TPU v7x, 32 devices: a whole 2x2x4 slice. The times are simulated.
32 devices in a mesh: fibre: 8 (over z, x), tm: 4 (over y, core).
Axes of the slice: x: 2, y: 2, z: 4, core: 2. Of those that a mesh axis runs over, the one named last changes fastest.
Arguments:
- record: bfloat16 [128, 131072], P('fibre', 'tm'), may hold values from -6 to 6
- offsets: int32 [128], P('tm'), may hold values from 0 to 1023
- src_idx: int32 [32], P('fibre'), may hold values from 0 to 127, as said below
Outputs:
- correlation: float32 [32, 128, 256], P('tm', 'fibre')
Inputs may be any that keep to these rules, and one draw needn't show every extreme that they name: `src_idx`: the 4 entries at positions b * 4 .. (b + 1) * 4 - 1 are distinct channels among b * 16 .. (b + 1) * 16 - 1.
All inputs are finite; a program needn't handle non-finite values.
Results may differ from a plain program's by a relative error of at most 0.012.
Values may be sent and summed in bfloat16 or wider, within the bound.
No kernel may reach another device: no remote copies, remote signals or barrier semaphores. Data moves between devices by JAX's collectives and lax.ppermute only.
A program may use at most 128 MiB of HBM per device.

v0:
```python
import math

import jax
import jax.numpy as jnp
from jax import lax
from jax.sharding import PartitionSpec as P

W = 2048
HOP = 1024
NB = 384
B0 = 20
SMOOTH = 64
LAGS = 256


def from_behind(shard, axis, by):
    peers = lax.axis_size(axis)
    pairs = [(i, i + by) for i in range(peers) if 0 <= i + by < peers]
    return lax.ppermute(shard, axis, pairs)


def forward_table():
    samples = jnp.arange(W, dtype=jnp.int32)
    freqs = B0 + jnp.arange(NB, dtype=jnp.int32)
    turns = (samples[:, None] * freqs[None, :] % W).astype(jnp.float32) * (2.0 * math.pi / W)
    taper = 0.5 - 0.5 * jnp.cos(samples.astype(jnp.float32) * (2.0 * math.pi / W))
    return jnp.concatenate(
        [taper[:, None] * jnp.cos(turns), -taper[:, None] * jnp.sin(turns)], axis=1
    ).astype(jnp.bfloat16)


def smoothing():
    rows = jnp.arange(NB, dtype=jnp.int32)[:, None]
    cols = jnp.arange(NB, dtype=jnp.int32)[None, :]
    first = jnp.clip(cols - SMOOTH // 2, 0, NB - SMOOTH)
    inside = (rows >= first) & (rows < first + SMOOTH)
    return jnp.where(inside, 1.0 / SMOOTH, 0.0).astype(jnp.float32)


def lag_table():
    freqs = B0 + jnp.arange(NB, dtype=jnp.int32)
    shifts = jnp.arange(LAGS, dtype=jnp.int32) - LAGS // 2
    turns = (freqs[:, None] * shifts[None, :] % W).astype(jnp.float32) * (2.0 * math.pi / W)
    return jnp.concatenate([jnp.cos(turns), -jnp.sin(turns)], axis=0).astype(jnp.bfloat16)


def whiten(spectra, smooth_mat):
    real = spectra[..., :NB]
    imag = spectra[..., NB:]
    power = real * real + imag * imag
    smoothed = jnp.dot(power.reshape(-1, NB), smooth_mat, precision=lax.Precision.HIGHEST).reshape(
        power.shape
    )
    factor = 1.0 / jnp.sqrt(smoothed + 1e-05)
    return jnp.concatenate([real * factor, imag * factor], axis=-1).astype(jnp.bfloat16)


def cross_parts(src_real, src_imag, rec_real, rec_imag):
    form = "swf,cwf->scf"
    real = jnp.einsum(form, src_real, rec_real, preferred_element_type=jnp.float32) + jnp.einsum(
        form, src_imag, rec_imag, preferred_element_type=jnp.float32
    )
    imag = jnp.einsum(form, src_real, rec_imag, preferred_element_type=jnp.float32) - jnp.einsum(
        form, src_imag, rec_real, preferred_element_type=jnp.float32
    )
    return (real, imag)


def body(record, offsets, src_idx):
    c_dev = record.shape[0]
    n_win = offsets.shape[0]
    n_tm = lax.axis_size("tm")
    factor = 1.0 / math.sqrt(n_win * n_tm * NB)
    lag_tab = lag_table()
    after = from_behind(record[:, :W], "tm", -1)
    padded = jnp.concatenate([record, after], axis=1)
    starts = jnp.arange(n_win, dtype=jnp.int32) * HOP + offsets

    def cut_window(first):
        return lax.dynamic_slice_in_dim(padded, first, W, 1)

    segments = jax.vmap(cut_window, out_axes=1)(starts)
    spectra = jnp.dot(
        segments.reshape(-1, W), forward_table(), preferred_element_type=jnp.float32
    ).reshape(c_dev, n_win, 2 * NB)
    whitened = whiten(spectra, smoothing())
    local = src_idx - lax.axis_index("fibre") * c_dev
    picker = (local[:, None] == jnp.arange(c_dev, dtype=jnp.int32)[None, :]).astype(jnp.bfloat16)
    own_sources = jnp.einsum(
        "sc,cwf->swf", picker, whitened, preferred_element_type=jnp.float32
    ).astype(jnp.bfloat16)
    piece = lax.all_gather(own_sources, "fibre", axis=0, tiled=True)
    real, imag = cross_parts(
        piece[..., :NB], piece[..., NB:], whitened[..., :NB], whitened[..., NB:]
    )
    cross = jnp.concatenate([real, imag], axis=-1).astype(jnp.bfloat16)
    lagged = (
        jnp.dot(cross.reshape(-1, 2 * NB), lag_tab, preferred_element_type=jnp.float32) * factor
    )
    partial_lags = lagged.reshape(piece.shape[0], c_dev, LAGS)
    summed = lax.psum(partial_lags.astype(jnp.bfloat16), "tm").astype(jnp.float32)
    share = summed.shape[0] // n_tm
    return lax.dynamic_slice_in_dim(summed, lax.axis_index("tm") * share, share, 0)


def solution(mesh):
    return jax.shard_map(
        body,
        mesh=mesh,
        in_specs=(P("fibre", "tm"), P("tm"), P("fibre")),
        out_specs=P("tm", "fibre", None),
        check_vma=False,
    )
```

profile of v0, /device:TPU:0, one launch (start us, length us, event | category | flops | bytes accessed | tf_op | source)
XLA Modules:
  0.0 221.1 jit_solution(6536390652008965608)
XLA Ops:
  10.2 14.4 %multiply_convert_fusion.1 = (bf16[2048,384]{1,0:T(8,128)(2,1)S(1)}, bf16[2048,384]{1,0:T(8,128)(2,1)}) fusion(s32[384]{0:T(512)S(1)} %iota_add_fusion, f32[2048]{0:T(1024)S(1)} %get-tuple-element.29, f32[2048]{0:T(1024)S(1)} %get-tuple-element.30), kind=kLoop, calls=%fused_computation.15 | loop fusion | flops 14155776 | bytes 3163648 | tf_op jit(solution)/shard_map/convert.10
  24.7 65.7 %while.1 = (s32[]{:T(128)}, bf16[16,34816]{1,0:T(8,128)(2,1)S(1)}, s32[32,2]{0,1:T(2,128)S(1)}, bf16[32,16,2048]{2,1,0:T(8,128)(2,1)}, s32[]{:T(128)}) while((s32[]{:T(128)}, bf16[16,34816]{1,0:T(8,128)(2,1)S(1)}, s32[32,2]{0,1:T(2,128)S(1)}, bf16[32,16,2048]{2,1,0:T(8,128)(2,1)}, s32[]{:T(128)}) %tuple.22), condition=%wide.while_cond, body=%wide.while_body.sunk | while | flops 2 | bytes 132185 | solution.py:80
  27.4 1.4 bitcast_dynamic-update-slice_fusion.2
  29.5 1.4 bitcast_dynamic-update-slice_fusion.2
  31.5 1.4 bitcast_dynamic-update-slice_fusion.2
  33.6 1.4 bitcast_dynamic-update-slice_fusion.2
  35.6 1.4 bitcast_dynamic-update-slice_fusion.2
  37.7 1.4 bitcast_dynamic-update-slice_fusion.2
  39.7 1.4 bitcast_dynamic-update-slice_fusion.2
  43.8 1.4 bitcast_dynamic-update-slice_fusion.2
  45.9 1.4 bitcast_dynamic-update-slice_fusion.2
  47.9 1.4 bitcast_dynamic-update-slice_fusion.2
  50.0 1.4 bitcast_dynamic-update-slice_fusion.2
  52.1 1.4 bitcast_dynamic-update-slice_fusion.2
  54.1 1.4 bitcast_dynamic-update-slice_fusion.2
  56.2 1.4 bitcast_dynamic-update-slice_fusion.2
  60.3 1.4 bitcast_dynamic-update-slice_fusion.2
  62.3 1.4 bitcast_dynamic-update-slice_fusion.2
  64.4 1.4 bitcast_dynamic-update-slice_fusion.2
  66.4 1.4 bitcast_dynamic-update-slice_fusion.2
  68.5 1.4 bitcast_dynamic-update-slice_fusion.2
  72.6 1.4 bitcast_dynamic-update-slice_fusion.2
  74.6 1.4 bitcast_dynamic-update-slice_fusion.2
  76.7 1.4 bitcast_dynamic-update-slice_fusion.2
  78.7 1.4 bitcast_dynamic-update-slice_fusion.2
  80.8 1.4 bitcast_dynamic-update-slice_fusion.2
  82.9 1.4 bitcast_dynamic-update-slice_fusion.2
  84.9 1.4 bitcast_dynamic-update-slice_fusion.2
  87.0 1.4 bitcast_dynamic-update-slice_fusion.2
  89.0 1.4 bitcast_dynamic-update-slice_fusion.2
  90.4 4.8 %fusion.3 = f32[16,32,768]{2,1,0:T(8,128)S(1)} fusion(bf16[2048,384]{1,0:T(8,128)(2,1)} %get-tuple-element.28, bf16[2048,384]{1,0:T(8,128)(2,1)S(1)} %get-tuple-element.27, bf16[16,32,2048]{2,0,1:T(8,128)(2,1)} %bitcast.39), kind=kOutput, calls=%fused_computation.9 | convolution fusion | flops 1616904192 | bytes 6815744 | tf_op jit(solution)/shard_map/dot_general | solution.py:83
  95.3 1.8 multiply_convert_fusion.3
  98.7 2.6 %cosine_convert_fusion = (bf16[384,256]{1,0:T(8,128)(2,1)}, bf16[384,256]{1,0:T(8,128)(2,1)}) fusion(s32[256]{0:T(256)S(1)} %iota_add_fusion.1, s32[384]{0:T(512)S(1)} %iota_add_fusion), kind=kLoop, calls=%fused_computation.57 | loop fusion | flops 1671168 | bytes 395776 | tf_op jit(solution)/shard_map/convert
  101.3 1.9 copy.30
  103.2 1.9 copy.32
  105.1 41.2 %all-gather.2.cloned.1.call-done = bf16[32,32,768]{2,1,0:T(8,128)(2,1)} async-done(((bf16[4,32,768]{2,1,0:T(8,128)(2,1)}), bf16[32,32,768]{2,1,0:T(8,128)(2,1)}) %all-gather.2.cloned.1.call-update) | async-done | bytes 1572880 | tf_op jit(solution)/shard_map/all_gather | solution.py:92
  146.3 2.5 %fusion.46 = (bf16[32,32,384]{2,1,0:T(8,128)(2,1)}, bf16[32,32,384]{2,1,0:T(8,128)(2,1)S(1)}) fusion(bf16[32,32,768]{2,1,0:T(8,128)(2,1)} %all-gather.2.cloned.1.call-done), kind=kLoop, calls=%fused_computation.79 | loop fusion | bytes 3145728 | tf_op jit(solution)/shard_map/slice | solution.py:94
  148.7 5.1 %copy.37 = bf16[32,32,384]{1,0,2:T(8,128)(2,1)} copy(bf16[32,32,384]{2,1,0:T(8,128)(2,1)S(1)} %get-tuple-element.24) | data formatting | bytes 1572864
  153.8 5.3 %copy.38 = bf16[32,32,384]{1,0,2:T(8,128)(2,1)S(1)} copy(bf16[32,32,384]{2,1,0:T(8,128)(2,1)} %get-tuple-element.23) | data formatting | bytes 1572864
  159.1 4.2 %fusion.47 = f32[384,16,32]{2,1,0:T(8,128)S(1)} fusion(bf16[16,32,384]{1,0,2:T(8,128)(2,1)} %copy.30, bf16[32,32,384]{1,0,2:T(8,128)(2,1)} %copy.37), kind=kOutput, calls=%fused_computation.80 | convolution fusion | flops 12582912 | bytes 1966080 | tf_op jit(solution)/shard_map/swf,cwf->scf/dot_general | solution.py:60
  163.3 3.4 %fusion.48 = f32[384,16,32]{2,1,0:T(8,128)} fusion(bf16[16,32,384]{1,0,2:T(8,128)(2,1)S(1)} %copy-done.1, bf16[32,32,384]{1,0,2:T(8,128)(2,1)S(1)} %copy-done), kind=kOutput, calls=%fused_computation.81 | convolution fusion | flops 12582912 | bytes 1966080 | tf_op jit(solution)/shard_map/swf,cwf->scf/dot_general | solution.py:63
  166.7 3.1 %fusion.10 = bf16[32,16,384]{0,1,2:T(8,128)(2,1)} fusion(f32[384,16,32]{2,1,0:T(8,128)S(1)} %fusion.47, bf16[16,32,384]{1,0,2:T(8,128)(2,1)S(1)} %copy-done.1, bf16[32,32,384]{1,0,2:T(8,128)(2,1)S(1)} %copy.38), kind=kOutput, calls=%fused_computation.20 | convolution fusion | flops 12976128 | bytes 2359296 | tf_op jit(solution)/shard_map/swf,cwf->scf/dot_general | solution.py:60
  169.8 2.3 %copy.33 = bf16[32,16,384]{2,1,0:T(8,128)(2,1)S(1)} copy(bf16[32,16,384]{0,1,2:T(8,128)(2,1)} %fusion.10) | data formatting | bytes 786432 | tf_op jit(solution)/shard_map/add | solution.py:60
  172.1 5.3 %fusion.11 = bf16[32,16,384]{0,1,2:T(8,128)(2,1)} fusion(f32[384,16,32]{2,1,0:T(8,128)} %fusion.48, bf16[16,32,384]{1,0,2:T(8,128)(2,1)} %copy.30, bf16[32,32,384]{1,0,2:T(8,128)(2,1)S(1)} %copy.38), kind=kOutput, calls=%fused_computation.21 | convolution fusion | flops 12976128 | bytes 2359296 | tf_op jit(solution)/shard_map/swf,cwf->scf/dot_general | solution.py:63
  177.4 2.3 %copy.36 = bf16[32,16,384]{2,1,0:T(8,128)(2,1)S(1)} copy(bf16[32,16,384]{0,1,2:T(8,128)(2,1)} %fusion.11) | data formatting | bytes 786432 | tf_op jit(solution)/shard_map/sub | solution.py:63
  179.7 2.1 fusion.13
  181.8 30.9 %all-reduce.3.cloned.1.call-done = bf16[32,16,256]{2,1,0:T(8,128)(2,1)} async-done(((bf16[32,16,256]{2,1,0:T(8,128)(2,1)}), bf16[32,16,256]{2,1,0:T(8,128)(2,1)}) %all-reduce.3.cloned.1.call-update) | async-done | bytes 262160 | tf_op jit(solution)/shard_map/psum | solution.py:101
  212.7 1.5 dynamic-slice_convert_fusion
  (93 shorter events, 31.9 us)
Async XLA Ops:
  6.5 139.7 %all-gather.2.cloned.1.call-start = ((), (), s32[]{:S(2)}) async-start(), calls=%async_computation | async-start | bytes 1769472 | tf_op jit(solution)/shard_map/all_gather | solution.py:92
  7.4 17.2 %collective-permute-start = (bf16[16,2048]{1,0:T(8,128)(2,1)S(1)}, bf16[16,2048]{1,0:T(8,128)(2,1)S(1)}, u32[]{:S(2)}, u32[]{:S(2)}) collective-permute-start(bf16[16,2048]{1,0:T(8,128)(2,1)S(1)} %slice.21), channel_id=1, source_target_pairs={{1,0},{2,1},{3,2},{5,4},{6,5},{7,6},{9,8},{10,9},{11,10},{13,12},{... | collective-permute-start | bytes 196616 | tf_op jit(solution)/shard_map/ppermute | solution.py:19
  9.4 15.2 %copy-start.2 = (bf16[16,32768]{1,0:T(8,128)(2,1)S(1)}, bf16[16,32768]{1,0:T(8,128)(2,1)}, u32[]{:S(2)}) copy-start(bf16[16,32768]{1,0:T(8,128)(2,1)} %param.3) | copy-start | bytes 3145732
  98.5 114.3 %all-reduce.3.cloned.1.call-start = ((), (), s32[]{:S(2)}) async-start(), calls=%async_computation.1 | async-start | bytes 524288 | tf_op jit(solution)/shard_map/psum | solution.py:101
  159.1 4.3 %copy-start = (bf16[32,32,384]{1,0,2:T(8,128)(2,1)S(1)}, bf16[32,32,384]{1,0,2:T(8,128)(2,1)}, u32[]{:S(2)}) copy-start(bf16[32,32,384]{1,0,2:T(8,128)(2,1)} %copy.37) | copy-start | bytes 2359300
  159.1 4.2 %copy-start.1 = (bf16[16,32,384]{1,0,2:T(8,128)(2,1)S(1)}, bf16[16,32,384]{1,0,2:T(8,128)(2,1)}, u32[]{:S(2)}) copy-start(bf16[16,32,384]{1,0,2:T(8,128)(2,1)} %copy.32) | copy-start | bytes 1179652
Sparse Core Ops, SparseCore 0:
  98.6 47.6 all-gather.1
  181.9 30.7 all-reduce.2
where the time goes:
time: 222 us; the launch traced here: 221 us
  local copies, waits for them, and re-layouts  88.4 us (40%)
  waiting for transfers between devices  72.2 us (33%)
  matrix products  25.3 us (11%)
  other arithmetic  20.1 us (9%)
  between operations  13.5 us (6%)
    gather x96, local copies, waits for them, and re-layouts  65.7 us
    all_gather x1, waiting for transfers between devices, body(): piece = lax.all_gather(own_sources, 'fibre', axis=0, tiled=True)  41.2 us
    psum x1, waiting for transfers between devices, body(): lax.psum(partial_lags.astype(jnp.bfloat16), 'tm').astype(jnp.float32)  30.9 us
    another operation x2, other arithmetic  17 us
    unnamed x8, local copies, waits for them, and re-layouts  10.4 us
    dot_general x1, matrix products, cross_parts(): jnp.einsum(form, src_imag, rec_real, preferred_element_type=jnp.float32)  5.29 us
    dot_general x1, matrix products, body(): jnp.dot(segments.reshape(-1, W), forward_table(), preferred_element_type=...  4.83 us
  transfers between devices with their start and end apart: 3, of which 2 were waited for; matrix products, arithmetic and copies ran while one was open for 10% of the time, Pallas kernels for 0%

commit v1 on v0

v1 whole, which is shorter than its diff:
```python
import functools
import math

import jax
import jax.numpy as jnp
import numpy as np
from jax import lax
from jax.experimental import pallas as pl
from jax.experimental.pallas import tpu as pltpu
from jax.sharding import PartitionSpec as P

W = 2048
HOP = 1024
NB = 384
B0 = 20
SMOOTH = 64
LAGS = 256
LANE = 128
CUT = W + LANE


def forward_table():
    samples = np.arange(W, dtype=np.int64)
    freqs = B0 + np.arange(NB, dtype=np.int64)
    turns = (samples[:, None] * freqs[None, :] % W) * (2.0 * math.pi / W)
    taper = 0.5 - 0.5 * np.cos(samples * (2.0 * math.pi / W))
    table = np.concatenate([taper[:, None] * np.cos(turns), -taper[:, None] * np.sin(turns)], axis=1)
    return table.astype(np.float32).astype(jnp.bfloat16)


def smoothing():
    rows = np.arange(NB)[:, None]
    cols = np.arange(NB)[None, :]
    first = np.clip(cols - SMOOTH // 2, 0, NB - SMOOTH)
    return np.where((rows >= first) & (rows < first + SMOOTH), 1.0 / SMOOTH, 0.0).astype(jnp.bfloat16)


def lag_table():
    freqs = B0 + np.arange(NB, dtype=np.int64)
    shifts = np.arange(LAGS, dtype=np.int64) - LAGS // 2
    turns = (freqs[:, None] * shifts[None, :] % W) * (2.0 * math.pi / W)
    table = np.concatenate([np.cos(turns), -np.sin(turns)], axis=0)
    return table.astype(np.float32).astype(jnp.bfloat16)


def spectra_kernel(first, count, tail_at, n_src, offs, local, *refs):
    if tail_at is None:
        rec, ftab, smooth, out_r, out_s, seg = refs
    else:
        rec, halo, ftab, smooth, out_r, out_s, seg, tail = refs
        body_len = rec.shape[1] - tail_at * HOP
        tail[:, :body_len] = rec[:, tail_at * HOP :]
        tail[:, body_len:] = halo[...]
    c_dev = rec.shape[0]
    lanes = lax.broadcasted_iota(jnp.int32, (c_dev, LANE), 1)

    def cut(source, base, slot):
        start = base + offs[first + slot]
        begin = pl.multiple_of(start // LANE * LANE, LANE)
        rest = start % LANE
        keep = lanes < LANE - rest
        shift = (LANE - rest) % LANE
        chunk = source[:, pl.ds(begin, CUT)].astype(jnp.float32)
        turned = [
            pltpu.roll(chunk[:, i * LANE : (i + 1) * LANE], shift, 1) for i in range(CUT // LANE)
        ]
        row = pl.multiple_of(slot * c_dev, c_dev)
        for i in range(W // LANE):
            seg[pl.ds(row, c_dev), i * LANE : (i + 1) * LANE] = jnp.where(
                keep, turned[i], turned[i + 1]
            ).astype(jnp.bfloat16)

    plain = count if tail_at is None else tail_at - first

    @pl.loop(0, plain)
    def _(slot):
        cut(rec, (first + slot) * HOP, slot)

    for slot in range(plain, count):
        cut(tail, (first + slot - tail_at) * HOP, slot)

    spectra = jnp.dot(seg[...], ftab[...], preferred_element_type=jnp.float32)
    real = spectra[:, :NB]
    imag = spectra[:, NB:]
    power = (real * real + imag * imag).astype(jnp.bfloat16)
    smoothed = jnp.dot(power, smooth[...], preferred_element_type=jnp.float32)
    factor = lax.rsqrt(smoothed + 1e-05)
    out_r[:, :NB] = (real * factor).astype(jnp.bfloat16)
    out_r[:, NB:] = (imag * factor).astype(jnp.bfloat16)
    rows = lax.broadcasted_iota(jnp.int32, (n_src * count, count * c_dev), 0)
    cols = lax.broadcasted_iota(jnp.int32, (n_src * count, count * c_dev), 1)
    wanted = jnp.zeros_like(rows)
    for s in range(n_src):
        wanted = jnp.where(rows // count == s, local[s] + (rows % count) * c_dev, wanted)
    picker = jnp.where(cols == wanted, 1.0, 0.0).astype(jnp.bfloat16)
    out_s[...] = jnp.dot(picker, out_r[...], preferred_element_type=jnp.float32).astype(jnp.bfloat16)


def spectra_call(record, halo, offsets, local, ftab, smooth, first, count):
    c_dev = record.shape[0]
    n_src = local.shape[0]
    n_win = offsets.shape[0]
    tail_at = None if halo is None else n_win - 2
    vmem = pl.BlockSpec(memory_space=pltpu.VMEM)
    smem = pl.BlockSpec(memory_space=pltpu.SMEM)
    arrays = [record] + ([] if halo is None else [halo]) + [ftab, smooth]
    scratch = [pltpu.VMEM((count * c_dev, W), jnp.bfloat16)]
    if halo is not None:
        scratch.append(pltpu.VMEM((c_dev, 2 * HOP + W), jnp.bfloat16))
    return pl.pallas_call(
        functools.partial(spectra_kernel, first, count, tail_at, n_src),
        out_shape=(
            jax.ShapeDtypeStruct((count * c_dev, 2 * NB), jnp.bfloat16),
            jax.ShapeDtypeStruct((n_src * count, 2 * NB), jnp.bfloat16),
        ),
        in_specs=[smem, smem] + [vmem] * len(arrays),
        out_specs=(vmem, vmem),
        scratch_shapes=scratch,
        compiler_params=pltpu.CompilerParams(vmem_limit_bytes=48 << 20),
        cost_estimate=pl.CostEstimate(
            flops=2 * count * c_dev * W * 2 * NB, bytes_accessed=6 << 20, transcendentals=0
        ),
        name="spectra",
    )(offsets, local, *arrays)


def cross_kernel(n_list, n_rec, n_src, count, c_dev, final, scale, *refs):
    srcs, refs = refs[:n_list], refs[n_list:]
    recs, refs = refs[:n_rec], refs[n_rec:]
    if final:
        before, ltab, out, wide, cross = refs
    else:
        out, wide = refs
    for k in range(n_list):
        wide[k * n_src * count : (k + 1) * n_src * count, :] = srcs[k][0].astype(jnp.float32)
    block = 8 if n_list * n_src % 8 == 0 else n_src
    tiles = NB // LANE

    @pl.loop(0, n_list * n_src // block * tiles)
    def _(step):
        at = step // tiles * block
        lo = pl.ds(pl.multiple_of(step % tiles * LANE, LANE), LANE)
        hi = pl.ds(pl.multiple_of(step % tiles * LANE + NB, LANE), LANE)
        src_row = pl.multiple_of(at * count, block * count)
        src = wide.at[pl.ds(src_row, block * count)]
        for q in range(n_rec):
            rows = [
                pl.ds(pl.multiple_of(((at + s) * n_rec + q) * c_dev, c_dev), c_dev) for s in range(block)
            ]
            sums = []
            for s in range(block):
                if final:
                    sums.append([before[rows[s], lo], before[rows[s], hi]])
                else:
                    sums.append([0.0, 0.0])
            for w in range(count):
                row = slice(w * c_dev, (w + 1) * c_dev)
                rec_real = recs[q][row, lo].astype(jnp.float32)
                rec_imag = recs[q][row, hi].astype(jnp.float32)
                for s in range(block):
                    src_real = src[s * count + w : s * count + w + 1, lo]
                    src_imag = src[s * count + w : s * count + w + 1, hi]
                    sums[s][0] += src_real * rec_real + src_imag * rec_imag
                    sums[s][1] += src_real * rec_imag - src_imag * rec_real
            for s in range(block):
                if final:
                    cross[rows[s], lo] = sums[s][0].astype(jnp.bfloat16)
                    cross[rows[s], hi] = sums[s][1].astype(jnp.bfloat16)
                else:
                    out[rows[s], lo] = sums[s][0]
                    out[rows[s], hi] = sums[s][1]

    if final:
        lagged = jnp.dot(cross[...], ltab[...], preferred_element_type=jnp.float32)
        out[...] = (lagged * scale).astype(jnp.bfloat16)


def cross_call(srcs, recs, before, ltab, n_src, count, c_dev, scale):
    n_list, n_rec = len(srcs), len(recs)
    groups = srcs[0].shape[0]
    final = before is not None
    rows = n_list * n_src * n_rec * c_dev
    whole = pl.BlockSpec(memory_space=pltpu.VMEM)
    src_spec = pl.BlockSpec((1,) + srcs[0].shape[1:], lambda g: (g, 0, 0))
    scratch = [pltpu.VMEM((n_list * n_src * count, 2 * NB), jnp.float32)]
    if final:
        scratch.append(pltpu.VMEM((rows, 2 * NB), jnp.bfloat16))
        out_shape = jax.ShapeDtypeStruct((groups * rows, LAGS), jnp.bfloat16)
    else:
        out_shape = jax.ShapeDtypeStruct((groups * rows, 2 * NB), jnp.float32)
    row_block = lambda width: pl.BlockSpec((rows, width), lambda g: (g, 0))
    return pl.pallas_call(
        functools.partial(cross_kernel, n_list, n_rec, n_src, count, c_dev, final, scale),
        grid=(groups,),
        out_shape=out_shape,
        in_specs=[src_spec] * n_list + [whole] * n_rec + ([row_block(2 * NB), whole] if final else []),
        out_specs=row_block(out_shape.shape[1]),
        scratch_shapes=scratch,
        compiler_params=pltpu.CompilerParams(vmem_limit_bytes=48 << 20),
        cost_estimate=pl.CostEstimate(
            flops=groups * rows * count * NB * 40, bytes_accessed=4 << 20, transcendentals=0
        ),
        name="cross",
    )(*srcs, *recs, *([before, ltab] if final else []))


def body(record, offsets, src_idx):
    c_dev = record.shape[0]
    n_win = offsets.shape[0]
    n_src = src_idx.shape[0]
    n_tm = lax.axis_size("tm")
    n_fibre = lax.axis_size("fibre")
    n_group = n_fibre // 2
    fibre = lax.axis_index("fibre")
    tm = lax.axis_index("tm")
    half = n_win // 2
    scale = 1.0 / math.sqrt(n_win * n_tm * NB)
    ftab = jnp.asarray(forward_table())
    smooth = jnp.asarray(smoothing())
    ltab = jnp.asarray(lag_table())
    swap = [(i, i ^ 1) for i in range(n_fibre)]
    direct = n_group == 4 and n_tm == 4

    halo = lax.ppermute(record[:, :W], "tm", [(i, i - 1) for i in range(1, n_tm)])
    local = src_idx - fibre * c_dev
    parts = []
    for first, edge in ((0, None), (half, halo)):
        rec, src = spectra_call(record, edge, offsets, local, ftab, smooth, first, half)
        other = lax.ppermute(rec, "fibre", swap)
        if direct:
            srcs = [src[None]] + [
                lax.ppermute(src, "fibre", [(i, i ^ (2 * k)) for i in range(n_fibre)])[None]
                for k in range(1, n_group)
            ]
        else:
            ranks = [[2 * j + p for j in range(n_group)] for p in range(2)]
            srcs = [lax.all_gather(src, "fibre", axis=0, axis_index_groups=ranks)]
        parts.append((srcs, [rec, other]))
    before = cross_call(*parts[0], None, None, n_src, half, c_dev, scale)
    lagged = cross_call(*parts[1], before, ltab, n_src, half, c_dev, scale)
    lagged = lagged.reshape(n_group, n_src, 2, c_dev, LAGS)

    def piece(owner, side):
        if direct:
            return lax.dynamic_index_in_dim(lagged[:, :, side], (fibre // 2) ^ owner, 0, keepdims=True)
        share = n_group // n_tm
        return lax.dynamic_slice_in_dim(lagged[:, :, side], owner * share, share, 0)

    totals = []
    for side in range(2):
        total = None
        for k in range(n_tm):
            mine = piece(tm ^ k, side)
            if side or k:
                pairs = [
                    (i * n_tm + t, (i ^ side) * n_tm + (t ^ k)) for i in range(n_fibre) for t in range(n_tm)
                ]
                mine = lax.ppermute(mine, ("fibre", "tm"), pairs)
            mine = mine.astype(jnp.float32)
            total = mine if total is None else total + mine
        totals.append(total)
    even = fibre % 2 == 0
    near, far = totals
    out = jnp.stack([jnp.where(even, near, far), jnp.where(even, far, near)], axis=1)
    return out.reshape(-1, c_dev, LAGS)


def solution(mesh):
    return jax.shard_map(
        body,
        mesh=mesh,
        in_specs=(P("fibre", "tm"), P("tm"), P("fibre")),
        out_specs=P("tm", "fibre", None),
        check_vma=False,
    )
```

time: 222 us -> 56 us (0.25)
  local copies, waits for them, and re-layouts: 88.4 us -> 5.63 us
  waiting for transfers between devices: 72.2 us -> 13.4 us
  matrix products: 25.3 us -> 0 us
  other arithmetic: 20.1 us -> 1.36 us
  starting transfers between devices: 1.5 us -> 20 us
  Pallas kernels: 0 us -> 15.2 us
  between operations: 13.5 us -> 0.12 us
    gather x96 -> x0, local copies, waits for them, and re-layouts: 65.7 us -> none
    all_gather x1 -> x0, waiting for transfers between devices: 41.2 us -> none  [body(): piece = lax.all_gather(own_sources, 'fibre', axis=0, tiled=True)]
    psum x1 -> x0, waiting for transfers between devices: 30.9 us -> none  [body(): lax.psum(partial_lags.astype(jnp.bfloat16), 'tm').astype(jnp.float32)]
    dot_general x8 -> x0, matrix products: 25.3 us -> none  [the longest x1 5.29 us: cross_parts(): jnp.einsum(form, src_imag, rec_real, preferred_element_type=jnp.float32)]
    ppermute x1 -> x16, starting transfers between devices: 1.28 us -> 20 us  [the longest x6 9.13 us: body(): lax.ppermute(src, 'fibre', [(i, i ^ 2 * k) for i in range(n_fibre)])[None]]
    another operation x2, other arithmetic: 17 us -> 0.7 us  [body(): jnp.stack([jnp.where(even, near, far), jnp.where(even, far, near)], axis=1)]
    pallas_call x0 -> x4, Pallas kernels: none -> 15.2 us  [the longest x2 7.71 us: cross_call(): pl.pallas_call(functools.partial(cross_kernel, n_list, n_rec, n_src, coun...]
    ppermute x1 -> x16, waiting for transfers between devices: 0.01 us -> 13.4 us  [the longest x6 8.76 us: body(): lax.ppermute(src, 'fibre', [(i, i ^ 2 * k) for i in range(n_fibre)])[None]]
  transfers between devices with their start and end apart: 3 -> 16, of which waited for: 2 -> 7; matrix products, arithmetic and copies ran while one was open for 10% -> 1% of each run, Pallas kernels for 0% -> 20%
where the time goes in v1:
time: 56 us; the launch traced here: 55.7 us
  starting transfers between devices  20 us (36%)
  Pallas kernels  15.2 us (27%)
  waiting for transfers between devices  13.4 us (24%)
  local copies, waits for them, and re-layouts  5.63 us (10%)
  other arithmetic  1.36 us (2%)
    ppermute x6, starting transfers between devices, body(): lax.ppermute(src, 'fibre', [(i, i ^ 2 * k) for i in range(n_fibre)])[None]  9.13 us
    ppermute x6, waiting for transfers between devices, body(): lax.ppermute(src, 'fibre', [(i, i ^ 2 * k) for i in range(n_fibre)])[None]  8.76 us
    pallas_call x2, Pallas kernels, cross_call(): pl.pallas_call(functools.partial(cross_kernel, n_list, n_rec, n_src, coun...  7.71 us
    pallas_call x2, Pallas kernels, spectra_call(): pl.pallas_call(functools.partial(spectra_kernel, first, count, tail_at, n...  7.54 us
    ppermute x7, starting transfers between devices, body(): mine = lax.ppermute(mine, ('fibre', 'tm'), pairs)  6.52 us
    unnamed x12, local copies, waits for them, and re-layouts  4.74 us
    ppermute x7, waiting for transfers between devices, body(): mine = lax.ppermute(mine, ('fibre', 'tm'), pairs)  4.59 us
    ppermute x2, starting transfers between devices, body(): other = lax.ppermute(rec, 'fibre', swap)  3.1 us
  transfers between devices with their start and end apart: 16, of which 7 were waited for; matrix products, arithmetic and copies ran while one was open for 1% of the time, Pallas kernels for 20%

profile of v1, /device:TPU:0, one launch (start us, length us, event | category | flops | bytes accessed | tf_op | source)
XLA Modules:
  0.0 55.7 jit_solution(3836474575092602891)
XLA Ops:
  0.0 0.8 %slice.6 = bf16[16,2048]{1,0:T(8,128)(2,1)S(1)} slice(bf16[16,32768]{1,0:T(8,128)(2,1)} %refs_0_.3), slice={[0:16], [0:2048]} | slice | bytes 131072 | tf_op jit(solution)/shard_map/slice | solution.py:224
  0.8 1.3 %collective-permute-start = (bf16[16,2048]{1,0:T(8,128)(2,1)S(1)}, bf16[16,2048]{1,0:T(8,128)(2,1)S(1)}, u32[]{:S(2)}, u32[]{:S(2)}) collective-permute-start(bf16[16,2048]{1,0:T(8,128)(2,1)S(1)} %slice.6), channel_id=1, source_target_pairs={{1,0},{2,1},{3,2},{5,4},{6,5},{7,6},{9,8},{10,9},{11,10},{13,12},{... | collective-permute-start | bytes 196616 | tf_op jit(solution)/shard_map/ppermute | solution.py:224
  2.1 0.7 %broadcast_subtract_fusion.local = s32[4]{0:T(128)S(1)} fusion(s32[4]{0:T(128)} %param.8, s32[]{:T(128)S(6)} %mul.3), kind=kLoop, calls=%fused_computation.14 | loop fusion | flops 4 | bytes 36 | tf_op jit(solution)/shard_map/sub | solution.py:225
  2.8 0.0 copy-start
  2.8 1.9 %copy-done = bf16[2048,768]{1,0:T(8,128)(2,1)S(1)} copy-done((bf16[2048,768]{1,0:T(8,128)(2,1)S(1)}, bf16[2048,768]{1,0:T(8,128)(2,1)}, u32[]{:S(2)}) %copy-start) | copy-done | bytes 3145752
  4.7 0.0 copy-start.2
  4.7 1.2 %copy-done.2 = bf16[16,32768]{1,0:T(8,128)(2,1)S(1)} copy-done((bf16[16,32768]{1,0:T(8,128)(2,1)S(1)}, bf16[16,32768]{1,0:T(8,128)(2,1)}, u32[]{:S(2)}) %copy-start.2) | copy-done | bytes 1048600
  5.9 1.0 %copy-done.3 = bf16[384,384]{1,0:T(8,128)(2,1)S(1)} copy-done((bf16[384,384]{1,0:T(8,128)(2,1)S(1)}, bf16[384,384]{1,0:T(8,128)(2,1)}, u32[]{:S(2)}) %copy-start.3) | copy-done | bytes 294936
  6.9 0.7 %copy-done.5 = s32[32]{0:T(128)S(1)} copy-done((s32[32]{0:T(128)S(1)}, s32[32]{0:T(128)}, u32[]{:S(2)}) %copy-start.5) | copy-done | bytes 152
  7.5 3.8 %spectra.3 = (bf16[256,768]{1,0:T(8,128)(2,1)S(1)}, bf16[64,768]{1,0:T(8,128)(2,1)S(1)}) custom-call(s32[32]{0:T(128)S(1)} %copy-done.5, s32[4]{0:T(128)S(1)} %broadcast_subtract_fusion.local, bf16[16,32768]{1,0:T(8,128)(2,1)S(1)} %copy-done.2, bf16[2048,768]{1,0:T(8,128)(2,1)S(1)} %copy-done, bf16[384,384]{1,0:T(8,128)(2,1)S(1)} %copy-done.3), custom_call_target="tpu_custom_call" | custom-call | flops 805306368 | bytes 6291456 | tf_op jit(solution)/shard_map/spectra/pallas_call | solution.py:110
  11.4 0.0 copy-start.4
  11.4 3.0 %collective-permute-start.8 = (bf16[256,768]{1,0:T(8,128)(2,1)S(1)}, bf16[256,768]{1,0:T(8,128)(2,1)S(1)}, u32[]{:S(2)}, u32[]{:S(2)}) collective-permute-start(bf16[256,768]{1,0:T(8,128)(2,1)S(1)} %get-tuple-element.12.refs_4_), channel_id=1, source_target_pairs={{0,4},{4,0},{8,12},{12,8},{16,20},{20,16},{24,28},{28,24},{1,5},{5... | collective-permute-start | bytes 1179656 | tf_op jit(solution)/shard_map/ppermute | solution.py:229
  14.4 0.0 collective-permute-done.refs_1_
  14.4 0.0 copy-done.1
  14.4 3.7 %spectra.2 = (bf16[256,768]{1,0:T(8,128)(2,1)S(1)}, bf16[64,768]{1,0:T(8,128)(2,1)S(1)}) custom-call(s32[32]{0:T(128)S(1)} %copy-done.5, s32[4]{0:T(128)S(1)} %broadcast_subtract_fusion.local, bf16[16,32768]{1,0:T(8,128)(2,1)S(1)} %copy-done.2, bf16[16,2048]{1,0:T(8,128)(2,1)S(1)} %collective-permute-done.refs_1_, bf16[2048,768]{1,0:T(8,128)(2,1)S(1)} %copy-done.1, ...), custom_call_target="tpu_custom_call" | custom-call | flops 805306368 | bytes 6291456 | tf_op jit(solution)/shard_map/spectra/pallas_call | solution.py:110
  18.1 0.1 collective-permute-start.4
  18.2 2.1 %collective-permute-start.5 = (bf16[64,768]{1,0:T(8,128)(2,1)S(1)}, bf16[64,768]{1,0:T(8,128)(2,1)S(1)}, u32[]{:S(2)}, u32[]{:S(2)}) collective-permute-start(bf16[64,768]{1,0:T(8,128)(2,1)S(1)} %get-tuple-element.11), channel_id=1, source_target_pairs={{0,8},{4,12},{8,0},{12,4},{16,24},{20,28},{24,16},{28,20},{1,9},{5... | collective-permute-start | bytes 294920 | tf_op jit(solution)/shard_map/ppermute | solution.py:232
  20.3 2.6 %collective-permute-start.6 = (bf16[64,768]{1,0:T(8,128)(2,1)S(1)}, bf16[64,768]{1,0:T(8,128)(2,1)S(1)}, u32[]{:S(2)}, u32[]{:S(2)}) collective-permute-start(bf16[64,768]{1,0:T(8,128)(2,1)S(1)} %get-tuple-element.11), channel_id=1, source_target_pairs={{0,16},{4,20},{8,24},{12,28},{16,0},{20,4},{24,8},{28,12},{1,17},{... | collective-permute-start | bytes 294920 | tf_op jit(solution)/shard_map/ppermute | solution.py:232
  22.9 0.0 collective-permute-start.7
  22.9 0.9 %collective-permute-done.5 = bf16[64,768]{1,0:T(8,128)(2,1)S(1)} collective-permute-done((bf16[64,768]{1,0:T(8,128)(2,1)S(1)}, bf16[64,768]{1,0:T(8,128)(2,1)S(1)}, u32[]{:S(2)}, u32[]{:S(2)}) %collective-permute-start.5) | collective-permute-done | bytes 98336 | tf_op jit(solution)/shard_map/ppermute | solution.py:232
  23.8 1.7 %collective-permute-start.1 = (bf16[64,768]{1,0:T(8,128)(2,1)S(1)}, bf16[64,768]{1,0:T(8,128)(2,1)S(1)}, u32[]{:S(2)}, u32[]{:S(2)}) collective-permute-start(bf16[64,768]{1,0:T(8,128)(2,1)S(1)} %get-tuple-element.9), channel_id=1, source_target_pairs={{0,8},{4,12},{8,0},{12,4},{16,24},{20,28},{24,16},{28,20},{1,9},{5... | collective-permute-start | bytes 294920 | tf_op jit(solution)/shard_map/ppermute | solution.py:232
  25.6 5.5 %collective-permute-done.6 = bf16[64,768]{1,0:T(8,128)(2,1)S(1)} collective-permute-done((bf16[64,768]{1,0:T(8,128)(2,1)S(1)}, bf16[64,768]{1,0:T(8,128)(2,1)S(1)}, u32[]{:S(2)}, u32[]{:S(2)}) %collective-permute-start.6) | collective-permute-done | bytes 98336 | tf_op jit(solution)/shard_map/ppermute | solution.py:232
  31.1 0.0 collective-permute-start.2
  31.1 0.0 collective-permute-done.7
  31.1 2.7 %collective-permute-start.3 = (bf16[64,768]{1,0:T(8,128)(2,1)S(1)}, bf16[64,768]{1,0:T(8,128)(2,1)S(1)}, u32[]{:S(2)}, u32[]{:S(2)}) collective-permute-start(bf16[64,768]{1,0:T(8,128)(2,1)S(1)} %get-tuple-element.9), channel_id=1, source_target_pairs={{0,24},{4,28},{8,16},{12,20},{16,8},{20,12},{24,0},{28,4},{1,25},{... | collective-permute-start | bytes 294920 | tf_op jit(solution)/shard_map/ppermute | solution.py:232
  33.8 0.0 collective-permute-done.8.refs_5_
  33.8 3.7 %cross.2.refs_6_ = f32[512,768]{1,0:T(8,128)S(1)} custom-call(bf16[1,64,768]{2,1,0:T(8,128)(2,1)S(1)} %bitcast.36, bf16[1,64,768]{2,1,0:T(8,128)(2,1)S(1)} %bitcast.37, bf16[1,64,768]{2,1,0:T(8,128)(2,1)S(1)} %bitcast.38, bf16[1,64,768]{2,1,0:T(8,128)(2,1)S(1)} %bitcast.39, bf16[256,768]{1,0:T(8,128)(2,1)S(1)} %get-tuple-element.12.refs_4_, ...), custom_call_target="tpu_custom_call" | custom-call | flops 125829120 | bytes 4194304 | tf_op jit(solution)/shard_map/cross/pallas_call | solution.py:192
  37.5 0.0 collective-permute-done.1
  37.5 2.3 %collective-permute-done.2 = bf16[64,768]{1,0:T(8,128)(2,1)S(1)} collective-permute-done((bf16[64,768]{1,0:T(8,128)(2,1)S(1)}, bf16[64,768]{1,0:T(8,128)(2,1)S(1)}, u32[]{:S(2)}, u32[]{:S(2)}) %collective-permute-start.2) | collective-permute-done | bytes 98336 | tf_op jit(solution)/shard_map/ppermute | solution.py:232
  39.8 0.0 collective-permute-done.3
  39.8 0.0 collective-permute-done.4.refs_5_
  39.8 0.0 copy-done.4
  39.8 4.0 %cross.3 = bf16[512,256]{1,0:T(8,128)(2,1)S(1)} custom-call(bf16[1,64,768]{2,1,0:T(8,128)(2,1)S(1)} %bitcast.40, bf16[1,64,768]{2,1,0:T(8,128)(2,1)S(1)} %bitcast.41, bf16[1,64,768]{2,1,0:T(8,128)(2,1)S(1)} %bitcast.42, bf16[1,64,768]{2,1,0:T(8,128)(2,1)S(1)} %bitcast.43, bf16[256,768]{1,0:T(8,128)(2,1)S(1)} %get-tuple-element.10.refs_4_, ...), custom_call_target="tpu_custom_call" | custom-call | flops 125829120 | bytes 4194304 | tf_op jit(solution)/shard_map/cross/pallas_call | solution.py:192
  43.9 1.7 %collective-permute-start.10 = (bf16[1,4,16,256]{3,2,1,0:T(8,128)(2,1)S(1)}, bf16[1,4,16,256]{3,2,1,0:T(8,128)(2,1)S(1)}, u32[]{:S(2)}, u32[]{:S(2)}) collective-permute-start(bf16[1,4,16,256]{3,2,1,0:T(8,128)(2,1)S(1)} %get-tuple-element.19), channel_id=1, source_target_pairs={{0,2},{1,3},{2,0},{3,1},{4,6},{5,7},{6,4},{7,5},{8,10},{9,11},{10,... | collective-permute-start | bytes 98312 | tf_op jit(solution)/shard_map/ppermute | solution.py:258
  45.6 0.0 collective-permute-start.11
  45.6 0.5 collective-permute-start.9
  46.1 1.6 %collective-permute-start.12 = (bf16[1,4,16,256]{3,2,1,0:T(8,128)(2,1)S(1)}, bf16[1,4,16,256]{3,2,1,0:T(8,128)(2,1)S(1)}, u32[]{:S(2)}, u32[]{:S(2)}) collective-permute-start(bf16[1,4,16,256]{3,2,1,0:T(8,128)(2,1)S(1)} %get-tuple-element.20), channel_id=1, source_target_pairs={{0,4},{1,5},{2,6},{3,7},{4,0},{5,1},{6,2},{7,3},{8,12},{9,13},{10,... | collective-permute-start | bytes 98312 | tf_op jit(solution)/shard_map/ppermute | solution.py:258
  47.7 0.0 collective-permute-start.13
  47.7 0.2 collective-permute-done.10
  47.9 2.7 %collective-permute-start.14 = (bf16[1,4,16,256]{3,2,1,0:T(8,128)(2,1)S(1)}, bf16[1,4,16,256]{3,2,1,0:T(8,128)(2,1)S(1)}, u32[]{:S(2)}, u32[]{:S(2)}) collective-permute-start(bf16[1,4,16,256]{3,2,1,0:T(8,128)(2,1)S(1)} %get-tuple-element.22), channel_id=1, source_target_pairs={{0,6},{1,7},{2,4},{3,5},{4,2},{5,3},{6,0},{7,1},{8,14},{9,15},{10,... | collective-permute-start | bytes 98312 | tf_op jit(solution)/shard_map/ppermute | solution.py:258
  50.6 0.0 collective-permute-done.11
  50.6 0.0 collective-permute-start.15
  50.6 0.0 collective-permute-done.9
  50.6 0.0 collective-permute-done.12
  50.7 0.6 %collective-permute-done.13 = bf16[1,4,16,256]{3,2,1,0:T(8,128)(2,1)S(1)} collective-permute-done((bf16[1,4,16,256]{3,2,1,0:T(8,128)(2,1)S(1)}, bf16[1,4,16,256]{3,2,1,0:T(8,128)(2,1)S(1)}, u32[]{:S(2)}, u32[]{:S(2)}) %collective-permute-start.13) | collective-permute-done | bytes 32800 | tf_op jit(solution)/shard_map/ppermute | solution.py:258
  51.3 1.7 %collective-permute-done.14 = bf16[1,4,16,256]{3,2,1,0:T(8,128)(2,1)S(1)} collective-permute-done((bf16[1,4,16,256]{3,2,1,0:T(8,128)(2,1)S(1)}, bf16[1,4,16,256]{3,2,1,0:T(8,128)(2,1)S(1)}, u32[]{:S(2)}, u32[]{:S(2)}) %collective-permute-start.14) | collective-permute-done | bytes 32800 | tf_op jit(solution)/shard_map/ppermute | solution.py:258
  53.0 2.0 %collective-permute-done.15 = bf16[1,4,16,256]{3,2,1,0:T(8,128)(2,1)S(1)} collective-permute-done((bf16[1,4,16,256]{3,2,1,0:T(8,128)(2,1)S(1)}, bf16[1,4,16,256]{3,2,1,0:T(8,128)(2,1)S(1)}, u32[]{:S(2)}, u32[]{:S(2)}) %collective-permute-start.15) | collective-permute-done | bytes 32800 | tf_op jit(solution)/shard_map/ppermute | solution.py:258
  55.1 0.7 %pad_maximum_fusion = f32[1,2,4,16,256]{4,3,2,1,0:T(8,128)} fusion(f32[1,1,4,16,256]{4,3,2,1,0:T(8,128)S(1)} %get-tuple-element.14, f32[1,1,4,16,256]{4,3,2,1,0:T(8,128)S(1)} %get-tuple-element.13), kind=kLoop, calls=%fused_computation | loop fusion | flops 32768 | bytes 262144 | tf_op jit(solution)/shard_map/stack | solution.py:264
  (7 shorter events, 0.1 us)
Async XLA Ops:
  0.8 13.6 %collective-permute-start = (bf16[16,2048]{1,0:T(8,128)(2,1)S(1)}, bf16[16,2048]{1,0:T(8,128)(2,1)S(1)}, u32[]{:S(2)}, u32[]{:S(2)}) collective-permute-start(bf16[16,2048]{1,0:T(8,128)(2,1)S(1)} %slice.6), channel_id=1, source_target_pairs={{1,0},{2,1},{3,2},{5,4},{6,5},{7,6},{9,8},{10,9},{11,10},{13,12},{... | collective-permute-start | bytes 196616 | tf_op jit(solution)/shard_map/ppermute | solution.py:224
  2.8 1.9 %copy-start = (bf16[2048,768]{1,0:T(8,128)(2,1)S(1)}, bf16[2048,768]{1,0:T(8,128)(2,1)}, u32[]{:S(2)}) copy-start(bf16[2048,768]{1,0:T(8,128)(2,1)} %constant.86.clone.refs_2_.refs_1_) | copy-start | bytes 9437188
  4.7 1.2 %copy-start.2 = (bf16[16,32768]{1,0:T(8,128)(2,1)S(1)}, bf16[16,32768]{1,0:T(8,128)(2,1)}, u32[]{:S(2)}) copy-start(bf16[16,32768]{1,0:T(8,128)(2,1)} %refs_0_.3) | copy-start | bytes 3145732
  5.9 1.0 %copy-start.3 = (bf16[384,384]{1,0:T(8,128)(2,1)S(1)}, bf16[384,384]{1,0:T(8,128)(2,1)}, u32[]{:S(2)}) copy-start(bf16[384,384]{1,0:T(8,128)(2,1)} %constant.87.clone.refs_3_.refs_2_) | copy-start | bytes 884740
  6.9 0.7 %copy-start.5 = (s32[32]{0:T(128)S(1)}, s32[32]{0:T(128)}, u32[]{:S(2)}) copy-start(s32[32]{0:T(128)} %offs.3) | copy-start | bytes 388
  7.5 6.9 %copy-start.1 = (bf16[2048,768]{1,0:T(8,128)(2,1)S(1)}, bf16[2048,768]{1,0:T(8,128)(2,1)}, u32[]{:S(2)}) copy-start(bf16[2048,768]{1,0:T(8,128)(2,1)} %constant.86.clone.refs_2_.refs_1_) | copy-start | bytes 9437188
  11.4 28.4 %copy-start.4 = (bf16[768,256]{1,0:T(8,128)(2,1)S(1)}, bf16[768,256]{1,0:T(8,128)(2,1)}, u32[]{:S(2)}) copy-start(bf16[768,256]{1,0:T(8,128)(2,1)} %constant.88.clone.refs_7_) | copy-start | bytes 1179652
  11.4 22.4 %collective-permute-start.8 = (bf16[256,768]{1,0:T(8,128)(2,1)S(1)}, bf16[256,768]{1,0:T(8,128)(2,1)S(1)}, u32[]{:S(2)}, u32[]{:S(2)}) collective-permute-start(bf16[256,768]{1,0:T(8,128)(2,1)S(1)} %get-tuple-element.12.refs_4_), channel_id=1, source_target_pairs={{0,4},{4,0},{8,12},{12,8},{16,20},{20,16},{24,28},{28,24},{1,5},{5... | collective-permute-start | bytes 1179656 | tf_op jit(solution)/shard_map/ppermute | solution.py:229
  18.1 21.7 %collective-permute-start.4 = (bf16[256,768]{1,0:T(8,128)(2,1)S(1)}, bf16[256,768]{1,0:T(8,128)(2,1)S(1)}, u32[]{:S(2)}, u32[]{:S(2)}) collective-permute-start(bf16[256,768]{1,0:T(8,128)(2,1)S(1)} %get-tuple-element.10.refs_4_), channel_id=1, source_target_pairs={{0,4},{4,0},{8,12},{12,8},{16,20},{20,16},{24,28},{28,24},{1,5},{5... | collective-permute-start | bytes 1179656 | tf_op jit(solution)/shard_map/ppermute | solution.py:229
  18.2 5.6 %collective-permute-start.5 = (bf16[64,768]{1,0:T(8,128)(2,1)S(1)}, bf16[64,768]{1,0:T(8,128)(2,1)S(1)}, u32[]{:S(2)}, u32[]{:S(2)}) collective-permute-start(bf16[64,768]{1,0:T(8,128)(2,1)S(1)} %get-tuple-element.11), channel_id=1, source_target_pairs={{0,8},{4,12},{8,0},{12,4},{16,24},{20,28},{24,16},{28,20},{1,9},{5... | collective-permute-start | bytes 294920 | tf_op jit(solution)/shard_map/ppermute | solution.py:232
  20.3 10.8 %collective-permute-start.6 = (bf16[64,768]{1,0:T(8,128)(2,1)S(1)}, bf16[64,768]{1,0:T(8,128)(2,1)S(1)}, u32[]{:S(2)}, u32[]{:S(2)}) collective-permute-start(bf16[64,768]{1,0:T(8,128)(2,1)S(1)} %get-tuple-element.11), channel_id=1, source_target_pairs={{0,16},{4,20},{8,24},{12,28},{16,0},{20,4},{24,8},{28,12},{1,17},{... | collective-permute-start | bytes 294920 | tf_op jit(solution)/shard_map/ppermute | solution.py:232
  22.9 8.2 %collective-permute-start.7 = (bf16[64,768]{1,0:T(8,128)(2,1)S(1)}, bf16[64,768]{1,0:T(8,128)(2,1)S(1)}, u32[]{:S(2)}, u32[]{:S(2)}) collective-permute-start(bf16[64,768]{1,0:T(8,128)(2,1)S(1)} %get-tuple-element.11), channel_id=1, source_target_pairs={{0,24},{4,28},{8,16},{12,20},{16,8},{20,12},{24,0},{28,4},{1,25},{... | collective-permute-start | bytes 294920 | tf_op jit(solution)/shard_map/ppermute | solution.py:232
  23.8 13.7 %collective-permute-start.1 = (bf16[64,768]{1,0:T(8,128)(2,1)S(1)}, bf16[64,768]{1,0:T(8,128)(2,1)S(1)}, u32[]{:S(2)}, u32[]{:S(2)}) collective-permute-start(bf16[64,768]{1,0:T(8,128)(2,1)S(1)} %get-tuple-element.9), channel_id=1, source_target_pairs={{0,8},{4,12},{8,0},{12,4},{16,24},{20,28},{24,16},{28,20},{1,9},{5... | collective-permute-start | bytes 294920 | tf_op jit(solution)/shard_map/ppermute | solution.py:232
  31.1 8.7 %collective-permute-start.2 = (bf16[64,768]{1,0:T(8,128)(2,1)S(1)}, bf16[64,768]{1,0:T(8,128)(2,1)S(1)}, u32[]{:S(2)}, u32[]{:S(2)}) collective-permute-start(bf16[64,768]{1,0:T(8,128)(2,1)S(1)} %get-tuple-element.9), channel_id=1, source_target_pairs={{0,16},{4,20},{8,24},{12,28},{16,0},{20,4},{24,8},{28,12},{1,17},{... | collective-permute-start | bytes 294920 | tf_op jit(solution)/shard_map/ppermute | solution.py:232
  31.1 8.7 %collective-permute-start.3 = (bf16[64,768]{1,0:T(8,128)(2,1)S(1)}, bf16[64,768]{1,0:T(8,128)(2,1)S(1)}, u32[]{:S(2)}, u32[]{:S(2)}) collective-permute-start(bf16[64,768]{1,0:T(8,128)(2,1)S(1)} %get-tuple-element.9), channel_id=1, source_target_pairs={{0,24},{4,28},{8,16},{12,20},{16,8},{20,12},{24,0},{28,4},{1,25},{... | collective-permute-start | bytes 294920 | tf_op jit(solution)/shard_map/ppermute | solution.py:232
  43.9 4.0 %collective-permute-start.10 = (bf16[1,4,16,256]{3,2,1,0:T(8,128)(2,1)S(1)}, bf16[1,4,16,256]{3,2,1,0:T(8,128)(2,1)S(1)}, u32[]{:S(2)}, u32[]{:S(2)}) collective-permute-start(bf16[1,4,16,256]{3,2,1,0:T(8,128)(2,1)S(1)} %get-tuple-element.19), channel_id=1, source_target_pairs={{0,2},{1,3},{2,0},{3,1},{4,6},{5,7},{6,4},{7,5},{8,10},{9,11},{10,... | collective-permute-start | bytes 98312 | tf_op jit(solution)/shard_map/ppermute | solution.py:258
  45.6 5.0 %collective-permute-start.11 = (bf16[1,4,16,256]{3,2,1,0:T(8,128)(2,1)S(1)}, bf16[1,4,16,256]{3,2,1,0:T(8,128)(2,1)S(1)}, u32[]{:S(2)}, u32[]{:S(2)}) collective-permute-start(bf16[1,4,16,256]{3,2,1,0:T(8,128)(2,1)S(1)} %get-tuple-element.18), channel_id=1, source_target_pairs={{0,3},{1,2},{2,1},{3,0},{4,7},{5,6},{6,5},{7,4},{8,11},{9,10},{10,... | collective-permute-start | bytes 98312 | tf_op jit(solution)/shard_map/ppermute | solution.py:258
  45.6 5.0 %collective-permute-start.9 = (bf16[1,4,16,256]{3,2,1,0:T(8,128)(2,1)S(1)}, bf16[1,4,16,256]{3,2,1,0:T(8,128)(2,1)S(1)}, u32[]{:S(2)}, u32[]{:S(2)}) collective-permute-start(bf16[1,4,16,256]{3,2,1,0:T(8,128)(2,1)S(1)} %get-tuple-element.17), channel_id=1, source_target_pairs={{0,1},{1,0},{2,3},{3,2},{4,5},{5,4},{6,7},{7,6},{8,9},{9,8},{10,11... | collective-permute-start | bytes 98312 | tf_op jit(solution)/shard_map/ppermute | solution.py:258
  46.1 4.5 %collective-permute-start.12 = (bf16[1,4,16,256]{3,2,1,0:T(8,128)(2,1)S(1)}, bf16[1,4,16,256]{3,2,1,0:T(8,128)(2,1)S(1)}, u32[]{:S(2)}, u32[]{:S(2)}) collective-permute-start(bf16[1,4,16,256]{3,2,1,0:T(8,128)(2,1)S(1)} %get-tuple-element.20), channel_id=1, source_target_pairs={{0,4},{1,5},{2,6},{3,7},{4,0},{5,1},{6,2},{7,3},{8,12},{9,13},{10,... | collective-permute-start | bytes 98312 | tf_op jit(solution)/shard_map/ppermute | solution.py:258
  47.7 3.6 %collective-permute-start.13 = (bf16[1,4,16,256]{3,2,1,0:T(8,128)(2,1)S(1)}, bf16[1,4,16,256]{3,2,1,0:T(8,128)(2,1)S(1)}, u32[]{:S(2)}, u32[]{:S(2)}) collective-permute-start(bf16[1,4,16,256]{3,2,1,0:T(8,128)(2,1)S(1)} %get-tuple-element.23), channel_id=1, source_target_pairs={{0,5},{1,4},{2,7},{3,6},{4,1},{5,0},{6,3},{7,2},{8,13},{9,12},{10,... | collective-permute-start | bytes 98312 | tf_op jit(solution)/shard_map/ppermute | solution.py:258
  47.9 5.2 %collective-permute-start.14 = (bf16[1,4,16,256]{3,2,1,0:T(8,128)(2,1)S(1)}, bf16[1,4,16,256]{3,2,1,0:T(8,128)(2,1)S(1)}, u32[]{:S(2)}, u32[]{:S(2)}) collective-permute-start(bf16[1,4,16,256]{3,2,1,0:T(8,128)(2,1)S(1)} %get-tuple-element.22), channel_id=1, source_target_pairs={{0,6},{1,7},{2,4},{3,5},{4,2},{5,3},{6,0},{7,1},{8,14},{9,15},{10,... | collective-permute-start | bytes 98312 | tf_op jit(solution)/shard_map/ppermute | solution.py:258
  50.6 4.4 %collective-permute-start.15 = (bf16[1,4,16,256]{3,2,1,0:T(8,128)(2,1)S(1)}, bf16[1,4,16,256]{3,2,1,0:T(8,128)(2,1)S(1)}, u32[]{:S(2)}, u32[]{:S(2)}) collective-permute-start(bf16[1,4,16,256]{3,2,1,0:T(8,128)(2,1)S(1)} %get-tuple-element.21), channel_id=1, source_target_pairs={{0,7},{1,6},{2,5},{3,4},{4,3},{5,2},{6,1},{7,0},{8,15},{9,14},{10,... | collective-permute-start | bytes 98312 | tf_op jit(solution)/shard_map/ppermute | solution.py:258

commit v2 on v1

--- a/solution.py
+++ b/solution.py
@@ -17,111 +17,165 @@
 LAGS = 256
 LANE = 128
 CUT = W + LANE
-
-
-def forward_table():
-    samples = np.arange(W, dtype=np.int64)
-    freqs = B0 + np.arange(NB, dtype=np.int64)
-    turns = (samples[:, None] * freqs[None, :] % W) * (2.0 * math.pi / W)
-    taper = 0.5 - 0.5 * np.cos(samples * (2.0 * math.pi / W))
-    table = np.concatenate([taper[:, None] * np.cos(turns), -taper[:, None] * np.sin(turns)], axis=1)
-    return table.astype(np.float32).astype(jnp.bfloat16)
+FOLD = W // 2
+BINS = np.concatenate(
+    [np.arange(0, 256, 2), np.arange(1, 256, 2), np.arange(256, NB, 2), np.arange(257, NB, 2)]
+)
+
+
+def taper_table():
+    return (0.5 - 0.5 * np.cos(np.arange(W) * (2.0 * math.pi / W))).astype(np.float32)[None, :]
+
+
+def half_tables():
+    samples = np.arange(FOLD, dtype=np.int64)[:, None]
+
+    def waves(bins):
+        turns = (samples * (B0 + bins)[None, :] % W) * (2.0 * math.pi / W)
+        return np.cos(turns), -np.sin(turns)
+
+    even_cos, even_sin = waves(np.arange(0, NB, 2))
+    odd_cos, odd_sin = waves(np.arange(1, NB, 2))
+    cut = LANE
+    columns = [
+        even_cos[:, :cut], even_sin[:, :cut], even_cos[:, cut:], even_sin[:, cut:],
+        odd_cos[:, :cut], odd_sin[:, :cut], odd_sin[:, cut:], odd_cos[:, cut:],
+    ]
+    return np.concatenate(columns, axis=1).astype(np.float32).astype(jnp.bfloat16)
 
 
 def smoothing():
-    rows = np.arange(NB)[:, None]
-    cols = np.arange(NB)[None, :]
+    rows = BINS[:, None]
+    cols = BINS[None, :]
     first = np.clip(cols - SMOOTH // 2, 0, NB - SMOOTH)
     return np.where((rows >= first) & (rows < first + SMOOTH), 1.0 / SMOOTH, 0.0).astype(jnp.bfloat16)
 
 
 def lag_table():
-    freqs = B0 + np.arange(NB, dtype=np.int64)
     shifts = np.arange(LAGS, dtype=np.int64) - LAGS // 2
-    turns = (freqs[:, None] * shifts[None, :] % W) * (2.0 * math.pi / W)
+    turns = ((B0 + BINS)[:, None] * shifts[None, :] % W) * (2.0 * math.pi / W)
     table = np.concatenate([np.cos(turns), -np.sin(turns)], axis=0)
     return table.astype(np.float32).astype(jnp.bfloat16)
 
 
-def spectra_kernel(first, count, tail_at, n_src, offs, local, *refs):
-    if tail_at is None:
-        rec, ftab, smooth, out_r, out_s, seg = refs
+def spectra_kernel(first, count, edge, c_dev, n_src, *refs):
+    offs, sources, rec, *refs = refs
+    if edge:
+        halo, table, taper, smooth, out_r, out_s, *refs = refs
     else:
-        rec, halo, ftab, smooth, out_r, out_s, seg, tail = refs
-        body_len = rec.shape[1] - tail_at * HOP
-        tail[:, :body_len] = rec[:, tail_at * HOP :]
-        tail[:, body_len:] = halo[...]
-    c_dev = rec.shape[0]
+        table, taper, smooth, out_r, out_s, out_h, *refs = refs
+    sums, diffs, held, table_v, taper_v, smooth_v, offs_v, sources_v, sems = refs
+    begin = first * HOP
+    width = (count + 2) * HOP
+    copies = []
+
+    def fetch(source, target):
+        copy = pltpu.make_async_copy(source, target, sems.at[len(copies)])
+        copy.start()
+        copies.append(copy)
+
+    fetch(offs, offs_v)
+    fetch(sources, sources_v)
+    fetch(taper, taper_v)
+    inside = width - (W if edge else 0)
+    step = inside // 2
+    for at in range(0, inside, step):
+        fetch(rec.at[:, pl.ds(begin + at, step)], held.at[:, pl.ds(at, step)])
+    if edge:
+        fetch(halo, held.at[:, pl.ds(inside, W)])
+    else:
+        fetch(rec.at[:, pl.ds(0, W)], out_h)
+    ready = len(copies)
+    rows = FOLD // 4
+    for at in range(0, FOLD, rows):
+        fetch(table.at[pl.ds(at, rows)], table_v.at[pl.ds(at, rows)])
+    fetch(smooth, smooth_v)
+    for copy in copies[:ready]:
+        copy.wait()
+
     lanes = lax.broadcasted_iota(jnp.int32, (c_dev, LANE), 1)
 
-    def cut(source, base, slot):
-        start = base + offs[first + slot]
-        begin = pl.multiple_of(start // LANE * LANE, LANE)
+    def cut(slot):
+        start = slot * HOP + offs_v[first + slot]
         rest = start % LANE
         keep = lanes < LANE - rest
         shift = (LANE - rest) % LANE
-        chunk = source[:, pl.ds(begin, CUT)].astype(jnp.float32)
-        turned = [
-            pltpu.roll(chunk[:, i * LANE : (i + 1) * LANE], shift, 1) for i in range(CUT // LANE)
-        ]
-        row = pl.multiple_of(slot * c_dev, c_dev)
-        for i in range(W // LANE):
-            seg[pl.ds(row, c_dev), i * LANE : (i + 1) * LANE] = jnp.where(
-                keep, turned[i], turned[i + 1]
-            ).astype(jnp.bfloat16)
-
-    plain = count if tail_at is None else tail_at - first
-
-    @pl.loop(0, plain)
-    def _(slot):
-        cut(rec, (first + slot) * HOP, slot)
-
-    for slot in range(plain, count):
-        cut(tail, (first + slot - tail_at) * HOP, slot)
-
-    spectra = jnp.dot(seg[...], ftab[...], preferred_element_type=jnp.float32)
-    real = spectra[:, :NB]
-    imag = spectra[:, NB:]
-    power = (real * real + imag * imag).astype(jnp.bfloat16)
-    smoothed = jnp.dot(power, smooth[...], preferred_element_type=jnp.float32)
+        chunk = held[:, pl.ds(pl.multiple_of(start // LANE * LANE, LANE), CUT)].astype(jnp.float32)
+        turned = [pltpu.roll(chunk[:, i * LANE : (i + 1) * LANE], shift, 1) for i in range(CUT // LANE)]
+        row = pl.ds(pl.multiple_of(slot * c_dev, c_dev), c_dev)
+        tiles = FOLD // LANE
+        for i in range(tiles):
+            lo = slice(i * LANE, (i + 1) * LANE)
+            hi = slice(FOLD + i * LANE, FOLD + (i + 1) * LANE)
+            near = jnp.where(keep, turned[i], turned[i + 1]) * taper_v[:, lo]
+            far = jnp.where(keep, turned[tiles + i], turned[tiles + i + 1]) * taper_v[:, hi]
+            sums[row, lo] = (near + far).astype(jnp.bfloat16)
+            diffs[row, lo] = (near - far).astype(jnp.bfloat16)
+
+    pl.loop(0, count, unroll=4)(cut)
+    for copy in copies[ready:]:
+        copy.wait()
+
+    split = 3 * LANE
+    even = jnp.dot(sums[...], table_v[:, :split], preferred_element_type=jnp.float32)
+    odd = jnp.dot(diffs[...], table_v[:, split:], preferred_element_type=jnp.float32)
+    left = lax.broadcasted_iota(jnp.int32, (1, LANE), 1) < LANE // 2
+    mixed_even, mixed_odd = even[:, 2 * LANE :], odd[:, 2 * LANE :]
+    real = [even[:, :LANE], odd[:, :LANE], jnp.where(left, mixed_even, mixed_odd)]
+    swapped = pltpu.roll(jnp.where(left, mixed_odd, mixed_even), LANE // 2, 1)
+    imag = [even[:, LANE : 2 * LANE], odd[:, LANE : 2 * LANE], swapped]
+    power = jnp.concatenate([r * r + i * i for r, i in zip(real, imag)], axis=1).astype(jnp.bfloat16)
+    smoothed = jnp.dot(power, smooth_v[...], preferred_element_type=jnp.float32)
     factor = lax.rsqrt(smoothed + 1e-05)
-    out_r[:, :NB] = (real * factor).astype(jnp.bfloat16)
-    out_r[:, NB:] = (imag * factor).astype(jnp.bfloat16)
-    rows = lax.broadcasted_iota(jnp.int32, (n_src * count, count * c_dev), 0)
+    for i in range(NB // LANE):
+        lo = slice(i * LANE, (i + 1) * LANE)
+        hi = slice(NB + i * LANE, NB + (i + 1) * LANE)
+        out_r[:, lo] = (real[i] * factor[:, lo]).astype(jnp.bfloat16)
+        out_r[:, hi] = (imag[i] * factor[:, lo]).astype(jnp.bfloat16)
+    rows = lax.broadcasted_iota(jnp.int32, (n_src * count, 1), 0)
     cols = lax.broadcasted_iota(jnp.int32, (n_src * count, count * c_dev), 1)
     wanted = jnp.zeros_like(rows)
     for s in range(n_src):
-        wanted = jnp.where(rows // count == s, local[s] + (rows % count) * c_dev, wanted)
+        wanted = jnp.where(rows // count == s, sources_v[s] % c_dev + (rows % count) * c_dev, wanted)
     picker = jnp.where(cols == wanted, 1.0, 0.0).astype(jnp.bfloat16)
     out_s[...] = jnp.dot(picker, out_r[...], preferred_element_type=jnp.float32).astype(jnp.bfloat16)
 
 
-def spectra_call(record, halo, offsets, local, ftab, smooth, first, count):
+def spectra_call(record, halo, offsets, src_idx, tables, first, count):
     c_dev = record.shape[0]
-    n_src = local.shape[0]
-    n_win = offsets.shape[0]
-    tail_at = None if halo is None else n_win - 2
+    n_src = src_idx.shape[0]
+    edge = halo is not None
     vmem = pl.BlockSpec(memory_space=pltpu.VMEM)
-    smem = pl.BlockSpec(memory_space=pltpu.SMEM)
-    arrays = [record] + ([] if halo is None else [halo]) + [ftab, smooth]
-    scratch = [pltpu.VMEM((count * c_dev, W), jnp.bfloat16)]
-    if halo is not None:
-        scratch.append(pltpu.VMEM((c_dev, 2 * HOP + W), jnp.bfloat16))
+    hbm = pl.BlockSpec(memory_space=pl.ANY)
+    arrays = [offsets, src_idx, record] + ([halo] if edge else []) + list(tables)
+    out_shape = [
+        jax.ShapeDtypeStruct((count * c_dev, 2 * NB), jnp.bfloat16),
+        jax.ShapeDtypeStruct((n_src * count, 2 * NB), jnp.bfloat16),
+    ]
+    if not edge:
+        out_shape.append(jax.ShapeDtypeStruct((c_dev, W), jnp.bfloat16))
     return pl.pallas_call(
-        functools.partial(spectra_kernel, first, count, tail_at, n_src),
-        out_shape=(
-            jax.ShapeDtypeStruct((count * c_dev, 2 * NB), jnp.bfloat16),
-            jax.ShapeDtypeStruct((n_src * count, 2 * NB), jnp.bfloat16),
-        ),
-        in_specs=[smem, smem] + [vmem] * len(arrays),
-        out_specs=(vmem, vmem),
-        scratch_shapes=scratch,
-        compiler_params=pltpu.CompilerParams(vmem_limit_bytes=48 << 20),
+        functools.partial(spectra_kernel, first, count, edge, c_dev, n_src),
+        out_shape=out_shape,
+        in_specs=[hbm] * len(arrays),
+        out_specs=[vmem] * len(out_shape),
+        scratch_shapes=[
+            pltpu.VMEM((count * c_dev, FOLD), jnp.bfloat16),
+            pltpu.VMEM((count * c_dev, FOLD), jnp.bfloat16),
+            pltpu.VMEM((c_dev, (count + 2) * HOP), jnp.bfloat16),
+            pltpu.VMEM((FOLD, 2 * NB), jnp.bfloat16),
+            pltpu.VMEM((1, W), jnp.float32),
+            pltpu.VMEM((NB, NB), jnp.bfloat16),
+            pltpu.SMEM(offsets.shape, jnp.int32),
+            pltpu.SMEM(src_idx.shape, jnp.int32),
+            pltpu.SemaphoreType.DMA((16,)),
+        ],
+        compiler_params=pltpu.CompilerParams(vmem_limit_bytes=32 << 20),
         cost_estimate=pl.CostEstimate(
             flops=2 * count * c_dev * W * 2 * NB, bytes_accessed=6 << 20, transcendentals=0
         ),
         name="spectra",
-    )(offsets, local, *arrays)
+    )(*arrays)
 
 
 def cross_kernel(n_list, n_rec, n_src, count, c_dev, final, scale, *refs):
@@ -213,19 +267,14 @@
     n_group = n_fibre // 2
     fibre = lax.axis_index("fibre")
     tm = lax.axis_index("tm")
-    half = n_win // 2
+    early = n_win * 3 // 4
     scale = 1.0 / math.sqrt(n_win * n_tm * NB)
-    ftab = jnp.asarray(forward_table())
-    smooth = jnp.asarray(smoothing())
+    tables = [jnp.asarray(t) for t in (half_tables(), taper_table(), smoothing())]
     ltab = jnp.asarray(lag_table())
     swap = [(i, i ^ 1) for i in range(n_fibre)]
     direct = n_group == 4 and n_tm == 4
 
-    halo = lax.ppermute(record[:, :W], "tm", [(i, i - 1) for i in range(1, n_tm)])
-    local = src_idx - fibre * c_dev
-    parts = []
-    for first, edge in ((0, None), (half, halo)):
-        rec, src = spectra_call(record, edge, offsets, local, ftab, smooth, first, half)
+    def spread(rec, src):
         other = lax.ppermute(rec, "fibre", swap)
         if direct:
             srcs = [src[None]] + [
@@ -235,9 +284,15 @@
         else:
             ranks = [[2 * j + p for j in range(n_group)] for p in range(2)]
             srcs = [lax.all_gather(src, "fibre", axis=0, axis_index_groups=ranks)]
-        parts.append((srcs, [rec, other]))
-    before = cross_call(*parts[0], None, None, n_src, half, c_dev, scale)
-    lagged = cross_call(*parts[1], before, ltab, n_src, half, c_dev, scale)
+        return srcs, [rec, other]
+
+    rec, src, edge = spectra_call(record, None, offsets, src_idx, tables, 0, early)
+    halo = lax.ppermute(edge, "tm", [(i, i - 1) for i in range(1, n_tm)])
+    first = spread(rec, src)
+    late = n_win - early
+    second = spread(*spectra_call(record, halo, offsets, src_idx, tables, early, late))
+    before = cross_call(*first, None, None, n_src, early, c_dev, scale)
+    lagged = cross_call(*second, before, ltab, n_src, late, c_dev, scale)
     lagged = lagged.reshape(n_group, n_src, 2, c_dev, LAGS)
 
     def piece(owner, side):

time: 56 us -> 52.7 us (0.941)
  the two profiles are of different devices: /device:TPU:0 before, /device:TPU:11 now
where the time goes in v2:
time: 52.7 us; the launch traced here: 52.4 us
  starting transfers between devices  21.9 us (42%)
  Pallas kernels  14.1 us (27%)
  waiting for transfers between devices  9.95 us (19%)
  local copies, waits for them, and re-layouts  5.65 us (11%)
  other arithmetic  0.7 us (1%)
    ppermute x6, starting transfers between devices, spread(): lax.ppermute(src, 'fibre', [(i, i ^ 2 * k) for i in range(n_fibre)])[None]  9.54 us
    ppermute x7, starting transfers between devices, body(): mine = lax.ppermute(mine, ('fibre', 'tm'), pairs)  7.94 us
    pallas_call x2, Pallas kernels, cross_call(): pl.pallas_call(functools.partial(cross_kernel, n_list, n_rec, n_src, coun...  7.86 us
    pallas_call x2, Pallas kernels, spectra_call(): pl.pallas_call(functools.partial(spectra_kernel, first, count, edge, c_de...  6.21 us
    unnamed x14, local copies, waits for them, and re-layouts  5.6 us
    ppermute x6, waiting for transfers between devices, spread(): lax.ppermute(src, 'fibre', [(i, i ^ 2 * k) for i in range(n_fibre)])[None]  5.08 us
    ppermute x7, waiting for transfers between devices, body(): mine = lax.ppermute(mine, ('fibre', 'tm'), pairs)  4.23 us
    ppermute x1, starting transfers between devices, body(): halo = lax.ppermute(edge, 'tm', [(i, i - 1) for i in range(1, n_tm)])  2.85 us
  transfers between devices with their start and end apart: 16, of which 6 were waited for; matrix products, arithmetic and copies ran while one was open for 0% of the time, Pallas kernels for 15%

profile of v2, /device:TPU:11, one launch (start us, length us, event | category | flops | bytes accessed | tf_op | source)
XLA Modules:
  0.0 52.4 jit_solution(8633360286604527106)
XLA Ops:
  0.0 0.0 copy-start
  0.0 1.4 %copy-done = bf16[1024,768]{1,0:T(8,128)(2,1)S(1)} copy-done((bf16[1024,768]{1,0:T(8,128)(2,1)S(1)}, bf16[1024,768]{1,0:T(8,128)(2,1)}, u32[]{:S(2)}) %copy-start) | copy-done | bytes 1572888
  1.4 0.0 copy-start.1
  1.4 1.2 %copy-done.1 = bf16[16,32768]{1,0:T(8,128)(2,1)S(1)} copy-done((bf16[16,32768]{1,0:T(8,128)(2,1)S(1)}, bf16[16,32768]{1,0:T(8,128)(2,1)}, u32[]{:S(2)}) %copy-start.1) | copy-done | bytes 1048600
  2.6 0.0 copy-start.3
  2.6 1.0 %copy-done.3 = bf16[384,384]{1,0:T(8,128)(2,1)S(1)} copy-done((bf16[384,384]{1,0:T(8,128)(2,1)S(1)}, bf16[384,384]{1,0:T(8,128)(2,1)}, u32[]{:S(2)}) %copy-start.3) | copy-done | bytes 294936
  3.6 0.0 copy-start.4
  3.6 0.7 %copy-done.4 = f32[1,2048]{1,0:T(1,128)S(1)} copy-done((f32[1,2048]{1,0:T(1,128)S(1)}, f32[1,2048]{1,0:T(1,128)}, u32[]{:S(2)}) %copy-start.4) | copy-done | bytes 8216
  4.3 0.7 %copy-done.5 = s32[32]{0:T(128)S(1)} copy-done((s32[32]{0:T(128)S(1)}, s32[32]{0:T(128)}, u32[]{:S(2)}) %copy-start.5) | copy-done | bytes 152
  5.0 0.7 %copy-done.6 = s32[4]{0:T(128)S(1)} copy-done((s32[4]{0:T(128)S(1)}, s32[4]{0:T(128)}, u32[]{:S(2)}) %copy-start.6) | copy-done | bytes 40
  5.6 3.9 %spectra.2 = (bf16[384,768]{1,0:T(8,128)(2,1)S(1)}, bf16[96,768]{1,0:T(8,128)(2,1)S(1)}, bf16[16,2048]{1,0:T(8,128)(2,1)S(1)}) custom-call(s32[32]{0:T(128)S(1)} %copy-done.5, s32[4]{0:T(128)S(1)} %copy-done.6, bf16[16,32768]{1,0:T(8,128)(2,1)S(1)} %copy-done.1, bf16[1024,768]{1,0:T(8,128)(2,1)S(1)} %copy-done, f32[1,2048]{1,0:T(1,128)S(1)} %copy-done.4, ...), custom_call_target="tpu_custom_call" | custom-call | flops 1207959552 | bytes 6291456 | tf_op jit(solution)/shard_map/spectra/pallas_call | solution.py:157
  9.5 0.3 collective-permute-start.8
  9.8 2.9 %collective-permute-start = (bf16[16,2048]{1,0:T(8,128)(2,1)S(1)}, bf16[16,2048]{1,0:T(8,128)(2,1)S(1)}, u32[]{:S(2)}, u32[]{:S(2)}) collective-permute-start(bf16[16,2048]{1,0:T(8,128)(2,1)S(1)} %get-tuple-element.10), channel_id=1, source_target_pairs={{1,0},{2,1},{3,2},{5,4},{6,5},{7,6},{9,8},{10,9},{11,10},{13,12},{... | collective-permute-start | bytes 196616 | tf_op jit(solution)/shard_map/ppermute | solution.py:290
  12.7 0.1 collective-permute-start.5
  12.7 2.5 %collective-permute-start.6 = (bf16[96,768]{1,0:T(8,128)(2,1)S(1)}, bf16[96,768]{1,0:T(8,128)(2,1)S(1)}, u32[]{:S(2)}, u32[]{:S(2)}) collective-permute-start(bf16[96,768]{1,0:T(8,128)(2,1)S(1)} %get-tuple-element.13), channel_id=1, source_target_pairs={{0,16},{4,20},{8,24},{12,28},{16,0},{20,4},{24,8},{28,12},{1,17},{... | collective-permute-start | bytes 442376 | tf_op jit(solution)/shard_map/ppermute | solution.py:281
  15.2 0.2 collective-permute-start.7
  15.4 0.6 %collective-permute-done.refs_3_ = bf16[16,2048]{1,0:T(8,128)(2,1)S(1)} collective-permute-done((bf16[16,2048]{1,0:T(8,128)(2,1)S(1)}, bf16[16,2048]{1,0:T(8,128)(2,1)S(1)}, u32[]{:S(2)}, u32[]{:S(2)}) %collective-permute-start) | collective-permute-done | bytes 65568 | tf_op jit(solution)/shard_map/ppermute | solution.py:290
  16.0 2.4 %spectra.3 = (bf16[128,768]{1,0:T(8,128)(2,1)S(1)}, bf16[32,768]{1,0:T(8,128)(2,1)S(1)}) custom-call(s32[32]{0:T(128)S(1)} %copy-done.5, s32[4]{0:T(128)S(1)} %copy-done.6, bf16[16,32768]{1,0:T(8,128)(2,1)S(1)} %copy-done.1, bf16[16,2048]{1,0:T(8,128)(2,1)S(1)} %collective-permute-done.refs_3_, bf16[1024,768]{1,0:T(8,128)(2,1)S(1)} %copy-done, ...), custom_call_target="tpu_custom_call" | custom-call | flops 402653184 | bytes 6291456 | tf_op jit(solution)/shard_map/spectra/pallas_call | solution.py:157
  18.4 1.3 %collective-permute-start.4 = (bf16[128,768]{1,0:T(8,128)(2,1)S(1)}, bf16[128,768]{1,0:T(8,128)(2,1)S(1)}, u32[]{:S(2)}, u32[]{:S(2)}) collective-permute-start(bf16[128,768]{1,0:T(8,128)(2,1)S(1)} %get-tuple-element.12.refs_4_), channel_id=1, source_target_pairs={{0,4},{4,0},{8,12},{12,8},{16,20},{20,16},{24,28},{28,24},{1,5},{5... | collective-permute-start | bytes 589832 | tf_op jit(solution)/shard_map/ppermute | solution.py:278
  19.7 0.0 collective-permute-done.5
  19.7 1.4 %collective-permute-start.1 = (bf16[32,768]{1,0:T(8,128)(2,1)S(1)}, bf16[32,768]{1,0:T(8,128)(2,1)S(1)}, u32[]{:S(2)}, u32[]{:S(2)}) collective-permute-start(bf16[32,768]{1,0:T(8,128)(2,1)S(1)} %get-tuple-element.11), channel_id=1, source_target_pairs={{0,8},{4,12},{8,0},{12,4},{16,24},{20,28},{24,16},{28,20},{1,9},{5... | collective-permute-start | bytes 147464 | tf_op jit(solution)/shard_map/ppermute | solution.py:281
  21.0 4.1 %collective-permute-done.6 = bf16[96,768]{1,0:T(8,128)(2,1)S(1)} collective-permute-done((bf16[96,768]{1,0:T(8,128)(2,1)S(1)}, bf16[96,768]{1,0:T(8,128)(2,1)S(1)}, u32[]{:S(2)}, u32[]{:S(2)}) %collective-permute-start.6) | collective-permute-done | bytes 147488 | tf_op jit(solution)/shard_map/ppermute | solution.py:281
  25.1 3.1 %collective-permute-start.2 = (bf16[32,768]{1,0:T(8,128)(2,1)S(1)}, bf16[32,768]{1,0:T(8,128)(2,1)S(1)}, u32[]{:S(2)}, u32[]{:S(2)}) collective-permute-start(bf16[32,768]{1,0:T(8,128)(2,1)S(1)} %get-tuple-element.11), channel_id=1, source_target_pairs={{0,16},{4,20},{8,24},{12,28},{16,0},{20,4},{24,8},{28,12},{1,17},{... | collective-permute-start | bytes 147464 | tf_op jit(solution)/shard_map/ppermute | solution.py:281
  28.2 1.0 %collective-permute-done.7 = bf16[96,768]{1,0:T(8,128)(2,1)S(1)} collective-permute-done((bf16[96,768]{1,0:T(8,128)(2,1)S(1)}, bf16[96,768]{1,0:T(8,128)(2,1)S(1)}, u32[]{:S(2)}, u32[]{:S(2)}) %collective-permute-start.7) | collective-permute-done | bytes 147488 | tf_op jit(solution)/shard_map/ppermute | solution.py:281
  29.2 2.3 %collective-permute-start.3 = (bf16[32,768]{1,0:T(8,128)(2,1)S(1)}, bf16[32,768]{1,0:T(8,128)(2,1)S(1)}, u32[]{:S(2)}, u32[]{:S(2)}) collective-permute-start(bf16[32,768]{1,0:T(8,128)(2,1)S(1)} %get-tuple-element.11), channel_id=1, source_target_pairs={{0,24},{4,28},{8,16},{12,20},{16,8},{20,12},{24,0},{28,4},{1,25},{... | collective-permute-start | bytes 147464 | tf_op jit(solution)/shard_map/ppermute | solution.py:281
  31.6 0.0 collective-permute-done.8.refs_5_
  31.6 5.6 %cross.2.refs_6_ = f32[512,768]{1,0:T(8,128)S(1)} custom-call(bf16[1,96,768]{2,1,0:T(8,128)(2,1)S(1)} %bitcast.36, bf16[1,96,768]{2,1,0:T(8,128)(2,1)S(1)} %bitcast.37, bf16[1,96,768]{2,1,0:T(8,128)(2,1)S(1)} %bitcast.38, bf16[1,96,768]{2,1,0:T(8,128)(2,1)S(1)} %bitcast.39, bf16[384,768]{1,0:T(8,128)(2,1)S(1)} %get-tuple-element.14.refs_4_, ...), custom_call_target="tpu_custom_call" | custom-call | flops 188743680 | bytes 4194304 | tf_op jit(solution)/shard_map/cross/pallas_call | solution.py:246
  37.2 0.0 collective-permute-done.1
  37.2 0.0 collective-permute-done.2
  37.2 0.0 collective-permute-done.3
  37.2 0.0 collective-permute-done.4.refs_5_
  37.2 0.0 copy-done.2
  37.2 2.3 %cross.3 = bf16[512,256]{1,0:T(8,128)(2,1)S(1)} custom-call(bf16[1,32,768]{2,1,0:T(8,128)(2,1)S(1)} %bitcast.40, bf16[1,32,768]{2,1,0:T(8,128)(2,1)S(1)} %bitcast.41, bf16[1,32,768]{2,1,0:T(8,128)(2,1)S(1)} %bitcast.42, bf16[1,32,768]{2,1,0:T(8,128)(2,1)S(1)} %bitcast.43, bf16[128,768]{1,0:T(8,128)(2,1)S(1)} %get-tuple-element.12.refs_4_, ...), custom_call_target="tpu_custom_call" | custom-call | flops 62914560 | bytes 4194304 | tf_op jit(solution)/shard_map/cross/pallas_call | solution.py:246
  39.5 0.2 collective-permute-start.10
  39.7 2.9 %collective-permute-start.11 = (bf16[1,4,16,256]{3,2,1,0:T(8,128)(2,1)S(1)}, bf16[1,4,16,256]{3,2,1,0:T(8,128)(2,1)S(1)}, u32[]{:S(2)}, u32[]{:S(2)}) collective-permute-start(bf16[1,4,16,256]{3,2,1,0:T(8,128)(2,1)S(1)} %get-tuple-element.20), channel_id=1, source_target_pairs={{0,3},{1,2},{2,1},{3,0},{4,7},{5,6},{6,5},{7,4},{8,11},{9,10},{10,... | collective-permute-start | bytes 98312 | tf_op jit(solution)/shard_map/ppermute | solution.py:313
  42.7 0.3 collective-permute-start.9
  43.0 1.3 %collective-permute-start.12 = (bf16[1,4,16,256]{3,2,1,0:T(8,128)(2,1)S(1)}, bf16[1,4,16,256]{3,2,1,0:T(8,128)(2,1)S(1)}, u32[]{:S(2)}, u32[]{:S(2)}) collective-permute-start(bf16[1,4,16,256]{3,2,1,0:T(8,128)(2,1)S(1)} %get-tuple-element.22), channel_id=1, source_target_pairs={{0,4},{1,5},{2,6},{3,7},{4,0},{5,1},{6,2},{7,3},{8,12},{9,13},{10,... | collective-permute-start | bytes 98312 | tf_op jit(solution)/shard_map/ppermute | solution.py:313
  44.3 0.6 %collective-permute-start.13 = (bf16[1,4,16,256]{3,2,1,0:T(8,128)(2,1)S(1)}, bf16[1,4,16,256]{3,2,1,0:T(8,128)(2,1)S(1)}, u32[]{:S(2)}, u32[]{:S(2)}) collective-permute-start(bf16[1,4,16,256]{3,2,1,0:T(8,128)(2,1)S(1)} %get-tuple-element.25), channel_id=1, source_target_pairs={{0,5},{1,4},{2,7},{3,6},{4,1},{5,0},{6,3},{7,2},{8,13},{9,12},{10,... | collective-permute-start | bytes 98312 | tf_op jit(solution)/shard_map/ppermute | solution.py:313
  44.9 0.0 collective-permute-done.10
  44.9 2.6 %collective-permute-start.14 = (bf16[1,4,16,256]{3,2,1,0:T(8,128)(2,1)S(1)}, bf16[1,4,16,256]{3,2,1,0:T(8,128)(2,1)S(1)}, u32[]{:S(2)}, u32[]{:S(2)}) collective-permute-start(bf16[1,4,16,256]{3,2,1,0:T(8,128)(2,1)S(1)} %get-tuple-element.24), channel_id=1, source_target_pairs={{0,6},{1,7},{2,4},{3,5},{4,2},{5,3},{6,0},{7,1},{8,14},{9,15},{10,... | collective-permute-start | bytes 98312 | tf_op jit(solution)/shard_map/ppermute | solution.py:313
  47.5 0.0 collective-permute-done.11
  47.5 0.0 collective-permute-start.15
  47.5 0.0 collective-permute-done.9
  47.5 0.0 collective-permute-done.12
  47.5 0.3 collective-permute-done.13
  47.8 2.1 %collective-permute-done.14 = bf16[1,4,16,256]{3,2,1,0:T(8,128)(2,1)S(1)} collective-permute-done((bf16[1,4,16,256]{3,2,1,0:T(8,128)(2,1)S(1)}, bf16[1,4,16,256]{3,2,1,0:T(8,128)(2,1)S(1)}, u32[]{:S(2)}, u32[]{:S(2)}) %collective-permute-start.14) | collective-permute-done | bytes 32800 | tf_op jit(solution)/shard_map/ppermute | solution.py:313
  49.9 1.8 %collective-permute-done.15 = bf16[1,4,16,256]{3,2,1,0:T(8,128)(2,1)S(1)} collective-permute-done((bf16[1,4,16,256]{3,2,1,0:T(8,128)(2,1)S(1)}, bf16[1,4,16,256]{3,2,1,0:T(8,128)(2,1)S(1)}, u32[]{:S(2)}, u32[]{:S(2)}) %collective-permute-start.15) | collective-permute-done | bytes 32800 | tf_op jit(solution)/shard_map/ppermute | solution.py:313
  51.8 0.7 %pad_maximum_fusion = f32[1,2,4,16,256]{4,3,2,1,0:T(8,128)} fusion(f32[1,1,4,16,256]{4,3,2,1,0:T(8,128)S(1)} %get-tuple-element.16, f32[1,1,4,16,256]{4,3,2,1,0:T(8,128)S(1)} %get-tuple-element.15), kind=kLoop, calls=%fused_computation | loop fusion | flops 32768 | bytes 262144 | tf_op jit(solution)/shard_map/stack | solution.py:319
  (7 shorter events, 0.1 us)
Async XLA Ops:
  0.0 1.4 %copy-start = (bf16[1024,768]{1,0:T(8,128)(2,1)S(1)}, bf16[1024,768]{1,0:T(8,128)(2,1)}, u32[]{:S(2)}) copy-start(bf16[1024,768]{1,0:T(8,128)(2,1)} %constant.86.clone.refs_3_.refs_4_) | copy-start | bytes 4718596
  1.4 1.2 %copy-start.1 = (bf16[16,32768]{1,0:T(8,128)(2,1)S(1)}, bf16[16,32768]{1,0:T(8,128)(2,1)}, u32[]{:S(2)}) copy-start(bf16[16,32768]{1,0:T(8,128)(2,1)} %refs_2_.3) | copy-start | bytes 3145732
  2.6 1.0 %copy-start.3 = (bf16[384,384]{1,0:T(8,128)(2,1)S(1)}, bf16[384,384]{1,0:T(8,128)(2,1)}, u32[]{:S(2)}) copy-start(bf16[384,384]{1,0:T(8,128)(2,1)} %constant.88.clone.refs_5_.refs_6_) | copy-start | bytes 884740
  3.6 0.7 %copy-start.4 = (f32[1,2048]{1,0:T(1,128)S(1)}, f32[1,2048]{1,0:T(1,128)}, u32[]{:S(2)}) copy-start(f32[1,2048]{1,0:T(1,128)} %constant.87.clone.refs_4_.refs_5_) | copy-start | bytes 24580
  4.3 0.7 %copy-start.5 = (s32[32]{0:T(128)S(1)}, s32[32]{0:T(128)}, u32[]{:S(2)}) copy-start(s32[32]{0:T(128)} %refs_0_.3) | copy-start | bytes 388
  4.9 0.7 %copy-start.6 = (s32[4]{0:T(128)S(1)}, s32[4]{0:T(128)}, u32[]{:S(2)}) copy-start(s32[4]{0:T(128)} %refs_1_.3) | copy-start | bytes 52
  9.5 22.1 %collective-permute-start.8 = (bf16[384,768]{1,0:T(8,128)(2,1)S(1)}, bf16[384,768]{1,0:T(8,128)(2,1)S(1)}, u32[]{:S(2)}, u32[]{:S(2)}) collective-permute-start(bf16[384,768]{1,0:T(8,128)(2,1)S(1)} %get-tuple-element.14.refs_4_), channel_id=1, source_target_pairs={{0,4},{4,0},{8,12},{12,8},{16,20},{20,16},{24,28},{28,24},{1,5},{5... | collective-permute-start | bytes 1769480 | tf_op jit(solution)/shard_map/ppermute | solution.py:278
  9.8 6.2 %collective-permute-start = (bf16[16,2048]{1,0:T(8,128)(2,1)S(1)}, bf16[16,2048]{1,0:T(8,128)(2,1)S(1)}, u32[]{:S(2)}, u32[]{:S(2)}) collective-permute-start(bf16[16,2048]{1,0:T(8,128)(2,1)S(1)} %get-tuple-element.10), channel_id=1, source_target_pairs={{1,0},{2,1},{3,2},{5,4},{6,5},{7,6},{9,8},{10,9},{11,10},{13,12},{... | collective-permute-start | bytes 196616 | tf_op jit(solution)/shard_map/ppermute | solution.py:290
  12.7 7.0 %collective-permute-start.5 = (bf16[96,768]{1,0:T(8,128)(2,1)S(1)}, bf16[96,768]{1,0:T(8,128)(2,1)S(1)}, u32[]{:S(2)}, u32[]{:S(2)}) collective-permute-start(bf16[96,768]{1,0:T(8,128)(2,1)S(1)} %get-tuple-element.13), channel_id=1, source_target_pairs={{0,8},{4,12},{8,0},{12,4},{16,24},{20,28},{24,16},{28,20},{1,9},{5... | collective-permute-start | bytes 442376 | tf_op jit(solution)/shard_map/ppermute | solution.py:281
  12.7 12.4 %collective-permute-start.6 = (bf16[96,768]{1,0:T(8,128)(2,1)S(1)}, bf16[96,768]{1,0:T(8,128)(2,1)S(1)}, u32[]{:S(2)}, u32[]{:S(2)}) collective-permute-start(bf16[96,768]{1,0:T(8,128)(2,1)S(1)} %get-tuple-element.13), channel_id=1, source_target_pairs={{0,16},{4,20},{8,24},{12,28},{16,0},{20,4},{24,8},{28,12},{1,17},{... | collective-permute-start | bytes 442376 | tf_op jit(solution)/shard_map/ppermute | solution.py:281
  15.2 14.0 %collective-permute-start.7 = (bf16[96,768]{1,0:T(8,128)(2,1)S(1)}, bf16[96,768]{1,0:T(8,128)(2,1)S(1)}, u32[]{:S(2)}, u32[]{:S(2)}) collective-permute-start(bf16[96,768]{1,0:T(8,128)(2,1)S(1)} %get-tuple-element.13), channel_id=1, source_target_pairs={{0,24},{4,28},{8,16},{12,20},{16,8},{20,12},{24,0},{28,4},{1,25},{... | collective-permute-start | bytes 442376 | tf_op jit(solution)/shard_map/ppermute | solution.py:281
  18.4 18.8 %collective-permute-start.4 = (bf16[128,768]{1,0:T(8,128)(2,1)S(1)}, bf16[128,768]{1,0:T(8,128)(2,1)S(1)}, u32[]{:S(2)}, u32[]{:S(2)}) collective-permute-start(bf16[128,768]{1,0:T(8,128)(2,1)S(1)} %get-tuple-element.12.refs_4_), channel_id=1, source_target_pairs={{0,4},{4,0},{8,12},{12,8},{16,20},{20,16},{24,28},{28,24},{1,5},{5... | collective-permute-start | bytes 589832 | tf_op jit(solution)/shard_map/ppermute | solution.py:278
  19.7 17.5 %collective-permute-start.1 = (bf16[32,768]{1,0:T(8,128)(2,1)S(1)}, bf16[32,768]{1,0:T(8,128)(2,1)S(1)}, u32[]{:S(2)}, u32[]{:S(2)}) collective-permute-start(bf16[32,768]{1,0:T(8,128)(2,1)S(1)} %get-tuple-element.11), channel_id=1, source_target_pairs={{0,8},{4,12},{8,0},{12,4},{16,24},{20,28},{24,16},{28,20},{1,9},{5... | collective-permute-start | bytes 147464 | tf_op jit(solution)/shard_map/ppermute | solution.py:281
  25.1 12.0 %collective-permute-start.2 = (bf16[32,768]{1,0:T(8,128)(2,1)S(1)}, bf16[32,768]{1,0:T(8,128)(2,1)S(1)}, u32[]{:S(2)}, u32[]{:S(2)}) collective-permute-start(bf16[32,768]{1,0:T(8,128)(2,1)S(1)} %get-tuple-element.11), channel_id=1, source_target_pairs={{0,16},{4,20},{8,24},{12,28},{16,0},{20,4},{24,8},{28,12},{1,17},{... | collective-permute-start | bytes 147464 | tf_op jit(solution)/shard_map/ppermute | solution.py:281
  29.2 8.0 %collective-permute-start.3 = (bf16[32,768]{1,0:T(8,128)(2,1)S(1)}, bf16[32,768]{1,0:T(8,128)(2,1)S(1)}, u32[]{:S(2)}, u32[]{:S(2)}) collective-permute-start(bf16[32,768]{1,0:T(8,128)(2,1)S(1)} %get-tuple-element.11), channel_id=1, source_target_pairs={{0,24},{4,28},{8,16},{12,20},{16,8},{20,12},{24,0},{28,4},{1,25},{... | collective-permute-start | bytes 147464 | tf_op jit(solution)/shard_map/ppermute | solution.py:281
  31.6 5.6 %copy-start.2 = (bf16[768,256]{1,0:T(8,128)(2,1)S(1)}, bf16[768,256]{1,0:T(8,128)(2,1)}, u32[]{:S(2)}) copy-start(bf16[768,256]{1,0:T(8,128)(2,1)} %constant.89.clone.refs_7_) | copy-start | bytes 1179652
  39.5 5.3 %collective-permute-start.10 = (bf16[1,4,16,256]{3,2,1,0:T(8,128)(2,1)S(1)}, bf16[1,4,16,256]{3,2,1,0:T(8,128)(2,1)S(1)}, u32[]{:S(2)}, u32[]{:S(2)}) collective-permute-start(bf16[1,4,16,256]{3,2,1,0:T(8,128)(2,1)S(1)} %get-tuple-element.21), channel_id=1, source_target_pairs={{0,2},{1,3},{2,0},{3,1},{4,6},{5,7},{6,4},{7,5},{8,10},{9,11},{10,... | collective-permute-start | bytes 98312 | tf_op jit(solution)/shard_map/ppermute | solution.py:313
  39.7 7.8 %collective-permute-start.11 = (bf16[1,4,16,256]{3,2,1,0:T(8,128)(2,1)S(1)}, bf16[1,4,16,256]{3,2,1,0:T(8,128)(2,1)S(1)}, u32[]{:S(2)}, u32[]{:S(2)}) collective-permute-start(bf16[1,4,16,256]{3,2,1,0:T(8,128)(2,1)S(1)} %get-tuple-element.20), channel_id=1, source_target_pairs={{0,3},{1,2},{2,1},{3,0},{4,7},{5,6},{6,5},{7,4},{8,11},{9,10},{10,... | collective-permute-start | bytes 98312 | tf_op jit(solution)/shard_map/ppermute | solution.py:313
  42.7 4.8 %collective-permute-start.9 = (bf16[1,4,16,256]{3,2,1,0:T(8,128)(2,1)S(1)}, bf16[1,4,16,256]{3,2,1,0:T(8,128)(2,1)S(1)}, u32[]{:S(2)}, u32[]{:S(2)}) collective-permute-start(bf16[1,4,16,256]{3,2,1,0:T(8,128)(2,1)S(1)} %get-tuple-element.19), channel_id=1, source_target_pairs={{0,1},{1,0},{2,3},{3,2},{4,5},{5,4},{6,7},{7,6},{8,9},{9,8},{10,11... | collective-permute-start | bytes 98312 | tf_op jit(solution)/shard_map/ppermute | solution.py:313
  43.0 4.5 %collective-permute-start.12 = (bf16[1,4,16,256]{3,2,1,0:T(8,128)(2,1)S(1)}, bf16[1,4,16,256]{3,2,1,0:T(8,128)(2,1)S(1)}, u32[]{:S(2)}, u32[]{:S(2)}) collective-permute-start(bf16[1,4,16,256]{3,2,1,0:T(8,128)(2,1)S(1)} %get-tuple-element.22), channel_id=1, source_target_pairs={{0,4},{1,5},{2,6},{3,7},{4,0},{5,1},{6,2},{7,3},{8,12},{9,13},{10,... | collective-permute-start | bytes 98312 | tf_op jit(solution)/shard_map/ppermute | solution.py:313
  44.3 3.5 %collective-permute-start.13 = (bf16[1,4,16,256]{3,2,1,0:T(8,128)(2,1)S(1)}, bf16[1,4,16,256]{3,2,1,0:T(8,128)(2,1)S(1)}, u32[]{:S(2)}, u32[]{:S(2)}) collective-permute-start(bf16[1,4,16,256]{3,2,1,0:T(8,128)(2,1)S(1)} %get-tuple-element.25), channel_id=1, source_target_pairs={{0,5},{1,4},{2,7},{3,6},{4,1},{5,0},{6,3},{7,2},{8,13},{9,12},{10,... | collective-permute-start | bytes 98312 | tf_op jit(solution)/shard_map/ppermute | solution.py:313
  44.9 5.0 %collective-permute-start.14 = (bf16[1,4,16,256]{3,2,1,0:T(8,128)(2,1)S(1)}, bf16[1,4,16,256]{3,2,1,0:T(8,128)(2,1)S(1)}, u32[]{:S(2)}, u32[]{:S(2)}) collective-permute-start(bf16[1,4,16,256]{3,2,1,0:T(8,128)(2,1)S(1)} %get-tuple-element.24), channel_id=1, source_target_pairs={{0,6},{1,7},{2,4},{3,5},{4,2},{5,3},{6,0},{7,1},{8,14},{9,15},{10,... | collective-permute-start | bytes 98312 | tf_op jit(solution)/shard_map/ppermute | solution.py:313
  47.5 4.2 %collective-permute-start.15 = (bf16[1,4,16,256]{3,2,1,0:T(8,128)(2,1)S(1)}, bf16[1,4,16,256]{3,2,1,0:T(8,128)(2,1)S(1)}, u32[]{:S(2)}, u32[]{:S(2)}) collective-permute-start(bf16[1,4,16,256]{3,2,1,0:T(8,128)(2,1)S(1)} %get-tuple-element.23), channel_id=1, source_target_pairs={{0,7},{1,6},{2,5},{3,4},{4,3},{5,2},{6,1},{7,0},{8,15},{9,14},{10,... | collective-permute-start | bytes 98312 | tf_op jit(solution)/shard_map/ppermute | solution.py:313

commit v3 on v2

v3 whole, which is shorter than its diff:
```python
import functools
import math

import jax
import jax.numpy as jnp
import numpy as np
from jax import lax
from jax.experimental import pallas as pl
from jax.experimental.pallas import tpu as pltpu
from jax.sharding import PartitionSpec as P

W = 2048
HOP = 1024
NB = 384
B0 = 20
SMOOTH = 64
LAGS = 256
LANE = 128
CUT = W + LANE
FOLD = W // 2
BINS = np.concatenate(
    [np.arange(0, 256, 2), np.arange(1, 256, 2), np.arange(256, NB, 2), np.arange(257, NB, 2)]
)


def taper_table():
    return (0.5 - 0.5 * np.cos(np.arange(W) * (2.0 * math.pi / W))).astype(np.float32)[None, :]


def half_tables():
    samples = np.arange(FOLD, dtype=np.int64)[:, None]

    def waves(bins):
        turns = (samples * (B0 + bins)[None, :] % W) * (2.0 * math.pi / W)
        return np.cos(turns), -np.sin(turns)

    even_cos, even_sin = waves(np.arange(0, NB, 2))
    odd_cos, odd_sin = waves(np.arange(1, NB, 2))
    cut = LANE
    columns = [
        even_cos[:, :cut], even_sin[:, :cut], even_cos[:, cut:], even_sin[:, cut:],
        odd_cos[:, :cut], odd_sin[:, :cut], odd_sin[:, cut:], odd_cos[:, cut:],
    ]
    return np.concatenate(columns, axis=1).astype(np.float32).astype(jnp.bfloat16)


def smoothing():
    rows = BINS[:, None]
    cols = BINS[None, :]
    first = np.clip(cols - SMOOTH // 2, 0, NB - SMOOTH)
    return np.where((rows >= first) & (rows < first + SMOOTH), 1.0 / SMOOTH, 0.0).astype(jnp.bfloat16)


def lag_table():
    shifts = np.arange(LAGS, dtype=np.int64) - LAGS // 2
    turns = ((B0 + BINS)[:, None] * shifts[None, :] % W) * (2.0 * math.pi / W)
    table = np.concatenate([np.cos(turns), -np.sin(turns)], axis=0)
    return table.astype(np.float32).astype(jnp.bfloat16)


def spectra_kernel(first, count, late, c_dev, n_src, *refs):
    if late:
        offs, sources, rec, halo, table_v, taper_v, smooth_v, before_s, out_r, out_s, *refs = refs
        sums, diffs, held, offs_v, sources_v, sems = refs
    else:
        offs, sources, rec, table, taper, smooth, out_r, out_s, table_v, taper_v, smooth_v, *refs = refs
        sums, diffs, held, offs_v, sources_v, sems = refs
    begin = first * HOP
    width = (count + 2) * HOP
    copies = []

    def fetch(source, target):
        copy = pltpu.make_async_copy(source, target, sems.at[len(copies)])
        copy.start()
        copies.append(copy)

    fetch(offs, offs_v)
    fetch(sources, sources_v)
    inside = width - (W if late else 0)
    step = inside // 2
    if not late:
        fetch(taper, taper_v)
    for at in range(0, inside, step):
        fetch(rec.at[:, pl.ds(begin + at, step)], held.at[:, pl.ds(at, step)])
    ready = len(copies)
    if late:
        held[:, inside:] = halo[...]
    else:
        rows = FOLD // 4
        for at in range(0, FOLD, rows):
            fetch(table.at[pl.ds(at, rows)], table_v.at[pl.ds(at, rows)])
        fetch(smooth, smooth_v)
    for copy in copies[:ready]:
        copy.wait()

    lanes = lax.broadcasted_iota(jnp.int32, (c_dev, LANE), 1)

    def cut(slot):
        start = slot * HOP + offs_v[first + slot]
        rest = start % LANE
        keep = lanes < LANE - rest
        shift = (LANE - rest) % LANE
        chunk = held[:, pl.ds(pl.multiple_of(start // LANE * LANE, LANE), CUT)].astype(jnp.float32)
        turned = [pltpu.roll(chunk[:, i * LANE : (i + 1) * LANE], shift, 1) for i in range(CUT // LANE)]
        row = pl.ds(pl.multiple_of(slot * c_dev, c_dev), c_dev)
        tiles = FOLD // LANE
        for i in range(tiles):
            lo = slice(i * LANE, (i + 1) * LANE)
            hi = slice(FOLD + i * LANE, FOLD + (i + 1) * LANE)
            near = jnp.where(keep, turned[i], turned[i + 1]) * taper_v[:, lo]
            far = jnp.where(keep, turned[tiles + i], turned[tiles + i + 1]) * taper_v[:, hi]
            sums[row, lo] = (near + far).astype(jnp.bfloat16)
            diffs[row, lo] = (near - far).astype(jnp.bfloat16)

    pl.loop(0, count, unroll=4)(cut)
    for copy in copies[ready:]:
        copy.wait()

    split = 3 * LANE
    even = jnp.dot(sums[...], table_v[:, :split], preferred_element_type=jnp.float32)
    odd = jnp.dot(diffs[...], table_v[:, split:], preferred_element_type=jnp.float32)
    left = lax.broadcasted_iota(jnp.int32, (1, LANE), 1) < LANE // 2
    mixed_even, mixed_odd = even[:, 2 * LANE :], odd[:, 2 * LANE :]
    real = [even[:, :LANE], odd[:, :LANE], jnp.where(left, mixed_even, mixed_odd)]
    swapped = pltpu.roll(jnp.where(left, mixed_odd, mixed_even), LANE // 2, 1)
    imag = [even[:, LANE : 2 * LANE], odd[:, LANE : 2 * LANE], swapped]
    power = jnp.concatenate([r * r + i * i for r, i in zip(real, imag)], axis=1).astype(jnp.bfloat16)
    smoothed = jnp.dot(power, smooth_v[...], preferred_element_type=jnp.float32)
    factor = lax.rsqrt(smoothed + 1e-05)
    for i in range(NB // LANE):
        lo = slice(i * LANE, (i + 1) * LANE)
        hi = slice(NB + i * LANE, NB + (i + 1) * LANE)
        out_r[:, lo] = (real[i] * factor[:, lo]).astype(jnp.bfloat16)
        out_r[:, hi] = (imag[i] * factor[:, lo]).astype(jnp.bfloat16)
    rows = lax.broadcasted_iota(jnp.int32, (n_src * count, 1), 0)
    cols = lax.broadcasted_iota(jnp.int32, (n_src * count, count * c_dev), 1)
    wanted = jnp.zeros_like(rows)
    for s in range(n_src):
        wanted = jnp.where(rows // count == s, sources_v[s] % c_dev + (rows % count) * c_dev, wanted)
    picker = jnp.where(cols == wanted, 1.0, 0.0).astype(jnp.bfloat16)
    at = 0
    if late:
        at = before_s.shape[0]
        out_s[:at] = before_s[...]
    out_s[at:] = jnp.dot(picker, out_r[...], preferred_element_type=jnp.float32).astype(jnp.bfloat16)


def spectra_call(record, offsets, src_idx, tables, first, count, late=None):
    c_dev = record.shape[0]
    n_src = src_idx.shape[0]
    vmem = pl.BlockSpec(memory_space=pltpu.VMEM)
    hbm = pl.BlockSpec(memory_space=pltpu.HBM)
    arrays = [offsets, src_idx, record]
    specs = [hbm] * 3
    out_rows = n_src * count
    if late is None:
        arrays += tables
        specs += [hbm] * 3
    else:
        halo, earlier = late
        arrays += [halo, *tables, earlier]
        specs += [vmem] * 5
        out_rows += earlier.shape[0]
    out_shape = [
        jax.ShapeDtypeStruct((count * c_dev, 2 * NB), jnp.bfloat16),
        jax.ShapeDtypeStruct((out_rows, 2 * NB), jnp.bfloat16),
    ]
    if late is None:
        out_shape += [jax.ShapeDtypeStruct(t.shape, t.dtype) for t in tables]
    return pl.pallas_call(
        functools.partial(spectra_kernel, first, count, late is not None, c_dev, n_src),
        out_shape=out_shape,
        in_specs=specs,
        out_specs=[vmem] * len(out_shape),
        scratch_shapes=[
            pltpu.VMEM((count * c_dev, FOLD), jnp.bfloat16),
            pltpu.VMEM((count * c_dev, FOLD), jnp.bfloat16),
            pltpu.VMEM((c_dev, (count + 2) * HOP), jnp.bfloat16),
            pltpu.SMEM(offsets.shape, jnp.int32),
            pltpu.SMEM(src_idx.shape, jnp.int32),
            pltpu.SemaphoreType.DMA((16,)),
        ],
        compiler_params=pltpu.CompilerParams(vmem_limit_bytes=24 << 20),
        cost_estimate=pl.CostEstimate(
            flops=2 * count * c_dev * W * 2 * NB, bytes_accessed=4 << 20, transcendentals=0
        ),
        name="spectra",
    )(*arrays)


def cross_kernel(n_list, sides, cuts, n_src, c_dev, scale, has_before, last, *refs):
    srcs, refs = refs[:n_list], refs[n_list:]
    recs = []
    for parts in sides:
        recs.append([(refs[i], part) for i, part in enumerate(parts)])
        refs = refs[len(parts) :]
    if has_before:
        before, *refs = refs
    if last:
        ltab, out, wide, cross = refs
    else:
        out, wide = refs
    n_win = cuts[-1]
    for k in range(n_list):
        wide[k * n_src * n_win : (k + 1) * n_src * n_win, :] = srcs[k][0].astype(jnp.float32)
    tiles = NB // LANE
    block = 8 if n_list * n_src % 8 == 0 else n_src
    groups = block // n_src
    n_side = len(sides)

    @pl.loop(0, n_list // groups * tiles)
    def _(step):
        group = step // tiles * groups
        lo = pl.ds(pl.multiple_of(step % tiles * LANE, LANE), LANE)
        hi = pl.ds(pl.multiple_of(step % tiles * LANE + NB, LANE), LANE)
        base = pl.multiple_of(group * (n_src * n_win), 8)
        src = wide.at[pl.ds(base, groups * n_src * n_win)]
        for q, parts in enumerate(recs):
            rows = [
                pl.ds(pl.multiple_of(((group * n_src + s) * n_side + q) * c_dev, c_dev), c_dev)
                for s in range(block)
            ]
            sums = [[before[r, lo], before[r, hi]] if has_before else [0.0, 0.0] for r in rows]
            for rec, part in parts:
                start, stop = cuts[part], cuts[part + 1]
                for w in range(stop - start):
                    row = slice(w * c_dev, (w + 1) * c_dev)
                    rec_real = rec[row, lo].astype(jnp.float32)
                    rec_imag = rec[row, hi].astype(jnp.float32)
                    for s in range(block):
                        at = s // n_src * n_src * n_win
                        at += start * n_src + s % n_src * (stop - start) + w
                        src_real = src[at : at + 1, lo]
                        src_imag = src[at : at + 1, hi]
                        sums[s][0] += src_real * rec_real + src_imag * rec_imag
                        sums[s][1] += src_real * rec_imag - src_imag * rec_real
            target = cross if last else out
            for s in range(block):
                for i, place in enumerate((lo, hi)):
                    target[rows[s], place] = (sums[s][i] + jnp.zeros((c_dev, LANE), jnp.float32)).astype(
                        target.dtype
                    )

    if last:
        lagged = jnp.dot(cross[...], ltab[...], preferred_element_type=jnp.float32)
        out[...] = (lagged * scale).astype(jnp.bfloat16)


def cross_call(srcs, sides, cuts, n_src, c_dev, scale, before=None, ltab=None):
    n_list, n_side = len(srcs), len(sides)
    groups = srcs[0].shape[0]
    last = ltab is not None
    rows = n_list * n_src * n_side * c_dev
    whole = pl.BlockSpec(memory_space=pltpu.VMEM)
    src_spec = pl.BlockSpec((1,) + srcs[0].shape[1:], lambda g: (g, 0, 0))
    row_block = lambda width: pl.BlockSpec((rows, width), lambda g: (g, 0))
    arrays, specs = list(srcs), [src_spec] * n_list
    for parts in sides:
        arrays += list(parts.values())
        specs += [whole] * len(parts)
    if before is not None:
        arrays.append(before)
        specs.append(row_block(2 * NB))
    scratch = [pltpu.VMEM((n_list * n_src * cuts[-1], 2 * NB), jnp.float32)]
    if last:
        arrays.append(ltab)
        specs.append(whole)
        scratch.append(pltpu.VMEM((rows, 2 * NB), jnp.bfloat16))
        out_shape = jax.ShapeDtypeStruct((groups * rows, LAGS), jnp.bfloat16)
    else:
        out_shape = jax.ShapeDtypeStruct((groups * rows, 2 * NB), jnp.float32)
    windows = sum(cuts[p + 1] - cuts[p] for parts in sides for p in parts) // n_side
    return pl.pallas_call(
        functools.partial(
            cross_kernel, n_list, [list(p) for p in sides], cuts, n_src, c_dev, scale,
            before is not None, last,
        ),
        grid=(groups,),
        out_shape=out_shape,
        in_specs=specs,
        out_specs=row_block(out_shape.shape[1]),
        scratch_shapes=scratch,
        compiler_params=pltpu.CompilerParams(vmem_limit_bytes=24 << 20),
        cost_estimate=pl.CostEstimate(
            flops=groups * rows * windows * NB * 40, bytes_accessed=4 << 20, transcendentals=0
        ),
        name="cross",
    )(*arrays)


def body(record, offsets, src_idx):
    c_dev = record.shape[0]
    n_win = offsets.shape[0]
    n_src = src_idx.shape[0]
    n_tm = lax.axis_size("tm")
    n_fibre = lax.axis_size("fibre")
    n_group = n_fibre // 2
    fibre = lax.axis_index("fibre")
    tm = lax.axis_index("tm")
    early = n_win * 5 // 8
    cuts = (0, early, n_win)
    scale = 1.0 / math.sqrt(n_win * n_tm * NB)
    tables = [jnp.asarray(t) for t in (half_tables(), taper_table(), smoothing())]
    ltab = jnp.asarray(lag_table())
    direct = n_group == 4 and n_tm == 4

    def trade(array, by):
        return lax.ppermute(array, "fibre", [(i, i ^ by) for i in range(n_fibre)])

    halo = lax.ppermute(record[:, :W], "tm", [(i, i - 1) for i in range(1, n_tm)])
    rec_a, src_a, *tables = spectra_call(record, offsets, src_idx, tables, 0, early)
    far_a = trade(rec_a, 1)
    rec_b, src = spectra_call(record, offsets, src_idx, tables, early, n_win - early, (halo, src_a))
    cross = functools.partial(cross_call, cuts=cuts, n_src=n_src, c_dev=c_dev, scale=scale)
    if direct:
        by_2 = trade(src, 4)
        by_1 = trade(src, 2)
        far_b = trade(rec_b, 1)
        by_3 = trade(by_2, 2)
        srcs = [s[None] for s in (src, by_1, by_2, by_3)]
        part = cross(srcs[:3], [{0: rec_a, 1: rec_b}, {0: far_a}])
        near = cross(srcs[:3], [{}, {1: far_b}], before=part, ltab=ltab)
        last = cross(srcs[3:], [{0: rec_a, 1: rec_b}, {0: far_a, 1: far_b}], ltab=ltab)
        lagged = jnp.concatenate([near, last], axis=0)
    else:
        ranks = [[2 * j + p for j in range(n_group)] for p in range(2)]
        srcs = [lax.all_gather(src, "fibre", axis=0, axis_index_groups=ranks)]
        far_b = trade(rec_b, 1)
        lagged = cross(srcs, [{0: rec_a, 1: rec_b}, {0: far_a, 1: far_b}], ltab=ltab)
    lagged = lagged.reshape(n_group, n_src, 2, c_dev, LAGS)

    def piece(owner, side):
        if direct:
            return lax.dynamic_index_in_dim(lagged[:, :, side], (fibre // 2) ^ owner, 0, keepdims=True)
        share = n_group // n_tm
        return lax.dynamic_slice_in_dim(lagged[:, :, side], owner * share, share, 0)

    totals = []
    for side in range(2):
        total = None
        for k in range(n_tm):
            mine = piece(tm ^ k, side)
            if side or k:
                pairs = [
                    (i * n_tm + t, (i ^ side) * n_tm + (t ^ k)) for i in range(n_fibre) for t in range(n_tm)
                ]
                mine = lax.ppermute(mine, ("fibre", "tm"), pairs)
            mine = mine.astype(jnp.float32)
            total = mine if total is None else total + mine
        totals.append(total)
    even = fibre % 2 == 0
    near, far = totals
    out = jnp.stack([jnp.where(even, near, far), jnp.where(even, far, near)], axis=1)
    return out.reshape(-1, c_dev, LAGS)


def solution(mesh):
    return jax.shard_map(
        body,
        mesh=mesh,
        in_specs=(P("fibre", "tm"), P("tm"), P("fibre")),
        out_specs=P("tm", "fibre", None),
        check_vma=False,
    )
```

time: 52.7 us -> 57.5 us (1.091)
  the two profiles are of different devices: /device:TPU:11 before, /device:TPU:0 now
where the time goes in v3:
time: 57.5 us; the launch traced here: 57.2 us
  waiting for transfers between devices  19.1 us (33%)
  starting transfers between devices  16.2 us (28%)
  Pallas kernels  14.5 us (25%)
  local copies, waits for them, and re-layouts  6.49 us (11%)
  other arithmetic  0.72 us (1%)
    ppermute x5, waiting for transfers between devices, trade(): return lax.ppermute(array, 'fibre', [(i, i ^ by) for i in range(n_fibre)])  16.3 us
    pallas_call x3, Pallas kernels, cross_call(): pl.pallas_call(functools.partial(cross_kernel, n_list, [list(p) for p in...  8.95 us
    ppermute x5, starting transfers between devices, trade(): return lax.ppermute(array, 'fibre', [(i, i ^ by) for i in range(n_fibre)])  8.22 us
    ppermute x7, starting transfers between devices, body(): mine = lax.ppermute(mine, ('fibre', 'tm'), pairs)  6.66 us
    unnamed x14, local copies, waits for them, and re-layouts  5.6 us
    pallas_call x2, Pallas kernels, spectra_call(): pl.pallas_call(functools.partial(spectra_kernel, first, count, late is no...  5.58 us
    ppermute x7, waiting for transfers between devices, body(): mine = lax.ppermute(mine, ('fibre', 'tm'), pairs)  2.83 us
    ppermute x1, starting transfers between devices, body(): lax.ppermute(record[:, :W], 'tm', [(i, i - 1) for i in range(1, n_tm)])  1.28 us
  transfers between devices with their start and end apart: 13, of which 6 were waited for; matrix products, arithmetic and copies ran while one was open for 0% of the time, Pallas kernels for 14%

profile of v3, /device:TPU:0, one launch (start us, length us, event | category | flops | bytes accessed | tf_op | source)
XLA Modules:
  0.0 57.2 jit_solution(13159686488129971020)
XLA Ops:
  0.0 0.8 %slice.6 = bf16[16,2048]{1,0:T(8,128)(2,1)S(1)} slice(bf16[16,32768]{1,0:T(8,128)(2,1)} %refs_2_.3), slice={[0:16], [0:2048]} | slice | bytes 131072 | tf_op jit(solution)/shard_map/slice | solution.py:310
  0.8 1.3 %collective-permute-start = (bf16[16,2048]{1,0:T(8,128)(2,1)S(1)}, bf16[16,2048]{1,0:T(8,128)(2,1)S(1)}, u32[]{:S(2)}, u32[]{:S(2)}) collective-permute-start(bf16[16,2048]{1,0:T(8,128)(2,1)S(1)} %slice.6), channel_id=1, source_target_pairs={{1,0},{2,1},{3,2},{5,4},{6,5},{7,6},{9,8},{10,9},{11,10},{13,12},{... | collective-permute-start | bytes 196616 | tf_op jit(solution)/shard_map/ppermute | solution.py:310
  2.1 0.0 copy-start.1
  2.1 1.2 %copy-done.1 = bf16[16,32768]{1,0:T(8,128)(2,1)S(1)} copy-done((bf16[16,32768]{1,0:T(8,128)(2,1)S(1)}, bf16[16,32768]{1,0:T(8,128)(2,1)}, u32[]{:S(2)}) %copy-start.1) | copy-done | bytes 1048600
  3.4 0.0 copy-start.2
  3.4 0.7 %copy-done.2 = s32[32]{0:T(128)S(1)} copy-done((s32[32]{0:T(128)S(1)}, s32[32]{0:T(128)}, u32[]{:S(2)}) %copy-start.2) | copy-done | bytes 152
  4.0 0.0 copy-start.3
  4.0 0.7 %copy-done.3 = s32[4]{0:T(128)S(1)} copy-done((s32[4]{0:T(128)S(1)}, s32[4]{0:T(128)}, u32[]{:S(2)}) %copy-start.3) | copy-done | bytes 40
  4.7 0.0 copy-start.4
  4.7 1.4 %copy-done.4 = bf16[1024,768]{1,0:T(8,128)(2,1)S(1)} copy-done((bf16[1024,768]{1,0:T(8,128)(2,1)S(1)}, bf16[1024,768]{1,0:T(8,128)(2,1)}, u32[]{:S(2)}) %copy-start.4) | copy-done | bytes 1572888
  6.1 0.0 copy-start.5
  6.1 1.0 %copy-done.5 = bf16[384,384]{1,0:T(8,128)(2,1)S(1)} copy-done((bf16[384,384]{1,0:T(8,128)(2,1)S(1)}, bf16[384,384]{1,0:T(8,128)(2,1)}, u32[]{:S(2)}) %copy-start.5) | copy-done | bytes 294936
  7.0 0.0 copy-start.6
  7.0 0.7 %copy-done.6 = f32[1,2048]{1,0:T(1,128)S(1)} copy-done((f32[1,2048]{1,0:T(1,128)S(1)}, f32[1,2048]{1,0:T(1,128)}, u32[]{:S(2)}) %copy-start.6) | copy-done | bytes 8216
  7.7 3.4 %spectra.2 = (bf16[320,768]{1,0:T(8,128)(2,1)S(1)}, bf16[80,768]{1,0:T(8,128)(2,1)S(1)}, bf16[1024,768]{1,0:T(8,128)(2,1)S(1)}, f32[1,2048]{1,0:T(1,128)S(1)}, bf16[384,384]{1,0:T(8,128)(2,1)S(1)}) custom-call(s32[32]{0:T(128)S(1)} %copy-done.2, s32[4]{0:T(128)S(1)} %copy-done.3, bf16[16,32768]{1,0:T(8,128)(2,1)S(1)} %copy-done.1, ...), custom_call_target="tpu_custom_call" | custom-call | flops 1006632960 | bytes 4194304 | tf_op jit(solution)/shard_map/spectra/pallas_call | solution.py:170
  11.1 3.0 %collective-permute-start.4 = (bf16[320,768]{1,0:T(8,128)(2,1)S(1)}, bf16[320,768]{1,0:T(8,128)(2,1)S(1)}, u32[]{:S(2)}, u32[]{:S(2)}) collective-permute-start(bf16[320,768]{1,0:T(8,128)(2,1)S(1)} %get-tuple-element.18.refs_3_.refs_1_), channel_id=1, source_target_pairs={{0,4},{4,0},{8,12},{12,8},{16,20},{20,16},{24,28},{28,24},{1,5},{5... | collective-permute-start | bytes 1474568 | tf_op jit(solution)/shard_map/ppermute | solution.py:308
  14.1 0.0 collective-permute-done.refs_3_
  14.1 0.0 copy-start
  14.1 2.2 %spectra.3 = (bf16[192,768]{1,0:T(8,128)(2,1)S(1)}, bf16[128,768]{1,0:T(8,128)(2,1)S(1)}) custom-call(s32[32]{0:T(128)S(1)} %copy-done.2, s32[4]{0:T(128)S(1)} %copy-done.3, bf16[16,32768]{1,0:T(8,128)(2,1)S(1)} %copy-done.1, bf16[16,2048]{1,0:T(8,128)(2,1)S(1)} %collective-permute-done.refs_3_, bf16[1024,768]{1,0:T(8,128)(2,1)S(1)} %get-tuple-element.12.refs_4_, ...), custom_call_target="tpu_custom_call" | custom-call | flops 603979776 | bytes 4194304 | tf_op jit(solution)/shard_map/spectra/pallas_call | solution.py:170
  16.3 2.6 %collective-permute-start.2 = (bf16[128,768]{1,0:T(8,128)(2,1)S(1)}, bf16[128,768]{1,0:T(8,128)(2,1)S(1)}, u32[]{:S(2)}, u32[]{:S(2)}) collective-permute-start(bf16[128,768]{1,0:T(8,128)(2,1)S(1)} %get-tuple-element.16), channel_id=1, source_target_pairs={{0,16},{4,20},{8,24},{12,28},{16,0},{20,4},{24,8},{28,12},{1,17},{... | collective-permute-start | bytes 589832 | tf_op jit(solution)/shard_map/ppermute | solution.py:308
  19.0 0.5 collective-permute-start.3
  19.5 9.6 %collective-permute-done.2 = bf16[128,768]{1,0:T(8,128)(2,1)S(1)} collective-permute-done((bf16[128,768]{1,0:T(8,128)(2,1)S(1)}, bf16[128,768]{1,0:T(8,128)(2,1)S(1)}, u32[]{:S(2)}, u32[]{:S(2)}) %collective-permute-start.2) | collective-permute-done | bytes 196640 | tf_op jit(solution)/shard_map/ppermute | solution.py:308
  29.2 0.7 %collective-permute-start.5 = (bf16[128,768]{1,0:T(8,128)(2,1)S(1)}, bf16[128,768]{1,0:T(8,128)(2,1)S(1)}, u32[]{:S(2)}, u32[]{:S(2)}) collective-permute-start(bf16[128,768]{1,0:T(8,128)(2,1)S(1)} %collective-permute-done.2), channel_id=1, source_target_pairs={{0,8},{4,12},{8,0},{12,4},{16,24},{20,28},{24,16},{28,20},{1,9},{5... | collective-permute-start | bytes 589832 | tf_op jit(solution)/shard_map/ppermute | solution.py:308
  29.8 1.4 %collective-permute-start.1 = (bf16[128,768]{1,0:T(8,128)(2,1)S(1)}, bf16[128,768]{1,0:T(8,128)(2,1)S(1)}, u32[]{:S(2)}, u32[]{:S(2)}) collective-permute-start(bf16[128,768]{1,0:T(8,128)(2,1)S(1)} %get-tuple-element.16), channel_id=1, source_target_pairs={{0,8},{4,12},{8,0},{12,4},{16,24},{20,28},{24,16},{28,20},{1,9},{5... | collective-permute-start | bytes 589832 | tf_op jit(solution)/shard_map/ppermute | solution.py:308
  31.2 1.0 %collective-permute-done.3.refs_3_.refs_4_ = bf16[192,768]{1,0:T(8,128)(2,1)S(1)} collective-permute-done((bf16[192,768]{1,0:T(8,128)(2,1)S(1)}, bf16[192,768]{1,0:T(8,128)(2,1)S(1)}, u32[]{:S(2)}, u32[]{:S(2)}) %collective-permute-start.3) | collective-permute-done | bytes 294944 | tf_op jit(solution)/shard_map/ppermute | solution.py:308
  32.2 4.8 %collective-permute-done.5 = bf16[128,768]{1,0:T(8,128)(2,1)S(1)} collective-permute-done((bf16[128,768]{1,0:T(8,128)(2,1)S(1)}, bf16[128,768]{1,0:T(8,128)(2,1)S(1)}, u32[]{:S(2)}, u32[]{:S(2)}) %collective-permute-start.5) | collective-permute-done | bytes 196640 | tf_op jit(solution)/shard_map/ppermute | solution.py:308
  36.9 0.0 collective-permute-done.4.refs_5_.refs_3_
  36.9 0.0 copy-done
  37.0 2.3 %cross.5 = bf16[128,256]{1,0:T(8,128)(2,1)S(1)} custom-call(bf16[1,128,768]{2,1,0:T(8,128)(2,1)S(1)} %bitcast.37, bf16[320,768]{1,0:T(8,128)(2,1)S(1)} %get-tuple-element.18.refs_3_.refs_1_, bf16[192,768]{1,0:T(8,128)(2,1)S(1)} %get-tuple-element.17.refs_4_.refs_2_, bf16[320,768]{1,0:T(8,128)(2,1)S(1)} %collective-permute-done.4.refs_5_.refs_3_, ...), custom_call_target="tpu_custom_call" | custom-call | flops 62914560 | bytes 4194304 | tf_op jit(solution)/shard_map/cross/pallas_call | solution.py:273
  39.3 0.9 %collective-permute-done.1 = bf16[128,768]{1,0:T(8,128)(2,1)S(1)} collective-permute-done((bf16[128,768]{1,0:T(8,128)(2,1)S(1)}, bf16[128,768]{1,0:T(8,128)(2,1)S(1)}, u32[]{:S(2)}, u32[]{:S(2)}) %collective-permute-start.1) | collective-permute-done | bytes 196640 | tf_op jit(solution)/shard_map/ppermute | solution.py:308
  40.2 5.0 %cross.3.refs_4_ = f32[384,768]{1,0:T(8,128)S(1)} custom-call(bf16[1,128,768]{2,1,0:T(8,128)(2,1)S(1)} %bitcast.31, bf16[1,128,768]{2,1,0:T(8,128)(2,1)S(1)} %bitcast.35, bf16[1,128,768]{2,1,0:T(8,128)(2,1)S(1)} %bitcast.33, bf16[320,768]{1,0:T(8,128)(2,1)S(1)} %get-tuple-element.18.refs_3_.refs_1_, bf16[192,768]{1,0:T(8,128)(2,1)S(1)} %get-tuple-element.17.refs_4_.refs_2_, ...), custom_call_target="tpu_custom_call" | custom-call | flops 153354240 | bytes 4194304 | tf_op jit(solution)/shard_map/cross/pallas_call | solution.py:273
  45.2 1.7 %cross.4 = bf16[384,256]{1,0:T(8,128)(2,1)S(1)} custom-call(bf16[1,128,768]{2,1,0:T(8,128)(2,1)S(1)} %bitcast.32, bf16[1,128,768]{2,1,0:T(8,128)(2,1)S(1)} %bitcast.36, bf16[1,128,768]{2,1,0:T(8,128)(2,1)S(1)} %bitcast.34, bf16[192,768]{1,0:T(8,128)(2,1)S(1)} %collective-permute-done.3.refs_3_.refs_4_, f32[384,768]{1,0:T(8,128)S(1)} %cross.3.refs_4_, ...), custom_call_target="tpu_custom_call" | custom-call | flops 35389440 | bytes 4194304 | tf_op jit(solution)/shard_map/cross/pallas_call | solution.py:273
  46.9 0.4 collective-permute-start.9
  47.3 0.0 collective-permute-start.12
  47.3 2.1 %collective-permute-start.11 = (bf16[1,4,16,256]{3,2,1,0:T(8,128)(2,1)S(1)}, bf16[1,4,16,256]{3,2,1,0:T(8,128)(2,1)S(1)}, u32[]{:S(2)}, u32[]{:S(2)}) collective-permute-start(bf16[1,4,16,256]{3,2,1,0:T(8,128)(2,1)S(1)} %get-tuple-element.28), channel_id=1, source_target_pairs={{0,6},{1,7},{2,4},{3,5},{4,2},{5,3},{6,0},{7,1},{8,14},{9,15},{10,... | collective-permute-start | bytes 98312 | tf_op jit(solution)/shard_map/ppermute | solution.py:347
  49.4 2.0 %collective-permute-start.10 = (bf16[1,4,16,256]{3,2,1,0:T(8,128)(2,1)S(1)}, bf16[1,4,16,256]{3,2,1,0:T(8,128)(2,1)S(1)}, u32[]{:S(2)}, u32[]{:S(2)}) collective-permute-start(bf16[1,4,16,256]{3,2,1,0:T(8,128)(2,1)S(1)} %get-tuple-element.29), channel_id=1, source_target_pairs={{0,5},{1,4},{2,7},{3,6},{4,1},{5,0},{6,3},{7,2},{8,13},{9,12},{10,... | collective-permute-start | bytes 98312 | tf_op jit(solution)/shard_map/ppermute | solution.py:347
  51.4 0.1 collective-permute-start.6
  51.5 0.0 collective-permute-done.9
  51.5 1.0 %collective-permute-start.8 = (bf16[1,4,16,256]{3,2,1,0:T(8,128)(2,1)S(1)}, bf16[1,4,16,256]{3,2,1,0:T(8,128)(2,1)S(1)}, u32[]{:S(2)}, u32[]{:S(2)}) collective-permute-start(bf16[1,4,16,256]{3,2,1,0:T(8,128)(2,1)S(1)} %get-tuple-element.24), channel_id=1, source_target_pairs={{0,3},{1,2},{2,1},{3,0},{4,7},{5,6},{6,5},{7,4},{8,11},{9,10},{10,... | collective-permute-start | bytes 98312 | tf_op jit(solution)/shard_map/ppermute | solution.py:347
  52.5 0.0 collective-permute-done.12
  52.5 1.1 %collective-permute-start.7 = (bf16[1,4,16,256]{3,2,1,0:T(8,128)(2,1)S(1)}, bf16[1,4,16,256]{3,2,1,0:T(8,128)(2,1)S(1)}, u32[]{:S(2)}, u32[]{:S(2)}) collective-permute-start(bf16[1,4,16,256]{3,2,1,0:T(8,128)(2,1)S(1)} %get-tuple-element.25), channel_id=1, source_target_pairs={{0,2},{1,3},{2,0},{3,1},{4,6},{5,7},{6,4},{7,5},{8,10},{9,11},{10,... | collective-permute-start | bytes 98312 | tf_op jit(solution)/shard_map/ppermute | solution.py:347
  53.6 0.0 collective-permute-done.11
  53.6 0.0 collective-permute-done.10
  53.6 0.0 collective-permute-done.6
  53.6 1.3 %collective-permute-done.8 = bf16[1,4,16,256]{3,2,1,0:T(8,128)(2,1)S(1)} collective-permute-done((bf16[1,4,16,256]{3,2,1,0:T(8,128)(2,1)S(1)}, bf16[1,4,16,256]{3,2,1,0:T(8,128)(2,1)S(1)}, u32[]{:S(2)}, u32[]{:S(2)}) %collective-permute-start.8) | collective-permute-done | bytes 32800 | tf_op jit(solution)/shard_map/ppermute | solution.py:347
  54.9 1.6 %collective-permute-done.7 = bf16[1,4,16,256]{3,2,1,0:T(8,128)(2,1)S(1)} collective-permute-done((bf16[1,4,16,256]{3,2,1,0:T(8,128)(2,1)S(1)}, bf16[1,4,16,256]{3,2,1,0:T(8,128)(2,1)S(1)}, u32[]{:S(2)}, u32[]{:S(2)}) %collective-permute-start.7) | collective-permute-done | bytes 32800 | tf_op jit(solution)/shard_map/ppermute | solution.py:347
  56.5 0.7 %pad_maximum_fusion.1 = f32[1,2,4,16,256]{4,3,2,1,0:T(8,128)} fusion(f32[1,1,4,16,256]{4,3,2,1,0:T(8,128)S(1)} %get-tuple-element.20, f32[1,1,4,16,256]{4,3,2,1,0:T(8,128)S(1)} %get-tuple-element.19), kind=kLoop, calls=%fused_computation.1 | loop fusion | flops 32768 | bytes 262144 | tf_op jit(solution)/shard_map/stack | solution.py:353
  (5 shorter events, 0.1 us)
Async XLA Ops:
  0.8 13.3 %collective-permute-start = (bf16[16,2048]{1,0:T(8,128)(2,1)S(1)}, bf16[16,2048]{1,0:T(8,128)(2,1)S(1)}, u32[]{:S(2)}, u32[]{:S(2)}) collective-permute-start(bf16[16,2048]{1,0:T(8,128)(2,1)S(1)} %slice.6), channel_id=1, source_target_pairs={{1,0},{2,1},{3,2},{5,4},{6,5},{7,6},{9,8},{10,9},{11,10},{13,12},{... | collective-permute-start | bytes 196616 | tf_op jit(solution)/shard_map/ppermute | solution.py:310
  2.1 1.2 %copy-start.1 = (bf16[16,32768]{1,0:T(8,128)(2,1)S(1)}, bf16[16,32768]{1,0:T(8,128)(2,1)}, u32[]{:S(2)}) copy-start(bf16[16,32768]{1,0:T(8,128)(2,1)} %refs_2_.3) | copy-start | bytes 3145732
  3.4 0.7 %copy-start.2 = (s32[32]{0:T(128)S(1)}, s32[32]{0:T(128)}, u32[]{:S(2)}) copy-start(s32[32]{0:T(128)} %refs_0_.3) | copy-start | bytes 388
  4.0 0.7 %copy-start.3 = (s32[4]{0:T(128)S(1)}, s32[4]{0:T(128)}, u32[]{:S(2)}) copy-start(s32[4]{0:T(128)} %refs_1_.3) | copy-start | bytes 52
  4.7 1.4 %copy-start.4 = (bf16[1024,768]{1,0:T(8,128)(2,1)S(1)}, bf16[1024,768]{1,0:T(8,128)(2,1)}, u32[]{:S(2)}) copy-start(bf16[1024,768]{1,0:T(8,128)(2,1)} %constant.86.clone.refs_3_) | copy-start | bytes 4718596
  6.1 1.0 %copy-start.5 = (bf16[384,384]{1,0:T(8,128)(2,1)S(1)}, bf16[384,384]{1,0:T(8,128)(2,1)}, u32[]{:S(2)}) copy-start(bf16[384,384]{1,0:T(8,128)(2,1)} %constant.88.clone.refs_5_) | copy-start | bytes 884740
  7.0 0.7 %copy-start.6 = (f32[1,2048]{1,0:T(1,128)S(1)}, f32[1,2048]{1,0:T(1,128)}, u32[]{:S(2)}) copy-start(f32[1,2048]{1,0:T(1,128)} %constant.87.clone.refs_4_) | copy-start | bytes 24580
  11.1 25.8 %collective-permute-start.4 = (bf16[320,768]{1,0:T(8,128)(2,1)S(1)}, bf16[320,768]{1,0:T(8,128)(2,1)S(1)}, u32[]{:S(2)}, u32[]{:S(2)}) collective-permute-start(bf16[320,768]{1,0:T(8,128)(2,1)S(1)} %get-tuple-element.18.refs_3_.refs_1_), channel_id=1, source_target_pairs={{0,4},{4,0},{8,12},{12,8},{16,20},{20,16},{24,28},{28,24},{1,5},{5... | collective-permute-start | bytes 1474568 | tf_op jit(solution)/shard_map/ppermute | solution.py:308
  14.1 22.8 %copy-start = (bf16[768,256]{1,0:T(8,128)(2,1)S(1)}, bf16[768,256]{1,0:T(8,128)(2,1)}, u32[]{:S(2)}) copy-start(bf16[768,256]{1,0:T(8,128)(2,1)} %constant.89.clone.refs_5_) | copy-start | bytes 1179652
  16.3 12.8 %collective-permute-start.2 = (bf16[128,768]{1,0:T(8,128)(2,1)S(1)}, bf16[128,768]{1,0:T(8,128)(2,1)S(1)}, u32[]{:S(2)}, u32[]{:S(2)}) collective-permute-start(bf16[128,768]{1,0:T(8,128)(2,1)S(1)} %get-tuple-element.16), channel_id=1, source_target_pairs={{0,16},{4,20},{8,24},{12,28},{16,0},{20,4},{24,8},{28,12},{1,17},{... | collective-permute-start | bytes 589832 | tf_op jit(solution)/shard_map/ppermute | solution.py:308
  19.0 13.2 %collective-permute-start.3 = (bf16[192,768]{1,0:T(8,128)(2,1)S(1)}, bf16[192,768]{1,0:T(8,128)(2,1)S(1)}, u32[]{:S(2)}, u32[]{:S(2)}) collective-permute-start(bf16[192,768]{1,0:T(8,128)(2,1)S(1)} %get-tuple-element.17.refs_4_.refs_2_), channel_id=1, source_target_pairs={{0,4},{4,0},{8,12},{12,8},{16,20},{20,16},{24,28},{28,24},{1,5},{5... | collective-permute-start | bytes 884744 | tf_op jit(solution)/shard_map/ppermute | solution.py:308
  29.2 7.8 %collective-permute-start.5 = (bf16[128,768]{1,0:T(8,128)(2,1)S(1)}, bf16[128,768]{1,0:T(8,128)(2,1)S(1)}, u32[]{:S(2)}, u32[]{:S(2)}) collective-permute-start(bf16[128,768]{1,0:T(8,128)(2,1)S(1)} %collective-permute-done.2), channel_id=1, source_target_pairs={{0,8},{4,12},{8,0},{12,4},{16,24},{20,28},{24,16},{28,20},{1,9},{5... | collective-permute-start | bytes 589832 | tf_op jit(solution)/shard_map/ppermute | solution.py:308
  29.8 10.3 %collective-permute-start.1 = (bf16[128,768]{1,0:T(8,128)(2,1)S(1)}, bf16[128,768]{1,0:T(8,128)(2,1)S(1)}, u32[]{:S(2)}, u32[]{:S(2)}) collective-permute-start(bf16[128,768]{1,0:T(8,128)(2,1)S(1)} %get-tuple-element.16), channel_id=1, source_target_pairs={{0,8},{4,12},{8,0},{12,4},{16,24},{20,28},{24,16},{28,20},{1,9},{5... | collective-permute-start | bytes 589832 | tf_op jit(solution)/shard_map/ppermute | solution.py:308
  46.9 4.5 %collective-permute-start.9 = (bf16[1,4,16,256]{3,2,1,0:T(8,128)(2,1)S(1)}, bf16[1,4,16,256]{3,2,1,0:T(8,128)(2,1)S(1)}, u32[]{:S(2)}, u32[]{:S(2)}) collective-permute-start(bf16[1,4,16,256]{3,2,1,0:T(8,128)(2,1)S(1)} %get-tuple-element.26), channel_id=1, source_target_pairs={{0,4},{1,5},{2,6},{3,7},{4,0},{5,1},{6,2},{7,3},{8,12},{9,13},{10,... | collective-permute-start | bytes 98312 | tf_op jit(solution)/shard_map/ppermute | solution.py:347
  47.3 5.2 %collective-permute-start.12 = (bf16[1,4,16,256]{3,2,1,0:T(8,128)(2,1)S(1)}, bf16[1,4,16,256]{3,2,1,0:T(8,128)(2,1)S(1)}, u32[]{:S(2)}, u32[]{:S(2)}) collective-permute-start(bf16[1,4,16,256]{3,2,1,0:T(8,128)(2,1)S(1)} %get-tuple-element.27), channel_id=1, source_target_pairs={{0,7},{1,6},{2,5},{3,4},{4,3},{5,2},{6,1},{7,0},{8,15},{9,14},{10,... | collective-permute-start | bytes 98312 | tf_op jit(solution)/shard_map/ppermute | solution.py:347
  47.3 6.3 %collective-permute-start.11 = (bf16[1,4,16,256]{3,2,1,0:T(8,128)(2,1)S(1)}, bf16[1,4,16,256]{3,2,1,0:T(8,128)(2,1)S(1)}, u32[]{:S(2)}, u32[]{:S(2)}) collective-permute-start(bf16[1,4,16,256]{3,2,1,0:T(8,128)(2,1)S(1)} %get-tuple-element.28), channel_id=1, source_target_pairs={{0,6},{1,7},{2,4},{3,5},{4,2},{5,3},{6,0},{7,1},{8,14},{9,15},{10,... | collective-permute-start | bytes 98312 | tf_op jit(solution)/shard_map/ppermute | solution.py:347
  49.4 4.2 %collective-permute-start.10 = (bf16[1,4,16,256]{3,2,1,0:T(8,128)(2,1)S(1)}, bf16[1,4,16,256]{3,2,1,0:T(8,128)(2,1)S(1)}, u32[]{:S(2)}, u32[]{:S(2)}) collective-permute-start(bf16[1,4,16,256]{3,2,1,0:T(8,128)(2,1)S(1)} %get-tuple-element.29), channel_id=1, source_target_pairs={{0,5},{1,4},{2,7},{3,6},{4,1},{5,0},{6,3},{7,2},{8,13},{9,12},{10,... | collective-permute-start | bytes 98312 | tf_op jit(solution)/shard_map/ppermute | solution.py:347
  51.4 2.2 %collective-permute-start.6 = (bf16[1,4,16,256]{3,2,1,0:T(8,128)(2,1)S(1)}, bf16[1,4,16,256]{3,2,1,0:T(8,128)(2,1)S(1)}, u32[]{:S(2)}, u32[]{:S(2)}) collective-permute-start(bf16[1,4,16,256]{3,2,1,0:T(8,128)(2,1)S(1)} %get-tuple-element.23), channel_id=1, source_target_pairs={{0,1},{1,0},{2,3},{3,2},{4,5},{5,4},{6,7},{7,6},{8,9},{9,8},{10,11... | collective-permute-start | bytes 98312 | tf_op jit(solution)/shard_map/ppermute | solution.py:347
  51.5 3.4 %collective-permute-start.8 = (bf16[1,4,16,256]{3,2,1,0:T(8,128)(2,1)S(1)}, bf16[1,4,16,256]{3,2,1,0:T(8,128)(2,1)S(1)}, u32[]{:S(2)}, u32[]{:S(2)}) collective-permute-start(bf16[1,4,16,256]{3,2,1,0:T(8,128)(2,1)S(1)} %get-tuple-element.24), channel_id=1, source_target_pairs={{0,3},{1,2},{2,1},{3,0},{4,7},{5,6},{6,5},{7,4},{8,11},{9,10},{10,... | collective-permute-start | bytes 98312 | tf_op jit(solution)/shard_map/ppermute | solution.py:347
  52.5 3.9 %collective-permute-start.7 = (bf16[1,4,16,256]{3,2,1,0:T(8,128)(2,1)S(1)}, bf16[1,4,16,256]{3,2,1,0:T(8,128)(2,1)S(1)}, u32[]{:S(2)}, u32[]{:S(2)}) collective-permute-start(bf16[1,4,16,256]{3,2,1,0:T(8,128)(2,1)S(1)} %get-tuple-element.25), channel_id=1, source_target_pairs={{0,2},{1,3},{2,0},{3,1},{4,6},{5,7},{6,4},{7,5},{8,10},{9,11},{10,... | collective-permute-start | bytes 98312 | tf_op jit(solution)/shard_map/ppermute | solution.py:347

commit v4 on v3

--- a/solution.py
+++ b/solution.py
@@ -60,7 +60,7 @@
 
 def spectra_kernel(first, count, late, c_dev, n_src, *refs):
     if late:
-        offs, sources, rec, halo, table_v, taper_v, smooth_v, before_s, out_r, out_s, *refs = refs
+        offs, sources, rec, halo, table_v, taper_v, smooth_v, before_s, out_r, out_s, out_all, *refs = refs
         sums, diffs, held, offs_v, sources_v, sems = refs
     else:
         offs, sources, rec, table, taper, smooth, out_r, out_s, table_v, taper_v, smooth_v, *refs = refs
@@ -138,11 +138,11 @@
     for s in range(n_src):
         wanted = jnp.where(rows // count == s, sources_v[s] % c_dev + (rows % count) * c_dev, wanted)
     picker = jnp.where(cols == wanted, 1.0, 0.0).astype(jnp.bfloat16)
-    at = 0
+    out_s[...] = jnp.dot(picker, out_r[...], preferred_element_type=jnp.float32).astype(jnp.bfloat16)
     if late:
         at = before_s.shape[0]
-        out_s[:at] = before_s[...]
-    out_s[at:] = jnp.dot(picker, out_r[...], preferred_element_type=jnp.float32).astype(jnp.bfloat16)
+        out_all[:at] = before_s[...]
+        out_all[at:] = out_s[...]
 
 
 def spectra_call(record, offsets, src_idx, tables, first, count, late=None):
@@ -151,22 +151,21 @@
     vmem = pl.BlockSpec(memory_space=pltpu.VMEM)
     hbm = pl.BlockSpec(memory_space=pltpu.HBM)
     arrays = [offsets, src_idx, record]
-    specs = [hbm] * 3
-    out_rows = n_src * count
     if late is None:
         arrays += tables
-        specs += [hbm] * 3
+    arrays = [pltpu.with_memory_space_constraint(a, pltpu.HBM) for a in arrays]
+    specs = [hbm] * len(arrays)
+    out_shape = [
+        jax.ShapeDtypeStruct((count * c_dev, 2 * NB), jnp.bfloat16),
+        jax.ShapeDtypeStruct((n_src * count, 2 * NB), jnp.bfloat16),
+    ]
+    if late is None:
+        out_shape += [jax.ShapeDtypeStruct(t.shape, t.dtype) for t in tables]
     else:
         halo, earlier = late
         arrays += [halo, *tables, earlier]
         specs += [vmem] * 5
-        out_rows += earlier.shape[0]
-    out_shape = [
-        jax.ShapeDtypeStruct((count * c_dev, 2 * NB), jnp.bfloat16),
-        jax.ShapeDtypeStruct((out_rows, 2 * NB), jnp.bfloat16),
-    ]
-    if late is None:
-        out_shape += [jax.ShapeDtypeStruct(t.shape, t.dtype) for t in tables]
+        out_shape.append(jax.ShapeDtypeStruct((earlier.shape[0] + n_src * count, 2 * NB), jnp.bfloat16))
     return pl.pallas_call(
         functools.partial(spectra_kernel, first, count, late is not None, c_dev, n_src),
         out_shape=out_shape,
@@ -188,39 +187,51 @@
     )(*arrays)
 
 
-def cross_kernel(n_list, sides, cuts, n_src, c_dev, scale, has_before, last, *refs):
-    srcs, refs = refs[:n_list], refs[n_list:]
+def cross_kernel(shares, sides, cuts, n_src, c_dev, scale, n_before, last, *refs):
+    n_list = len(shares)
+    srcs = []
+    for share in shares:
+        srcs.append(refs[:share])
+        refs = refs[share:]
     recs = []
     for parts in sides:
         recs.append([(refs[i], part) for i, part in enumerate(parts)])
         refs = refs[len(parts) :]
-    if has_before:
-        before, *refs = refs
+    before, refs = refs[:n_before], refs[n_before:]
     if last:
         ltab, out, wide, cross = refs
     else:
         out, wide = refs
     n_win = cuts[-1]
-    for k in range(n_list):
-        wide[k * n_src * n_win : (k + 1) * n_src * n_win, :] = srcs[k][0].astype(jnp.float32)
+    at = 0
+    for src in srcs:
+        for part in src:
+            height = part.shape[1]
+            wide[at : at + height, :] = part[0].astype(jnp.float32)
+            at += height
     tiles = NB // LANE
     block = 8 if n_list * n_src % 8 == 0 else n_src
     groups = block // n_src
     n_side = len(sides)
 
-    @pl.loop(0, n_list // groups * tiles)
-    def _(step):
-        group = step // tiles * groups
+    span = n_list // max(len(before), 1)
+
+    def run(step, first, earlier):
+        local = step // tiles * groups
+        group = first + local
         lo = pl.ds(pl.multiple_of(step % tiles * LANE, LANE), LANE)
         hi = pl.ds(pl.multiple_of(step % tiles * LANE + NB, LANE), LANE)
         base = pl.multiple_of(group * (n_src * n_win), 8)
         src = wide.at[pl.ds(base, groups * n_src * n_win)]
+
+        def places(group, q):
+            starts = [((group * n_src + s) * n_side + q) * c_dev for s in range(block)]
+            return [pl.ds(pl.multiple_of(start, c_dev), c_dev) for start in starts]
+
         for q, parts in enumerate(recs):
-            rows = [
-                pl.ds(pl.multiple_of(((group * n_src + s) * n_side + q) * c_dev, c_dev), c_dev)
-                for s in range(block)
-            ]
-            sums = [[before[r, lo], before[r, hi]] if has_before else [0.0, 0.0] for r in rows]
+            sums = [[0.0, 0.0] for _ in range(block)]
+            if earlier is not None:
+                sums = [[earlier[r, lo], earlier[r, hi]] for r in places(local, q)]
             for rec, part in parts:
                 start, stop = cuts[part], cuts[part + 1]
                 for w in range(stop - start):
@@ -235,11 +246,13 @@
                         sums[s][0] += src_real * rec_real + src_imag * rec_imag
                         sums[s][1] += src_real * rec_imag - src_imag * rec_real
             target = cross if last else out
-            for s in range(block):
-                for i, place in enumerate((lo, hi)):
-                    target[rows[s], place] = (sums[s][i] + jnp.zeros((c_dev, LANE), jnp.float32)).astype(
-                        target.dtype
-                    )
+            for r, pair in zip(places(group, q), sums):
+                for place, value in zip((lo, hi), pair):
+                    target[r, place] = jnp.broadcast_to(value, (c_dev, LANE)).astype(target.dtype)
+
+    for i in range(max(len(before), 1)):
+        earlier = before[i] if before else None
+        pl.loop(0, span // groups * tiles)(functools.partial(run, first=i * span, earlier=earlier))
 
     if last:
         lagged = jnp.dot(cross[...], ltab[...], preferred_element_type=jnp.float32)
@@ -248,19 +261,19 @@
 
 def cross_call(srcs, sides, cuts, n_src, c_dev, scale, before=None, ltab=None):
     n_list, n_side = len(srcs), len(sides)
-    groups = srcs[0].shape[0]
+    groups = srcs[0][0].shape[0]
     last = ltab is not None
     rows = n_list * n_src * n_side * c_dev
     whole = pl.BlockSpec(memory_space=pltpu.VMEM)
-    src_spec = pl.BlockSpec((1,) + srcs[0].shape[1:], lambda g: (g, 0, 0))
     row_block = lambda width: pl.BlockSpec((rows, width), lambda g: (g, 0))
-    arrays, specs = list(srcs), [src_spec] * n_list
+    arrays = [part for src in srcs for part in src]
+    specs = [pl.BlockSpec((1,) + a.shape[1:], lambda g: (g, 0, 0)) for a in arrays]
     for parts in sides:
         arrays += list(parts.values())
         specs += [whole] * len(parts)
     if before is not None:
-        arrays.append(before)
-        specs.append(row_block(2 * NB))
+        arrays += before
+        specs += [whole] * len(before)
     scratch = [pltpu.VMEM((n_list * n_src * cuts[-1], 2 * NB), jnp.float32)]
     if last:
         arrays.append(ltab)
@@ -272,8 +285,8 @@
     windows = sum(cuts[p + 1] - cuts[p] for parts in sides for p in parts) // n_side
     return pl.pallas_call(
         functools.partial(
-            cross_kernel, n_list, [list(p) for p in sides], cuts, n_src, c_dev, scale,
-            before is not None, last,
+            cross_kernel, [len(src) for src in srcs], [list(p) for p in sides], cuts, n_src, c_dev, scale,
+            0 if before is None else len(before), last,
         ),
         grid=(groups,),
         out_shape=out_shape,
@@ -297,7 +310,7 @@
     n_group = n_fibre // 2
     fibre = lax.axis_index("fibre")
     tm = lax.axis_index("tm")
-    early = n_win * 5 // 8
+    early = n_win * 3 // 4
     cuts = (0, early, n_win)
     scale = 1.0 / math.sqrt(n_win * n_tm * NB)
     tables = [jnp.asarray(t) for t in (half_tables(), taper_table(), smoothing())]
@@ -310,42 +323,50 @@
     halo = lax.ppermute(record[:, :W], "tm", [(i, i - 1) for i in range(1, n_tm)])
     rec_a, src_a, *tables = spectra_call(record, offsets, src_idx, tables, 0, early)
     far_a = trade(rec_a, 1)
-    rec_b, src = spectra_call(record, offsets, src_idx, tables, early, n_win - early, (halo, src_a))
+    if direct:
+        by_2a = trade(src_a, 4)
+    rec_b, src_b, src = spectra_call(record, offsets, src_idx, tables, early, n_win - early, (halo, src_a))
     cross = functools.partial(cross_call, cuts=cuts, n_src=n_src, c_dev=c_dev, scale=scale)
     if direct:
-        by_2 = trade(src, 4)
+        far_b = trade(rec_b, 1)
+        by_2b = trade(src_b, 4)
         by_1 = trade(src, 2)
-        far_b = trade(rec_b, 1)
-        by_3 = trade(by_2, 2)
-        srcs = [s[None] for s in (src, by_1, by_2, by_3)]
-        part = cross(srcs[:3], [{0: rec_a, 1: rec_b}, {0: far_a}])
-        near = cross(srcs[:3], [{}, {1: far_b}], before=part, ltab=ltab)
-        last = cross(srcs[3:], [{0: rec_a, 1: rec_b}, {0: far_a, 1: far_b}], ltab=ltab)
-        lagged = jnp.concatenate([near, last], axis=0)
+        by_3a = trade(by_2a, 2)
+        by_3b = trade(by_2b, 2)
+        srcs = [[part[None] for part in s] for s in ([src], [by_1], [by_2a, by_2b], [by_3a, by_3b])]
+        sides = [{0: rec_a, 1: rec_b}, {0: far_a}]
+        parts = [cross(srcs[:2], sides), cross(srcs[2:], sides)]
+        lagged = cross(srcs, [{}, {1: far_b}], before=parts, ltab=ltab)
     else:
         ranks = [[2 * j + p for j in range(n_group)] for p in range(2)]
-        srcs = [lax.all_gather(src, "fibre", axis=0, axis_index_groups=ranks)]
+        srcs = [[lax.all_gather(src, "fibre", axis=0, axis_index_groups=ranks)]]
         far_b = trade(rec_b, 1)
         lagged = cross(srcs, [{0: rec_a, 1: rec_b}, {0: far_a, 1: far_b}], ltab=ltab)
     lagged = lagged.reshape(n_group, n_src, 2, c_dev, LAGS)
 
-    def piece(owner, side):
+    def piece(owner):
         if direct:
-            return lax.dynamic_index_in_dim(lagged[:, :, side], (fibre // 2) ^ owner, 0, keepdims=True)
+            return lax.dynamic_index_in_dim(lagged, (fibre // 2) ^ owner, 0, keepdims=True)
         share = n_group // n_tm
-        return lax.dynamic_slice_in_dim(lagged[:, :, side], owner * share, share, 0)
-
+        return lax.dynamic_slice_in_dim(lagged, owner * share, share, 0)
+
+    keep = jnp.stack([piece(tm ^ k) for k in range(0, n_tm, 2)])
+    give = jnp.stack([piece(tm ^ k) for k in range(1, n_tm, 2)])
+    got = lax.ppermute(give, "tm", [(i, i ^ 1) for i in range(n_tm)])
+    pairs = keep.astype(jnp.float32) + got.astype(jnp.float32)
     totals = []
     for side in range(2):
         total = None
-        for k in range(n_tm):
-            mine = piece(tm ^ k, side)
+        for k in range(n_tm // 2):
+            mine = pairs[k, :, :, side]
             if side or k:
-                pairs = [
-                    (i * n_tm + t, (i ^ side) * n_tm + (t ^ k)) for i in range(n_fibre) for t in range(n_tm)
+                routes = [
+                    (i * n_tm + t, (i ^ side) * n_tm + (t ^ (2 * k)))
+                    for i in range(n_fibre)
+                    for t in range(n_tm)
                 ]
-                mine = lax.ppermute(mine, ("fibre", "tm"), pairs)
-            mine = mine.astype(jnp.float32)
+                mine = lax.ppermute(mine.astype(jnp.bfloat16), ("fibre", "tm"), routes)
+                mine = mine.astype(jnp.float32)
             total = mine if total is None else total + mine
         totals.append(total)
     even = fibre % 2 == 0

time: 57.5 us -> 47 us (0.82)
  waiting for transfers between devices: 19.1 us -> 10.7 us
  local copies, waits for them, and re-layouts: 6.49 us -> 0.89 us
  starting transfers between devices: 16.2 us -> 19.9 us
    ppermute x5 -> x7, waiting for transfers between devices: 16.3 us -> 5.8 us  [trade(): return lax.ppermute(array, 'fibre', [(i, i ^ by) for i in range(n_fibre)])]
    ppermute x5 -> x7, starting transfers between devices: 8.22 us -> 15 us  [trade(): return lax.ppermute(array, 'fibre', [(i, i ^ by) for i in range(n_fibre)])]
    unnamed x14 -> x2, local copies, waits for them, and re-layouts: 5.6 us -> 0.01 us
    ppermute x7 -> x4, starting transfers between devices: 6.66 us -> 3.62 us  [the longest x3 3.55 us: body(): mine = lax.ppermute(mine.astype(jnp.bfloat16), ('fibre', 'tm'), routes)]
    ppermute x7 -> x4, waiting for transfers between devices: 2.83 us -> 4.86 us  [the longest x3 3.53 us: body(): mine = lax.ppermute(mine.astype(jnp.bfloat16), ('fibre', 'tm'), routes)]
    pallas_call x3, Pallas kernels: 8.95 us -> 8.24 us  [cross_call(): pl.pallas_call(functools.partial(cross_kernel, [len(src) for src in srcs]...]
    pallas_call x2, Pallas kernels: 5.58 us -> 6.18 us  [spectra_call(): pl.pallas_call(functools.partial(spectra_kernel, first, count, late is no...]
  transfers between devices with their start and end apart: 13 -> 12, of which waited for: 6 -> 6; matrix products, arithmetic and copies ran while one was open for 0% -> 2% of each run, Pallas kernels for 14% -> 19%
where the time goes in v4:
time: 47 us; the launch traced here: 46.8 us
  starting transfers between devices  19.9 us (42%)
  Pallas kernels  14.4 us (31%)
  waiting for transfers between devices  10.7 us (23%)
  local copies, waits for them, and re-layouts  0.89 us (2%)
  other arithmetic  0.74 us (2%)
    ppermute x7, starting transfers between devices, trade(): return lax.ppermute(array, 'fibre', [(i, i ^ by) for i in range(n_fibre)])  15 us
    pallas_call x3, Pallas kernels, cross_call(): pl.pallas_call(functools.partial(cross_kernel, [len(src) for src in srcs]...  8.24 us
    pallas_call x2, Pallas kernels, spectra_call(): pl.pallas_call(functools.partial(spectra_kernel, first, count, late is no...  6.18 us
    ppermute x7, waiting for transfers between devices, trade(): return lax.ppermute(array, 'fibre', [(i, i ^ by) for i in range(n_fibre)])  5.8 us
    ppermute x3, starting transfers between devices, body(): mine = lax.ppermute(mine.astype(jnp.bfloat16), ('fibre', 'tm'), routes)  3.55 us
    ppermute x3, waiting for transfers between devices, body(): mine = lax.ppermute(mine.astype(jnp.bfloat16), ('fibre', 'tm'), routes)  3.53 us
    ppermute x1, waiting for transfers between devices, body(): got = lax.ppermute(give, 'tm', [(i, i ^ 1) for i in range(n_tm)])  1.33 us
    ppermute x1, starting transfers between devices, body(): lax.ppermute(record[:, :W], 'tm', [(i, i - 1) for i in range(1, n_tm)])  1.28 us
  transfers between devices with their start and end apart: 12, of which 6 were waited for; matrix products, arithmetic and copies ran while one was open for 2% of the time, Pallas kernels for 19%

profile of v4, /device:TPU:0, one launch (start us, length us, event | category | flops | bytes accessed | tf_op | source)
XLA Modules:
  0.0 46.8 jit_solution(467367788123965614)
XLA Ops:
  0.0 3.9 %spectra.2 = (bf16[384,768]{1,0:T(8,128)(2,1)S(1)}, bf16[96,768]{1,0:T(8,128)(2,1)S(1)}, bf16[1024,768]{1,0:T(8,128)(2,1)S(1)}, f32[1,2048]{1,0:T(1,128)S(1)}, bf16[384,384]{1,0:T(8,128)(2,1)S(1)}) custom-call(s32[32]{0:T(128)} %refs_0_.3, s32[4]{0:T(128)} %refs_1_.3, bf16[16,32768]{1,0:T(8,128)(2,1)} %refs_2_.3, bf16[1024,768]{1,0:T(8,128)(2,1)} %constant.62.clone.refs_3_, ...), custom_call_target="tpu_custom_call" | custom-call | flops 1207959552 | bytes 4194304 | tf_op jit(solution)/shard_map/spectra/pallas_call | solution.py:169
  3.9 3.0 %collective-permute-start.7 = (bf16[384,768]{1,0:T(8,128)(2,1)S(1)}, bf16[384,768]{1,0:T(8,128)(2,1)S(1)}, u32[]{:S(2)}, u32[]{:S(2)}) collective-permute-start(bf16[384,768]{1,0:T(8,128)(2,1)S(1)} %get-tuple-element.20.refs_2_.refs_4_), channel_id=1, source_target_pairs={{0,4},{4,0},{8,12},{12,8},{16,20},{20,16},{24,28},{28,24},{1,5},{5... | collective-permute-start | bytes 1769480 | tf_op jit(solution)/shard_map/ppermute | solution.py:321
  6.9 0.8 %slice.18 = bf16[16,2048]{1,0:T(8,128)(2,1)S(1)} slice(bf16[16,32768]{1,0:T(8,128)(2,1)} %refs_2_.3), slice={[0:16], [0:2048]} | slice | bytes 131072 | tf_op jit(solution)/shard_map/slice | solution.py:323
  7.7 1.3 %collective-permute-start = (bf16[16,2048]{1,0:T(8,128)(2,1)S(1)}, bf16[16,2048]{1,0:T(8,128)(2,1)S(1)}, u32[]{:S(2)}, u32[]{:S(2)}) collective-permute-start(bf16[16,2048]{1,0:T(8,128)(2,1)S(1)} %slice.18), channel_id=1, source_target_pairs={{1,0},{2,1},{3,2},{5,4},{6,5},{7,6},{9,8},{10,9},{11,10},{13,12},{... | collective-permute-start | bytes 196616 | tf_op jit(solution)/shard_map/ppermute | solution.py:323
  9.0 2.7 %collective-permute-start.2 = (bf16[96,768]{1,0:T(8,128)(2,1)S(1)}, bf16[96,768]{1,0:T(8,128)(2,1)S(1)}, u32[]{:S(2)}, u32[]{:S(2)}) collective-permute-start(bf16[96,768]{1,0:T(8,128)(2,1)S(1)} %get-tuple-element.16.refs_7_), channel_id=1, source_target_pairs={{0,16},{4,20},{8,24},{12,28},{16,0},{20,4},{24,8},{28,12},{1,17},{... | collective-permute-start | bytes 442376 | tf_op jit(solution)/shard_map/ppermute | solution.py:321
  11.7 0.0 collective-permute-done.refs_3_
  11.7 2.3 %spectra.3 = (bf16[128,768]{1,0:T(8,128)(2,1)S(1)}, bf16[32,768]{1,0:T(8,128)(2,1)S(1)}, bf16[128,768]{1,0:T(8,128)(2,1)S(1)}) custom-call(s32[32]{0:T(128)} %refs_0_.3, s32[4]{0:T(128)} %refs_1_.3, bf16[16,32768]{1,0:T(8,128)(2,1)} %refs_2_.3, bf16[16,2048]{1,0:T(8,128)(2,1)S(1)} %collective-permute-done.refs_3_, ...), custom_call_target="tpu_custom_call" | custom-call | flops 402653184 | bytes 4194304 | tf_op jit(solution)/shard_map/spectra/pallas_call | solution.py:169
  14.0 1.6 %collective-permute-start.1 = (bf16[128,768]{1,0:T(8,128)(2,1)S(1)}, bf16[128,768]{1,0:T(8,128)(2,1)S(1)}, u32[]{:S(2)}, u32[]{:S(2)}) collective-permute-start(bf16[128,768]{1,0:T(8,128)(2,1)S(1)} %get-tuple-element.17), channel_id=1, source_target_pairs={{0,8},{4,12},{8,0},{12,4},{16,24},{20,28},{24,16},{28,20},{1,9},{5... | collective-permute-start | bytes 589832 | tf_op jit(solution)/shard_map/ppermute | solution.py:321
  15.6 0.5 %collective-permute-start.6 = (bf16[128,768]{1,0:T(8,128)(2,1)S(1)}, bf16[128,768]{1,0:T(8,128)(2,1)S(1)}, u32[]{:S(2)}, u32[]{:S(2)}) collective-permute-start(bf16[128,768]{1,0:T(8,128)(2,1)S(1)} %get-tuple-element.19.refs_3_.refs_5_), channel_id=1, source_target_pairs={{0,4},{4,0},{8,12},{12,8},{16,20},{20,16},{24,28},{28,24},{1,5},{5... | collective-permute-start | bytes 589832 | tf_op jit(solution)/shard_map/ppermute | solution.py:321
  16.2 3.7 %collective-permute-done.2 = bf16[96,768]{1,0:T(8,128)(2,1)S(1)} collective-permute-done((bf16[96,768]{1,0:T(8,128)(2,1)S(1)}, bf16[96,768]{1,0:T(8,128)(2,1)S(1)}, u32[]{:S(2)}, u32[]{:S(2)}) %collective-permute-start.2) | collective-permute-done | bytes 147488 | tf_op jit(solution)/shard_map/ppermute | solution.py:321
  19.8 0.8 %collective-permute-start.4 = (bf16[96,768]{1,0:T(8,128)(2,1)S(1)}, bf16[96,768]{1,0:T(8,128)(2,1)S(1)}, u32[]{:S(2)}, u32[]{:S(2)}) collective-permute-start(bf16[96,768]{1,0:T(8,128)(2,1)S(1)} %collective-permute-done.2), channel_id=1, source_target_pairs={{0,8},{4,12},{8,0},{12,4},{16,24},{20,28},{24,16},{28,20},{1,9},{5... | collective-permute-start | bytes 442376 | tf_op jit(solution)/shard_map/ppermute | solution.py:321
  20.6 3.4 %collective-permute-start.3 = (bf16[32,768]{1,0:T(8,128)(2,1)S(1)}, bf16[32,768]{1,0:T(8,128)(2,1)S(1)}, u32[]{:S(2)}, u32[]{:S(2)}) collective-permute-start(bf16[32,768]{1,0:T(8,128)(2,1)S(1)} %get-tuple-element.18), channel_id=1, source_target_pairs={{0,16},{4,20},{8,24},{12,28},{16,0},{20,4},{24,8},{28,12},{1,17},{... | collective-permute-start | bytes 147464 | tf_op jit(solution)/shard_map/ppermute | solution.py:321
  24.0 2.1 %collective-permute-done.3 = bf16[32,768]{1,0:T(8,128)(2,1)S(1)} collective-permute-done((bf16[32,768]{1,0:T(8,128)(2,1)S(1)}, bf16[32,768]{1,0:T(8,128)(2,1)S(1)}, u32[]{:S(2)}, u32[]{:S(2)}) %collective-permute-start.3) | collective-permute-done | bytes 49184 | tf_op jit(solution)/shard_map/ppermute | solution.py:321
  26.2 3.0 %collective-permute-start.5 = (bf16[32,768]{1,0:T(8,128)(2,1)S(1)}, bf16[32,768]{1,0:T(8,128)(2,1)S(1)}, u32[]{:S(2)}, u32[]{:S(2)}) collective-permute-start(bf16[32,768]{1,0:T(8,128)(2,1)S(1)} %collective-permute-done.3), channel_id=1, source_target_pairs={{0,8},{4,12},{8,0},{12,4},{16,24},{20,28},{24,16},{28,20},{1,9},{5... | collective-permute-start | bytes 147464 | tf_op jit(solution)/shard_map/ppermute | solution.py:321
  29.2 0.0 collective-permute-done.1
  29.2 0.0 collective-permute-done.7.refs_4_.refs_6_
  29.2 3.3 %cross.3.refs_7_ = f32[256,768]{1,0:T(8,128)S(1)} custom-call(bf16[1,128,768]{2,1,0:T(8,128)(2,1)S(1)} %bitcast.41, bf16[1,128,768]{2,1,0:T(8,128)(2,1)S(1)} %bitcast.43, bf16[384,768]{1,0:T(8,128)(2,1)S(1)} %get-tuple-element.20.refs_2_.refs_4_, bf16[128,768]{1,0:T(8,128)(2,1)S(1)} %get-tuple-element.19.refs_3_.refs_5_, ...), custom_call_target="tpu_custom_call" | custom-call | flops 110100480 | bytes 4194304 | tf_op jit(solution)/shard_map/cross/pallas_call | solution.py:286
  32.5 0.0 copy-start
  32.5 0.0 collective-permute-done.5
  32.5 0.0 collective-permute-done.4
  32.5 3.3 %cross.4.refs_8_ = f32[256,768]{1,0:T(8,128)S(1)} custom-call(bf16[1,96,768]{2,1,0:T(8,128)(2,1)S(1)} %bitcast.45, bf16[1,32,768]{2,1,0:T(8,128)(2,1)S(1)} %bitcast.49, bf16[1,96,768]{2,1,0:T(8,128)(2,1)S(1)} %bitcast.47, bf16[1,32,768]{2,1,0:T(8,128)(2,1)S(1)} %bitcast.51, bf16[384,768]{1,0:T(8,128)(2,1)S(1)} %get-tuple-element.20.refs_2_.refs_4_, ...), custom_call_target="tpu_custom_call" | custom-call | flops 110100480 | bytes 4194304 | tf_op jit(solution)/shard_map/cross/pallas_call | solution.py:286
  35.9 0.0 collective-permute-done.6.refs_6_
  35.9 0.0 copy-done
  35.9 1.6 %cross.5 = bf16[512,256]{1,0:T(8,128)(2,1)S(1)} custom-call(bf16[1,128,768]{2,1,0:T(8,128)(2,1)S(1)} %bitcast.42, bf16[1,128,768]{2,1,0:T(8,128)(2,1)S(1)} %bitcast.44, bf16[1,96,768]{2,1,0:T(8,128)(2,1)S(1)} %bitcast.46, bf16[1,32,768]{2,1,0:T(8,128)(2,1)S(1)} %bitcast.50, bf16[1,96,768]{2,1,0:T(8,128)(2,1)S(1)} %bitcast.48, ...), custom_call_target="tpu_custom_call" | custom-call | flops 31457280 | bytes 4194304 | tf_op jit(solution)/shard_map/cross/pallas_call | solution.py:286
  37.5 0.1 collective-permute-start.8
  37.6 1.3 %collective-permute-done.8 = bf16[2,1,4,2,16,256]{5,4,3,2,1,0:T(8,128)(2,1)S(1)} collective-permute-done((bf16[2,1,4,2,16,256]{5,4,3,2,1,0:T(8,128)(2,1)S(1)}, bf16[2,1,4,2,16,256]{5,4,3,2,1,0:T(8,128)(2,1)S(1)}, u32[]{:S(2)}, u32[]{:S(2)}) %collective-permute-start.8) | collective-permute-done | bytes 131104 | tf_op jit(solution)/shard_map/ppermute | solution.py:355
  39.0 0.6 %collective-permute-start.10 = (bf16[1,4,16,256]{3,2,1,0:T(8,128)(2,1)S(1)}, bf16[1,4,16,256]{3,2,1,0:T(8,128)(2,1)S(1)}, u32[]{:S(2)}, u32[]{:S(2)}) collective-permute-start(bf16[1,4,16,256]{3,2,1,0:T(8,128)(2,1)S(1)} %get-tuple-element.31), channel_id=1, source_target_pairs={{0,4},{1,5},{2,6},{3,7},{4,0},{5,1},{6,2},{7,3},{8,12},{9,13},{10,... | collective-permute-start | bytes 98312 | tf_op jit(solution)/shard_map/ppermute | solution.py:368
  39.6 2.6 %collective-permute-start.11 = (bf16[1,4,16,256]{3,2,1,0:T(8,128)(2,1)S(1)}, bf16[1,4,16,256]{3,2,1,0:T(8,128)(2,1)S(1)}, u32[]{:S(2)}, u32[]{:S(2)}) collective-permute-start(bf16[1,4,16,256]{3,2,1,0:T(8,128)(2,1)S(1)} %get-tuple-element.30), channel_id=1, source_target_pairs={{0,6},{1,7},{2,4},{3,5},{4,2},{5,3},{6,0},{7,1},{8,14},{9,15},{10,... | collective-permute-start | bytes 98312 | tf_op jit(solution)/shard_map/ppermute | solution.py:368
  42.2 0.4 collective-permute-start.9
  42.6 0.4 collective-permute-done.10
  43.0 1.4 %collective-permute-done.11 = bf16[1,4,16,256]{3,2,1,0:T(8,128)(2,1)S(1)} collective-permute-done((bf16[1,4,16,256]{3,2,1,0:T(8,128)(2,1)S(1)}, bf16[1,4,16,256]{3,2,1,0:T(8,128)(2,1)S(1)}, u32[]{:S(2)}, u32[]{:S(2)}) %collective-permute-start.11) | collective-permute-done | bytes 32800 | tf_op jit(solution)/shard_map/ppermute | solution.py:368
  44.4 1.7 %collective-permute-done.9 = bf16[1,4,16,256]{3,2,1,0:T(8,128)(2,1)S(1)} collective-permute-done((bf16[1,4,16,256]{3,2,1,0:T(8,128)(2,1)S(1)}, bf16[1,4,16,256]{3,2,1,0:T(8,128)(2,1)S(1)}, u32[]{:S(2)}, u32[]{:S(2)}) %collective-permute-start.9) | collective-permute-done | bytes 32800 | tf_op jit(solution)/shard_map/ppermute | solution.py:368
  46.1 0.7 %pad_maximum_fusion.1 = f32[1,2,4,16,256]{4,3,2,1,0:T(8,128)} fusion(f32[1,1,4,16,256]{4,3,2,1,0:T(8,128)S(1)} %get-tuple-element.22, f32[1,1,4,16,256]{4,3,2,1,0:T(8,128)S(1)} %get-tuple-element.21), kind=kLoop, calls=%fused_computation.2 | loop fusion | flops 32768 | bytes 262144 | tf_op jit(solution)/shard_map/stack | solution.py:374
  (5 shorter events, 0.1 us)
Async XLA Ops:
  3.9 25.3 %collective-permute-start.7 = (bf16[384,768]{1,0:T(8,128)(2,1)S(1)}, bf16[384,768]{1,0:T(8,128)(2,1)S(1)}, u32[]{:S(2)}, u32[]{:S(2)}) collective-permute-start(bf16[384,768]{1,0:T(8,128)(2,1)S(1)} %get-tuple-element.20.refs_2_.refs_4_), channel_id=1, source_target_pairs={{0,4},{4,0},{8,12},{12,8},{16,20},{20,16},{24,28},{28,24},{1,5},{5... | collective-permute-start | bytes 1769480 | tf_op jit(solution)/shard_map/ppermute | solution.py:321
  7.7 4.0 %collective-permute-start = (bf16[16,2048]{1,0:T(8,128)(2,1)S(1)}, bf16[16,2048]{1,0:T(8,128)(2,1)S(1)}, u32[]{:S(2)}, u32[]{:S(2)}) collective-permute-start(bf16[16,2048]{1,0:T(8,128)(2,1)S(1)} %slice.18), channel_id=1, source_target_pairs={{1,0},{2,1},{3,2},{5,4},{6,5},{7,6},{9,8},{10,9},{11,10},{13,12},{... | collective-permute-start | bytes 196616 | tf_op jit(solution)/shard_map/ppermute | solution.py:323
  9.0 10.8 %collective-permute-start.2 = (bf16[96,768]{1,0:T(8,128)(2,1)S(1)}, bf16[96,768]{1,0:T(8,128)(2,1)S(1)}, u32[]{:S(2)}, u32[]{:S(2)}) collective-permute-start(bf16[96,768]{1,0:T(8,128)(2,1)S(1)} %get-tuple-element.16.refs_7_), channel_id=1, source_target_pairs={{0,16},{4,20},{8,24},{12,28},{16,0},{20,4},{24,8},{28,12},{1,17},{... | collective-permute-start | bytes 442376 | tf_op jit(solution)/shard_map/ppermute | solution.py:321
  14.0 15.2 %collective-permute-start.1 = (bf16[128,768]{1,0:T(8,128)(2,1)S(1)}, bf16[128,768]{1,0:T(8,128)(2,1)S(1)}, u32[]{:S(2)}, u32[]{:S(2)}) collective-permute-start(bf16[128,768]{1,0:T(8,128)(2,1)S(1)} %get-tuple-element.17), channel_id=1, source_target_pairs={{0,8},{4,12},{8,0},{12,4},{16,24},{20,28},{24,16},{28,20},{1,9},{5... | collective-permute-start | bytes 589832 | tf_op jit(solution)/shard_map/ppermute | solution.py:321
  15.6 20.2 %collective-permute-start.6 = (bf16[128,768]{1,0:T(8,128)(2,1)S(1)}, bf16[128,768]{1,0:T(8,128)(2,1)S(1)}, u32[]{:S(2)}, u32[]{:S(2)}) collective-permute-start(bf16[128,768]{1,0:T(8,128)(2,1)S(1)} %get-tuple-element.19.refs_3_.refs_5_), channel_id=1, source_target_pairs={{0,4},{4,0},{8,12},{12,8},{16,20},{20,16},{24,28},{28,24},{1,5},{5... | collective-permute-start | bytes 589832 | tf_op jit(solution)/shard_map/ppermute | solution.py:321
  19.8 12.7 %collective-permute-start.4 = (bf16[96,768]{1,0:T(8,128)(2,1)S(1)}, bf16[96,768]{1,0:T(8,128)(2,1)S(1)}, u32[]{:S(2)}, u32[]{:S(2)}) collective-permute-start(bf16[96,768]{1,0:T(8,128)(2,1)S(1)} %collective-permute-done.2), channel_id=1, source_target_pairs={{0,8},{4,12},{8,0},{12,4},{16,24},{20,28},{24,16},{28,20},{1,9},{5... | collective-permute-start | bytes 442376 | tf_op jit(solution)/shard_map/ppermute | solution.py:321
  20.6 5.6 %collective-permute-start.3 = (bf16[32,768]{1,0:T(8,128)(2,1)S(1)}, bf16[32,768]{1,0:T(8,128)(2,1)S(1)}, u32[]{:S(2)}, u32[]{:S(2)}) collective-permute-start(bf16[32,768]{1,0:T(8,128)(2,1)S(1)} %get-tuple-element.18), channel_id=1, source_target_pairs={{0,16},{4,20},{8,24},{12,28},{16,0},{20,4},{24,8},{28,12},{1,17},{... | collective-permute-start | bytes 147464 | tf_op jit(solution)/shard_map/ppermute | solution.py:321
  26.2 6.3 %collective-permute-start.5 = (bf16[32,768]{1,0:T(8,128)(2,1)S(1)}, bf16[32,768]{1,0:T(8,128)(2,1)S(1)}, u32[]{:S(2)}, u32[]{:S(2)}) collective-permute-start(bf16[32,768]{1,0:T(8,128)(2,1)S(1)} %collective-permute-done.3), channel_id=1, source_target_pairs={{0,8},{4,12},{8,0},{12,4},{16,24},{20,28},{24,16},{28,20},{1,9},{5... | collective-permute-start | bytes 147464 | tf_op jit(solution)/shard_map/ppermute | solution.py:321
  32.5 3.4 %copy-start = (bf16[768,256]{1,0:T(8,128)(2,1)S(1)}, bf16[768,256]{1,0:T(8,128)(2,1)}, u32[]{:S(2)}) copy-start(bf16[768,256]{1,0:T(8,128)(2,1)} %constant.65.clone.refs_9_) | copy-start | bytes 1179652
  37.5 1.4 %collective-permute-start.8 = (bf16[2,1,4,2,16,256]{5,4,3,2,1,0:T(8,128)(2,1)S(1)}, bf16[2,1,4,2,16,256]{5,4,3,2,1,0:T(8,128)(2,1)S(1)}, u32[]{:S(2)}, u32[]{:S(2)}) collective-permute-start(bf16[2,1,4,2,16,256]{5,4,3,2,1,0:T(8,128)(2,1)S(1)} %pad_maximum_fusion), channel_id=1, source_target_pairs={{0,1},{1,0},{2,3},{3,2},{4,5},{5,4},{6,7},{7,6},{8,9},{9,8},{10,11... | collective-permute-start | bytes 393224 | tf_op jit(solution)/shard_map/ppermute | solution.py:355
  39.0 4.0 %collective-permute-start.10 = (bf16[1,4,16,256]{3,2,1,0:T(8,128)(2,1)S(1)}, bf16[1,4,16,256]{3,2,1,0:T(8,128)(2,1)S(1)}, u32[]{:S(2)}, u32[]{:S(2)}) collective-permute-start(bf16[1,4,16,256]{3,2,1,0:T(8,128)(2,1)S(1)} %get-tuple-element.31), channel_id=1, source_target_pairs={{0,4},{1,5},{2,6},{3,7},{4,0},{5,1},{6,2},{7,3},{8,12},{9,13},{10,... | collective-permute-start | bytes 98312 | tf_op jit(solution)/shard_map/ppermute | solution.py:368
  39.6 4.8 %collective-permute-start.11 = (bf16[1,4,16,256]{3,2,1,0:T(8,128)(2,1)S(1)}, bf16[1,4,16,256]{3,2,1,0:T(8,128)(2,1)S(1)}, u32[]{:S(2)}, u32[]{:S(2)}) collective-permute-start(bf16[1,4,16,256]{3,2,1,0:T(8,128)(2,1)S(1)} %get-tuple-element.30), channel_id=1, source_target_pairs={{0,6},{1,7},{2,4},{3,5},{4,2},{5,3},{6,0},{7,1},{8,14},{9,15},{10,... | collective-permute-start | bytes 98312 | tf_op jit(solution)/shard_map/ppermute | solution.py:368
  42.2 3.9 %collective-permute-start.9 = (bf16[1,4,16,256]{3,2,1,0:T(8,128)(2,1)S(1)}, bf16[1,4,16,256]{3,2,1,0:T(8,128)(2,1)S(1)}, u32[]{:S(2)}, u32[]{:S(2)}) collective-permute-start(bf16[1,4,16,256]{3,2,1,0:T(8,128)(2,1)S(1)} %get-tuple-element.29), channel_id=1, source_target_pairs={{0,2},{1,3},{2,0},{3,1},{4,6},{5,7},{6,4},{7,5},{8,10},{9,11},{10,... | collective-permute-start | bytes 98312 | tf_op jit(solution)/shard_map/ppermute | solution.py:368

commit v5 on v4

--- a/solution.py
+++ b/solution.py
@@ -63,7 +63,8 @@
         offs, sources, rec, halo, table_v, taper_v, smooth_v, before_s, out_r, out_s, out_all, *refs = refs
         sums, diffs, held, offs_v, sources_v, sems = refs
     else:
-        offs, sources, rec, table, taper, smooth, out_r, out_s, table_v, taper_v, smooth_v, *refs = refs
+        offs, sources, rec, table, taper, smooth, *refs = refs
+        out_r, out_s, out_edge, table_v, taper_v, smooth_v, *refs = refs
         sums, diffs, held, offs_v, sources_v, sems = refs
     begin = first * HOP
     width = (count + 2) * HOP
@@ -90,6 +91,7 @@
         for at in range(0, FOLD, rows):
             fetch(table.at[pl.ds(at, rows)], table_v.at[pl.ds(at, rows)])
         fetch(smooth, smooth_v)
+        fetch(rec.at[:, pl.ds(0, W)], out_edge)
     for copy in copies[:ready]:
         copy.wait()
 
@@ -160,6 +162,7 @@
         jax.ShapeDtypeStruct((n_src * count, 2 * NB), jnp.bfloat16),
     ]
     if late is None:
+        out_shape.append(jax.ShapeDtypeStruct((c_dev, W), record.dtype))
         out_shape += [jax.ShapeDtypeStruct(t.shape, t.dtype) for t in tables]
     else:
         halo, earlier = late
@@ -320,45 +323,47 @@
     def trade(array, by):
         return lax.ppermute(array, "fibre", [(i, i ^ by) for i in range(n_fibre)])
 
-    halo = lax.ppermute(record[:, :W], "tm", [(i, i - 1) for i in range(1, n_tm)])
-    rec_a, src_a, *tables = spectra_call(record, offsets, src_idx, tables, 0, early)
+    rec_a, src_a, edge, *tables = spectra_call(record, offsets, src_idx, tables, 0, early)
     far_a = trade(rec_a, 1)
     if direct:
         by_2a = trade(src_a, 4)
+    halo = lax.ppermute(edge, "tm", [(i, i - 1) for i in range(1, n_tm)])
     rec_b, src_b, src = spectra_call(record, offsets, src_idx, tables, early, n_win - early, (halo, src_a))
+    far_b = trade(rec_b, 1)
     cross = functools.partial(cross_call, cuts=cuts, n_src=n_src, c_dev=c_dev, scale=scale)
+    own = [{0: rec_a, 1: rec_b}]
     if direct:
-        far_b = trade(rec_b, 1)
-        by_2b = trade(src_b, 4)
+        by_2 = jnp.concatenate([by_2a, trade(src_b, 4)], axis=0)
         by_1 = trade(src, 2)
-        by_3a = trade(by_2a, 2)
-        by_3b = trade(by_2b, 2)
-        srcs = [[part[None] for part in s] for s in ([src], [by_1], [by_2a, by_2b], [by_3a, by_3b])]
-        sides = [{0: rec_a, 1: rec_b}, {0: far_a}]
-        parts = [cross(srcs[:2], sides), cross(srcs[2:], sides)]
-        lagged = cross(srcs, [{}, {1: far_b}], before=parts, ltab=ltab)
+        by_3 = trade(by_2, 2)
+        srcs = [[part[None]] for part in (src, by_1, by_2, by_3)]
+        halves = (srcs[:2], srcs[2:])
+        near = [cross(half, own, ltab=ltab) for half in halves]
+        near = jnp.concatenate(near, axis=0)
+        parts = [cross(half, [{0: far_a}]) for half in halves]
+        far = cross(srcs, [{1: far_b}], before=parts, ltab=ltab)
     else:
         ranks = [[2 * j + p for j in range(n_group)] for p in range(2)]
         srcs = [[lax.all_gather(src, "fibre", axis=0, axis_index_groups=ranks)]]
-        far_b = trade(rec_b, 1)
-        lagged = cross(srcs, [{0: rec_a, 1: rec_b}, {0: far_a, 1: far_b}], ltab=ltab)
-    lagged = lagged.reshape(n_group, n_src, 2, c_dev, LAGS)
-
-    def piece(owner):
+        near = cross(srcs, own, ltab=ltab)
+        far = cross(srcs, [{0: far_a, 1: far_b}], ltab=ltab)
+    near, far = (r.reshape(n_group, n_src, c_dev, LAGS) for r in (near, far))
+
+    def piece(lagged, owner):
         if direct:
             return lax.dynamic_index_in_dim(lagged, (fibre // 2) ^ owner, 0, keepdims=True)
         share = n_group // n_tm
         return lax.dynamic_slice_in_dim(lagged, owner * share, share, 0)
 
-    keep = jnp.stack([piece(tm ^ k) for k in range(0, n_tm, 2)])
-    give = jnp.stack([piece(tm ^ k) for k in range(1, n_tm, 2)])
+    keep = jnp.stack([piece(r, tm ^ k) for r in (near, far) for k in range(0, n_tm, 2)])
+    give = jnp.stack([piece(r, tm ^ k) for r in (near, far) for k in range(1, n_tm, 2)])
     got = lax.ppermute(give, "tm", [(i, i ^ 1) for i in range(n_tm)])
     pairs = keep.astype(jnp.float32) + got.astype(jnp.float32)
     totals = []
     for side in range(2):
         total = None
         for k in range(n_tm // 2):
-            mine = pairs[k, :, :, side]
+            mine = pairs[side * (n_tm // 2) + k]
             if side or k:
                 routes = [
                     (i * n_tm + t, (i ^ side) * n_tm + (t ^ (2 * k)))

time: 47 us -> 42.8 us (0.911)
  starting transfers between devices: 19.9 us -> 16.2 us
  local copies, waits for them, and re-layouts: 0.89 us -> 0.06 us
  Pallas kernels: 14.4 us -> 15.1 us
    ppermute x7 -> x6, starting transfers between devices: 15 us -> 10.6 us  [trade(): return lax.ppermute(array, 'fibre', [(i, i ^ by) for i in range(n_fibre)])]
    slice x1 -> x0, local copies, waits for them, and re-layouts: 0.84 us -> none  [body(): record[:, :W]]
    ppermute x1, starting transfers between devices: 0.07 us -> 0.74 us  [body(): got = lax.ppermute(give, 'tm', [(i, i ^ 1) for i in range(n_tm)])]
    pallas_call x3 -> x5, Pallas kernels: 8.24 us -> 8.88 us  [cross_call(): pl.pallas_call(functools.partial(cross_kernel, [len(src) for src in srcs]...]
    ppermute x7 -> x6, waiting for transfers between devices: 5.8 us -> 5.44 us  [trade(): return lax.ppermute(array, 'fibre', [(i, i ^ by) for i in range(n_fibre)])]
  transfers between devices with their start and end apart: 12 -> 11, of which waited for: 6 -> 7; matrix products, arithmetic and copies ran while one was open for 2% -> 0% of each run, Pallas kernels for 19% -> 23%
where the time goes in v5:
time: 42.8 us; the launch traced here: 42.6 us
  starting transfers between devices  16.2 us (38%)
  Pallas kernels  15.1 us (35%)
  waiting for transfers between devices  10.3 us (24%)
  other arithmetic  0.76 us (2%)
    ppermute x6, starting transfers between devices, trade(): return lax.ppermute(array, 'fibre', [(i, i ^ by) for i in range(n_fibre)])  10.6 us
    pallas_call x5, Pallas kernels, cross_call(): pl.pallas_call(functools.partial(cross_kernel, [len(src) for src in srcs]...  8.88 us
    pallas_call x2, Pallas kernels, spectra_call(): pl.pallas_call(functools.partial(spectra_kernel, first, count, late is no...  6.22 us
    ppermute x6, waiting for transfers between devices, trade(): return lax.ppermute(array, 'fibre', [(i, i ^ by) for i in range(n_fibre)])  5.44 us
    ppermute x3, waiting for transfers between devices, body(): mine = lax.ppermute(mine.astype(jnp.bfloat16), ('fibre', 'tm'), routes)  3.63 us
    ppermute x3, starting transfers between devices, body(): mine = lax.ppermute(mine.astype(jnp.bfloat16), ('fibre', 'tm'), routes)  3.57 us
    ppermute x1, starting transfers between devices, body(): halo = lax.ppermute(edge, 'tm', [(i, i - 1) for i in range(1, n_tm)])  1.28 us
    ppermute x1, waiting for transfers between devices, body(): got = lax.ppermute(give, 'tm', [(i, i ^ 1) for i in range(n_tm)])  0.99 us
  transfers between devices with their start and end apart: 11, of which 7 were waited for; matrix products, arithmetic and copies ran while one was open for 0% of the time, Pallas kernels for 23%

profile of v5, /device:TPU:0, one launch (start us, length us, event | category | flops | bytes accessed | tf_op | source)
XLA Modules:
  0.0 42.6 jit_solution(17981268414219910308)
XLA Ops:
  0.0 3.9 %spectra.2 = (bf16[384,768]{1,0:T(8,128)(2,1)S(1)}, bf16[96,768]{1,0:T(8,128)(2,1)S(1)}, bf16[16,2048]{1,0:T(8,128)(2,1)S(1)}, bf16[1024,768]{1,0:T(8,128)(2,1)S...) custom-call(s32[32]{0:T(128)} %refs_0_.3, s32[4]{0:T(128)} %refs_1_.3, bf16[16,32768]{1,0:T(8,128)(2,1)} %refs_2_.3, ...), custom_call_target="tpu_custom_call" | custom-call | flops 1207959552 | bytes 4194304 | tf_op jit(solution)/shard_map/spectra/pallas_call | solution.py:172
  3.9 4.1 %collective-permute-start.2 = (bf16[96,768]{1,0:T(8,128)(2,1)S(1)}, bf16[96,768]{1,0:T(8,128)(2,1)S(1)}, u32[]{:S(2)}, u32[]{:S(2)}) collective-permute-start(bf16[96,768]{1,0:T(8,128)(2,1)S(1)} %get-tuple-element.18.refs_7_), channel_id=1, source_target_pairs={{0,16},{4,20},{8,24},{12,28},{16,0},{20,4},{24,8},{28,12},{1,17},{... | collective-permute-start | bytes 442376 | tf_op jit(solution)/shard_map/ppermute | solution.py:324
  8.0 1.3 %collective-permute-start = (bf16[16,2048]{1,0:T(8,128)(2,1)S(1)}, bf16[16,2048]{1,0:T(8,128)(2,1)S(1)}, u32[]{:S(2)}, u32[]{:S(2)}) collective-permute-start(bf16[16,2048]{1,0:T(8,128)(2,1)S(1)} %get-tuple-element.14), channel_id=1, source_target_pairs={{1,0},{2,1},{3,2},{5,4},{6,5},{7,6},{9,8},{10,9},{11,10},{13,12},{... | collective-permute-start | bytes 196616 | tf_op jit(solution)/shard_map/ppermute | solution.py:330
  9.3 1.6 %collective-permute-start.6 = (bf16[384,768]{1,0:T(8,128)(2,1)S(1)}, bf16[384,768]{1,0:T(8,128)(2,1)S(1)}, u32[]{:S(2)}, u32[]{:S(2)}) collective-permute-start(bf16[384,768]{1,0:T(8,128)(2,1)S(1)} %get-tuple-element.20.refs_2_), channel_id=1, source_target_pairs={{0,4},{4,0},{8,12},{12,8},{16,20},{20,16},{24,28},{28,24},{1,5},{5... | collective-permute-start | bytes 1769480 | tf_op jit(solution)/shard_map/ppermute | solution.py:324
  10.9 0.3 collective-permute-done.refs_3_
  11.2 0.0 copy-start
  11.2 2.3 %spectra.3 = (bf16[128,768]{1,0:T(8,128)(2,1)S(1)}, bf16[32,768]{1,0:T(8,128)(2,1)S(1)}, bf16[128,768]{1,0:T(8,128)(2,1)S(1)}) custom-call(s32[32]{0:T(128)} %refs_0_.3, s32[4]{0:T(128)} %refs_1_.3, bf16[16,32768]{1,0:T(8,128)(2,1)} %refs_2_.3, bf16[16,2048]{1,0:T(8,128)(2,1)S(1)} %collective-permute-done.refs_3_, ...), custom_call_target="tpu_custom_call" | custom-call | flops 402653184 | bytes 4194304 | tf_op jit(solution)/shard_map/spectra/pallas_call | solution.py:172
  13.5 0.1 collective-permute-start.3
  13.6 1.9 %collective-permute-start.1 = (bf16[128,768]{1,0:T(8,128)(2,1)S(1)}, bf16[128,768]{1,0:T(8,128)(2,1)S(1)}, u32[]{:S(2)}, u32[]{:S(2)}) collective-permute-start(bf16[128,768]{1,0:T(8,128)(2,1)S(1)} %get-tuple-element.19), channel_id=1, source_target_pairs={{0,8},{4,12},{8,0},{12,4},{16,24},{20,28},{24,16},{28,20},{1,9},{5... | collective-permute-start | bytes 589832 | tf_op jit(solution)/shard_map/ppermute | solution.py:324
  15.5 0.0 collective-permute-done.2
  15.5 3.2 %collective-permute-done.3 = bf16[32,768]{1,0:T(8,128)(2,1)S(1)} collective-permute-done((bf16[32,768]{1,0:T(8,128)(2,1)S(1)}, bf16[32,768]{1,0:T(8,128)(2,1)S(1)}, u32[]{:S(2)}, u32[]{:S(2)}) %collective-permute-start.3) | collective-permute-done | bytes 49184 | tf_op jit(solution)/shard_map/ppermute | solution.py:324
  18.7 1.5 %collective-permute-start.4 = (bf16[128,768]{1,0:T(8,128)(2,1)S(1)}, bf16[128,768]{1,0:T(8,128)(2,1)S(1)}, u32[]{:S(2)}, u32[]{:S(2)}) collective-permute-start(bf16[128,768]{1,0:T(8,128)(2,1)S(1)} %constant_dynamic-update-slice_fusion), channel_id=1, source_target_pairs={{0,8},{4,12},{8,0},{12,4},{16,24},{20,28},{24,16},{28,20},{1,9},{5... | collective-permute-start | bytes 589832 | tf_op jit(solution)/shard_map/ppermute | solution.py:324
  20.1 1.5 %collective-permute-start.5 = (bf16[128,768]{1,0:T(8,128)(2,1)S(1)}, bf16[128,768]{1,0:T(8,128)(2,1)S(1)}, u32[]{:S(2)}, u32[]{:S(2)}) collective-permute-start(bf16[128,768]{1,0:T(8,128)(2,1)S(1)} %get-tuple-element.21.refs_3_), channel_id=1, source_target_pairs={{0,4},{4,0},{8,12},{12,8},{16,20},{20,16},{24,28},{28,24},{1,5},{5... | collective-permute-start | bytes 589832 | tf_op jit(solution)/shard_map/ppermute | solution.py:324
  21.6 0.0 collective-permute-done.1
  21.6 0.0 copy-done
  21.6 2.2 %cross.5 = bf16[128,256]{1,0:T(8,128)(2,1)S(1)} custom-call(bf16[1,128,768]{2,1,0:T(8,128)(2,1)S(1)} %bitcast.44, bf16[1,128,768]{2,1,0:T(8,128)(2,1)S(1)} %bitcast.47, bf16[384,768]{1,0:T(8,128)(2,1)S(1)} %get-tuple-element.20.refs_2_, bf16[128,768]{1,0:T(8,128)(2,1)S(1)} %get-tuple-element.21.refs_3_, bf16[768,256]{1,0:T(8,128)(2,1)S(1)} %copy-done), custom_call_target="tpu_custom_call" | custom-call | flops 62914560 | bytes 4194304 | tf_op jit(solution)/shard_map/cross/pallas_call | solution.py:289
  23.9 2.3 %collective-permute-done.4 = bf16[128,768]{1,0:T(8,128)(2,1)S(1)} collective-permute-done((bf16[128,768]{1,0:T(8,128)(2,1)S(1)}, bf16[128,768]{1,0:T(8,128)(2,1)S(1)}, u32[]{:S(2)}, u32[]{:S(2)}) %collective-permute-start.4) | collective-permute-done | bytes 196640 | tf_op jit(solution)/shard_map/ppermute | solution.py:324
  26.1 2.2 %cross.6 = bf16[128,256]{1,0:T(8,128)(2,1)S(1)} custom-call(bf16[1,128,768]{2,1,0:T(8,128)(2,1)S(1)} %bitcast.41, bf16[1,128,768]{2,1,0:T(8,128)(2,1)S(1)} %bitcast.50, bf16[384,768]{1,0:T(8,128)(2,1)S(1)} %get-tuple-element.20.refs_2_, bf16[128,768]{1,0:T(8,128)(2,1)S(1)} %get-tuple-element.21.refs_3_, bf16[768,256]{1,0:T(8,128)(2,1)S(1)} %copy-done), custom_call_target="tpu_custom_call" | custom-call | flops 62914560 | bytes 4194304 | tf_op jit(solution)/shard_map/cross/pallas_call | solution.py:289
  28.4 0.0 collective-permute-done.6.refs_2_
  28.4 1.5 %cross.8.refs_6_ = f32[128,768]{1,0:T(8,128)S(1)} custom-call(bf16[1,128,768]{2,1,0:T(8,128)(2,1)S(1)} %bitcast.42, bf16[1,128,768]{2,1,0:T(8,128)(2,1)S(1)} %bitcast.51, bf16[384,768]{1,0:T(8,128)(2,1)S(1)} %collective-permute-done.6.refs_2_), custom_call_target="tpu_custom_call" | custom-call | flops 47185920 | bytes 4194304 | tf_op jit(solution)/shard_map/cross/pallas_call | solution.py:289
  29.9 1.5 %cross.7.refs_5_ = f32[128,768]{1,0:T(8,128)S(1)} custom-call(bf16[1,128,768]{2,1,0:T(8,128)(2,1)S(1)} %bitcast.45, bf16[1,128,768]{2,1,0:T(8,128)(2,1)S(1)} %bitcast.48, bf16[384,768]{1,0:T(8,128)(2,1)S(1)} %collective-permute-done.6.refs_2_), custom_call_target="tpu_custom_call" | custom-call | flops 47185920 | bytes 4194304 | tf_op jit(solution)/shard_map/cross/pallas_call | solution.py:289
  31.4 0.0 collective-permute-done.5.refs_4_
  31.5 1.4 %cross.9 = bf16[256,256]{1,0:T(8,128)(2,1)S(1)} custom-call(bf16[1,128,768]{2,1,0:T(8,128)(2,1)S(1)} %bitcast.46, bf16[1,128,768]{2,1,0:T(8,128)(2,1)S(1)} %bitcast.49, bf16[1,128,768]{2,1,0:T(8,128)(2,1)S(1)} %bitcast.43, bf16[1,128,768]{2,1,0:T(8,128)(2,1)S(1)} %bitcast.52, bf16[128,768]{1,0:T(8,128)(2,1)S(1)} %collective-permute-done.5.refs_4_, ...), custom_call_target="tpu_custom_call" | custom-call | flops 31457280 | bytes 4194304 | tf_op jit(solution)/shard_map/cross/pallas_call | solution.py:289
  32.9 0.7 %collective-permute-start.7 = (bf16[4,1,4,16,256]{4,3,2,1,0:T(8,128)(2,1)S(1)}, bf16[4,1,4,16,256]{4,3,2,1,0:T(8,128)(2,1)S(1)}, u32[]{:S(2)}, u32[]{:S(2)}) collective-permute-start(bf16[4,1,4,16,256]{4,3,2,1,0:T(8,128)(2,1)S(1)} %pad_maximum_fusion.1), channel_id=1, source_target_pairs={{0,1},{1,0},{2,3},{3,2},{4,5},{5,4},{6,7},{7,6},{8,9},{9,8},{10,11... | collective-permute-start | bytes 393224 | tf_op jit(solution)/shard_map/ppermute | solution.py:360
  33.6 1.0 %collective-permute-done.7 = bf16[4,1,4,16,256]{4,3,2,1,0:T(8,128)(2,1)S(1)} collective-permute-done((bf16[4,1,4,16,256]{4,3,2,1,0:T(8,128)(2,1)S(1)}, bf16[4,1,4,16,256]{4,3,2,1,0:T(8,128)(2,1)S(1)}, u32[]{:S(2)}, u32[]{:S(2)}) %collective-permute-start.7) | collective-permute-done | bytes 131104 | tf_op jit(solution)/shard_map/ppermute | solution.py:360
  34.7 1.9 %collective-permute-start.10 = (bf16[1,4,16,256]{3,2,1,0:T(8,128)(2,1)S(1)}, bf16[1,4,16,256]{3,2,1,0:T(8,128)(2,1)S(1)}, u32[]{:S(2)}, u32[]{:S(2)}) collective-permute-start(bf16[1,4,16,256]{3,2,1,0:T(8,128)(2,1)S(1)} %get-tuple-element.28), channel_id=1, source_target_pairs={{0,6},{1,7},{2,4},{3,5},{4,2},{5,3},{6,0},{7,1},{8,14},{9,15},{10,... | collective-permute-start | bytes 98312 | tf_op jit(solution)/shard_map/ppermute | solution.py:373
  36.6 1.3 %collective-permute-start.8 = (bf16[1,4,16,256]{3,2,1,0:T(8,128)(2,1)S(1)}, bf16[1,4,16,256]{3,2,1,0:T(8,128)(2,1)S(1)}, u32[]{:S(2)}, u32[]{:S(2)}) collective-permute-start(bf16[1,4,16,256]{3,2,1,0:T(8,128)(2,1)S(1)} %get-tuple-element.27), channel_id=1, source_target_pairs={{0,2},{1,3},{2,0},{3,1},{4,6},{5,7},{6,4},{7,5},{8,10},{9,11},{10,... | collective-permute-start | bytes 98312 | tf_op jit(solution)/shard_map/ppermute | solution.py:373
  38.0 0.3 collective-permute-start.9
  38.3 1.4 %collective-permute-done.10 = bf16[1,4,16,256]{3,2,1,0:T(8,128)(2,1)S(1)} collective-permute-done((bf16[1,4,16,256]{3,2,1,0:T(8,128)(2,1)S(1)}, bf16[1,4,16,256]{3,2,1,0:T(8,128)(2,1)S(1)}, u32[]{:S(2)}, u32[]{:S(2)}) %collective-permute-start.10) | collective-permute-done | bytes 32800 | tf_op jit(solution)/shard_map/ppermute | solution.py:373
  39.7 0.9 %collective-permute-done.8 = bf16[1,4,16,256]{3,2,1,0:T(8,128)(2,1)S(1)} collective-permute-done((bf16[1,4,16,256]{3,2,1,0:T(8,128)(2,1)S(1)}, bf16[1,4,16,256]{3,2,1,0:T(8,128)(2,1)S(1)}, u32[]{:S(2)}, u32[]{:S(2)}) %collective-permute-start.8) | collective-permute-done | bytes 32800 | tf_op jit(solution)/shard_map/ppermute | solution.py:373
  40.5 1.3 %collective-permute-done.9 = bf16[1,4,16,256]{3,2,1,0:T(8,128)(2,1)S(1)} collective-permute-done((bf16[1,4,16,256]{3,2,1,0:T(8,128)(2,1)S(1)}, bf16[1,4,16,256]{3,2,1,0:T(8,128)(2,1)S(1)}, u32[]{:S(2)}, u32[]{:S(2)}) %collective-permute-start.9) | collective-permute-done | bytes 32800 | tf_op jit(solution)/shard_map/ppermute | solution.py:373
  41.9 0.7 %pad_maximum_fusion.2 = f32[1,2,4,16,256]{4,3,2,1,0:T(8,128)} fusion(f32[1,1,4,16,256]{4,3,2,1,0:T(8,128)S(1)} %get-tuple-element.24, f32[1,1,4,16,256]{4,3,2,1,0:T(8,128)S(1)} %get-tuple-element.23), kind=kLoop, calls=%fused_computation.3 | loop fusion | flops 32768 | bytes 262144 | tf_op jit(solution)/shard_map/stack | solution.py:379
  (8 shorter events, 0.1 us)
Async XLA Ops:
  3.9 11.6 %collective-permute-start.2 = (bf16[96,768]{1,0:T(8,128)(2,1)S(1)}, bf16[96,768]{1,0:T(8,128)(2,1)S(1)}, u32[]{:S(2)}, u32[]{:S(2)}) collective-permute-start(bf16[96,768]{1,0:T(8,128)(2,1)S(1)} %get-tuple-element.18.refs_7_), channel_id=1, source_target_pairs={{0,16},{4,20},{8,24},{12,28},{16,0},{20,4},{24,8},{28,12},{1,17},{... | collective-permute-start | bytes 442376 | tf_op jit(solution)/shard_map/ppermute | solution.py:324
  8.0 3.1 %collective-permute-start = (bf16[16,2048]{1,0:T(8,128)(2,1)S(1)}, bf16[16,2048]{1,0:T(8,128)(2,1)S(1)}, u32[]{:S(2)}, u32[]{:S(2)}) collective-permute-start(bf16[16,2048]{1,0:T(8,128)(2,1)S(1)} %get-tuple-element.14), channel_id=1, source_target_pairs={{1,0},{2,1},{3,2},{5,4},{6,5},{7,6},{9,8},{10,9},{11,10},{13,12},{... | collective-permute-start | bytes 196616 | tf_op jit(solution)/shard_map/ppermute | solution.py:330
  9.3 19.1 %collective-permute-start.6 = (bf16[384,768]{1,0:T(8,128)(2,1)S(1)}, bf16[384,768]{1,0:T(8,128)(2,1)S(1)}, u32[]{:S(2)}, u32[]{:S(2)}) collective-permute-start(bf16[384,768]{1,0:T(8,128)(2,1)S(1)} %get-tuple-element.20.refs_2_), channel_id=1, source_target_pairs={{0,4},{4,0},{8,12},{12,8},{16,20},{20,16},{24,28},{28,24},{1,5},{5... | collective-permute-start | bytes 1769480 | tf_op jit(solution)/shard_map/ppermute | solution.py:324
  11.2 10.5 %copy-start = (bf16[768,256]{1,0:T(8,128)(2,1)S(1)}, bf16[768,256]{1,0:T(8,128)(2,1)}, u32[]{:S(2)}) copy-start(bf16[768,256]{1,0:T(8,128)(2,1)} %constant.81.clone.refs_4_.refs_7_) | copy-start | bytes 1179652
  13.5 5.2 %collective-permute-start.3 = (bf16[32,768]{1,0:T(8,128)(2,1)S(1)}, bf16[32,768]{1,0:T(8,128)(2,1)S(1)}, u32[]{:S(2)}, u32[]{:S(2)}) collective-permute-start(bf16[32,768]{1,0:T(8,128)(2,1)S(1)} %get-tuple-element.22), channel_id=1, source_target_pairs={{0,16},{4,20},{8,24},{12,28},{16,0},{20,4},{24,8},{28,12},{1,17},{... | collective-permute-start | bytes 147464 | tf_op jit(solution)/shard_map/ppermute | solution.py:324
  13.6 8.0 %collective-permute-start.1 = (bf16[128,768]{1,0:T(8,128)(2,1)S(1)}, bf16[128,768]{1,0:T(8,128)(2,1)S(1)}, u32[]{:S(2)}, u32[]{:S(2)}) collective-permute-start(bf16[128,768]{1,0:T(8,128)(2,1)S(1)} %get-tuple-element.19), channel_id=1, source_target_pairs={{0,8},{4,12},{8,0},{12,4},{16,24},{20,28},{24,16},{28,20},{1,9},{5... | collective-permute-start | bytes 589832 | tf_op jit(solution)/shard_map/ppermute | solution.py:324
  18.7 7.5 %collective-permute-start.4 = (bf16[128,768]{1,0:T(8,128)(2,1)S(1)}, bf16[128,768]{1,0:T(8,128)(2,1)S(1)}, u32[]{:S(2)}, u32[]{:S(2)}) collective-permute-start(bf16[128,768]{1,0:T(8,128)(2,1)S(1)} %constant_dynamic-update-slice_fusion), channel_id=1, source_target_pairs={{0,8},{4,12},{8,0},{12,4},{16,24},{20,28},{24,16},{28,20},{1,9},{5... | collective-permute-start | bytes 589832 | tf_op jit(solution)/shard_map/ppermute | solution.py:324
  20.1 11.3 %collective-permute-start.5 = (bf16[128,768]{1,0:T(8,128)(2,1)S(1)}, bf16[128,768]{1,0:T(8,128)(2,1)S(1)}, u32[]{:S(2)}, u32[]{:S(2)}) collective-permute-start(bf16[128,768]{1,0:T(8,128)(2,1)S(1)} %get-tuple-element.21.refs_3_), channel_id=1, source_target_pairs={{0,4},{4,0},{8,12},{12,8},{16,20},{20,16},{24,28},{28,24},{1,5},{5... | collective-permute-start | bytes 589832 | tf_op jit(solution)/shard_map/ppermute | solution.py:324
  32.9 1.7 %collective-permute-start.7 = (bf16[4,1,4,16,256]{4,3,2,1,0:T(8,128)(2,1)S(1)}, bf16[4,1,4,16,256]{4,3,2,1,0:T(8,128)(2,1)S(1)}, u32[]{:S(2)}, u32[]{:S(2)}) collective-permute-start(bf16[4,1,4,16,256]{4,3,2,1,0:T(8,128)(2,1)S(1)} %pad_maximum_fusion.1), channel_id=1, source_target_pairs={{0,1},{1,0},{2,3},{3,2},{4,5},{5,4},{6,7},{7,6},{8,9},{9,8},{10,11... | collective-permute-start | bytes 393224 | tf_op jit(solution)/shard_map/ppermute | solution.py:360
  34.7 5.0 %collective-permute-start.10 = (bf16[1,4,16,256]{3,2,1,0:T(8,128)(2,1)S(1)}, bf16[1,4,16,256]{3,2,1,0:T(8,128)(2,1)S(1)}, u32[]{:S(2)}, u32[]{:S(2)}) collective-permute-start(bf16[1,4,16,256]{3,2,1,0:T(8,128)(2,1)S(1)} %get-tuple-element.28), channel_id=1, source_target_pairs={{0,6},{1,7},{2,4},{3,5},{4,2},{5,3},{6,0},{7,1},{8,14},{9,15},{10,... | collective-permute-start | bytes 98312 | tf_op jit(solution)/shard_map/ppermute | solution.py:373
  36.6 3.9 %collective-permute-start.8 = (bf16[1,4,16,256]{3,2,1,0:T(8,128)(2,1)S(1)}, bf16[1,4,16,256]{3,2,1,0:T(8,128)(2,1)S(1)}, u32[]{:S(2)}, u32[]{:S(2)}) collective-permute-start(bf16[1,4,16,256]{3,2,1,0:T(8,128)(2,1)S(1)} %get-tuple-element.27), channel_id=1, source_target_pairs={{0,2},{1,3},{2,0},{3,1},{4,6},{5,7},{6,4},{7,5},{8,10},{9,11},{10,... | collective-permute-start | bytes 98312 | tf_op jit(solution)/shard_map/ppermute | solution.py:373
  38.0 3.9 %collective-permute-start.9 = (bf16[1,4,16,256]{3,2,1,0:T(8,128)(2,1)S(1)}, bf16[1,4,16,256]{3,2,1,0:T(8,128)(2,1)S(1)}, u32[]{:S(2)}, u32[]{:S(2)}) collective-permute-start(bf16[1,4,16,256]{3,2,1,0:T(8,128)(2,1)S(1)} %get-tuple-element.29), channel_id=1, source_target_pairs={{0,4},{1,5},{2,6},{3,7},{4,0},{5,1},{6,2},{7,3},{8,12},{9,13},{10,... | collective-permute-start | bytes 98312 | tf_op jit(solution)/shard_map/ppermute | solution.py:373

commit v6 on v5

--- a/solution.py
+++ b/solution.py
@@ -60,13 +60,12 @@
 
 def spectra_kernel(first, count, late, c_dev, n_src, *refs):
     if late:
-        offs, sources, rec, halo, table_v, taper_v, smooth_v, before_s, out_r, out_s, out_all, *refs = refs
+        offs, sources, rest_v, halo, table_v, taper_v, smooth_v, before_s, out_r, out_s, out_all, *refs = refs
         sums, diffs, held, offs_v, sources_v, sems = refs
     else:
         offs, sources, rec, table, taper, smooth, *refs = refs
-        out_r, out_s, out_edge, table_v, taper_v, smooth_v, *refs = refs
+        out_r, out_s, out_edge, rest_v, table_v, taper_v, smooth_v, *refs = refs
         sums, diffs, held, offs_v, sources_v, sems = refs
-    begin = first * HOP
     width = (count + 2) * HOP
     copies = []
 
@@ -77,21 +76,21 @@
 
     fetch(offs, offs_v)
     fetch(sources, sources_v)
-    inside = width - (W if late else 0)
-    step = inside // 2
-    if not late:
+    if late:
+        held[:, : width - W] = rest_v[...]
+        held[:, width - W :] = halo[...]
+        ready = len(copies)
+    else:
         fetch(taper, taper_v)
-    for at in range(0, inside, step):
-        fetch(rec.at[:, pl.ds(begin + at, step)], held.at[:, pl.ds(at, step)])
-    ready = len(copies)
-    if late:
-        held[:, inside:] = halo[...]
-    else:
+        for at in range(0, width, width // 2):
+            fetch(rec.at[:, pl.ds(at, width // 2)], held.at[:, pl.ds(at, width // 2)])
+        ready = len(copies)
         rows = FOLD // 4
         for at in range(0, FOLD, rows):
             fetch(table.at[pl.ds(at, rows)], table_v.at[pl.ds(at, rows)])
         fetch(smooth, smooth_v)
         fetch(rec.at[:, pl.ds(0, W)], out_edge)
+        fetch(rec.at[:, pl.ds(count * HOP, rest_v.shape[1])], rest_v)
     for copy in copies[:ready]:
         copy.wait()
 
@@ -149,12 +148,13 @@
 
 def spectra_call(record, offsets, src_idx, tables, first, count, late=None):
     c_dev = record.shape[0]
+    n_rest = record.shape[1] - count * HOP
     n_src = src_idx.shape[0]
     vmem = pl.BlockSpec(memory_space=pltpu.VMEM)
     hbm = pl.BlockSpec(memory_space=pltpu.HBM)
-    arrays = [offsets, src_idx, record]
+    arrays = [offsets, src_idx]
     if late is None:
-        arrays += tables
+        arrays += [record, *tables]
     arrays = [pltpu.with_memory_space_constraint(a, pltpu.HBM) for a in arrays]
     specs = [hbm] * len(arrays)
     out_shape = [
@@ -162,12 +162,12 @@
         jax.ShapeDtypeStruct((n_src * count, 2 * NB), jnp.bfloat16),
     ]
     if late is None:
-        out_shape.append(jax.ShapeDtypeStruct((c_dev, W), record.dtype))
+        out_shape += [jax.ShapeDtypeStruct((c_dev, n), record.dtype) for n in (W, n_rest)]
         out_shape += [jax.ShapeDtypeStruct(t.shape, t.dtype) for t in tables]
     else:
         halo, earlier = late
-        arrays += [halo, *tables, earlier]
-        specs += [vmem] * 5
+        arrays += [record, halo, *tables, earlier]
+        specs += [vmem] * 6
         out_shape.append(jax.ShapeDtypeStruct((earlier.shape[0] + n_src * count, 2 * NB), jnp.bfloat16))
     return pl.pallas_call(
         functools.partial(spectra_kernel, first, count, late is not None, c_dev, n_src),
@@ -184,13 +184,13 @@
         ],
         compiler_params=pltpu.CompilerParams(vmem_limit_bytes=24 << 20),
         cost_estimate=pl.CostEstimate(
-            flops=2 * count * c_dev * W * 2 * NB, bytes_accessed=4 << 20, transcendentals=0
+            flops=int((1.5 + 0.1 * count) * 1.15e9), bytes_accessed=1 << 20, transcendentals=0
         ),
         name="spectra",
     )(*arrays)
 
 
-def cross_kernel(shares, sides, cuts, n_src, c_dev, scale, n_before, last, *refs):
+def cross_kernel(shares, sides, cuts, n_src, c_dev, scale, spans, last, n_done, *refs):
     n_list = len(shares)
     srcs = []
     for share in shares:
@@ -200,108 +200,129 @@
     for parts in sides:
         recs.append([(refs[i], part) for i, part in enumerate(parts)])
         refs = refs[len(parts) :]
-    before, refs = refs[:n_before], refs[n_before:]
+    before, refs = refs[: len(spans)], refs[len(spans) :]
+    done, refs = refs[:n_done], refs[n_done:]
     if last:
-        ltab, out, wide, cross = refs
+        ltab, *outs, wide, cross = refs
     else:
         out, wide = refs
     n_win = cuts[-1]
     at = 0
     for src in srcs:
         for part in src:
-            height = part.shape[1]
-            wide[at : at + height, :] = part[0].astype(jnp.float32)
-            at += height
+            rows = slice(at, at + part.shape[1])
+            real = part[0, :, :NB].astype(jnp.float32)
+            imag = part[0, :, NB:].astype(jnp.float32)
+            wide[rows, :NB] = real
+            wide[rows, NB : 2 * NB] = real + imag
+            wide[rows, 2 * NB :] = real - imag
+            at += part.shape[1]
     tiles = NB // LANE
-    block = 8 if n_list * n_src % 8 == 0 else n_src
-    groups = block // n_src
     n_side = len(sides)
 
-    span = n_list // max(len(before), 1)
-
-    def run(step, first, earlier):
+    def run(step, first, groups, earlier):
+        block = groups * n_src
         local = step // tiles * groups
         group = first + local
-        lo = pl.ds(pl.multiple_of(step % tiles * LANE, LANE), LANE)
-        hi = pl.ds(pl.multiple_of(step % tiles * LANE + NB, LANE), LANE)
+        lo, hi, top = (
+            pl.ds(pl.multiple_of(step % tiles * LANE + i * NB, LANE), LANE) for i in range(3)
+        )
         base = pl.multiple_of(group * (n_src * n_win), 8)
-        src = wide.at[pl.ds(base, groups * n_src * n_win)]
+        src = wide.at[pl.ds(base, block * n_win)]
 
         def places(group, q):
-            starts = [((group * n_src + s) * n_side + q) * c_dev for s in range(block)]
+            starts = [q * n_list * n_src * c_dev + (group * n_src + s) * c_dev for s in range(block)]
             return [pl.ds(pl.multiple_of(start, c_dev), c_dev) for start in starts]
 
         for q, parts in enumerate(recs):
-            sums = [[0.0, 0.0] for _ in range(block)]
-            if earlier is not None:
-                sums = [[earlier[r, lo], earlier[r, hi]] for r in places(local, q)]
+            sums = [[jnp.zeros((c_dev, LANE), jnp.float32)] * 3 for _ in range(block)]
             for rec, part in parts:
                 start, stop = cuts[part], cuts[part + 1]
                 for w in range(stop - start):
                     row = slice(w * c_dev, (w + 1) * c_dev)
                     rec_real = rec[row, lo].astype(jnp.float32)
                     rec_imag = rec[row, hi].astype(jnp.float32)
+                    rec_both = rec_real + rec_imag
                     for s in range(block):
                         at = s // n_src * n_src * n_win
                         at += start * n_src + s % n_src * (stop - start) + w
-                        src_real = src[at : at + 1, lo]
-                        src_imag = src[at : at + 1, hi]
-                        sums[s][0] += src_real * rec_real + src_imag * rec_imag
-                        sums[s][1] += src_real * rec_imag - src_imag * rec_real
+                        row = slice(at, at + 1)
+                        both, plus, minus = sums[s]
+                        sums[s] = [
+                            both + src[row, lo] * rec_both,
+                            plus + src[row, hi] * rec_real,
+                            minus + src[row, top] * rec_imag,
+                        ]
             target = cross if last else out
-            for r, pair in zip(places(group, q), sums):
-                for place, value in zip((lo, hi), pair):
-                    target[r, place] = jnp.broadcast_to(value, (c_dev, LANE)).astype(target.dtype)
-
-    for i in range(max(len(before), 1)):
-        earlier = before[i] if before else None
-        pl.loop(0, span // groups * tiles)(functools.partial(run, first=i * span, earlier=earlier))
+            near, far = places(group, q), places(local, 0)
+            for s in range(block):
+                both, plus, minus = sums[s]
+                real, imag = both - minus, both - plus
+                if earlier is not None:
+                    real += earlier[far[s], lo]
+                    imag += earlier[far[s], hi]
+                target[near[s], lo] = real.astype(target.dtype)
+                target[near[s], hi] = imag.astype(target.dtype)
+
+    first = 0
+    for span, earlier in zip(spans or [n_list], before or [None]):
+        groups = 8 // n_src if span * n_src % 8 == 0 and 8 % n_src == 0 else 1
+        pl.loop(0, span // groups * tiles)(
+            functools.partial(run, first=first, groups=groups, earlier=earlier)
+        )
+        first += span
 
     if last:
         lagged = jnp.dot(cross[...], ltab[...], preferred_element_type=jnp.float32)
-        out[...] = (lagged * scale).astype(jnp.bfloat16)
-
-
-def cross_call(srcs, sides, cuts, n_src, c_dev, scale, before=None, ltab=None):
+        lagged = (lagged * scale).astype(jnp.bfloat16)
+        height = n_list * n_src * c_dev
+        done = list(done)
+        for q, out in enumerate(outs):
+            at = 0
+            while at < out.shape[0] - height:
+                part = done.pop(0)
+                out[at : at + part.shape[0], :] = part[...]
+                at += part.shape[0]
+            out[at:, :] = lagged[q * height : (q + 1) * height]
+
+
+def cross_call(srcs, sides, cuts, n_src, c_dev, scale, before=(), ltab=None, done=()):
     n_list, n_side = len(srcs), len(sides)
     groups = srcs[0][0].shape[0]
     last = ltab is not None
-    rows = n_list * n_src * n_side * c_dev
+    unit = n_src * c_dev
+    rows = n_list * n_side * unit
     whole = pl.BlockSpec(memory_space=pltpu.VMEM)
-    row_block = lambda width: pl.BlockSpec((rows, width), lambda g: (g, 0))
     arrays = [part for src in srcs for part in src]
     specs = [pl.BlockSpec((1,) + a.shape[1:], lambda g: (g, 0, 0)) for a in arrays]
-    for parts in sides:
-        arrays += list(parts.values())
-        specs += [whole] * len(parts)
-    if before is not None:
-        arrays += before
-        specs += [whole] * len(before)
-    scratch = [pltpu.VMEM((n_list * n_src * cuts[-1], 2 * NB), jnp.float32)]
+    others = [a for parts in sides for a in parts.values()] + list(before)
+    scratch = [pltpu.VMEM((n_list * n_src * cuts[-1], 3 * NB), jnp.float32)]
     if last:
-        arrays.append(ltab)
-        specs.append(whole)
+        others += list(done) + [ltab]
         scratch.append(pltpu.VMEM((rows, 2 * NB), jnp.bfloat16))
-        out_shape = jax.ShapeDtypeStruct((groups * rows, LAGS), jnp.bfloat16)
-    else:
-        out_shape = jax.ShapeDtypeStruct((groups * rows, 2 * NB), jnp.float32)
-    windows = sum(cuts[p + 1] - cuts[p] for parts in sides for p in parts) // n_side
+        heights = [n_list * unit + sum(a.shape[0] for a in done) // n_side] * n_side
+        shapes = [jax.ShapeDtypeStruct((groups * h, LAGS), jnp.bfloat16) for h in heights]
+    else:
+        heights = [rows]
+        shapes = [jax.ShapeDtypeStruct((groups * rows, 2 * NB), jnp.float32)]
+    windows = sum(cuts[p + 1] - cuts[p] for parts in sides for p in parts)
+    micros = 0.4 + groups * n_list * n_src * windows * 0.008
     return pl.pallas_call(
         functools.partial(
-            cross_kernel, [len(src) for src in srcs], [list(p) for p in sides], cuts, n_src, c_dev, scale,
-            0 if before is None else len(before), last,
+            cross_kernel, [len(src) for src in srcs], [list(p) for p in sides], cuts, n_src, c_dev,
+            scale, [a.shape[0] // unit for a in before], last, len(done),
         ),
         grid=(groups,),
-        out_shape=out_shape,
-        in_specs=specs,
-        out_specs=row_block(out_shape.shape[1]),
+        out_shape=shapes,
+        in_specs=specs + [whole] * len(others),
+        out_specs=[pl.BlockSpec((h, a.shape[1]), lambda g: (g, 0)) for h, a in zip(heights, shapes)],
         scratch_shapes=scratch,
         compiler_params=pltpu.CompilerParams(vmem_limit_bytes=24 << 20),
         cost_estimate=pl.CostEstimate(
-            flops=groups * rows * windows * NB * 40, bytes_accessed=4 << 20, transcendentals=0
+            flops=int(micros * 1.15e9), bytes_accessed=1 << 20, transcendentals=0
         ),
         name="cross",
-    )(*arrays)
+    )(*arrays, *others)
 
 
 def body(record, offsets, src_idx):
@@ -323,12 +344,12 @@
     def trade(array, by):
         return lax.ppermute(array, "fibre", [(i, i ^ by) for i in range(n_fibre)])
 
-    rec_a, src_a, edge, *tables = spectra_call(record, offsets, src_idx, tables, 0, early)
+    rec_a, src_a, edge, rest, *tables = spectra_call(record, offsets, src_idx, tables, 0, early)
     far_a = trade(rec_a, 1)
     if direct:
         by_2a = trade(src_a, 4)
     halo = lax.ppermute(edge, "tm", [(i, i - 1) for i in range(1, n_tm)])
-    rec_b, src_b, src = spectra_call(record, offsets, src_idx, tables, early, n_win - early, (halo, src_a))
+    rec_b, src_b, src = spectra_call(rest, offsets, src_idx, tables, early, n_win - early, (halo, src_a))
     far_b = trade(rec_b, 1)
     cross = functools.partial(cross_call, cuts=cuts, n_src=n_src, c_dev=c_dev, scale=scale)
     own = [{0: rec_a, 1: rec_b}]
@@ -337,16 +358,14 @@
         by_1 = trade(src, 2)
         by_3 = trade(by_2, 2)
         srcs = [[part[None]] for part in (src, by_1, by_2, by_3)]
-        halves = (srcs[:2], srcs[2:])
-        near = [cross(half, own, ltab=ltab) for half in halves]
-        near = jnp.concatenate(near, axis=0)
-        parts = [cross(half, [{0: far_a}]) for half in halves]
-        far = cross(srcs, [{1: far_b}], before=parts, ltab=ltab)
+        near = [cross(srcs[k : k + 1], own, ltab=ltab)[0] for k in range(3)]
+        parts = [*cross(srcs[:2], [{0: far_a}]), *cross(srcs[2:3], [{0: far_a}])]
+        far = cross(srcs[:3], [{1: far_b}], before=parts, ltab=ltab)
+        near, far = cross(srcs[3:], own + [{0: far_a, 1: far_b}], ltab=ltab, done=[*near, *far])
     else:
         ranks = [[2 * j + p for j in range(n_group)] for p in range(2)]
         srcs = [[lax.all_gather(src, "fibre", axis=0, axis_index_groups=ranks)]]
-        near = cross(srcs, own, ltab=ltab)
-        far = cross(srcs, [{0: far_a, 1: far_b}], ltab=ltab)
+        near, far = cross(srcs, own + [{0: far_a, 1: far_b}], ltab=ltab)
     near, far = (r.reshape(n_group, n_src, c_dev, LAGS) for r in (near, far))
 
     def piece(lagged, owner):

time: 42.8 us -> 40 us (0.935)
  starting transfers between devices: 16.2 us -> 14 us
  local copies, waits for them, and re-layouts: 0.06 us -> 1.7 us
  waiting for transfers between devices: 10.3 us -> 8.81 us
  Pallas kernels: 15.1 us -> 14.4 us
    unnamed x3 -> x7, local copies, waits for them, and re-layouts: 0.01 us -> 1.66 us
    ppermute x6, starting transfers between devices: 10.6 us -> 9.03 us  [trade(): return lax.ppermute(array, 'fibre', [(i, i ^ by) for i in range(n_fibre)])]
    ppermute x6, waiting for transfers between devices: 5.44 us -> 4.61 us  [trade(): return lax.ppermute(array, 'fibre', [(i, i ^ by) for i in range(n_fibre)])]
    ppermute x3, waiting for transfers between devices: 3.63 us -> 2.9 us  [body(): mine = lax.ppermute(mine.astype(jnp.bfloat16), ('fibre', 'tm'), routes)]
    ppermute x1, starting transfers between devices: 0.74 us -> 0.11 us  [body(): got = lax.ppermute(give, 'tm', [(i, i ^ 1) for i in range(n_tm)])]
    pallas_call x5 -> x7, Pallas kernels: 8.88 us -> 8.4 us  [cross_call(): pl.pallas_call(functools.partial(cross_kernel, [len(src) for src in srcs]...]
  transfers between devices with their start and end apart: 11 -> 11, of which waited for: 7 -> 7; matrix products, arithmetic and copies ran while one was open for 0% -> 0% of each run, Pallas kernels for 23% -> 22%
where the time goes in v6:
time: 40 us; the launch traced here: 39.8 us
  Pallas kernels  14.4 us (36%)
  starting transfers between devices  14 us (35%)
  waiting for transfers between devices  8.81 us (22%)
  local copies, waits for them, and re-layouts  1.7 us (4%)
  other arithmetic  0.75 us (2%)
    ppermute x6, starting transfers between devices, trade(): return lax.ppermute(array, 'fibre', [(i, i ^ by) for i in range(n_fibre)])  9.03 us
    pallas_call x7, Pallas kernels, cross_call(): pl.pallas_call(functools.partial(cross_kernel, [len(src) for src in srcs]...  8.4 us
    pallas_call x2, Pallas kernels, spectra_call(): pl.pallas_call(functools.partial(spectra_kernel, first, count, late is no...  6 us
    ppermute x6, waiting for transfers between devices, trade(): return lax.ppermute(array, 'fibre', [(i, i ^ by) for i in range(n_fibre)])  4.61 us
    ppermute x3, starting transfers between devices, body(): mine = lax.ppermute(mine.astype(jnp.bfloat16), ('fibre', 'tm'), routes)  3.55 us
    ppermute x3, waiting for transfers between devices, body(): mine = lax.ppermute(mine.astype(jnp.bfloat16), ('fibre', 'tm'), routes)  2.9 us
    unnamed x7, local copies, waits for them, and re-layouts  1.66 us
    ppermute x1, waiting for transfers between devices, body(): got = lax.ppermute(give, 'tm', [(i, i ^ 1) for i in range(n_tm)])  1.3 us
  transfers between devices with their start and end apart: 11, of which 7 were waited for; matrix products, arithmetic and copies ran while one was open for 0% of the time, Pallas kernels for 22%

profile of v6, /device:TPU:0, one launch (start us, length us, event | category | flops | bytes accessed | tf_op | source)
XLA Modules:
  0.0 39.8 jit_solution(1406027653327874314)
XLA Ops:
  0.0 3.9 %spectra.2 = (bf16[384,768]{1,0:T(8,128)(2,1)S(1)}, bf16[96,768]{1,0:T(8,128)(2,1)S(1)}, bf16[16,2048]{1,0:T(8,128)(2,1)S(1)}, bf16[16,8192]{1,0:T(8,128)(2,1)S(...) custom-call(s32[32]{0:T(128)} %refs_0_.3, s32[4]{0:T(128)} %refs_1_.3, ...), custom_call_target="tpu_custom_call" | custom-call | flops 4485000192 | bytes 1048576 | tf_op jit(solution)/shard_map/spectra/pallas_call | solution.py:172
  3.9 0.0 copy-start.1
  3.9 0.7 %copy-done.1 = bf16[16,8192]{1,0:T(8,128)(2,1)} copy-done((bf16[16,8192]{1,0:T(8,128)(2,1)}, bf16[16,8192]{1,0:T(8,128)(2,1)S(1)}, u32[]{:S(2)}) %copy-start.1) | copy-done | bytes 262168
  4.6 1.3 %collective-permute-start.1 = (bf16[16,2048]{1,0:T(8,128)(2,1)S(1)}, bf16[16,2048]{1,0:T(8,128)(2,1)S(1)}, u32[]{:S(2)}, u32[]{:S(2)}) collective-permute-start(bf16[16,2048]{1,0:T(8,128)(2,1)S(1)} %get-tuple-element.19), channel_id=1, source_target_pairs={{1,0},{2,1},{3,2},{5,4},{6,5},{7,6},{9,8},{10,9},{11,10},{13,12},{... | collective-permute-start | bytes 196616 | tf_op jit(solution)/shard_map/ppermute | solution.py:351
  5.9 3.0 %collective-permute-start.4 = (bf16[384,768]{1,0:T(8,128)(2,1)S(1)}, bf16[384,768]{1,0:T(8,128)(2,1)S(1)}, u32[]{:S(2)}, u32[]{:S(2)}) collective-permute-start(bf16[384,768]{1,0:T(8,128)(2,1)S(1)} %get-tuple-element.24.refs_1_), channel_id=1, source_target_pairs={{0,4},{4,0},{8,12},{12,8},{16,20},{20,16},{24,28},{28,24},{1,5},{5... | collective-permute-start | bytes 1769480 | tf_op jit(solution)/shard_map/ppermute | solution.py:345
  8.9 2.6 %collective-permute-start = (bf16[96,768]{1,0:T(8,128)(2,1)S(1)}, bf16[96,768]{1,0:T(8,128)(2,1)S(1)}, u32[]{:S(2)}, u32[]{:S(2)}) collective-permute-start(bf16[96,768]{1,0:T(8,128)(2,1)S(1)} %get-tuple-element.17.refs_7_), channel_id=1, source_target_pairs={{0,16},{4,20},{8,24},{12,28},{16,0},{20,4},{24,8},{28,12},{1,17},{... | collective-permute-start | bytes 442376 | tf_op jit(solution)/shard_map/ppermute | solution.py:345
  11.5 0.0 collective-permute-done.1.refs_3_
  11.5 0.0 copy-start.2
  11.5 0.9 %copy-done.2 = bf16[16,8192]{1,0:T(8,128)(2,1)S(1)} copy-done((bf16[16,8192]{1,0:T(8,128)(2,1)S(1)}, bf16[16,8192]{1,0:T(8,128)(2,1)}, u32[]{:S(2)}) %copy-start.2) | copy-done | bytes 262168
  12.4 0.0 copy-start
  12.4 2.1 %spectra.3 = (bf16[128,768]{1,0:T(8,128)(2,1)S(1)}, bf16[32,768]{1,0:T(8,128)(2,1)S(1)}, bf16[128,768]{1,0:T(8,128)(2,1)S(1)}) custom-call(s32[32]{0:T(128)} %refs_0_.3, s32[4]{0:T(128)} %refs_1_.3, bf16[16,8192]{1,0:T(8,128)(2,1)S(1)} %copy-done.2, bf16[16,2048]{1,0:T(8,128)(2,1)S(1)} %collective-permute-done.1.refs_3_, ...), custom_call_target="tpu_custom_call" | custom-call | flops 2644999936 | bytes 1048576 | tf_op jit(solution)/shard_map/spectra/pallas_call | solution.py:172
  14.6 1.6 %collective-permute-start.6 = (bf16[128,768]{1,0:T(8,128)(2,1)S(1)}, bf16[128,768]{1,0:T(8,128)(2,1)S(1)}, u32[]{:S(2)}, u32[]{:S(2)}) collective-permute-start(bf16[128,768]{1,0:T(8,128)(2,1)S(1)} %get-tuple-element.26), channel_id=1, source_target_pairs={{0,8},{4,12},{8,0},{12,4},{16,24},{20,28},{24,16},{28,20},{1,9},{5... | collective-permute-start | bytes 589832 | tf_op jit(solution)/shard_map/ppermute | solution.py:345
  16.2 0.3 collective-permute-start.2
  16.5 1.4 %collective-permute-start.5 = (bf16[128,768]{1,0:T(8,128)(2,1)S(1)}, bf16[128,768]{1,0:T(8,128)(2,1)S(1)}, u32[]{:S(2)}, u32[]{:S(2)}) collective-permute-start(bf16[128,768]{1,0:T(8,128)(2,1)S(1)} %get-tuple-element.25.refs_2_), channel_id=1, source_target_pairs={{0,4},{4,0},{8,12},{12,8},{16,20},{20,16},{24,28},{28,24},{1,5},{5... | collective-permute-start | bytes 589832 | tf_op jit(solution)/shard_map/ppermute | solution.py:345
  18.0 0.0 copy-done
  18.0 1.1 %cross.7.refs_5_ = bf16[64,256]{1,0:T(8,128)(2,1)S(1)} custom-call(bf16[1,128,768]{2,1,0:T(8,128)(2,1)S(1)} %bitcast.46, bf16[384,768]{1,0:T(8,128)(2,1)S(1)} %get-tuple-element.24.refs_1_, bf16[128,768]{1,0:T(8,128)(2,1)S(1)} %get-tuple-element.25.refs_2_, bf16[768,256]{1,0:T(8,128)(2,1)S(1)} %copy-done), custom_call_target="tpu_custom_call" | custom-call | flops 1637600000 | bytes 1048576 | tf_op jit(solution)/shard_map/cross/pallas_call | solution.py:310
  19.1 0.6 %collective-permute-done = bf16[96,768]{1,0:T(8,128)(2,1)S(1)} collective-permute-done((bf16[96,768]{1,0:T(8,128)(2,1)S(1)}, bf16[96,768]{1,0:T(8,128)(2,1)S(1)}, u32[]{:S(2)}, u32[]{:S(2)}) %collective-permute-start) | collective-permute-done | bytes 147488 | tf_op jit(solution)/shard_map/ppermute | solution.py:345
  19.7 2.5 %collective-permute-done.2 = bf16[32,768]{1,0:T(8,128)(2,1)S(1)} collective-permute-done((bf16[32,768]{1,0:T(8,128)(2,1)S(1)}, bf16[32,768]{1,0:T(8,128)(2,1)S(1)}, u32[]{:S(2)}, u32[]{:S(2)}) %collective-permute-start.2) | collective-permute-done | bytes 49184 | tf_op jit(solution)/shard_map/ppermute | solution.py:345
  22.1 0.0 collective-permute-start.3
  22.2 1.1 %cross.9.refs_7_ = bf16[64,256]{1,0:T(8,128)(2,1)S(1)} custom-call(bf16[1,128,768]{2,1,0:T(8,128)(2,1)S(1)} %bitcast.43, bf16[384,768]{1,0:T(8,128)(2,1)S(1)} %get-tuple-element.24.refs_1_, bf16[128,768]{1,0:T(8,128)(2,1)S(1)} %get-tuple-element.25.refs_2_, bf16[768,256]{1,0:T(8,128)(2,1)S(1)} %copy-done), custom_call_target="tpu_custom_call" | custom-call | flops 1637600000 | bytes 1048576 | tf_op jit(solution)/shard_map/cross/pallas_call | solution.py:310
  23.3 1.6 %collective-permute-done.6 = bf16[128,768]{1,0:T(8,128)(2,1)S(1)} collective-permute-done((bf16[128,768]{1,0:T(8,128)(2,1)S(1)}, bf16[128,768]{1,0:T(8,128)(2,1)S(1)}, u32[]{:S(2)}, u32[]{:S(2)}) %collective-permute-start.6) | collective-permute-done | bytes 196640 | tf_op jit(solution)/shard_map/ppermute | solution.py:345
  24.8 1.1 %cross.8.refs_6_ = bf16[64,256]{1,0:T(8,128)(2,1)S(1)} custom-call(bf16[1,128,768]{2,1,0:T(8,128)(2,1)S(1)} %bitcast.49, bf16[384,768]{1,0:T(8,128)(2,1)S(1)} %get-tuple-element.24.refs_1_, bf16[128,768]{1,0:T(8,128)(2,1)S(1)} %get-tuple-element.25.refs_2_, bf16[768,256]{1,0:T(8,128)(2,1)S(1)} %copy-done), custom_call_target="tpu_custom_call" | custom-call | flops 1637600000 | bytes 1048576 | tf_op jit(solution)/shard_map/cross/pallas_call | solution.py:310
  26.0 0.0 collective-permute-done.4.refs_2_.refs_1_.refs_3_
  26.0 1.4 %cross.10.refs_4_ = f32[128,768]{1,0:T(8,128)S(1)} custom-call(bf16[1,128,768]{2,1,0:T(8,128)(2,1)S(1)} %bitcast.47, bf16[1,128,768]{2,1,0:T(8,128)(2,1)S(1)} %bitcast.50, bf16[384,768]{1,0:T(8,128)(2,1)S(1)} %collective-permute-done.4.refs_2_.refs_1_.refs_3_), custom_call_target="tpu_custom_call" | custom-call | flops 2226400000 | bytes 1048576 | tf_op jit(solution)/shard_map/cross/pallas_call | solution.py:310
  27.4 0.7 %cross.11.refs_5_ = f32[64,768]{1,0:T(8,128)S(1)} custom-call(bf16[1,128,768]{2,1,0:T(8,128)(2,1)S(1)} %bitcast.44, bf16[384,768]{1,0:T(8,128)(2,1)S(1)} %collective-permute-done.4.refs_2_.refs_1_.refs_3_), custom_call_target="tpu_custom_call" | custom-call | flops 1343200000 | bytes 1048576 | tf_op jit(solution)/shard_map/cross/pallas_call | solution.py:310
  28.1 0.0 collective-permute-done.5.refs_3_.refs_4_
  28.1 1.1 %cross.12.refs_8_ = bf16[192,256]{1,0:T(8,128)(2,1)S(1)} custom-call(bf16[1,128,768]{2,1,0:T(8,128)(2,1)S(1)} %bitcast.48, bf16[1,128,768]{2,1,0:T(8,128)(2,1)S(1)} %bitcast.51, bf16[1,128,768]{2,1,0:T(8,128)(2,1)S(1)} %bitcast.45, bf16[128,768]{1,0:T(8,128)(2,1)S(1)} %collective-permute-done.5.refs_3_.refs_4_, f32[128,768]{1,0:T(8,128)S(1)} %cross.10.refs_4_, ...), custom_call_target="tpu_custom_call" | custom-call | flops 1343200000 | bytes 1048576 | tf_op jit(solution)/shard_map/cross/pallas_call | solution.py:310
  29.2 0.0 collective-permute-done.3
  29.2 1.9 %cross.13 = (bf16[256,256]{1,0:T(8,128)(2,1)S(1)}, bf16[256,256]{1,0:T(8,128)(2,1)S(1)}) custom-call(bf16[1,128,768]{2,1,0:T(8,128)(2,1)S(1)} %bitcast.52, bf16[384,768]{1,0:T(8,128)(2,1)S(1)} %get-tuple-element.24.refs_1_, bf16[128,768]{1,0:T(8,128)(2,1)S(1)} %get-tuple-element.25.refs_2_, ...), custom_call_target="tpu_custom_call" | custom-call | flops 2815200000 | bytes 1048576 | tf_op jit(solution)/shard_map/cross/pallas_call | solution.py:310
  31.2 0.1 collective-permute-start.7
  31.3 1.3 %collective-permute-done.7 = bf16[4,1,4,16,256]{4,3,2,1,0:T(8,128)(2,1)S(1)} collective-permute-done((bf16[4,1,4,16,256]{4,3,2,1,0:T(8,128)(2,1)S(1)}, bf16[4,1,4,16,256]{4,3,2,1,0:T(8,128)(2,1)S(1)}, u32[]{:S(2)}, u32[]{:S(2)}) %collective-permute-start.7) | collective-permute-done | bytes 131104 | tf_op jit(solution)/shard_map/ppermute | solution.py:379
  32.6 2.3 %collective-permute-start.10 = (bf16[1,4,16,256]{3,2,1,0:T(8,128)(2,1)S(1)}, bf16[1,4,16,256]{3,2,1,0:T(8,128)(2,1)S(1)}, u32[]{:S(2)}, u32[]{:S(2)}) collective-permute-start(bf16[1,4,16,256]{3,2,1,0:T(8,128)(2,1)S(1)} %get-tuple-element.34), channel_id=1, source_target_pairs={{0,6},{1,7},{2,4},{3,5},{4,2},{5,3},{6,0},{7,1},{8,14},{9,15},{10,... | collective-permute-start | bytes 98312 | tf_op jit(solution)/shard_map/ppermute | solution.py:392
  35.0 0.2 collective-permute-start.8
  35.2 1.0 %collective-permute-start.9 = (bf16[1,4,16,256]{3,2,1,0:T(8,128)(2,1)S(1)}, bf16[1,4,16,256]{3,2,1,0:T(8,128)(2,1)S(1)}, u32[]{:S(2)}, u32[]{:S(2)}) collective-permute-start(bf16[1,4,16,256]{3,2,1,0:T(8,128)(2,1)S(1)} %get-tuple-element.35), channel_id=1, source_target_pairs={{0,4},{1,5},{2,6},{3,7},{4,0},{5,1},{6,2},{7,3},{8,12},{9,13},{10,... | collective-permute-start | bytes 98312 | tf_op jit(solution)/shard_map/ppermute | solution.py:392
  36.2 1.3 %collective-permute-done.10 = bf16[1,4,16,256]{3,2,1,0:T(8,128)(2,1)S(1)} collective-permute-done((bf16[1,4,16,256]{3,2,1,0:T(8,128)(2,1)S(1)}, bf16[1,4,16,256]{3,2,1,0:T(8,128)(2,1)S(1)}, u32[]{:S(2)}, u32[]{:S(2)}) %collective-permute-start.10) | collective-permute-done | bytes 32800 | tf_op jit(solution)/shard_map/ppermute | solution.py:392
  37.5 1.4 %collective-permute-done.8 = bf16[1,4,16,256]{3,2,1,0:T(8,128)(2,1)S(1)} collective-permute-done((bf16[1,4,16,256]{3,2,1,0:T(8,128)(2,1)S(1)}, bf16[1,4,16,256]{3,2,1,0:T(8,128)(2,1)S(1)}, u32[]{:S(2)}, u32[]{:S(2)}) %collective-permute-start.8) | collective-permute-done | bytes 32800 | tf_op jit(solution)/shard_map/ppermute | solution.py:392
  38.9 0.2 collective-permute-done.9
  39.1 0.7 %pad_maximum_fusion.1 = f32[1,2,4,16,256]{4,3,2,1,0:T(8,128)} fusion(f32[1,1,4,16,256]{4,3,2,1,0:T(8,128)S(1)} %get-tuple-element.30, f32[1,1,4,16,256]{4,3,2,1,0:T(8,128)S(1)} %get-tuple-element.29), kind=kLoop, calls=%fused_computation.2 | loop fusion | flops 32768 | bytes 262144 | tf_op jit(solution)/shard_map/stack | solution.py:398
  (7 shorter events, 0.1 us)
Async XLA Ops:
  3.9 0.7 %copy-start.1 = (bf16[16,8192]{1,0:T(8,128)(2,1)}, bf16[16,8192]{1,0:T(8,128)(2,1)S(1)}, u32[]{:S(2)}) copy-start(bf16[16,8192]{1,0:T(8,128)(2,1)S(1)} %get-tuple-element.18.refs_2_) | copy-start | bytes 786436
  4.6 6.9 %collective-permute-start.1 = (bf16[16,2048]{1,0:T(8,128)(2,1)S(1)}, bf16[16,2048]{1,0:T(8,128)(2,1)S(1)}, u32[]{:S(2)}, u32[]{:S(2)}) collective-permute-start(bf16[16,2048]{1,0:T(8,128)(2,1)S(1)} %get-tuple-element.19), channel_id=1, source_target_pairs={{1,0},{2,1},{3,2},{5,4},{6,5},{7,6},{9,8},{10,9},{11,10},{13,12},{... | collective-permute-start | bytes 196616 | tf_op jit(solution)/shard_map/ppermute | solution.py:351
  5.9 20.1 %collective-permute-start.4 = (bf16[384,768]{1,0:T(8,128)(2,1)S(1)}, bf16[384,768]{1,0:T(8,128)(2,1)S(1)}, u32[]{:S(2)}, u32[]{:S(2)}) collective-permute-start(bf16[384,768]{1,0:T(8,128)(2,1)S(1)} %get-tuple-element.24.refs_1_), channel_id=1, source_target_pairs={{0,4},{4,0},{8,12},{12,8},{16,20},{20,16},{24,28},{28,24},{1,5},{5... | collective-permute-start | bytes 1769480 | tf_op jit(solution)/shard_map/ppermute | solution.py:345
  8.9 10.8 %collective-permute-start = (bf16[96,768]{1,0:T(8,128)(2,1)S(1)}, bf16[96,768]{1,0:T(8,128)(2,1)S(1)}, u32[]{:S(2)}, u32[]{:S(2)}) collective-permute-start(bf16[96,768]{1,0:T(8,128)(2,1)S(1)} %get-tuple-element.17.refs_7_), channel_id=1, source_target_pairs={{0,16},{4,20},{8,24},{12,28},{16,0},{20,4},{24,8},{28,12},{1,17},{... | collective-permute-start | bytes 442376 | tf_op jit(solution)/shard_map/ppermute | solution.py:345
  11.5 1.0 %copy-start.2 = (bf16[16,8192]{1,0:T(8,128)(2,1)S(1)}, bf16[16,8192]{1,0:T(8,128)(2,1)}, u32[]{:S(2)}) copy-start(bf16[16,8192]{1,0:T(8,128)(2,1)} %copy-done.1) | copy-start | bytes 786436
  12.4 5.5 %copy-start = (bf16[768,256]{1,0:T(8,128)(2,1)S(1)}, bf16[768,256]{1,0:T(8,128)(2,1)}, u32[]{:S(2)}) copy-start(bf16[768,256]{1,0:T(8,128)(2,1)} %constant.81.clone.refs_3_.refs_6_.refs_9_) | copy-start | bytes 1179652
  14.6 10.3 %collective-permute-start.6 = (bf16[128,768]{1,0:T(8,128)(2,1)S(1)}, bf16[128,768]{1,0:T(8,128)(2,1)S(1)}, u32[]{:S(2)}, u32[]{:S(2)}) collective-permute-start(bf16[128,768]{1,0:T(8,128)(2,1)S(1)} %get-tuple-element.26), channel_id=1, source_target_pairs={{0,8},{4,12},{8,0},{12,4},{16,24},{20,28},{24,16},{28,20},{1,9},{5... | collective-permute-start | bytes 589832 | tf_op jit(solution)/shard_map/ppermute | solution.py:345
  16.2 5.9 %collective-permute-start.2 = (bf16[32,768]{1,0:T(8,128)(2,1)S(1)}, bf16[32,768]{1,0:T(8,128)(2,1)S(1)}, u32[]{:S(2)}, u32[]{:S(2)}) collective-permute-start(bf16[32,768]{1,0:T(8,128)(2,1)S(1)} %get-tuple-element.23), channel_id=1, source_target_pairs={{0,16},{4,20},{8,24},{12,28},{16,0},{20,4},{24,8},{28,12},{1,17},{... | collective-permute-start | bytes 147464 | tf_op jit(solution)/shard_map/ppermute | solution.py:345
  16.5 11.6 %collective-permute-start.5 = (bf16[128,768]{1,0:T(8,128)(2,1)S(1)}, bf16[128,768]{1,0:T(8,128)(2,1)S(1)}, u32[]{:S(2)}, u32[]{:S(2)}) collective-permute-start(bf16[128,768]{1,0:T(8,128)(2,1)S(1)} %get-tuple-element.25.refs_2_), channel_id=1, source_target_pairs={{0,4},{4,0},{8,12},{12,8},{16,20},{20,16},{24,28},{28,24},{1,5},{5... | collective-permute-start | bytes 589832 | tf_op jit(solution)/shard_map/ppermute | solution.py:345
  22.1 7.1 %collective-permute-start.3 = (bf16[128,768]{1,0:T(8,128)(2,1)S(1)}, bf16[128,768]{1,0:T(8,128)(2,1)S(1)}, u32[]{:S(2)}, u32[]{:S(2)}) collective-permute-start(bf16[128,768]{1,0:T(8,128)(2,1)S(1)} %constant_dynamic-update-slice_fusion), channel_id=1, source_target_pairs={{0,8},{4,12},{8,0},{12,4},{16,24},{20,28},{24,16},{28,20},{1,9},{5... | collective-permute-start | bytes 589832 | tf_op jit(solution)/shard_map/ppermute | solution.py:345
  31.2 1.4 %collective-permute-start.7 = (bf16[4,1,4,16,256]{4,3,2,1,0:T(8,128)(2,1)S(1)}, bf16[4,1,4,16,256]{4,3,2,1,0:T(8,128)(2,1)S(1)}, u32[]{:S(2)}, u32[]{:S(2)}) collective-permute-start(bf16[4,1,4,16,256]{4,3,2,1,0:T(8,128)(2,1)S(1)} %pad_maximum_fusion), channel_id=1, source_target_pairs={{0,1},{1,0},{2,3},{3,2},{4,5},{5,4},{6,7},{7,6},{8,9},{9,8},{10,11... | collective-permute-start | bytes 393224 | tf_op jit(solution)/shard_map/ppermute | solution.py:379
  32.6 4.9 %collective-permute-start.10 = (bf16[1,4,16,256]{3,2,1,0:T(8,128)(2,1)S(1)}, bf16[1,4,16,256]{3,2,1,0:T(8,128)(2,1)S(1)}, u32[]{:S(2)}, u32[]{:S(2)}) collective-permute-start(bf16[1,4,16,256]{3,2,1,0:T(8,128)(2,1)S(1)} %get-tuple-element.34), channel_id=1, source_target_pairs={{0,6},{1,7},{2,4},{3,5},{4,2},{5,3},{6,0},{7,1},{8,14},{9,15},{10,... | collective-permute-start | bytes 98312 | tf_op jit(solution)/shard_map/ppermute | solution.py:392
  35.0 3.9 %collective-permute-start.8 = (bf16[1,4,16,256]{3,2,1,0:T(8,128)(2,1)S(1)}, bf16[1,4,16,256]{3,2,1,0:T(8,128)(2,1)S(1)}, u32[]{:S(2)}, u32[]{:S(2)}) collective-permute-start(bf16[1,4,16,256]{3,2,1,0:T(8,128)(2,1)S(1)} %get-tuple-element.33), channel_id=1, source_target_pairs={{0,2},{1,3},{2,0},{3,1},{4,6},{5,7},{6,4},{7,5},{8,10},{9,11},{10,... | collective-permute-start | bytes 98312 | tf_op jit(solution)/shard_map/ppermute | solution.py:392
  35.2 3.9 %collective-permute-start.9 = (bf16[1,4,16,256]{3,2,1,0:T(8,128)(2,1)S(1)}, bf16[1,4,16,256]{3,2,1,0:T(8,128)(2,1)S(1)}, u32[]{:S(2)}, u32[]{:S(2)}) collective-permute-start(bf16[1,4,16,256]{3,2,1,0:T(8,128)(2,1)S(1)} %get-tuple-element.35), channel_id=1, source_target_pairs={{0,4},{1,5},{2,6},{3,7},{4,0},{5,1},{6,2},{7,3},{8,12},{9,13},{10,... | collective-permute-start | bytes 98312 | tf_op jit(solution)/shard_map/ppermute | solution.py:392

commit v7 on v5

--- a/solution.py
+++ b/solution.py
@@ -66,7 +66,6 @@
         offs, sources, rec, table, taper, smooth, *refs = refs
         out_r, out_s, out_edge, table_v, taper_v, smooth_v, *refs = refs
         sums, diffs, held, offs_v, sources_v, sems = refs
-    begin = first * HOP
     width = (count + 2) * HOP
     copies = []
 
@@ -78,15 +77,14 @@
     fetch(offs, offs_v)
     fetch(sources, sources_v)
     inside = width - (W if late else 0)
-    step = inside // 2
-    if not late:
-        fetch(taper, taper_v)
-    for at in range(0, inside, step):
-        fetch(rec.at[:, pl.ds(begin + at, step)], held.at[:, pl.ds(at, step)])
-    ready = len(copies)
+    for at in range(0, inside, inside // 2):
+        fetch(rec.at[:, pl.ds(first * HOP + at, inside // 2)], held.at[:, pl.ds(at, inside // 2)])
     if late:
         held[:, inside:] = halo[...]
+        ready = len(copies)
     else:
+        fetch(taper, taper_v)
+        ready = len(copies)
         rows = FOLD // 4
         for at in range(0, FOLD, rows):
             fetch(table.at[pl.ds(at, rows)], table_v.at[pl.ds(at, rows)])
@@ -184,121 +182,135 @@
         ],
         compiler_params=pltpu.CompilerParams(vmem_limit_bytes=24 << 20),
         cost_estimate=pl.CostEstimate(
-            flops=2 * count * c_dev * W * 2 * NB, bytes_accessed=4 << 20, transcendentals=0
+            flops=int((1.5 + 0.1 * count) * 1.15e9), bytes_accessed=1 << 20, transcendentals=0
         ),
         name="spectra",
     )(*arrays)
 
 
-def cross_kernel(shares, sides, cuts, n_src, c_dev, scale, n_before, last, *refs):
-    n_list = len(shares)
-    srcs = []
-    for share in shares:
-        srcs.append(refs[:share])
-        refs = refs[share:]
-    recs = []
-    for parts in sides:
-        recs.append([(refs[i], part) for i, part in enumerate(parts)])
-        refs = refs[len(parts) :]
-    before, refs = refs[:n_before], refs[n_before:]
+def cross_kernel(plan, n_src, n_win, c_dev, scale, n_done, n_after, last, *refs):
+    runs = []
+    for n_group, parts, has_before in plan:
+        srcs, refs = refs[:n_group], refs[n_group:]
+        recs, refs = refs[: len(parts)], refs[len(parts) :]
+        before, refs = refs[: int(has_before)], refs[int(has_before) :]
+        runs.append((srcs, list(zip(recs, parts)), before))
+    done, refs = refs[:n_done], refs[n_done:]
     if last:
-        ltab, out, wide, cross = refs
+        ltab, refs = refs[0], refs[1:]
+    refs = refs[n_after:]
+    if last:
+        out, *assembled, wide, cross = refs
     else:
         out, wide = refs
-    n_win = cuts[-1]
+        cross = out
     at = 0
-    for src in srcs:
-        for part in src:
-            height = part.shape[1]
-            wide[at : at + height, :] = part[0].astype(jnp.float32)
-            at += height
+    for srcs, _, _ in runs:
+        for src in srcs:
+            rows = slice(at, at + src.shape[1])
+            real = src[0, :, :NB].astype(jnp.float32)
+            imag = src[0, :, NB:].astype(jnp.float32)
+            wide[rows, :NB] = real
+            wide[rows, NB : 2 * NB] = real + imag
+            wide[rows, 2 * NB :] = real - imag
+            at += src.shape[1]
     tiles = NB // LANE
-    block = 8 if n_list * n_src % 8 == 0 else n_src
-    groups = block // n_src
-    n_side = len(sides)
-
-    span = n_list // max(len(before), 1)
-
-    def run(step, first, earlier):
+
+    def run(step, first, groups, recs, before):
+        block = groups * n_src
         local = step // tiles * groups
-        group = first + local
-        lo = pl.ds(pl.multiple_of(step % tiles * LANE, LANE), LANE)
-        hi = pl.ds(pl.multiple_of(step % tiles * LANE + NB, LANE), LANE)
-        base = pl.multiple_of(group * (n_src * n_win), 8)
-        src = wide.at[pl.ds(base, groups * n_src * n_win)]
-
-        def places(group, q):
-            starts = [((group * n_src + s) * n_side + q) * c_dev for s in range(block)]
-            return [pl.ds(pl.multiple_of(start, c_dev), c_dev) for start in starts]
-
-        for q, parts in enumerate(recs):
-            sums = [[0.0, 0.0] for _ in range(block)]
-            if earlier is not None:
-                sums = [[earlier[r, lo], earlier[r, hi]] for r in places(local, q)]
-            for rec, part in parts:
-                start, stop = cuts[part], cuts[part + 1]
-                for w in range(stop - start):
-                    row = slice(w * c_dev, (w + 1) * c_dev)
-                    rec_real = rec[row, lo].astype(jnp.float32)
-                    rec_imag = rec[row, hi].astype(jnp.float32)
-                    for s in range(block):
-                        at = s // n_src * n_src * n_win
-                        at += start * n_src + s % n_src * (stop - start) + w
-                        src_real = src[at : at + 1, lo]
-                        src_imag = src[at : at + 1, hi]
-                        sums[s][0] += src_real * rec_real + src_imag * rec_imag
-                        sums[s][1] += src_real * rec_imag - src_imag * rec_real
-            target = cross if last else out
-            for r, pair in zip(places(group, q), sums):
-                for place, value in zip((lo, hi), pair):
-                    target[r, place] = jnp.broadcast_to(value, (c_dev, LANE)).astype(target.dtype)
-
-    for i in range(max(len(before), 1)):
-        earlier = before[i] if before else None
-        pl.loop(0, span // groups * tiles)(functools.partial(run, first=i * span, earlier=earlier))
+        lo, hi, top = (
+            pl.ds(pl.multiple_of(step % tiles * LANE + i * NB, LANE), LANE) for i in range(3)
+        )
+        base = pl.multiple_of((first + local) * (n_src * n_win), 8)
+        src = wide.at[pl.ds(base, block * n_win)]
+
+        def place(group, s):
+            return pl.ds(pl.multiple_of((group * n_src + s) * c_dev, c_dev), c_dev)
+
+        sums = [[jnp.zeros((c_dev, LANE), jnp.float32)] * 3 for _ in range(block)]
+        for rec, (start, stop) in recs:
+            for w in range(stop - start):
+                row = slice(w * c_dev, (w + 1) * c_dev)
+                rec_real = rec[row, lo].astype(jnp.float32)
+                rec_imag = rec[row, hi].astype(jnp.float32)
+                rec_both = rec_real + rec_imag
+                for s in range(block):
+                    at = s // n_src * n_src * n_win
+                    at += start * n_src + s % n_src * (stop - start) + w
+                    row = slice(at, at + 1)
+                    both, plus, minus = sums[s]
+                    sums[s] = [
+                        both + src[row, lo] * rec_both,
+                        plus + src[row, hi] * rec_real,
+                        minus + src[row, top] * rec_imag,
+                    ]
+        for s in range(block):
+            both, plus, minus = sums[s]
+            real, imag = both - minus, both - plus
+            for earlier in before:
+                real += earlier[place(local, s), lo]
+                imag += earlier[place(local, s), hi]
+            cross[place(first + local, s), lo] = real.astype(cross.dtype)
+            cross[place(first + local, s), hi] = imag.astype(cross.dtype)
+
+    first = 0
+    for srcs, recs, before in runs:
+        groups = 8 // n_src if len(srcs) * n_src % 8 == 0 and 8 % n_src == 0 else 1
+        pl.loop(0, len(srcs) // groups * tiles)(
+            functools.partial(run, first=first, groups=groups, recs=recs, before=before)
+        )
+        first += len(srcs)
 
     if last:
         lagged = jnp.dot(cross[...], ltab[...], preferred_element_type=jnp.float32)
         out[...] = (lagged * scale).astype(jnp.bfloat16)
-
-
-def cross_call(srcs, sides, cuts, n_src, c_dev, scale, before=None, ltab=None):
-    n_list, n_side = len(srcs), len(sides)
-    groups = srcs[0][0].shape[0]
+    at = 0
+    for part in done:
+        assembled[0][at : at + part.shape[0], :] = part[...]
+        at += part.shape[0]
+
+
+def cross_call(runs, n_src, n_win, c_dev, scale, ltab=None, done=(), after=()):
+    grid = runs[0][0][0].shape[0]
     last = ltab is not None
-    rows = n_list * n_src * n_side * c_dev
+    n_list = sum(len(srcs) for srcs, _, _ in runs)
+    rows = n_list * n_src * c_dev
     whole = pl.BlockSpec(memory_space=pltpu.VMEM)
-    row_block = lambda width: pl.BlockSpec((rows, width), lambda g: (g, 0))
-    arrays = [part for src in srcs for part in src]
-    specs = [pl.BlockSpec((1,) + a.shape[1:], lambda g: (g, 0, 0)) for a in arrays]
-    for parts in sides:
-        arrays += list(parts.values())
-        specs += [whole] * len(parts)
-    if before is not None:
-        arrays += before
-        specs += [whole] * len(before)
-    scratch = [pltpu.VMEM((n_list * n_src * cuts[-1], 2 * NB), jnp.float32)]
+    arrays, specs, plan, pairs = [], [], [], 0
+    for srcs, parts, before in runs:
+        arrays += srcs
+        specs += [pl.BlockSpec((1,) + a.shape[1:], lambda g: (g, 0, 0)) for a in srcs]
+        others = [rec for rec, _ in parts] + ([] if before is None else [before])
+        arrays += others
+        specs += [whole] * len(others)
+        plan.append((len(srcs), [cut for _, cut in parts], before is not None))
+        pairs += len(srcs) * n_src * sum(stop - start for _, (start, stop) in parts)
+    others = list(done) + ([ltab] if last else [])
+    arrays += others + list(after)
+    specs += [whole] * len(others) + [pl.BlockSpec(memory_space=pl.ANY)] * len(after)
+    scratch = [pltpu.VMEM((n_list * n_src * n_win, 3 * NB), jnp.float32)]
     if last:
-        arrays.append(ltab)
-        specs.append(whole)
         scratch.append(pltpu.VMEM((rows, 2 * NB), jnp.bfloat16))
-        out_shape = jax.ShapeDtypeStruct((groups * rows, LAGS), jnp.bfloat16)
-    else:
-        out_shape = jax.ShapeDtypeStruct((groups * rows, 2 * NB), jnp.float32)
-    windows = sum(cuts[p + 1] - cuts[p] for parts in sides for p in parts) // n_side
+    shapes = [
+        jax.ShapeDtypeStruct((grid * rows, LAGS), jnp.bfloat16)
+        if last
+        else jax.ShapeDtypeStruct((grid * rows, 2 * NB), jnp.float32)
+    ]
+    out_specs = [pl.BlockSpec((rows, shapes[0].shape[1]), lambda g: (g, 0))]
+    if done:
+        shapes.append(jax.ShapeDtypeStruct((sum(a.shape[0] for a in done), LAGS), jnp.bfloat16))
+        out_specs.append(whole)
     return pl.pallas_call(
-        functools.partial(
-            cross_kernel, [len(src) for src in srcs], [list(p) for p in sides], cuts, n_src, c_dev, scale,
-            0 if before is None else len(before), last,
-        ),
-        grid=(groups,),
-        out_shape=out_shape,
+        functools.partial(cross_kernel, plan, n_src, n_win, c_dev, scale, len(done), len(after), last),
+        grid=(grid,),
+        out_shape=shapes,
         in_specs=specs,
-        out_specs=row_block(out_shape.shape[1]),
+        out_specs=out_specs,
         scratch_shapes=scratch,
         compiler_params=pltpu.CompilerParams(vmem_limit_bytes=24 << 20),
         cost_estimate=pl.CostEstimate(
-            flops=groups * rows * windows * NB * 40, bytes_accessed=4 << 20, transcendentals=0
+            flops=int((0.4 + grid * pairs * 0.008) * 1.15e9), bytes_accessed=1 << 20, transcendentals=0
         ),
         name="cross",
     )(*arrays)
@@ -314,7 +326,6 @@
     fibre = lax.axis_index("fibre")
     tm = lax.axis_index("tm")
     early = n_win * 3 // 4
-    cuts = (0, early, n_win)
     scale = 1.0 / math.sqrt(n_win * n_tm * NB)
     tables = [jnp.asarray(t) for t in (half_tables(), taper_table(), smoothing())]
     ltab = jnp.asarray(lag_table())
@@ -330,23 +341,27 @@
     halo = lax.ppermute(edge, "tm", [(i, i - 1) for i in range(1, n_tm)])
     rec_b, src_b, src = spectra_call(record, offsets, src_idx, tables, early, n_win - early, (halo, src_a))
     far_b = trade(rec_b, 1)
-    cross = functools.partial(cross_call, cuts=cuts, n_src=n_src, c_dev=c_dev, scale=scale)
-    own = [{0: rec_a, 1: rec_b}]
+    cross = functools.partial(cross_call, n_src=n_src, n_win=n_win, c_dev=c_dev, scale=scale)
+    head, rest = (0, early), (early, n_win)
+    own = [(rec_a, head), (rec_b, rest)]
     if direct:
         by_2 = jnp.concatenate([by_2a, trade(src_b, 4)], axis=0)
         by_1 = trade(src, 2)
         by_3 = trade(by_2, 2)
-        srcs = [[part[None]] for part in (src, by_1, by_2, by_3)]
-        halves = (srcs[:2], srcs[2:])
-        near = [cross(half, own, ltab=ltab) for half in halves]
-        near = jnp.concatenate(near, axis=0)
-        parts = [cross(half, [{0: far_a}]) for half in halves]
-        far = cross(srcs, [{1: far_b}], before=parts, ltab=ltab)
+        srcs = [part[None] for part in (src, by_1, by_2, by_3)]
+        split = (srcs[:1], srcs[1:3], srcs[3:])
+        near, sums = [], []
+        for k, part in enumerate(split):
+            after = sums[-1:]
+            near += cross([(part, own, None)], ltab=ltab, after=after)
+            sums += cross([(part, [(far_a, head)], None)], after=near[-1:])
+        runs = [(part, [(far_b, rest)], before) for part, before in zip(split, sums)]
+        far, near = cross(runs, ltab=ltab, done=near)
     else:
         ranks = [[2 * j + p for j in range(n_group)] for p in range(2)]
-        srcs = [[lax.all_gather(src, "fibre", axis=0, axis_index_groups=ranks)]]
-        near = cross(srcs, own, ltab=ltab)
-        far = cross(srcs, [{0: far_a, 1: far_b}], ltab=ltab)
+        srcs = [lax.all_gather(src, "fibre", axis=0, axis_index_groups=ranks)]
+        near = cross([(srcs, own, None)], ltab=ltab)[0]
+        far = cross([(srcs, [(far_a, head), (far_b, rest)], None)], ltab=ltab)[0]
     near, far = (r.reshape(n_group, n_src, c_dev, LAGS) for r in (near, far))
 
     def piece(lagged, owner):

time: 42.8 us -> 39.8 us (0.930)
  starting transfers between devices: 16.2 us -> 14.5 us
  waiting for transfers between devices: 10.3 us -> 9.46 us
    ppermute x3, waiting for transfers between devices: 3.63 us -> 2.24 us  [body(): mine = lax.ppermute(mine.astype(jnp.bfloat16), ('fibre', 'tm'), routes)]
    ppermute x6, starting transfers between devices: 10.6 us -> 9.58 us  [trade(): return lax.ppermute(array, 'fibre', [(i, i ^ by) for i in range(n_fibre)])]
    ppermute x1, starting transfers between devices: 0.74 us -> 0.07 us  [body(): got = lax.ppermute(give, 'tm', [(i, i ^ 1) for i in range(n_tm)])]
    ppermute x6, waiting for transfers between devices: 5.44 us -> 5.88 us  [trade(): return lax.ppermute(array, 'fibre', [(i, i ^ by) for i in range(n_fibre)])]
    pallas_call x5 -> x7, Pallas kernels: 8.88 us -> 8.52 us  [cross_call(): pl.pallas_call(functools.partial(cross_kernel, plan, n_src, n_win, c_dev,...]
  transfers between devices with their start and end apart: 11 -> 11, of which waited for: 7 -> 8; matrix products, arithmetic and copies ran while one was open for 0% -> 0% of each run, Pallas kernels for 23% -> 24%
where the time goes in v7:
time: 39.8 us; the launch traced here: 39.6 us
  Pallas kernels  14.7 us (37%)
  starting transfers between devices  14.5 us (36%)
  waiting for transfers between devices  9.46 us (24%)
  other arithmetic  0.75 us (2%)
    ppermute x6, starting transfers between devices, trade(): return lax.ppermute(array, 'fibre', [(i, i ^ by) for i in range(n_fibre)])  9.58 us
    pallas_call x7, Pallas kernels, cross_call(): pl.pallas_call(functools.partial(cross_kernel, plan, n_src, n_win, c_dev,...  8.52 us
    pallas_call x2, Pallas kernels, spectra_call(): pl.pallas_call(functools.partial(spectra_kernel, first, count, late is no...  6.19 us
    ppermute x6, waiting for transfers between devices, trade(): return lax.ppermute(array, 'fibre', [(i, i ^ by) for i in range(n_fibre)])  5.88 us
    ppermute x3, starting transfers between devices, body(): mine = lax.ppermute(mine.astype(jnp.bfloat16), ('fibre', 'tm'), routes)  3.55 us
    ppermute x3, waiting for transfers between devices, body(): mine = lax.ppermute(mine.astype(jnp.bfloat16), ('fibre', 'tm'), routes)  2.24 us
    ppermute x1, waiting for transfers between devices, body(): got = lax.ppermute(give, 'tm', [(i, i ^ 1) for i in range(n_tm)])  1.33 us
    ppermute x1, starting transfers between devices, body(): halo = lax.ppermute(edge, 'tm', [(i, i - 1) for i in range(1, n_tm)])  1.29 us
  transfers between devices with their start and end apart: 11, of which 8 were waited for; matrix products, arithmetic and copies ran while one was open for 0% of the time, Pallas kernels for 24%

profile of v7, /device:TPU:0, one launch (start us, length us, event | category | flops | bytes accessed | tf_op | source)
XLA Modules:
  0.0 39.6 jit_solution(4077366745283907486)
XLA Ops:
  0.0 3.9 %spectra.2 = (bf16[384,768]{1,0:T(8,128)(2,1)S(1)}, bf16[96,768]{1,0:T(8,128)(2,1)S(1)}, bf16[16,2048]{1,0:T(8,128)(2,1)S(1)}, bf16[1024,768]{1,0:T(8,128)(2,1)S...) custom-call(s32[32]{0:T(128)} %refs_0_.3, s32[4]{0:T(128)} %refs_1_.3, bf16[16,32768]{1,0:T(8,128)(2,1)} %refs_2_.3, ...), custom_call_target="tpu_custom_call" | custom-call | flops 4485000192 | bytes 1048576 | tf_op jit(solution)/shard_map/spectra/pallas_call | solution.py:170
  3.9 1.3 %collective-permute-start = (bf16[16,2048]{1,0:T(8,128)(2,1)S(1)}, bf16[16,2048]{1,0:T(8,128)(2,1)S(1)}, u32[]{:S(2)}, u32[]{:S(2)}) collective-permute-start(bf16[16,2048]{1,0:T(8,128)(2,1)S(1)} %get-tuple-element.16), channel_id=1, source_target_pairs={{1,0},{2,1},{3,2},{5,4},{6,5},{7,6},{9,8},{10,9},{11,10},{13,12},{... | collective-permute-start | bytes 196616 | tf_op jit(solution)/shard_map/ppermute | solution.py:341
  5.2 3.0 %collective-permute-start.2 = (bf16[384,768]{1,0:T(8,128)(2,1)S(1)}, bf16[384,768]{1,0:T(8,128)(2,1)S(1)}, u32[]{:S(2)}, u32[]{:S(2)}) collective-permute-start(bf16[384,768]{1,0:T(8,128)(2,1)S(1)} %get-tuple-element.23.refs_1_.refs_2_), channel_id=1, source_target_pairs={{0,4},{4,0},{8,12},{12,8},{16,20},{20,16},{24,28},{28,24},{1,5},{5... | collective-permute-start | bytes 1769480 | tf_op jit(solution)/shard_map/ppermute | solution.py:335
  8.2 2.6 %collective-permute-start.4 = (bf16[96,768]{1,0:T(8,128)(2,1)S(1)}, bf16[96,768]{1,0:T(8,128)(2,1)S(1)}, u32[]{:S(2)}, u32[]{:S(2)}) collective-permute-start(bf16[96,768]{1,0:T(8,128)(2,1)S(1)} %get-tuple-element.20.refs_7_), channel_id=1, source_target_pairs={{0,16},{4,20},{8,24},{12,28},{16,0},{20,4},{24,8},{28,12},{1,17},{... | collective-permute-start | bytes 442376 | tf_op jit(solution)/shard_map/ppermute | solution.py:335
  10.8 0.0 collective-permute-done.refs_3_
  10.8 0.0 copy-start
  10.8 2.3 %spectra.3 = (bf16[128,768]{1,0:T(8,128)(2,1)S(1)}, bf16[32,768]{1,0:T(8,128)(2,1)S(1)}, bf16[128,768]{1,0:T(8,128)(2,1)S(1)}) custom-call(s32[32]{0:T(128)} %refs_0_.3, s32[4]{0:T(128)} %refs_1_.3, bf16[16,32768]{1,0:T(8,128)(2,1)} %refs_2_.3, bf16[16,2048]{1,0:T(8,128)(2,1)S(1)} %collective-permute-done.refs_3_, ...), custom_call_target="tpu_custom_call" | custom-call | flops 2644999936 | bytes 1048576 | tf_op jit(solution)/shard_map/spectra/pallas_call | solution.py:170
  13.1 0.4 collective-permute-start.5
  13.5 1.6 %collective-permute-start.3 = (bf16[128,768]{1,0:T(8,128)(2,1)S(1)}, bf16[128,768]{1,0:T(8,128)(2,1)S(1)}, u32[]{:S(2)}, u32[]{:S(2)}) collective-permute-start(bf16[128,768]{1,0:T(8,128)(2,1)S(1)} %get-tuple-element.21), channel_id=1, source_target_pairs={{0,8},{4,12},{8,0},{12,4},{16,24},{20,28},{24,16},{28,20},{1,9},{5... | collective-permute-start | bytes 589832 | tf_op jit(solution)/shard_map/ppermute | solution.py:335
  15.1 1.4 %collective-permute-start.1 = (bf16[128,768]{1,0:T(8,128)(2,1)S(1)}, bf16[128,768]{1,0:T(8,128)(2,1)S(1)}, u32[]{:S(2)}, u32[]{:S(2)}) collective-permute-start(bf16[128,768]{1,0:T(8,128)(2,1)S(1)} %get-tuple-element.22.refs_2_.refs_3_), channel_id=1, source_target_pairs={{0,4},{4,0},{8,12},{12,8},{16,20},{20,16},{24,28},{28,24},{1,5},{5... | collective-permute-start | bytes 589832 | tf_op jit(solution)/shard_map/ppermute | solution.py:335
  16.5 0.0 copy-done
  16.5 1.1 %cross.7.refs_2_.refs_10_ = bf16[64,256]{1,0:T(8,128)(2,1)S(1)} custom-call(bf16[1,128,768]{2,1,0:T(8,128)(2,1)S(1)} %bitcast.46, bf16[384,768]{1,0:T(8,128)(2,1)S(1)} %get-tuple-element.23.refs_1_.refs_2_, bf16[128,768]{1,0:T(8,128)(2,1)S(1)} %get-tuple-element.22.refs_2_.refs_3_, bf16[768,256]{1,0:T(8,128)(2,1)S(1)} %copy-done), custom_call_target="tpu_custom_call" | custom-call | flops 1637600000 | bytes 1048576 | tf_op jit(solution)/shard_map/cross/pallas_call | solution.py:304
  17.6 2.5 %collective-permute-done.4 = bf16[96,768]{1,0:T(8,128)(2,1)S(1)} collective-permute-done((bf16[96,768]{1,0:T(8,128)(2,1)S(1)}, bf16[96,768]{1,0:T(8,128)(2,1)S(1)}, u32[]{:S(2)}, u32[]{:S(2)}) %collective-permute-start.4) | collective-permute-done | bytes 147488 | tf_op jit(solution)/shard_map/ppermute | solution.py:335
  20.1 0.9 %collective-permute-done.5 = bf16[32,768]{1,0:T(8,128)(2,1)S(1)} collective-permute-done((bf16[32,768]{1,0:T(8,128)(2,1)S(1)}, bf16[32,768]{1,0:T(8,128)(2,1)S(1)}, u32[]{:S(2)}, u32[]{:S(2)}) %collective-permute-start.5) | collective-permute-done | bytes 49184 | tf_op jit(solution)/shard_map/ppermute | solution.py:335
  21.1 0.6 %collective-permute-start.6 = (bf16[128,768]{1,0:T(8,128)(2,1)S(1)}, bf16[128,768]{1,0:T(8,128)(2,1)S(1)}, u32[]{:S(2)}, u32[]{:S(2)}) collective-permute-start(bf16[128,768]{1,0:T(8,128)(2,1)S(1)} %constant_dynamic-update-slice_fusion), channel_id=1, source_target_pairs={{0,8},{4,12},{8,0},{12,4},{16,24},{20,28},{24,16},{28,20},{1,9},{5... | collective-permute-start | bytes 589832 | tf_op jit(solution)/shard_map/ppermute | solution.py:335
  21.6 0.4 collective-permute-done.2.refs_1_.refs_2_
  22.0 0.7 %cross.8.refs_5_.refs_2_ = f32[64,768]{1,0:T(8,128)S(1)} custom-call(bf16[1,128,768]{2,1,0:T(8,128)(2,1)S(1)} %bitcast.47, bf16[384,768]{1,0:T(8,128)(2,1)S(1)} %collective-permute-done.2.refs_1_.refs_2_, bf16[64,256]{1,0:T(8,128)(2,1)S(1)} %cross.7.refs_2_.refs_10_), custom_call_target="tpu_custom_call" | custom-call | flops 1343200000 | bytes 1048576 | tf_op jit(solution)/shard_map/cross/pallas_call | solution.py:304
  22.7 1.3 %collective-permute-done.3 = bf16[128,768]{1,0:T(8,128)(2,1)S(1)} collective-permute-done((bf16[128,768]{1,0:T(8,128)(2,1)S(1)}, bf16[128,768]{1,0:T(8,128)(2,1)S(1)}, u32[]{:S(2)}, u32[]{:S(2)}) %collective-permute-start.3) | collective-permute-done | bytes 196640 | tf_op jit(solution)/shard_map/ppermute | solution.py:335
  24.0 2.1 %cross.9.refs_3_.refs_11_ = bf16[128,256]{1,0:T(8,128)(2,1)S(1)} custom-call(bf16[1,128,768]{2,1,0:T(8,128)(2,1)S(1)} %bitcast.49, bf16[1,128,768]{2,1,0:T(8,128)(2,1)S(1)} %bitcast.43, bf16[384,768]{1,0:T(8,128)(2,1)S(1)} %get-tuple-element.23.refs_1_.refs_2_, bf16[128,768]{1,0:T(8,128)(2,1)S(1)} %get-tuple-element.22.refs_2_.refs_3_, ...), custom_call_target="tpu_custom_call" | custom-call | flops 2815200000 | bytes 1048576 | tf_op jit(solution)/shard_map/cross/pallas_call | solution.py:304
  26.1 1.4 %cross.10.refs_4_.refs_6_ = f32[128,768]{1,0:T(8,128)S(1)} custom-call(bf16[1,128,768]{2,1,0:T(8,128)(2,1)S(1)} %bitcast.50, bf16[1,128,768]{2,1,0:T(8,128)(2,1)S(1)} %bitcast.44, bf16[384,768]{1,0:T(8,128)(2,1)S(1)} %collective-permute-done.2.refs_1_.refs_2_, bf16[128,256]{1,0:T(8,128)(2,1)S(1)} %cross.9.refs_3_.refs_11_), custom_call_target="tpu_custom_call" | custom-call | flops 2226400000 | bytes 1048576 | tf_op jit(solution)/shard_map/cross/pallas_call | solution.py:304
  27.5 0.8 %collective-permute-done.6 = bf16[128,768]{1,0:T(8,128)(2,1)S(1)} collective-permute-done((bf16[128,768]{1,0:T(8,128)(2,1)S(1)}, bf16[128,768]{1,0:T(8,128)(2,1)S(1)}, u32[]{:S(2)}, u32[]{:S(2)}) %collective-permute-start.6) | collective-permute-done | bytes 196640 | tf_op jit(solution)/shard_map/ppermute | solution.py:335
  28.3 1.1 %cross.11.refs_2_.refs_12_ = bf16[64,256]{1,0:T(8,128)(2,1)S(1)} custom-call(bf16[1,128,768]{2,1,0:T(8,128)(2,1)S(1)} %bitcast.52, bf16[384,768]{1,0:T(8,128)(2,1)S(1)} %get-tuple-element.23.refs_1_.refs_2_, bf16[128,768]{1,0:T(8,128)(2,1)S(1)} %get-tuple-element.22.refs_2_.refs_3_, bf16[768,256]{1,0:T(8,128)(2,1)S(1)} %copy-done, ...), custom_call_target="tpu_custom_call" | custom-call | flops 1637600000 | bytes 1048576 | tf_op jit(solution)/shard_map/cross/pallas_call | solution.py:304
  29.4 0.7 %cross.12.refs_9_ = f32[64,768]{1,0:T(8,128)S(1)} custom-call(bf16[1,128,768]{2,1,0:T(8,128)(2,1)S(1)} %bitcast.53, bf16[384,768]{1,0:T(8,128)(2,1)S(1)} %collective-permute-done.2.refs_1_.refs_2_, bf16[64,256]{1,0:T(8,128)(2,1)S(1)} %cross.11.refs_2_.refs_12_), custom_call_target="tpu_custom_call" | custom-call | flops 1343200000 | bytes 1048576 | tf_op jit(solution)/shard_map/cross/pallas_call | solution.py:304
  30.2 0.0 collective-permute-done.1.refs_1_.refs_5_.refs_8_
  30.2 1.4 %cross.13 = (bf16[256,256]{1,0:T(8,128)(2,1)S(1)}, bf16[256,256]{1,0:T(8,128)(2,1)S(1)}) custom-call(bf16[1,128,768]{2,1,0:T(8,128)(2,1)S(1)} %bitcast.48, bf16[128,768]{1,0:T(8,128)(2,1)S(1)} %collective-permute-done.1.refs_1_.refs_5_.refs_8_, f32[64,768]{1,0:T(8,128)S(1)} %cross.8.refs_5_.refs_2_, bf16[1,128,768]{2,1,0:T(8,128)(2,1)S(1)} %bitcast.51, ...), custom_call_target="tpu_custom_call" | custom-call | flops 1637600000 | bytes 1048576 | tf_op jit(solution)/shard_map/cross/pallas_call | solution.py:304
  31.6 0.1 collective-permute-start.7
  31.7 1.3 %collective-permute-done.7 = bf16[4,1,4,16,256]{4,3,2,1,0:T(8,128)(2,1)S(1)} collective-permute-done((bf16[4,1,4,16,256]{4,3,2,1,0:T(8,128)(2,1)S(1)}, bf16[4,1,4,16,256]{4,3,2,1,0:T(8,128)(2,1)S(1)}, u32[]{:S(2)}, u32[]{:S(2)}) %collective-permute-start.7) | collective-permute-done | bytes 131104 | tf_op jit(solution)/shard_map/ppermute | solution.py:375
  33.1 1.9 %collective-permute-start.10 = (bf16[1,4,16,256]{3,2,1,0:T(8,128)(2,1)S(1)}, bf16[1,4,16,256]{3,2,1,0:T(8,128)(2,1)S(1)}, u32[]{:S(2)}, u32[]{:S(2)}) collective-permute-start(bf16[1,4,16,256]{3,2,1,0:T(8,128)(2,1)S(1)} %get-tuple-element.32), channel_id=1, source_target_pairs={{0,6},{1,7},{2,4},{3,5},{4,2},{5,3},{6,0},{7,1},{8,14},{9,15},{10,... | collective-permute-start | bytes 98312 | tf_op jit(solution)/shard_map/ppermute | solution.py:388
  35.0 0.0 collective-permute-start.8
  35.0 1.7 %collective-permute-start.9 = (bf16[1,4,16,256]{3,2,1,0:T(8,128)(2,1)S(1)}, bf16[1,4,16,256]{3,2,1,0:T(8,128)(2,1)S(1)}, u32[]{:S(2)}, u32[]{:S(2)}) collective-permute-start(bf16[1,4,16,256]{3,2,1,0:T(8,128)(2,1)S(1)} %get-tuple-element.33), channel_id=1, source_target_pairs={{0,4},{1,5},{2,6},{3,7},{4,0},{5,1},{6,2},{7,3},{8,12},{9,13},{10,... | collective-permute-start | bytes 98312 | tf_op jit(solution)/shard_map/ppermute | solution.py:388
  36.7 1.4 %collective-permute-done.10 = bf16[1,4,16,256]{3,2,1,0:T(8,128)(2,1)S(1)} collective-permute-done((bf16[1,4,16,256]{3,2,1,0:T(8,128)(2,1)S(1)}, bf16[1,4,16,256]{3,2,1,0:T(8,128)(2,1)S(1)}, u32[]{:S(2)}, u32[]{:S(2)}) %collective-permute-start.10) | collective-permute-done | bytes 32800 | tf_op jit(solution)/shard_map/ppermute | solution.py:388
  38.1 0.8 %collective-permute-done.8 = bf16[1,4,16,256]{3,2,1,0:T(8,128)(2,1)S(1)} collective-permute-done((bf16[1,4,16,256]{3,2,1,0:T(8,128)(2,1)S(1)}, bf16[1,4,16,256]{3,2,1,0:T(8,128)(2,1)S(1)}, u32[]{:S(2)}, u32[]{:S(2)}) %collective-permute-start.8) | collective-permute-done | bytes 32800 | tf_op jit(solution)/shard_map/ppermute | solution.py:388
  38.9 0.0 collective-permute-done.9
  38.9 0.7 %pad_maximum_fusion.1 = f32[1,2,4,16,256]{4,3,2,1,0:T(8,128)} fusion(f32[1,1,4,16,256]{4,3,2,1,0:T(8,128)S(1)} %get-tuple-element.28, f32[1,1,4,16,256]{4,3,2,1,0:T(8,128)S(1)} %get-tuple-element.27), kind=kLoop, calls=%fused_computation.2 | loop fusion | flops 32768 | bytes 262144 | tf_op jit(solution)/shard_map/stack | solution.py:394
  (7 shorter events, 0.1 us)
Async XLA Ops:
  3.9 6.9 %collective-permute-start = (bf16[16,2048]{1,0:T(8,128)(2,1)S(1)}, bf16[16,2048]{1,0:T(8,128)(2,1)S(1)}, u32[]{:S(2)}, u32[]{:S(2)}) collective-permute-start(bf16[16,2048]{1,0:T(8,128)(2,1)S(1)} %get-tuple-element.16), channel_id=1, source_target_pairs={{1,0},{2,1},{3,2},{5,4},{6,5},{7,6},{9,8},{10,9},{11,10},{13,12},{... | collective-permute-start | bytes 196616 | tf_op jit(solution)/shard_map/ppermute | solution.py:341
  5.2 16.8 %collective-permute-start.2 = (bf16[384,768]{1,0:T(8,128)(2,1)S(1)}, bf16[384,768]{1,0:T(8,128)(2,1)S(1)}, u32[]{:S(2)}, u32[]{:S(2)}) collective-permute-start(bf16[384,768]{1,0:T(8,128)(2,1)S(1)} %get-tuple-element.23.refs_1_.refs_2_), channel_id=1, source_target_pairs={{0,4},{4,0},{8,12},{12,8},{16,20},{20,16},{24,28},{28,24},{1,5},{5... | collective-permute-start | bytes 1769480 | tf_op jit(solution)/shard_map/ppermute | solution.py:335
  8.2 11.9 %collective-permute-start.4 = (bf16[96,768]{1,0:T(8,128)(2,1)S(1)}, bf16[96,768]{1,0:T(8,128)(2,1)S(1)}, u32[]{:S(2)}, u32[]{:S(2)}) collective-permute-start(bf16[96,768]{1,0:T(8,128)(2,1)S(1)} %get-tuple-element.20.refs_7_), channel_id=1, source_target_pairs={{0,16},{4,20},{8,24},{12,28},{16,0},{20,4},{24,8},{28,12},{1,17},{... | collective-permute-start | bytes 442376 | tf_op jit(solution)/shard_map/ppermute | solution.py:335
  10.8 5.7 %copy-start = (bf16[768,256]{1,0:T(8,128)(2,1)S(1)}, bf16[768,256]{1,0:T(8,128)(2,1)}, u32[]{:S(2)}) copy-start(bf16[768,256]{1,0:T(8,128)(2,1)} %constant.81.clone.refs_3_.refs_4_.refs_13_) | copy-start | bytes 1179652
  13.1 7.9 %collective-permute-start.5 = (bf16[32,768]{1,0:T(8,128)(2,1)S(1)}, bf16[32,768]{1,0:T(8,128)(2,1)S(1)}, u32[]{:S(2)}, u32[]{:S(2)}) collective-permute-start(bf16[32,768]{1,0:T(8,128)(2,1)S(1)} %get-tuple-element.24), channel_id=1, source_target_pairs={{0,16},{4,20},{8,24},{12,28},{16,0},{20,4},{24,8},{28,12},{1,17},{... | collective-permute-start | bytes 147464 | tf_op jit(solution)/shard_map/ppermute | solution.py:335
  13.5 10.5 %collective-permute-start.3 = (bf16[128,768]{1,0:T(8,128)(2,1)S(1)}, bf16[128,768]{1,0:T(8,128)(2,1)S(1)}, u32[]{:S(2)}, u32[]{:S(2)}) collective-permute-start(bf16[128,768]{1,0:T(8,128)(2,1)S(1)} %get-tuple-element.21), channel_id=1, source_target_pairs={{0,8},{4,12},{8,0},{12,4},{16,24},{20,28},{24,16},{28,20},{1,9},{5... | collective-permute-start | bytes 589832 | tf_op jit(solution)/shard_map/ppermute | solution.py:335
  15.1 15.1 %collective-permute-start.1 = (bf16[128,768]{1,0:T(8,128)(2,1)S(1)}, bf16[128,768]{1,0:T(8,128)(2,1)S(1)}, u32[]{:S(2)}, u32[]{:S(2)}) collective-permute-start(bf16[128,768]{1,0:T(8,128)(2,1)S(1)} %get-tuple-element.22.refs_2_.refs_3_), channel_id=1, source_target_pairs={{0,4},{4,0},{8,12},{12,8},{16,20},{20,16},{24,28},{28,24},{1,5},{5... | collective-permute-start | bytes 589832 | tf_op jit(solution)/shard_map/ppermute | solution.py:335
  21.1 7.3 %collective-permute-start.6 = (bf16[128,768]{1,0:T(8,128)(2,1)S(1)}, bf16[128,768]{1,0:T(8,128)(2,1)S(1)}, u32[]{:S(2)}, u32[]{:S(2)}) collective-permute-start(bf16[128,768]{1,0:T(8,128)(2,1)S(1)} %constant_dynamic-update-slice_fusion), channel_id=1, source_target_pairs={{0,8},{4,12},{8,0},{12,4},{16,24},{20,28},{24,16},{28,20},{1,9},{5... | collective-permute-start | bytes 589832 | tf_op jit(solution)/shard_map/ppermute | solution.py:335
  31.6 1.4 %collective-permute-start.7 = (bf16[4,1,4,16,256]{4,3,2,1,0:T(8,128)(2,1)S(1)}, bf16[4,1,4,16,256]{4,3,2,1,0:T(8,128)(2,1)S(1)}, u32[]{:S(2)}, u32[]{:S(2)}) collective-permute-start(bf16[4,1,4,16,256]{4,3,2,1,0:T(8,128)(2,1)S(1)} %pad_maximum_fusion), channel_id=1, source_target_pairs={{0,1},{1,0},{2,3},{3,2},{4,5},{5,4},{6,7},{7,6},{8,9},{9,8},{10,11... | collective-permute-start | bytes 393224 | tf_op jit(solution)/shard_map/ppermute | solution.py:375
  33.1 5.0 %collective-permute-start.10 = (bf16[1,4,16,256]{3,2,1,0:T(8,128)(2,1)S(1)}, bf16[1,4,16,256]{3,2,1,0:T(8,128)(2,1)S(1)}, u32[]{:S(2)}, u32[]{:S(2)}) collective-permute-start(bf16[1,4,16,256]{3,2,1,0:T(8,128)(2,1)S(1)} %get-tuple-element.32), channel_id=1, source_target_pairs={{0,6},{1,7},{2,4},{3,5},{4,2},{5,3},{6,0},{7,1},{8,14},{9,15},{10,... | collective-permute-start | bytes 98312 | tf_op jit(solution)/shard_map/ppermute | solution.py:388
  35.0 3.9 %collective-permute-start.8 = (bf16[1,4,16,256]{3,2,1,0:T(8,128)(2,1)S(1)}, bf16[1,4,16,256]{3,2,1,0:T(8,128)(2,1)S(1)}, u32[]{:S(2)}, u32[]{:S(2)}) collective-permute-start(bf16[1,4,16,256]{3,2,1,0:T(8,128)(2,1)S(1)} %get-tuple-element.31), channel_id=1, source_target_pairs={{0,2},{1,3},{2,0},{3,1},{4,6},{5,7},{6,4},{7,5},{8,10},{9,11},{10,... | collective-permute-start | bytes 98312 | tf_op jit(solution)/shard_map/ppermute | solution.py:388
  35.0 3.9 %collective-permute-start.9 = (bf16[1,4,16,256]{3,2,1,0:T(8,128)(2,1)S(1)}, bf16[1,4,16,256]{3,2,1,0:T(8,128)(2,1)S(1)}, u32[]{:S(2)}, u32[]{:S(2)}) collective-permute-start(bf16[1,4,16,256]{3,2,1,0:T(8,128)(2,1)S(1)} %get-tuple-element.33), channel_id=1, source_target_pairs={{0,4},{1,5},{2,6},{3,7},{4,0},{5,1},{6,2},{7,3},{8,12},{9,13},{10,... | collective-permute-start | bytes 98312 | tf_op jit(solution)/shard_map/ppermute | solution.py:388

commit v8 on v7

--- a/solution.py
+++ b/solution.py
@@ -182,7 +182,7 @@
         ],
         compiler_params=pltpu.CompilerParams(vmem_limit_bytes=24 << 20),
         cost_estimate=pl.CostEstimate(
-            flops=int((1.5 + 0.1 * count) * 1.15e9), bytes_accessed=1 << 20, transcendentals=0
+            flops=int((1.5 + 0.1 * count) * 0.3e9), bytes_accessed=1 << 20, transcendentals=0
         ),
         name="spectra",
     )(*arrays)
@@ -280,7 +280,10 @@
     arrays, specs, plan, pairs = [], [], [], 0
     for srcs, parts, before in runs:
         arrays += srcs
-        specs += [pl.BlockSpec((1,) + a.shape[1:], lambda g: (g, 0, 0)) for a in srcs]
+        if grid == 1:
+            specs += [whole] * len(srcs)
+        else:
+            specs += [pl.BlockSpec((1,) + a.shape[1:], lambda g: (g, 0, 0)) for a in srcs]
         others = [rec for rec, _ in parts] + ([] if before is None else [before])
         arrays += others
         specs += [whole] * len(others)
@@ -297,13 +300,13 @@
         if last
         else jax.ShapeDtypeStruct((grid * rows, 2 * NB), jnp.float32)
     ]
-    out_specs = [pl.BlockSpec((rows, shapes[0].shape[1]), lambda g: (g, 0))]
+    out_specs = [whole if grid == 1 else pl.BlockSpec((rows, shapes[0].shape[1]), lambda g: (g, 0))]
     if done:
         shapes.append(jax.ShapeDtypeStruct((sum(a.shape[0] for a in done), LAGS), jnp.bfloat16))
         out_specs.append(whole)
     return pl.pallas_call(
         functools.partial(cross_kernel, plan, n_src, n_win, c_dev, scale, len(done), len(after), last),
-        grid=(grid,),
+        grid=() if grid == 1 else (grid,),
         out_shape=shapes,
         in_specs=specs,
         out_specs=out_specs,

time: 39.8 us -> 39.9 us (level)
  starting transfers between devices: 14.5 us -> 15.3 us
  waiting for transfers between devices: 9.46 us -> 8.74 us
    ppermute x6, starting transfers between devices: 9.58 us -> 10.4 us  [trade(): return lax.ppermute(array, 'fibre', [(i, i ^ by) for i in range(n_fibre)])]
    ppermute x6, waiting for transfers between devices: 5.88 us -> 5.22 us  [trade(): return lax.ppermute(array, 'fibre', [(i, i ^ by) for i in range(n_fibre)])]
where the time goes in v8:
time: 39.9 us; the launch traced here: 39.7 us
  starting transfers between devices  15.3 us (38%)
  Pallas kernels  14.7 us (37%)
  waiting for transfers between devices  8.74 us (22%)
  other arithmetic  0.75 us (2%)
    ppermute x6, starting transfers between devices, trade(): return lax.ppermute(array, 'fibre', [(i, i ^ by) for i in range(n_fibre)])  10.4 us
    pallas_call x7, Pallas kernels, cross_call(): pl.pallas_call(functools.partial(cross_kernel, plan, n_src, n_win, c_dev,...  8.52 us
    pallas_call x2, Pallas kernels, spectra_call(): pl.pallas_call(functools.partial(spectra_kernel, first, count, late is no...  6.19 us
    ppermute x6, waiting for transfers between devices, trade(): return lax.ppermute(array, 'fibre', [(i, i ^ by) for i in range(n_fibre)])  5.22 us
    ppermute x3, starting transfers between devices, body(): mine = lax.ppermute(mine.astype(jnp.bfloat16), ('fibre', 'tm'), routes)  3.55 us
    ppermute x3, waiting for transfers between devices, body(): mine = lax.ppermute(mine.astype(jnp.bfloat16), ('fibre', 'tm'), routes)  2.18 us
    ppermute x1, waiting for transfers between devices, body(): got = lax.ppermute(give, 'tm', [(i, i ^ 1) for i in range(n_tm)])  1.33 us
    ppermute x1, starting transfers between devices, body(): halo = lax.ppermute(edge, 'tm', [(i, i - 1) for i in range(1, n_tm)])  1.28 us
  transfers between devices with their start and end apart: 11, of which 8 were waited for; matrix products, arithmetic and copies ran while one was open for 0% of the time, Pallas kernels for 24%

profile of v8, /device:TPU:0, one launch (start us, length us, event | category | flops | bytes accessed | tf_op | source)
XLA Modules:
  0.0 39.7 jit_solution(13035181826431393500)
XLA Ops:
  0.0 3.9 %spectra.2 = (bf16[384,768]{1,0:T(8,128)(2,1)S(1)}, bf16[96,768]{1,0:T(8,128)(2,1)S(1)}, bf16[16,2048]{1,0:T(8,128)(2,1)S(1)}, bf16[1024,768]{1,0:T(8,128)(2,1)S...) custom-call(s32[32]{0:T(128)} %refs_0_.3, s32[4]{0:T(128)} %refs_1_.3, bf16[16,32768]{1,0:T(8,128)(2,1)} %refs_2_.3, ...), custom_call_target="tpu_custom_call" | custom-call | flops 1170000000 | bytes 1048576 | tf_op jit(solution)/shard_map/spectra/pallas_call | solution.py:170
  3.9 3.0 %collective-permute-start.2 = (bf16[384,768]{1,0:T(8,128)(2,1)S(1)}, bf16[384,768]{1,0:T(8,128)(2,1)S(1)}, u32[]{:S(2)}, u32[]{:S(2)}) collective-permute-start(bf16[384,768]{1,0:T(8,128)(2,1)S(1)} %get-tuple-element.23.refs_1_.refs_2_), channel_id=1, source_target_pairs={{0,4},{4,0},{8,12},{12,8},{16,20},{20,16},{24,28},{28,24},{1,5},{5... | collective-permute-start | bytes 1769480 | tf_op jit(solution)/shard_map/ppermute | solution.py:338
  6.9 1.3 %collective-permute-start = (bf16[16,2048]{1,0:T(8,128)(2,1)S(1)}, bf16[16,2048]{1,0:T(8,128)(2,1)S(1)}, u32[]{:S(2)}, u32[]{:S(2)}) collective-permute-start(bf16[16,2048]{1,0:T(8,128)(2,1)S(1)} %get-tuple-element.16), channel_id=1, source_target_pairs={{1,0},{2,1},{3,2},{5,4},{6,5},{7,6},{9,8},{10,9},{11,10},{13,12},{... | collective-permute-start | bytes 196616 | tf_op jit(solution)/shard_map/ppermute | solution.py:344
  8.2 2.7 %collective-permute-start.4 = (bf16[96,768]{1,0:T(8,128)(2,1)S(1)}, bf16[96,768]{1,0:T(8,128)(2,1)S(1)}, u32[]{:S(2)}, u32[]{:S(2)}) collective-permute-start(bf16[96,768]{1,0:T(8,128)(2,1)S(1)} %get-tuple-element.20.refs_7_), channel_id=1, source_target_pairs={{0,16},{4,20},{8,24},{12,28},{16,0},{20,4},{24,8},{28,12},{1,17},{... | collective-permute-start | bytes 442376 | tf_op jit(solution)/shard_map/ppermute | solution.py:338
  10.8 0.0 collective-permute-done.refs_3_
  10.8 0.0 copy-start
  10.8 2.3 %spectra.3 = (bf16[128,768]{1,0:T(8,128)(2,1)S(1)}, bf16[32,768]{1,0:T(8,128)(2,1)S(1)}, bf16[128,768]{1,0:T(8,128)(2,1)S(1)}) custom-call(s32[32]{0:T(128)} %refs_0_.3, s32[4]{0:T(128)} %refs_1_.3, bf16[16,32768]{1,0:T(8,128)(2,1)} %refs_2_.3, bf16[16,2048]{1,0:T(8,128)(2,1)S(1)} %collective-permute-done.refs_3_, ...), custom_call_target="tpu_custom_call" | custom-call | flops 690000000 | bytes 1048576 | tf_op jit(solution)/shard_map/spectra/pallas_call | solution.py:170
  13.2 1.8 %collective-permute-start.5 = (bf16[32,768]{1,0:T(8,128)(2,1)S(1)}, bf16[32,768]{1,0:T(8,128)(2,1)S(1)}, u32[]{:S(2)}, u32[]{:S(2)}) collective-permute-start(bf16[32,768]{1,0:T(8,128)(2,1)S(1)} %get-tuple-element.24), channel_id=1, source_target_pairs={{0,16},{4,20},{8,24},{12,28},{16,0},{20,4},{24,8},{28,12},{1,17},{... | collective-permute-start | bytes 147464 | tf_op jit(solution)/shard_map/ppermute | solution.py:338
  15.0 1.6 %collective-permute-start.3 = (bf16[128,768]{1,0:T(8,128)(2,1)S(1)}, bf16[128,768]{1,0:T(8,128)(2,1)S(1)}, u32[]{:S(2)}, u32[]{:S(2)}) collective-permute-start(bf16[128,768]{1,0:T(8,128)(2,1)S(1)} %get-tuple-element.21), channel_id=1, source_target_pairs={{0,8},{4,12},{8,0},{12,4},{16,24},{20,28},{24,16},{28,20},{1,9},{5... | collective-permute-start | bytes 589832 | tf_op jit(solution)/shard_map/ppermute | solution.py:338
  16.6 0.5 %collective-permute-start.1 = (bf16[128,768]{1,0:T(8,128)(2,1)S(1)}, bf16[128,768]{1,0:T(8,128)(2,1)S(1)}, u32[]{:S(2)}, u32[]{:S(2)}) collective-permute-start(bf16[128,768]{1,0:T(8,128)(2,1)S(1)} %get-tuple-element.22.refs_2_.refs_3_), channel_id=1, source_target_pairs={{0,4},{4,0},{8,12},{12,8},{16,20},{20,16},{24,28},{28,24},{1,5},{5... | collective-permute-start | bytes 589832 | tf_op jit(solution)/shard_map/ppermute | solution.py:338
  17.1 0.0 copy-done
  17.1 1.1 %cross.7.refs_2_.refs_10_ = bf16[64,256]{1,0:T(8,128)(2,1)S(1)} custom-call(bf16[1,128,768]{2,1,0:T(8,128)(2,1)S(1)} %bitcast.46, bf16[384,768]{1,0:T(8,128)(2,1)S(1)} %get-tuple-element.23.refs_1_.refs_2_, bf16[128,768]{1,0:T(8,128)(2,1)S(1)} %get-tuple-element.22.refs_2_.refs_3_, bf16[768,256]{1,0:T(8,128)(2,1)S(1)} %copy-done), custom_call_target="tpu_custom_call" | custom-call | flops 1637600000 | bytes 1048576 | tf_op jit(solution)/shard_map/cross/pallas_call | solution.py:307
  18.2 1.3 %collective-permute-done.4 = bf16[96,768]{1,0:T(8,128)(2,1)S(1)} collective-permute-done((bf16[96,768]{1,0:T(8,128)(2,1)S(1)}, bf16[96,768]{1,0:T(8,128)(2,1)S(1)}, u32[]{:S(2)}, u32[]{:S(2)}) %collective-permute-start.4) | collective-permute-done | bytes 147488 | tf_op jit(solution)/shard_map/ppermute | solution.py:338
  19.5 1.5 %collective-permute-done.5 = bf16[32,768]{1,0:T(8,128)(2,1)S(1)} collective-permute-done((bf16[32,768]{1,0:T(8,128)(2,1)S(1)}, bf16[32,768]{1,0:T(8,128)(2,1)S(1)}, u32[]{:S(2)}, u32[]{:S(2)}) %collective-permute-start.5) | collective-permute-done | bytes 49184 | tf_op jit(solution)/shard_map/ppermute | solution.py:338
  21.0 0.8 %collective-permute-start.6 = (bf16[128,768]{1,0:T(8,128)(2,1)S(1)}, bf16[128,768]{1,0:T(8,128)(2,1)S(1)}, u32[]{:S(2)}, u32[]{:S(2)}) collective-permute-start(bf16[128,768]{1,0:T(8,128)(2,1)S(1)} %constant_dynamic-update-slice_fusion), channel_id=1, source_target_pairs={{0,8},{4,12},{8,0},{12,4},{16,24},{20,28},{24,16},{28,20},{1,9},{5... | collective-permute-start | bytes 589832 | tf_op jit(solution)/shard_map/ppermute | solution.py:338
  21.8 0.0 collective-permute-done.2.refs_1_.refs_2_
  21.8 0.7 %cross.8.refs_5_.refs_2_ = f32[64,768]{1,0:T(8,128)S(1)} custom-call(bf16[1,128,768]{2,1,0:T(8,128)(2,1)S(1)} %bitcast.47, bf16[384,768]{1,0:T(8,128)(2,1)S(1)} %collective-permute-done.2.refs_1_.refs_2_, bf16[64,256]{1,0:T(8,128)(2,1)S(1)} %cross.7.refs_2_.refs_10_), custom_call_target="tpu_custom_call" | custom-call | flops 1343200000 | bytes 1048576 | tf_op jit(solution)/shard_map/cross/pallas_call | solution.py:307
  22.6 0.9 %collective-permute-done.3 = bf16[128,768]{1,0:T(8,128)(2,1)S(1)} collective-permute-done((bf16[128,768]{1,0:T(8,128)(2,1)S(1)}, bf16[128,768]{1,0:T(8,128)(2,1)S(1)}, u32[]{:S(2)}, u32[]{:S(2)}) %collective-permute-start.3) | collective-permute-done | bytes 196640 | tf_op jit(solution)/shard_map/ppermute | solution.py:338
  23.5 2.1 %cross.9.refs_3_.refs_11_ = bf16[128,256]{1,0:T(8,128)(2,1)S(1)} custom-call(bf16[1,128,768]{2,1,0:T(8,128)(2,1)S(1)} %bitcast.49, bf16[1,128,768]{2,1,0:T(8,128)(2,1)S(1)} %bitcast.43, bf16[384,768]{1,0:T(8,128)(2,1)S(1)} %get-tuple-element.23.refs_1_.refs_2_, bf16[128,768]{1,0:T(8,128)(2,1)S(1)} %get-tuple-element.22.refs_2_.refs_3_, ...), custom_call_target="tpu_custom_call" | custom-call | flops 2815200000 | bytes 1048576 | tf_op jit(solution)/shard_map/cross/pallas_call | solution.py:307
  25.6 1.4 %cross.10.refs_4_.refs_6_ = f32[128,768]{1,0:T(8,128)S(1)} custom-call(bf16[1,128,768]{2,1,0:T(8,128)(2,1)S(1)} %bitcast.50, bf16[1,128,768]{2,1,0:T(8,128)(2,1)S(1)} %bitcast.44, bf16[384,768]{1,0:T(8,128)(2,1)S(1)} %collective-permute-done.2.refs_1_.refs_2_, bf16[128,256]{1,0:T(8,128)(2,1)S(1)} %cross.9.refs_3_.refs_11_), custom_call_target="tpu_custom_call" | custom-call | flops 2226400000 | bytes 1048576 | tf_op jit(solution)/shard_map/cross/pallas_call | solution.py:307
  27.0 1.5 %collective-permute-done.6 = bf16[128,768]{1,0:T(8,128)(2,1)S(1)} collective-permute-done((bf16[128,768]{1,0:T(8,128)(2,1)S(1)}, bf16[128,768]{1,0:T(8,128)(2,1)S(1)}, u32[]{:S(2)}, u32[]{:S(2)}) %collective-permute-start.6) | collective-permute-done | bytes 196640 | tf_op jit(solution)/shard_map/ppermute | solution.py:338
  28.5 1.1 %cross.11.refs_2_.refs_12_ = bf16[64,256]{1,0:T(8,128)(2,1)S(1)} custom-call(bf16[1,128,768]{2,1,0:T(8,128)(2,1)S(1)} %bitcast.52, bf16[384,768]{1,0:T(8,128)(2,1)S(1)} %get-tuple-element.23.refs_1_.refs_2_, bf16[128,768]{1,0:T(8,128)(2,1)S(1)} %get-tuple-element.22.refs_2_.refs_3_, bf16[768,256]{1,0:T(8,128)(2,1)S(1)} %copy-done, ...), custom_call_target="tpu_custom_call" | custom-call | flops 1637600000 | bytes 1048576 | tf_op jit(solution)/shard_map/cross/pallas_call | solution.py:307
  29.6 0.7 %cross.12.refs_9_ = f32[64,768]{1,0:T(8,128)S(1)} custom-call(bf16[1,128,768]{2,1,0:T(8,128)(2,1)S(1)} %bitcast.53, bf16[384,768]{1,0:T(8,128)(2,1)S(1)} %collective-permute-done.2.refs_1_.refs_2_, bf16[64,256]{1,0:T(8,128)(2,1)S(1)} %cross.11.refs_2_.refs_12_), custom_call_target="tpu_custom_call" | custom-call | flops 1343200000 | bytes 1048576 | tf_op jit(solution)/shard_map/cross/pallas_call | solution.py:307
  30.3 0.0 collective-permute-done.1.refs_1_.refs_5_.refs_8_
  30.4 1.4 %cross.13 = (bf16[256,256]{1,0:T(8,128)(2,1)S(1)}, bf16[256,256]{1,0:T(8,128)(2,1)S(1)}) custom-call(bf16[1,128,768]{2,1,0:T(8,128)(2,1)S(1)} %bitcast.48, bf16[128,768]{1,0:T(8,128)(2,1)S(1)} %collective-permute-done.1.refs_1_.refs_5_.refs_8_, f32[64,768]{1,0:T(8,128)S(1)} %cross.8.refs_5_.refs_2_, bf16[1,128,768]{2,1,0:T(8,128)(2,1)S(1)} %bitcast.51, ...), custom_call_target="tpu_custom_call" | custom-call | flops 1637600000 | bytes 1048576 | tf_op jit(solution)/shard_map/cross/pallas_call | solution.py:307
  31.8 0.1 collective-permute-start.7
  31.9 1.3 %collective-permute-done.7 = bf16[4,1,4,16,256]{4,3,2,1,0:T(8,128)(2,1)S(1)} collective-permute-done((bf16[4,1,4,16,256]{4,3,2,1,0:T(8,128)(2,1)S(1)}, bf16[4,1,4,16,256]{4,3,2,1,0:T(8,128)(2,1)S(1)}, u32[]{:S(2)}, u32[]{:S(2)}) %collective-permute-start.7) | collective-permute-done | bytes 131104 | tf_op jit(solution)/shard_map/ppermute | solution.py:378
  33.3 1.7 %collective-permute-start.10 = (bf16[1,4,16,256]{3,2,1,0:T(8,128)(2,1)S(1)}, bf16[1,4,16,256]{3,2,1,0:T(8,128)(2,1)S(1)}, u32[]{:S(2)}, u32[]{:S(2)}) collective-permute-start(bf16[1,4,16,256]{3,2,1,0:T(8,128)(2,1)S(1)} %get-tuple-element.32), channel_id=1, source_target_pairs={{0,6},{1,7},{2,4},{3,5},{4,2},{5,3},{6,0},{7,1},{8,14},{9,15},{10,... | collective-permute-start | bytes 98312 | tf_op jit(solution)/shard_map/ppermute | solution.py:391
  35.0 0.1 collective-permute-start.8
  35.1 1.7 %collective-permute-start.9 = (bf16[1,4,16,256]{3,2,1,0:T(8,128)(2,1)S(1)}, bf16[1,4,16,256]{3,2,1,0:T(8,128)(2,1)S(1)}, u32[]{:S(2)}, u32[]{:S(2)}) collective-permute-start(bf16[1,4,16,256]{3,2,1,0:T(8,128)(2,1)S(1)} %get-tuple-element.33), channel_id=1, source_target_pairs={{0,4},{1,5},{2,6},{3,7},{4,0},{5,1},{6,2},{7,3},{8,12},{9,13},{10,... | collective-permute-start | bytes 98312 | tf_op jit(solution)/shard_map/ppermute | solution.py:391
  36.9 1.3 %collective-permute-done.10 = bf16[1,4,16,256]{3,2,1,0:T(8,128)(2,1)S(1)} collective-permute-done((bf16[1,4,16,256]{3,2,1,0:T(8,128)(2,1)S(1)}, bf16[1,4,16,256]{3,2,1,0:T(8,128)(2,1)S(1)}, u32[]{:S(2)}, u32[]{:S(2)}) %collective-permute-start.10) | collective-permute-done | bytes 32800 | tf_op jit(solution)/shard_map/ppermute | solution.py:391
  38.2 0.7 %collective-permute-done.8 = bf16[1,4,16,256]{3,2,1,0:T(8,128)(2,1)S(1)} collective-permute-done((bf16[1,4,16,256]{3,2,1,0:T(8,128)(2,1)S(1)}, bf16[1,4,16,256]{3,2,1,0:T(8,128)(2,1)S(1)}, u32[]{:S(2)}, u32[]{:S(2)}) %collective-permute-start.8) | collective-permute-done | bytes 32800 | tf_op jit(solution)/shard_map/ppermute | solution.py:391
  38.9 0.1 collective-permute-done.9
  39.1 0.7 %pad_maximum_fusion.1 = f32[1,2,4,16,256]{4,3,2,1,0:T(8,128)} fusion(f32[1,1,4,16,256]{4,3,2,1,0:T(8,128)S(1)} %get-tuple-element.28, f32[1,1,4,16,256]{4,3,2,1,0:T(8,128)S(1)} %get-tuple-element.27), kind=kLoop, calls=%fused_computation.2 | loop fusion | flops 32768 | bytes 262144 | tf_op jit(solution)/shard_map/stack | solution.py:397
  (7 shorter events, 0.1 us)
Async XLA Ops:
  3.9 18.0 %collective-permute-start.2 = (bf16[384,768]{1,0:T(8,128)(2,1)S(1)}, bf16[384,768]{1,0:T(8,128)(2,1)S(1)}, u32[]{:S(2)}, u32[]{:S(2)}) collective-permute-start(bf16[384,768]{1,0:T(8,128)(2,1)S(1)} %get-tuple-element.23.refs_1_.refs_2_), channel_id=1, source_target_pairs={{0,4},{4,0},{8,12},{12,8},{16,20},{20,16},{24,28},{28,24},{1,5},{5... | collective-permute-start | bytes 1769480 | tf_op jit(solution)/shard_map/ppermute | solution.py:338
  6.9 3.9 %collective-permute-start = (bf16[16,2048]{1,0:T(8,128)(2,1)S(1)}, bf16[16,2048]{1,0:T(8,128)(2,1)S(1)}, u32[]{:S(2)}, u32[]{:S(2)}) collective-permute-start(bf16[16,2048]{1,0:T(8,128)(2,1)S(1)} %get-tuple-element.16), channel_id=1, source_target_pairs={{1,0},{2,1},{3,2},{5,4},{6,5},{7,6},{9,8},{10,9},{11,10},{13,12},{... | collective-permute-start | bytes 196616 | tf_op jit(solution)/shard_map/ppermute | solution.py:344
  8.2 11.3 %collective-permute-start.4 = (bf16[96,768]{1,0:T(8,128)(2,1)S(1)}, bf16[96,768]{1,0:T(8,128)(2,1)S(1)}, u32[]{:S(2)}, u32[]{:S(2)}) collective-permute-start(bf16[96,768]{1,0:T(8,128)(2,1)S(1)} %get-tuple-element.20.refs_7_), channel_id=1, source_target_pairs={{0,16},{4,20},{8,24},{12,28},{16,0},{20,4},{24,8},{28,12},{1,17},{... | collective-permute-start | bytes 442376 | tf_op jit(solution)/shard_map/ppermute | solution.py:338
  10.8 6.3 %copy-start = (bf16[768,256]{1,0:T(8,128)(2,1)S(1)}, bf16[768,256]{1,0:T(8,128)(2,1)}, u32[]{:S(2)}) copy-start(bf16[768,256]{1,0:T(8,128)(2,1)} %constant.81.clone.refs_3_.refs_4_.refs_13_) | copy-start | bytes 1179652
  13.2 7.8 %collective-permute-start.5 = (bf16[32,768]{1,0:T(8,128)(2,1)S(1)}, bf16[32,768]{1,0:T(8,128)(2,1)S(1)}, u32[]{:S(2)}, u32[]{:S(2)}) collective-permute-start(bf16[32,768]{1,0:T(8,128)(2,1)S(1)} %get-tuple-element.24), channel_id=1, source_target_pairs={{0,16},{4,20},{8,24},{12,28},{16,0},{20,4},{24,8},{28,12},{1,17},{... | collective-permute-start | bytes 147464 | tf_op jit(solution)/shard_map/ppermute | solution.py:338
  15.0 8.5 %collective-permute-start.3 = (bf16[128,768]{1,0:T(8,128)(2,1)S(1)}, bf16[128,768]{1,0:T(8,128)(2,1)S(1)}, u32[]{:S(2)}, u32[]{:S(2)}) collective-permute-start(bf16[128,768]{1,0:T(8,128)(2,1)S(1)} %get-tuple-element.21), channel_id=1, source_target_pairs={{0,8},{4,12},{8,0},{12,4},{16,24},{20,28},{24,16},{28,20},{1,9},{5... | collective-permute-start | bytes 589832 | tf_op jit(solution)/shard_map/ppermute | solution.py:338
  16.6 13.8 %collective-permute-start.1 = (bf16[128,768]{1,0:T(8,128)(2,1)S(1)}, bf16[128,768]{1,0:T(8,128)(2,1)S(1)}, u32[]{:S(2)}, u32[]{:S(2)}) collective-permute-start(bf16[128,768]{1,0:T(8,128)(2,1)S(1)} %get-tuple-element.22.refs_2_.refs_3_), channel_id=1, source_target_pairs={{0,4},{4,0},{8,12},{12,8},{16,20},{20,16},{24,28},{28,24},{1,5},{5... | collective-permute-start | bytes 589832 | tf_op jit(solution)/shard_map/ppermute | solution.py:338
  21.0 7.5 %collective-permute-start.6 = (bf16[128,768]{1,0:T(8,128)(2,1)S(1)}, bf16[128,768]{1,0:T(8,128)(2,1)S(1)}, u32[]{:S(2)}, u32[]{:S(2)}) collective-permute-start(bf16[128,768]{1,0:T(8,128)(2,1)S(1)} %constant_dynamic-update-slice_fusion), channel_id=1, source_target_pairs={{0,8},{4,12},{8,0},{12,4},{16,24},{20,28},{24,16},{28,20},{1,9},{5... | collective-permute-start | bytes 589832 | tf_op jit(solution)/shard_map/ppermute | solution.py:338
  31.8 1.4 %collective-permute-start.7 = (bf16[4,1,4,16,256]{4,3,2,1,0:T(8,128)(2,1)S(1)}, bf16[4,1,4,16,256]{4,3,2,1,0:T(8,128)(2,1)S(1)}, u32[]{:S(2)}, u32[]{:S(2)}) collective-permute-start(bf16[4,1,4,16,256]{4,3,2,1,0:T(8,128)(2,1)S(1)} %pad_maximum_fusion), channel_id=1, source_target_pairs={{0,1},{1,0},{2,3},{3,2},{4,5},{5,4},{6,7},{7,6},{8,9},{9,8},{10,11... | collective-permute-start | bytes 393224 | tf_op jit(solution)/shard_map/ppermute | solution.py:378
  33.3 4.9 %collective-permute-start.10 = (bf16[1,4,16,256]{3,2,1,0:T(8,128)(2,1)S(1)}, bf16[1,4,16,256]{3,2,1,0:T(8,128)(2,1)S(1)}, u32[]{:S(2)}, u32[]{:S(2)}) collective-permute-start(bf16[1,4,16,256]{3,2,1,0:T(8,128)(2,1)S(1)} %get-tuple-element.32), channel_id=1, source_target_pairs={{0,6},{1,7},{2,4},{3,5},{4,2},{5,3},{6,0},{7,1},{8,14},{9,15},{10,... | collective-permute-start | bytes 98312 | tf_op jit(solution)/shard_map/ppermute | solution.py:391
  35.0 3.9 %collective-permute-start.8 = (bf16[1,4,16,256]{3,2,1,0:T(8,128)(2,1)S(1)}, bf16[1,4,16,256]{3,2,1,0:T(8,128)(2,1)S(1)}, u32[]{:S(2)}, u32[]{:S(2)}) collective-permute-start(bf16[1,4,16,256]{3,2,1,0:T(8,128)(2,1)S(1)} %get-tuple-element.31), channel_id=1, source_target_pairs={{0,2},{1,3},{2,0},{3,1},{4,6},{5,7},{6,4},{7,5},{8,10},{9,11},{10,... | collective-permute-start | bytes 98312 | tf_op jit(solution)/shard_map/ppermute | solution.py:391
  35.1 3.9 %collective-permute-start.9 = (bf16[1,4,16,256]{3,2,1,0:T(8,128)(2,1)S(1)}, bf16[1,4,16,256]{3,2,1,0:T(8,128)(2,1)S(1)}, u32[]{:S(2)}, u32[]{:S(2)}) collective-permute-start(bf16[1,4,16,256]{3,2,1,0:T(8,128)(2,1)S(1)} %get-tuple-element.33), channel_id=1, source_target_pairs={{0,4},{1,5},{2,6},{3,7},{4,0},{5,1},{6,2},{7,3},{8,12},{9,13},{10,... | collective-permute-start | bytes 98312 | tf_op jit(solution)/shard_map/ppermute | solution.py:391

commit v9 on v8

--- a/solution.py
+++ b/solution.py
@@ -60,11 +60,12 @@
 
 def spectra_kernel(first, count, late, c_dev, n_src, *refs):
     if late:
-        offs, sources, rec, halo, table_v, taper_v, smooth_v, before_s, out_r, out_s, out_all, *refs = refs
+        offs, sources, rec, halo, table_v, taper_v, smooth_v, before_r, before_s, *refs = refs
+        out_r, out_s, out_all, *refs = refs
         sums, diffs, held, offs_v, sources_v, sems = refs
     else:
         offs, sources, rec, table, taper, smooth, *refs = refs
-        out_r, out_s, out_edge, table_v, taper_v, smooth_v, *refs = refs
+        out_r, out_mid, out_s, out_edge, table_v, taper_v, smooth_v, *refs = refs
         sums, diffs, held, offs_v, sources_v, sems = refs
     width = (count + 2) * HOP
     copies = []
@@ -127,25 +128,30 @@
     power = jnp.concatenate([r * r + i * i for r, i in zip(real, imag)], axis=1).astype(jnp.bfloat16)
     smoothed = jnp.dot(power, smooth_v[...], preferred_element_type=jnp.float32)
     factor = lax.rsqrt(smoothed + 1e-05)
-    for i in range(NB // LANE):
-        lo = slice(i * LANE, (i + 1) * LANE)
-        hi = slice(NB + i * LANE, NB + (i + 1) * LANE)
-        out_r[:, lo] = (real[i] * factor[:, lo]).astype(jnp.bfloat16)
-        out_r[:, hi] = (imag[i] * factor[:, lo]).astype(jnp.bfloat16)
+    parts = [value * factor[:, i % 3 * LANE : (i % 3 + 1) * LANE] for i, value in enumerate(real + imag)]
+    white = jnp.concatenate([part.astype(jnp.bfloat16) for part in parts], axis=1)
+    if late:
+        at = before_r.shape[0]
+        out_r[:at] = before_r[...]
+        out_r[at:] = white
+    else:
+        at = out_r.shape[0]
+        out_r[...] = white[:at]
+        out_mid[...] = white[at:]
     rows = lax.broadcasted_iota(jnp.int32, (n_src * count, 1), 0)
     cols = lax.broadcasted_iota(jnp.int32, (n_src * count, count * c_dev), 1)
     wanted = jnp.zeros_like(rows)
     for s in range(n_src):
         wanted = jnp.where(rows // count == s, sources_v[s] % c_dev + (rows % count) * c_dev, wanted)
     picker = jnp.where(cols == wanted, 1.0, 0.0).astype(jnp.bfloat16)
-    out_s[...] = jnp.dot(picker, out_r[...], preferred_element_type=jnp.float32).astype(jnp.bfloat16)
+    out_s[...] = jnp.dot(picker, white, preferred_element_type=jnp.float32).astype(jnp.bfloat16)
     if late:
         at = before_s.shape[0]
         out_all[:at] = before_s[...]
         out_all[at:] = out_s[...]
 
 
-def spectra_call(record, offsets, src_idx, tables, first, count, late=None):
+def spectra_call(record, offsets, src_idx, tables, first, count, head=None, late=None):
     c_dev = record.shape[0]
     n_src = src_idx.shape[0]
     vmem = pl.BlockSpec(memory_space=pltpu.VMEM)
@@ -155,18 +161,17 @@
         arrays += tables
     arrays = [pltpu.with_memory_space_constraint(a, pltpu.HBM) for a in arrays]
     specs = [hbm] * len(arrays)
-    out_shape = [
-        jax.ShapeDtypeStruct((count * c_dev, 2 * NB), jnp.bfloat16),
-        jax.ShapeDtypeStruct((n_src * count, 2 * NB), jnp.bfloat16),
-    ]
+    rows = [head, count - head] if late is None else [count + late[1].shape[0] // c_dev]
+    out_shape = [jax.ShapeDtypeStruct((n * c_dev, 2 * NB), jnp.bfloat16) for n in rows]
+    out_shape.append(jax.ShapeDtypeStruct((n_src * count, 2 * NB), jnp.bfloat16))
     if late is None:
         out_shape.append(jax.ShapeDtypeStruct((c_dev, W), record.dtype))
         out_shape += [jax.ShapeDtypeStruct(t.shape, t.dtype) for t in tables]
     else:
-        halo, earlier = late
-        arrays += [halo, *tables, earlier]
-        specs += [vmem] * 5
-        out_shape.append(jax.ShapeDtypeStruct((earlier.shape[0] + n_src * count, 2 * NB), jnp.bfloat16))
+        halo, middle, sources = late
+        arrays += [halo, *tables, middle, sources]
+        specs += [vmem] * 6
+        out_shape.append(jax.ShapeDtypeStruct((sources.shape[0] + n_src * count, 2 * NB), jnp.bfloat16))
     return pl.pallas_call(
         functools.partial(spectra_kernel, first, count, late is not None, c_dev, n_src),
         out_shape=out_shape,
@@ -182,13 +187,13 @@
         ],
         compiler_params=pltpu.CompilerParams(vmem_limit_bytes=24 << 20),
         cost_estimate=pl.CostEstimate(
-            flops=int((1.5 + 0.1 * count) * 0.3e9), bytes_accessed=1 << 20, transcendentals=0
+            flops=int((1.5 + 0.1 * count) * 0.01e9), bytes_accessed=1 << 20, transcendentals=0
         ),
         name="spectra",
     )(*arrays)
 
 
-def cross_kernel(plan, n_src, n_win, c_dev, scale, n_done, n_after, last, *refs):
+def cross_kernel(plan, n_src, n_win, early, c_dev, scale, n_done, n_after, last, *refs):
     runs = []
     for n_group, parts, has_before in plan:
         srcs, refs = refs[:n_group], refs[n_group:]
@@ -237,7 +242,10 @@
                 rec_both = rec_real + rec_imag
                 for s in range(block):
                     at = s // n_src * n_src * n_win
-                    at += start * n_src + s % n_src * (stop - start) + w
+                    if start + w < early:
+                        at += s % n_src * early + start + w
+                    else:
+                        at += n_src * early + s % n_src * (n_win - early) + start + w - early
                     row = slice(at, at + 1)
                     both, plus, minus = sums[s]
                     sums[s] = [
@@ -271,7 +279,7 @@
         at += part.shape[0]
 
 
-def cross_call(runs, n_src, n_win, c_dev, scale, ltab=None, done=(), after=()):
+def cross_call(runs, n_src, n_win, early, c_dev, scale, ltab=None, done=(), after=()):
     grid = runs[0][0][0].shape[0]
     last = ltab is not None
     n_list = sum(len(srcs) for srcs, _, _ in runs)
@@ -305,7 +313,7 @@
         shapes.append(jax.ShapeDtypeStruct((sum(a.shape[0] for a in done), LAGS), jnp.bfloat16))
         out_specs.append(whole)
     return pl.pallas_call(
-        functools.partial(cross_kernel, plan, n_src, n_win, c_dev, scale, len(done), len(after), last),
+        functools.partial(cross_kernel, plan, n_src, n_win, early, c_dev, scale, len(done), len(after), last),
         grid=() if grid == 1 else (grid,),
         out_shape=shapes,
         in_specs=specs,
@@ -313,7 +321,7 @@
         scratch_shapes=scratch,
         compiler_params=pltpu.CompilerParams(vmem_limit_bytes=24 << 20),
         cost_estimate=pl.CostEstimate(
-            flops=int((0.4 + grid * pairs * 0.008) * 1.15e9), bytes_accessed=1 << 20, transcendentals=0
+            flops=int((0.4 + grid * pairs * 0.008) * 0.6e9), bytes_accessed=1 << 20, transcendentals=0
         ),
         name="cross",
     )(*arrays)
@@ -328,7 +336,7 @@
     n_group = n_fibre // 2
     fibre = lax.axis_index("fibre")
     tm = lax.axis_index("tm")
-    early = n_win * 3 // 4
+    head, early = n_win * 3 // 4, n_win * 7 // 8
     scale = 1.0 / math.sqrt(n_win * n_tm * NB)
     tables = [jnp.asarray(t) for t in (half_tables(), taper_table(), smoothing())]
     ltab = jnp.asarray(lag_table())
@@ -337,15 +345,16 @@
     def trade(array, by):
         return lax.ppermute(array, "fibre", [(i, i ^ by) for i in range(n_fibre)])
 
-    rec_a, src_a, edge, *tables = spectra_call(record, offsets, src_idx, tables, 0, early)
+    rec_a, middle, src_a, edge, *tables = spectra_call(record, offsets, src_idx, tables, 0, early, head)
     far_a = trade(rec_a, 1)
     if direct:
         by_2a = trade(src_a, 4)
     halo = lax.ppermute(edge, "tm", [(i, i - 1) for i in range(1, n_tm)])
-    rec_b, src_b, src = spectra_call(record, offsets, src_idx, tables, early, n_win - early, (halo, src_a))
+    late = (halo, middle, src_a)
+    rec_b, src_b, src = spectra_call(record, offsets, src_idx, tables, early, n_win - early, late=late)
     far_b = trade(rec_b, 1)
-    cross = functools.partial(cross_call, n_src=n_src, n_win=n_win, c_dev=c_dev, scale=scale)
-    head, rest = (0, early), (early, n_win)
+    cross = functools.partial(cross_call, n_src=n_src, n_win=n_win, early=early, c_dev=c_dev, scale=scale)
+    head, rest = (0, head), (head, n_win)
     own = [(rec_a, head), (rec_b, rest)]
     if direct:
         by_2 = jnp.concatenate([by_2a, trade(src_b, 4)], axis=0)

time: 39.9 us -> 39.3 us (0.985)
  local copies, waits for them, and re-layouts: 0.06 us -> 0.98 us
  starting transfers between devices: 15.3 us -> 14.6 us
  Pallas kernels: 14.7 us -> 14.2 us
    ppermute x6, waiting for transfers between devices: 5.22 us -> 2.65 us  [trade(): return lax.ppermute(array, 'fibre', [(i, i ^ by) for i in range(n_fibre)])]
    ppermute x1, waiting for transfers between devices: 0.01 us -> 1.81 us  [body(): halo = lax.ppermute(edge, 'tm', [(i, i - 1) for i in range(1, n_tm)])]
    unnamed x3, local copies, waits for them, and re-layouts: 0.01 us -> 0.93 us
    ppermute x6, starting transfers between devices: 10.4 us -> 9.58 us  [trade(): return lax.ppermute(array, 'fibre', [(i, i ^ by) for i in range(n_fibre)])]
    ppermute x3, waiting for transfers between devices: 2.18 us -> 2.7 us  [body(): mine = lax.ppermute(mine.astype(jnp.bfloat16), ('fibre', 'tm'), routes)]
  transfers between devices with their start and end apart: 11 -> 11, of which waited for: 8 -> 8; matrix products, arithmetic and copies ran while one was open for 0% -> 2% of each run, Pallas kernels for 24% -> 22%
where the time goes in v9:
time: 39.3 us; the launch traced here: 39.1 us
  starting transfers between devices  14.6 us (37%)
  Pallas kernels  14.2 us (36%)
  waiting for transfers between devices  8.37 us (21%)
  local copies, waits for them, and re-layouts  0.98 us (2%)
  other arithmetic  0.75 us (2%)
    ppermute x6, starting transfers between devices, trade(): return lax.ppermute(array, 'fibre', [(i, i ^ by) for i in range(n_fibre)])  9.58 us
    pallas_call x7, Pallas kernels, cross_call(): pl.pallas_call(functools.partial(cross_kernel, plan, n_src, n_win, early,...  8.17 us
    pallas_call x2, Pallas kernels, spectra_call(): pl.pallas_call(functools.partial(spectra_kernel, first, count, late is no...  6.06 us
    ppermute x3, starting transfers between devices, body(): mine = lax.ppermute(mine.astype(jnp.bfloat16), ('fibre', 'tm'), routes)  3.55 us
    ppermute x3, waiting for transfers between devices, body(): mine = lax.ppermute(mine.astype(jnp.bfloat16), ('fibre', 'tm'), routes)  2.7 us
    ppermute x6, waiting for transfers between devices, trade(): return lax.ppermute(array, 'fibre', [(i, i ^ by) for i in range(n_fibre)])  2.65 us
    ppermute x1, waiting for transfers between devices, body(): halo = lax.ppermute(edge, 'tm', [(i, i - 1) for i in range(1, n_tm)])  1.81 us
    ppermute x1, starting transfers between devices, body(): halo = lax.ppermute(edge, 'tm', [(i, i - 1) for i in range(1, n_tm)])  1.28 us
  transfers between devices with their start and end apart: 11, of which 8 were waited for; matrix products, arithmetic and copies ran while one was open for 2% of the time, Pallas kernels for 22%

profile of v9, /device:TPU:0, one launch (start us, length us, event | category | flops | bytes accessed | tf_op | source)
XLA Modules:
  0.0 39.1 jit_solution(15676350836436296296)
XLA Ops:
  0.0 4.2 %spectra.2 = (bf16[384,768]{1,0:T(8,128)(2,1)S(1)}, bf16[64,768]{1,0:T(8,128)(2,1)S(1)}, bf16[112,768]{1,0:T(8,128)(2,1)S(1)}, bf16[16,2048]{1,0:T(8,128)(2,1)S(...) custom-call(s32[32]{0:T(128)} %refs_0_.3, s32[4]{0:T(128)} %refs_1_.3, ...), custom_call_target="tpu_custom_call" | custom-call | flops 43000000 | bytes 1048576 | tf_op jit(solution)/shard_map/spectra/pallas_call | solution.py:175
  4.2 3.0 %collective-permute-start.2 = (bf16[384,768]{1,0:T(8,128)(2,1)S(1)}, bf16[384,768]{1,0:T(8,128)(2,1)S(1)}, u32[]{:S(2)}, u32[]{:S(2)}) collective-permute-start(bf16[384,768]{1,0:T(8,128)(2,1)S(1)} %get-tuple-element.25.refs_1_.refs_2_), channel_id=1, source_target_pairs={{0,4},{4,0},{8,12},{12,8},{16,20},{20,16},{24,28},{28,24},{1,5},{5... | collective-permute-start | bytes 1769480 | tf_op jit(solution)/shard_map/ppermute | solution.py:346
  7.2 2.6 %collective-permute-start.4 = (bf16[112,768]{1,0:T(8,128)(2,1)S(1)}, bf16[112,768]{1,0:T(8,128)(2,1)}, u32[]{:S(2)}, u32[]{:S(2)}) collective-permute-start(bf16[112,768]{1,0:T(8,128)(2,1)S(1)} %get-tuple-element.22.refs_8_), channel_id=1, source_target_pairs={{0,16},{4,20},{8,24},{12,28},{16,0},{20,4},{24,8},{28,12},{1,17},{... | collective-permute-start | bytes 516104 | tf_op jit(solution)/shard_map/ppermute | solution.py:346
  9.8 1.3 %collective-permute-start = (bf16[16,2048]{1,0:T(8,128)(2,1)S(1)}, bf16[16,2048]{1,0:T(8,128)(2,1)S(1)}, u32[]{:S(2)}, u32[]{:S(2)}) collective-permute-start(bf16[16,2048]{1,0:T(8,128)(2,1)S(1)} %get-tuple-element.17), channel_id=1, source_target_pairs={{1,0},{2,1},{3,2},{5,4},{6,5},{7,6},{9,8},{10,9},{11,10},{13,12},{... | collective-permute-start | bytes 196616 | tf_op jit(solution)/shard_map/ppermute | solution.py:352
  11.1 1.8 %collective-permute-done.refs_3_ = bf16[16,2048]{1,0:T(8,128)(2,1)S(1)} collective-permute-done((bf16[16,2048]{1,0:T(8,128)(2,1)S(1)}, bf16[16,2048]{1,0:T(8,128)(2,1)S(1)}, u32[]{:S(2)}, u32[]{:S(2)}) %collective-permute-start) | collective-permute-done | bytes 65568 | tf_op jit(solution)/shard_map/ppermute | solution.py:352
  12.9 0.0 copy-start
  12.9 1.9 %spectra.3 = (bf16[128,768]{1,0:T(8,128)(2,1)S(1)}, bf16[16,768]{1,0:T(8,128)(2,1)S(1)}, bf16[128,768]{1,0:T(8,128)(2,1)S(1)}) custom-call(s32[32]{0:T(128)} %refs_0_.3, s32[4]{0:T(128)} %refs_1_.3, bf16[16,32768]{1,0:T(8,128)(2,1)} %refs_2_.3, bf16[16,2048]{1,0:T(8,128)(2,1)S(1)} %collective-permute-done.refs_3_, ...), custom_call_target="tpu_custom_call" | custom-call | flops 19000000 | bytes 1048576 | tf_op jit(solution)/shard_map/spectra/pallas_call | solution.py:175
  14.8 0.4 %collective-permute-start.5 = (bf16[16,768]{1,0:T(8,128)(2,1)S(1)}, bf16[16,768]{1,0:T(8,128)(2,1)S(1)}, u32[]{:S(2)}, u32[]{:S(2)}) collective-permute-start(bf16[16,768]{1,0:T(8,128)(2,1)S(1)} %get-tuple-element.26), channel_id=1, source_target_pairs={{0,16},{4,20},{8,24},{12,28},{16,0},{20,4},{24,8},{28,12},{1,17},{... | collective-permute-start | bytes 73736 | tf_op jit(solution)/shard_map/ppermute | solution.py:346
  15.2 1.6 %collective-permute-start.3 = (bf16[128,768]{1,0:T(8,128)(2,1)S(1)}, bf16[128,768]{1,0:T(8,128)(2,1)S(1)}, u32[]{:S(2)}, u32[]{:S(2)}) collective-permute-start(bf16[128,768]{1,0:T(8,128)(2,1)S(1)} %get-tuple-element.23), channel_id=1, source_target_pairs={{0,8},{4,12},{8,0},{12,4},{16,24},{20,28},{24,16},{28,20},{1,9},{5... | collective-permute-start | bytes 589832 | tf_op jit(solution)/shard_map/ppermute | solution.py:346
  16.8 0.5 %collective-permute-start.1 = (bf16[128,768]{1,0:T(8,128)(2,1)S(1)}, bf16[128,768]{1,0:T(8,128)(2,1)S(1)}, u32[]{:S(2)}, u32[]{:S(2)}) collective-permute-start(bf16[128,768]{1,0:T(8,128)(2,1)S(1)} %get-tuple-element.24.refs_2_.refs_3_), channel_id=1, source_target_pairs={{0,4},{4,0},{8,12},{12,8},{16,20},{20,16},{24,28},{28,24},{1,5},{5... | collective-permute-start | bytes 589832 | tf_op jit(solution)/shard_map/ppermute | solution.py:346
  17.3 0.0 copy-done
  17.3 1.1 %cross.7.refs_2_.refs_10_ = bf16[64,256]{1,0:T(8,128)(2,1)S(1)} custom-call(bf16[1,128,768]{2,1,0:T(8,128)(2,1)S(1)} %bitcast.46, bf16[384,768]{1,0:T(8,128)(2,1)S(1)} %get-tuple-element.25.refs_1_.refs_2_, bf16[128,768]{1,0:T(8,128)(2,1)S(1)} %get-tuple-element.24.refs_2_.refs_3_, bf16[768,256]{1,0:T(8,128)(2,1)S(1)} %copy-done), custom_call_target="tpu_custom_call" | custom-call | flops 854400000 | bytes 1048576 | tf_op jit(solution)/shard_map/cross/pallas_call | solution.py:315
  18.4 0.0 collective-permute-done.4
  18.4 0.9 %constant_dynamic-update-slice_fusion.1 = bf16[128,768]{1,0:T(8,128)(2,1)S(1)} fusion(bf16[112,768]{1,0:T(8,128)(2,1)} %collective-permute-done.4), kind=kLoop, calls=%fused_computation.20 | loop fusion | bytes 344064
  19.4 0.3 collective-permute-done.5
  19.7 1.5 %collective-permute-start.6 = (bf16[128,768]{1,0:T(8,128)(2,1)S(1)}, bf16[128,768]{1,0:T(8,128)(2,1)S(1)}, u32[]{:S(2)}, u32[]{:S(2)}) collective-permute-start(bf16[128,768]{1,0:T(8,128)(2,1)S(1)} %constant_dynamic-update-slice_fusion), channel_id=1, source_target_pairs={{0,8},{4,12},{8,0},{12,4},{16,24},{20,28},{24,16},{28,20},{1,9},{5... | collective-permute-start | bytes 589832 | tf_op jit(solution)/shard_map/ppermute | solution.py:346
  21.2 0.0 collective-permute-done.2.refs_1_.refs_2_
  21.2 0.7 %cross.8.refs_5_.refs_2_ = f32[64,768]{1,0:T(8,128)S(1)} custom-call(bf16[1,128,768]{2,1,0:T(8,128)(2,1)S(1)} %bitcast.47, bf16[384,768]{1,0:T(8,128)(2,1)S(1)} %collective-permute-done.2.refs_1_.refs_2_, bf16[64,256]{1,0:T(8,128)(2,1)S(1)} %cross.7.refs_2_.refs_10_), custom_call_target="tpu_custom_call" | custom-call | flops 700800000 | bytes 1048576 | tf_op jit(solution)/shard_map/cross/pallas_call | solution.py:315
  21.9 0.3 collective-permute-done.3
  22.2 1.9 %cross.9.refs_3_.refs_11_ = bf16[128,256]{1,0:T(8,128)(2,1)S(1)} custom-call(bf16[1,128,768]{2,1,0:T(8,128)(2,1)S(1)} %bitcast.49, bf16[1,128,768]{2,1,0:T(8,128)(2,1)S(1)} %bitcast.41, bf16[384,768]{1,0:T(8,128)(2,1)S(1)} %get-tuple-element.25.refs_1_.refs_2_, bf16[128,768]{1,0:T(8,128)(2,1)S(1)} %get-tuple-element.24.refs_2_.refs_3_, ...), custom_call_target="tpu_custom_call" | custom-call | flops 1468800000 | bytes 1048576 | tf_op jit(solution)/shard_map/cross/pallas_call | solution.py:315
  24.1 1.3 %cross.10.refs_4_.refs_6_ = f32[128,768]{1,0:T(8,128)S(1)} custom-call(bf16[1,128,768]{2,1,0:T(8,128)(2,1)S(1)} %bitcast.50, bf16[1,128,768]{2,1,0:T(8,128)(2,1)S(1)} %bitcast.42, bf16[384,768]{1,0:T(8,128)(2,1)S(1)} %collective-permute-done.2.refs_1_.refs_2_, bf16[128,256]{1,0:T(8,128)(2,1)S(1)} %cross.9.refs_3_.refs_11_), custom_call_target="tpu_custom_call" | custom-call | flops 1161600000 | bytes 1048576 | tf_op jit(solution)/shard_map/cross/pallas_call | solution.py:315
  25.4 2.0 %collective-permute-done.6 = bf16[128,768]{1,0:T(8,128)(2,1)S(1)} collective-permute-done((bf16[128,768]{1,0:T(8,128)(2,1)S(1)}, bf16[128,768]{1,0:T(8,128)(2,1)S(1)}, u32[]{:S(2)}, u32[]{:S(2)}) %collective-permute-start.6) | collective-permute-done | bytes 196640 | tf_op jit(solution)/shard_map/ppermute | solution.py:346
  27.4 1.1 %cross.11.refs_2_.refs_12_ = bf16[64,256]{1,0:T(8,128)(2,1)S(1)} custom-call(bf16[1,128,768]{2,1,0:T(8,128)(2,1)S(1)} %bitcast.52, bf16[384,768]{1,0:T(8,128)(2,1)S(1)} %get-tuple-element.25.refs_1_.refs_2_, bf16[128,768]{1,0:T(8,128)(2,1)S(1)} %get-tuple-element.24.refs_2_.refs_3_, bf16[768,256]{1,0:T(8,128)(2,1)S(1)} %copy-done, ...), custom_call_target="tpu_custom_call" | custom-call | flops 854400000 | bytes 1048576 | tf_op jit(solution)/shard_map/cross/pallas_call | solution.py:315
  28.5 0.7 %cross.12.refs_9_ = f32[64,768]{1,0:T(8,128)S(1)} custom-call(bf16[1,128,768]{2,1,0:T(8,128)(2,1)S(1)} %bitcast.53, bf16[384,768]{1,0:T(8,128)(2,1)S(1)} %collective-permute-done.2.refs_1_.refs_2_, bf16[64,256]{1,0:T(8,128)(2,1)S(1)} %cross.11.refs_2_.refs_12_), custom_call_target="tpu_custom_call" | custom-call | flops 700800000 | bytes 1048576 | tf_op jit(solution)/shard_map/cross/pallas_call | solution.py:315
  29.2 0.0 collective-permute-done.1.refs_1_.refs_5_.refs_8_
  29.2 1.4 %cross.13 = (bf16[256,256]{1,0:T(8,128)(2,1)S(1)}, bf16[256,256]{1,0:T(8,128)(2,1)S(1)}) custom-call(bf16[1,128,768]{2,1,0:T(8,128)(2,1)S(1)} %bitcast.48, bf16[128,768]{1,0:T(8,128)(2,1)S(1)} %collective-permute-done.1.refs_1_.refs_5_.refs_8_, f32[64,768]{1,0:T(8,128)S(1)} %cross.8.refs_5_.refs_2_, bf16[1,128,768]{2,1,0:T(8,128)(2,1)S(1)} %bitcast.51, ...), custom_call_target="tpu_custom_call" | custom-call | flops 854400000 | bytes 1048576 | tf_op jit(solution)/shard_map/cross/pallas_call | solution.py:315
  30.7 0.2 collective-permute-start.7
  30.9 1.2 %collective-permute-done.7 = bf16[4,1,4,16,256]{4,3,2,1,0:T(8,128)(2,1)S(1)} collective-permute-done((bf16[4,1,4,16,256]{4,3,2,1,0:T(8,128)(2,1)S(1)}, bf16[4,1,4,16,256]{4,3,2,1,0:T(8,128)(2,1)S(1)}, u32[]{:S(2)}, u32[]{:S(2)}) %collective-permute-start.7) | collective-permute-done | bytes 131104 | tf_op jit(solution)/shard_map/ppermute | solution.py:387
  32.2 1.0 %collective-permute-start.10 = (bf16[1,4,16,256]{3,2,1,0:T(8,128)(2,1)S(1)}, bf16[1,4,16,256]{3,2,1,0:T(8,128)(2,1)S(1)}, u32[]{:S(2)}, u32[]{:S(2)}) collective-permute-start(bf16[1,4,16,256]{3,2,1,0:T(8,128)(2,1)S(1)} %get-tuple-element.34), channel_id=1, source_target_pairs={{0,6},{1,7},{2,4},{3,5},{4,2},{5,3},{6,0},{7,1},{8,14},{9,15},{10,... | collective-permute-start | bytes 98312 | tf_op jit(solution)/shard_map/ppermute | solution.py:400
  33.1 1.4 %collective-permute-start.8 = (bf16[1,4,16,256]{3,2,1,0:T(8,128)(2,1)S(1)}, bf16[1,4,16,256]{3,2,1,0:T(8,128)(2,1)S(1)}, u32[]{:S(2)}, u32[]{:S(2)}) collective-permute-start(bf16[1,4,16,256]{3,2,1,0:T(8,128)(2,1)S(1)} %get-tuple-element.33), channel_id=1, source_target_pairs={{0,2},{1,3},{2,0},{3,1},{4,6},{5,7},{6,4},{7,5},{8,10},{9,11},{10,... | collective-permute-start | bytes 98312 | tf_op jit(solution)/shard_map/ppermute | solution.py:400
  34.5 1.2 %collective-permute-start.9 = (bf16[1,4,16,256]{3,2,1,0:T(8,128)(2,1)S(1)}, bf16[1,4,16,256]{3,2,1,0:T(8,128)(2,1)S(1)}, u32[]{:S(2)}, u32[]{:S(2)}) collective-permute-start(bf16[1,4,16,256]{3,2,1,0:T(8,128)(2,1)S(1)} %get-tuple-element.35), channel_id=1, source_target_pairs={{0,4},{1,5},{2,6},{3,7},{4,0},{5,1},{6,2},{7,3},{8,12},{9,13},{10,... | collective-permute-start | bytes 98312 | tf_op jit(solution)/shard_map/ppermute | solution.py:400
  35.7 1.6 %collective-permute-done.10 = bf16[1,4,16,256]{3,2,1,0:T(8,128)(2,1)S(1)} collective-permute-done((bf16[1,4,16,256]{3,2,1,0:T(8,128)(2,1)S(1)}, bf16[1,4,16,256]{3,2,1,0:T(8,128)(2,1)S(1)}, u32[]{:S(2)}, u32[]{:S(2)}) %collective-permute-start.10) | collective-permute-done | bytes 32800 | tf_op jit(solution)/shard_map/ppermute | solution.py:400
  37.3 0.1 collective-permute-done.8
  37.4 1.0 %collective-permute-done.9 = bf16[1,4,16,256]{3,2,1,0:T(8,128)(2,1)S(1)} collective-permute-done((bf16[1,4,16,256]{3,2,1,0:T(8,128)(2,1)S(1)}, bf16[1,4,16,256]{3,2,1,0:T(8,128)(2,1)S(1)}, u32[]{:S(2)}, u32[]{:S(2)}) %collective-permute-start.9) | collective-permute-done | bytes 32800 | tf_op jit(solution)/shard_map/ppermute | solution.py:400
  38.4 0.7 %pad_maximum_fusion.1 = f32[1,2,4,16,256]{4,3,2,1,0:T(8,128)} fusion(f32[1,1,4,16,256]{4,3,2,1,0:T(8,128)S(1)} %get-tuple-element.30, f32[1,1,4,16,256]{4,3,2,1,0:T(8,128)S(1)} %get-tuple-element.29), kind=kLoop, calls=%fused_computation.2 | loop fusion | flops 32768 | bytes 262144 | tf_op jit(solution)/shard_map/stack | solution.py:406
  (6 shorter events, 0.1 us)
Async XLA Ops:
  4.2 17.0 %collective-permute-start.2 = (bf16[384,768]{1,0:T(8,128)(2,1)S(1)}, bf16[384,768]{1,0:T(8,128)(2,1)S(1)}, u32[]{:S(2)}, u32[]{:S(2)}) collective-permute-start(bf16[384,768]{1,0:T(8,128)(2,1)S(1)} %get-tuple-element.25.refs_1_.refs_2_), channel_id=1, source_target_pairs={{0,4},{4,0},{8,12},{12,8},{16,20},{20,16},{24,28},{28,24},{1,5},{5... | collective-permute-start | bytes 1769480 | tf_op jit(solution)/shard_map/ppermute | solution.py:346
  7.2 11.3 %collective-permute-start.4 = (bf16[112,768]{1,0:T(8,128)(2,1)S(1)}, bf16[112,768]{1,0:T(8,128)(2,1)}, u32[]{:S(2)}, u32[]{:S(2)}) collective-permute-start(bf16[112,768]{1,0:T(8,128)(2,1)S(1)} %get-tuple-element.22.refs_8_), channel_id=1, source_target_pairs={{0,16},{4,20},{8,24},{12,28},{16,0},{20,4},{24,8},{28,12},{1,17},{... | collective-permute-start | bytes 516104 | tf_op jit(solution)/shard_map/ppermute | solution.py:346
  9.8 3.1 %collective-permute-start = (bf16[16,2048]{1,0:T(8,128)(2,1)S(1)}, bf16[16,2048]{1,0:T(8,128)(2,1)S(1)}, u32[]{:S(2)}, u32[]{:S(2)}) collective-permute-start(bf16[16,2048]{1,0:T(8,128)(2,1)S(1)} %get-tuple-element.17), channel_id=1, source_target_pairs={{1,0},{2,1},{3,2},{5,4},{6,5},{7,6},{9,8},{10,9},{11,10},{13,12},{... | collective-permute-start | bytes 196616 | tf_op jit(solution)/shard_map/ppermute | solution.py:352
  12.9 4.4 %copy-start = (bf16[768,256]{1,0:T(8,128)(2,1)S(1)}, bf16[768,256]{1,0:T(8,128)(2,1)}, u32[]{:S(2)}) copy-start(bf16[768,256]{1,0:T(8,128)(2,1)} %constant.81.clone.refs_3_.refs_4_.refs_13_) | copy-start | bytes 1179652
  14.8 4.9 %collective-permute-start.5 = (bf16[16,768]{1,0:T(8,128)(2,1)S(1)}, bf16[16,768]{1,0:T(8,128)(2,1)S(1)}, u32[]{:S(2)}, u32[]{:S(2)}) collective-permute-start(bf16[16,768]{1,0:T(8,128)(2,1)S(1)} %get-tuple-element.26), channel_id=1, source_target_pairs={{0,16},{4,20},{8,24},{12,28},{16,0},{20,4},{24,8},{28,12},{1,17},{... | collective-permute-start | bytes 73736 | tf_op jit(solution)/shard_map/ppermute | solution.py:346
  15.2 7.0 %collective-permute-start.3 = (bf16[128,768]{1,0:T(8,128)(2,1)S(1)}, bf16[128,768]{1,0:T(8,128)(2,1)S(1)}, u32[]{:S(2)}, u32[]{:S(2)}) collective-permute-start(bf16[128,768]{1,0:T(8,128)(2,1)S(1)} %get-tuple-element.23), channel_id=1, source_target_pairs={{0,8},{4,12},{8,0},{12,4},{16,24},{20,28},{24,16},{28,20},{1,9},{5... | collective-permute-start | bytes 589832 | tf_op jit(solution)/shard_map/ppermute | solution.py:346
  16.8 12.4 %collective-permute-start.1 = (bf16[128,768]{1,0:T(8,128)(2,1)S(1)}, bf16[128,768]{1,0:T(8,128)(2,1)S(1)}, u32[]{:S(2)}, u32[]{:S(2)}) collective-permute-start(bf16[128,768]{1,0:T(8,128)(2,1)S(1)} %get-tuple-element.24.refs_2_.refs_3_), channel_id=1, source_target_pairs={{0,4},{4,0},{8,12},{12,8},{16,20},{20,16},{24,28},{28,24},{1,5},{5... | collective-permute-start | bytes 589832 | tf_op jit(solution)/shard_map/ppermute | solution.py:346
  19.7 7.7 %collective-permute-start.6 = (bf16[128,768]{1,0:T(8,128)(2,1)S(1)}, bf16[128,768]{1,0:T(8,128)(2,1)S(1)}, u32[]{:S(2)}, u32[]{:S(2)}) collective-permute-start(bf16[128,768]{1,0:T(8,128)(2,1)S(1)} %constant_dynamic-update-slice_fusion), channel_id=1, source_target_pairs={{0,8},{4,12},{8,0},{12,4},{16,24},{20,28},{24,16},{28,20},{1,9},{5... | collective-permute-start | bytes 589832 | tf_op jit(solution)/shard_map/ppermute | solution.py:346
  30.7 1.4 %collective-permute-start.7 = (bf16[4,1,4,16,256]{4,3,2,1,0:T(8,128)(2,1)S(1)}, bf16[4,1,4,16,256]{4,3,2,1,0:T(8,128)(2,1)S(1)}, u32[]{:S(2)}, u32[]{:S(2)}) collective-permute-start(bf16[4,1,4,16,256]{4,3,2,1,0:T(8,128)(2,1)S(1)} %pad_maximum_fusion), channel_id=1, source_target_pairs={{0,1},{1,0},{2,3},{3,2},{4,5},{5,4},{6,7},{7,6},{8,9},{9,8},{10,11... | collective-permute-start | bytes 393224 | tf_op jit(solution)/shard_map/ppermute | solution.py:387
  32.2 5.2 %collective-permute-start.10 = (bf16[1,4,16,256]{3,2,1,0:T(8,128)(2,1)S(1)}, bf16[1,4,16,256]{3,2,1,0:T(8,128)(2,1)S(1)}, u32[]{:S(2)}, u32[]{:S(2)}) collective-permute-start(bf16[1,4,16,256]{3,2,1,0:T(8,128)(2,1)S(1)} %get-tuple-element.34), channel_id=1, source_target_pairs={{0,6},{1,7},{2,4},{3,5},{4,2},{5,3},{6,0},{7,1},{8,14},{9,15},{10,... | collective-permute-start | bytes 98312 | tf_op jit(solution)/shard_map/ppermute | solution.py:400
  33.1 4.3 %collective-permute-start.8 = (bf16[1,4,16,256]{3,2,1,0:T(8,128)(2,1)S(1)}, bf16[1,4,16,256]{3,2,1,0:T(8,128)(2,1)S(1)}, u32[]{:S(2)}, u32[]{:S(2)}) collective-permute-start(bf16[1,4,16,256]{3,2,1,0:T(8,128)(2,1)S(1)} %get-tuple-element.33), channel_id=1, source_target_pairs={{0,2},{1,3},{2,0},{3,1},{4,6},{5,7},{6,4},{7,5},{8,10},{9,11},{10,... | collective-permute-start | bytes 98312 | tf_op jit(solution)/shard_map/ppermute | solution.py:400
  34.5 3.9 %collective-permute-start.9 = (bf16[1,4,16,256]{3,2,1,0:T(8,128)(2,1)S(1)}, bf16[1,4,16,256]{3,2,1,0:T(8,128)(2,1)S(1)}, u32[]{:S(2)}, u32[]{:S(2)}) collective-permute-start(bf16[1,4,16,256]{3,2,1,0:T(8,128)(2,1)S(1)} %get-tuple-element.35), channel_id=1, source_target_pairs={{0,4},{1,5},{2,6},{3,7},{4,0},{5,1},{6,2},{7,3},{8,12},{9,13},{10,... | collective-permute-start | bytes 98312 | tf_op jit(solution)/shard_map/ppermute | solution.py:400

commit v10 on v9

--- a/solution.py
+++ b/solution.py
@@ -58,10 +58,10 @@
     return table.astype(np.float32).astype(jnp.bfloat16)
 
 
-def spectra_kernel(first, count, late, c_dev, n_src, *refs):
+def spectra_kernel(first, count, late, c_dev, n_src, n_after, *refs):
     if late:
         offs, sources, rec, halo, table_v, taper_v, smooth_v, before_r, before_s, *refs = refs
-        out_r, out_s, out_all, *refs = refs
+        out_r, out_s, out_all, *refs = refs[n_after:]
         sums, diffs, held, offs_v, sources_v, sems = refs
     else:
         offs, sources, rec, table, taper, smooth, *refs = refs
@@ -151,7 +151,7 @@
         out_all[at:] = out_s[...]
 
 
-def spectra_call(record, offsets, src_idx, tables, first, count, head=None, late=None):
+def spectra_call(record, offsets, src_idx, tables, first, count, head=None, late=None, after=()):
     c_dev = record.shape[0]
     n_src = src_idx.shape[0]
     vmem = pl.BlockSpec(memory_space=pltpu.VMEM)
@@ -169,11 +169,11 @@
         out_shape += [jax.ShapeDtypeStruct(t.shape, t.dtype) for t in tables]
     else:
         halo, middle, sources = late
-        arrays += [halo, *tables, middle, sources]
-        specs += [vmem] * 6
+        arrays += [halo, *tables, middle, sources, *after]
+        specs += [vmem] * 6 + [pl.BlockSpec(memory_space=pl.ANY)] * len(after)
         out_shape.append(jax.ShapeDtypeStruct((sources.shape[0] + n_src * count, 2 * NB), jnp.bfloat16))
     return pl.pallas_call(
-        functools.partial(spectra_kernel, first, count, late is not None, c_dev, n_src),
+        functools.partial(spectra_kernel, first, count, late is not None, c_dev, n_src, len(after)),
         out_shape=out_shape,
         in_specs=specs,
         out_specs=[vmem] * len(out_shape),
@@ -193,59 +193,48 @@
     )(*arrays)
 
 
-def cross_kernel(plan, n_src, n_win, early, c_dev, scale, n_done, n_after, last, *refs):
-    runs = []
-    for n_group, parts, has_before in plan:
-        srcs, refs = refs[:n_group], refs[n_group:]
-        recs, refs = refs[: len(parts)], refs[len(parts) :]
-        before, refs = refs[: int(has_before)], refs[int(has_before) :]
-        runs.append((srcs, list(zip(recs, parts)), before))
-    done, refs = refs[:n_done], refs[n_done:]
-    if last:
-        ltab, refs = refs[0], refs[1:]
-    refs = refs[n_after:]
-    if last:
-        out, *assembled, wide, cross = refs
-    else:
-        out, wide = refs
-        cross = out
-    at = 0
-    for srcs, _, _ in runs:
-        for src in srcs:
-            rows = slice(at, at + src.shape[1])
-            real = src[0, :, :NB].astype(jnp.float32)
-            imag = src[0, :, NB:].astype(jnp.float32)
-            wide[rows, :NB] = real
-            wide[rows, NB : 2 * NB] = real + imag
-            wide[rows, 2 * NB :] = real - imag
-            at += src.shape[1]
+def cross_kernel(runs, outs, counts, n_src, n_win, early, c_dev, scale, *refs):
+    groups = []
+    for count in counts:
+        groups.append(refs[:count])
+        refs = refs[count:]
+    srcs, recs, befores, done, tables, _ = groups
+    outputs, refs = refs[: len(outs)], refs[len(outs) :]
+    wide = refs[0]
+    span = n_src * n_win
+    for k, src in enumerate(srcs):
+        rows = slice(k * span, k * span + src.shape[1])
+        real = src[0, :, :NB].astype(jnp.float32)
+        imag = src[0, :, NB:].astype(jnp.float32)
+        wide[rows, :NB] = real
+        wide[rows, NB : 2 * NB] = real + imag
+        wide[rows, 2 * NB :] = real - imag
     tiles = NB // LANE
 
-    def run(step, first, groups, recs, before):
-        block = groups * n_src
-        local = step // tiles * groups
+    def run(step, first, wave, parts, before, target, offset):
+        block = wave * n_src
+        local = step // tiles * wave
         lo, hi, top = (
             pl.ds(pl.multiple_of(step % tiles * LANE + i * NB, LANE), LANE) for i in range(3)
         )
-        base = pl.multiple_of((first + local) * (n_src * n_win), 8)
-        src = wide.at[pl.ds(base, block * n_win)]
-
-        def place(group, s):
-            return pl.ds(pl.multiple_of((group * n_src + s) * c_dev, c_dev), c_dev)
+        src = wide.at[pl.ds(pl.multiple_of((first + local) * span, 8), wave * span)]
+
+        def place(start, s):
+            return pl.ds(pl.multiple_of(((start + local) * n_src + s) * c_dev, c_dev), c_dev)
 
         sums = [[jnp.zeros((c_dev, LANE), jnp.float32)] * 3 for _ in range(block)]
-        for rec, (start, stop) in recs:
-            for w in range(stop - start):
-                row = slice(w * c_dev, (w + 1) * c_dev)
-                rec_real = rec[row, lo].astype(jnp.float32)
-                rec_imag = rec[row, hi].astype(jnp.float32)
+        for index, base, start, stop in parts:
+            for w in range(start, stop):
+                row = slice((w - base) * c_dev, (w - base + 1) * c_dev)
+                rec_real = recs[index][row, lo].astype(jnp.float32)
+                rec_imag = recs[index][row, hi].astype(jnp.float32)
                 rec_both = rec_real + rec_imag
                 for s in range(block):
-                    at = s // n_src * n_src * n_win
-                    if start + w < early:
-                        at += s % n_src * early + start + w
+                    at = s // n_src * span
+                    if w < early:
+                        at += s % n_src * early + w
                     else:
-                        at += n_src * early + s % n_src * (n_win - early) + start + w - early
+                        at += n_src * early + s % n_src * (n_win - early) + w - early
                     row = slice(at, at + 1)
                     both, plus, minus = sums[s]
                     sums[s] = [
@@ -256,64 +245,71 @@
         for s in range(block):
             both, plus, minus = sums[s]
             real, imag = both - minus, both - plus
-            for earlier in before:
-                real += earlier[place(local, s), lo]
-                imag += earlier[place(local, s), hi]
-            cross[place(first + local, s), lo] = real.astype(cross.dtype)
-            cross[place(first + local, s), hi] = imag.astype(cross.dtype)
-
-    first = 0
-    for srcs, recs, before in runs:
-        groups = 8 // n_src if len(srcs) * n_src % 8 == 0 and 8 % n_src == 0 else 1
-        pl.loop(0, len(srcs) // groups * tiles)(
-            functools.partial(run, first=first, groups=groups, recs=recs, before=before)
+            if before is not None:
+                real += befores[before[0]][place(before[1], s), lo]
+                imag += befores[before[0]][place(before[1], s), hi]
+            target[place(offset, s), lo] = real.astype(target.dtype)
+            target[place(offset, s), hi] = imag.astype(target.dtype)
+
+    lagged = 0
+    for first, n_group, parts, before, place in runs:
+        if place is None:
+            target, offset = refs[1], lagged
+            lagged += n_group
+        else:
+            target, offset = outputs[place[0]], place[1]
+        wave = 8 // n_src if n_group * n_src % 8 == 0 and 8 % n_src == 0 else 1
+        pl.loop(0, n_group // wave * tiles)(
+            functools.partial(
+                run, first=first, wave=wave, parts=parts, before=before, target=target, offset=offset
+            )
         )
-        first += len(srcs)
-
-    if last:
-        lagged = jnp.dot(cross[...], ltab[...], preferred_element_type=jnp.float32)
-        out[...] = (lagged * scale).astype(jnp.bfloat16)
-    at = 0
-    for part in done:
-        assembled[0][at : at + part.shape[0], :] = part[...]
-        at += part.shape[0]
-
-
-def cross_call(runs, n_src, n_win, early, c_dev, scale, ltab=None, done=(), after=()):
-    grid = runs[0][0][0].shape[0]
-    last = ltab is not None
-    n_list = sum(len(srcs) for srcs, _, _ in runs)
-    rows = n_list * n_src * c_dev
+
+    if lagged:
+        lags = jnp.dot(refs[1][...], tables[0][...], preferred_element_type=jnp.float32)
+        lags = (lags * scale).astype(jnp.bfloat16)
+        unit = n_src * c_dev
+        start = 0
+        for out, pieces in zip(outputs, outs):
+            at = 0
+            for piece in pieces or ():
+                if isinstance(piece, str):
+                    part = done[0][...]
+                else:
+                    part = lags[start * unit : (start + piece) * unit]
+                    start += piece
+                out[at : at + part.shape[0], :] = part
+                at += part.shape[0]
+
+
+def cross_call(srcs, recs, runs, outs, n_src, n_win, early, c_dev, scale, befores=(), done=(), ltab=None, after=()):
+    grid = srcs[0].shape[0]
+    unit = n_src * c_dev
     whole = pl.BlockSpec(memory_space=pltpu.VMEM)
-    arrays, specs, plan, pairs = [], [], [], 0
-    for srcs, parts, before in runs:
-        arrays += srcs
-        if grid == 1:
-            specs += [whole] * len(srcs)
+    lists = [srcs, recs, befores, done, () if ltab is None else (ltab,), after]
+    arrays = [a for some in lists for a in some]
+    specs = [whole] * (len(arrays) - len(after)) + [pl.BlockSpec(memory_space=pl.ANY)] * len(after)
+    shapes = []
+    for out in outs:
+        if isinstance(out, int):
+            shapes.append(jax.ShapeDtypeStruct((out * unit, 2 * NB), jnp.float32))
         else:
-            specs += [pl.BlockSpec((1,) + a.shape[1:], lambda g: (g, 0, 0)) for a in srcs]
-        others = [rec for rec, _ in parts] + ([] if before is None else [before])
-        arrays += others
-        specs += [whole] * len(others)
-        plan.append((len(srcs), [cut for _, cut in parts], before is not None))
-        pairs += len(srcs) * n_src * sum(stop - start for _, (start, stop) in parts)
-    others = list(done) + ([ltab] if last else [])
-    arrays += others + list(after)
-    specs += [whole] * len(others) + [pl.BlockSpec(memory_space=pl.ANY)] * len(after)
-    scratch = [pltpu.VMEM((n_list * n_src * n_win, 3 * NB), jnp.float32)]
-    if last:
-        scratch.append(pltpu.VMEM((rows, 2 * NB), jnp.bfloat16))
-    shapes = [
-        jax.ShapeDtypeStruct((grid * rows, LAGS), jnp.bfloat16)
-        if last
-        else jax.ShapeDtypeStruct((grid * rows, 2 * NB), jnp.float32)
-    ]
-    out_specs = [whole if grid == 1 else pl.BlockSpec((rows, shapes[0].shape[1]), lambda g: (g, 0))]
-    if done:
-        shapes.append(jax.ShapeDtypeStruct((sum(a.shape[0] for a in done), LAGS), jnp.bfloat16))
-        out_specs.append(whole)
+            rows = sum(done[0].shape[0] if isinstance(p, str) else p * unit for p in out)
+            shapes.append(jax.ShapeDtypeStruct((grid * rows, LAGS), jnp.bfloat16))
+    out_specs = [whole] * len(shapes)
+    if grid > 1:
+        specs[: len(srcs)] = [pl.BlockSpec((1,) + a.shape[1:], lambda g: (g, 0, 0)) for a in srcs]
+        out_specs = [pl.BlockSpec((s.shape[0] // grid, s.shape[1]), lambda g: (g, 0)) for s in shapes]
+    scratch = [pltpu.VMEM((len(srcs) * n_src * n_win, 3 * NB), jnp.float32)]
+    lagged = sum(n for _, n, _, _, place in runs if place is None)
+    if lagged:
+        scratch.append(pltpu.VMEM((lagged * unit, 2 * NB), jnp.bfloat16))
+    pairs = sum(n * n_src * sum(p[3] - p[2] for p in parts) for _, n, parts, _, _ in runs)
+    kept = [None if isinstance(out, int) else out for out in outs]
     return pl.pallas_call(
-        functools.partial(cross_kernel, plan, n_src, n_win, early, c_dev, scale, len(done), len(after), last),
+        functools.partial(
+            cross_kernel, runs, kept, [len(some) for some in lists], n_src, n_win, early, c_dev, scale
+        ),
         grid=() if grid == 1 else (grid,),
         out_shape=shapes,
         in_specs=specs,
@@ -321,10 +317,31 @@
         scratch_shapes=scratch,
         compiler_params=pltpu.CompilerParams(vmem_limit_bytes=24 << 20),
         cost_estimate=pl.CostEstimate(
-            flops=int((0.4 + grid * pairs * 0.008) * 0.6e9), bytes_accessed=1 << 20, transcendentals=0
+            flops=int((0.4 + grid * pairs * 0.008) * 0.02e9), bytes_accessed=1 << 20, transcendentals=0
         ),
         name="cross",
     )(*arrays)
+
+
+def join_kernel(*refs):
+    *parts, out = refs
+    at = 0
+    for part in parts:
+        out[at : at + part.shape[0]] = part[...]
+        at += part.shape[0]
+
+
+def join_call(*parts):
+    rows = sum(part.shape[0] for part in parts)
+    vmem = pl.BlockSpec(memory_space=pltpu.VMEM)
+    return pl.pallas_call(
+        join_kernel,
+        out_shape=jax.ShapeDtypeStruct((rows, parts[0].shape[1]), parts[0].dtype),
+        in_specs=[vmem] * len(parts),
+        out_specs=vmem,
+        cost_estimate=pl.CostEstimate(flops=1 << 20, bytes_accessed=1 << 19, transcendentals=0),
+        name="join",
+    )(*parts)
 
 
 def body(record, offsets, src_idx):
@@ -350,30 +367,49 @@
     if direct:
         by_2a = trade(src_a, 4)
     halo = lax.ppermute(edge, "tm", [(i, i - 1) for i in range(1, n_tm)])
+    cross = functools.partial(
+        cross_call, n_src=n_src, n_win=n_win, early=early, c_dev=c_dev, scale=scale
+    )
     late = (halo, middle, src_a)
-    rec_b, src_b, src = spectra_call(record, offsets, src_idx, tables, early, n_win - early, late=late)
+    begun = []
+    if direct:
+        parts = [(0, 0, 0, head), (1, head, head, early)]
+        begun = cross([src_a[None]], [rec_a, middle], [(0, 1, parts, None, (0, 0))], [1])
+    rec_b, src_b, src = spectra_call(
+        record, offsets, src_idx, tables, early, n_win - early, late=late, after=begun
+    )
     far_b = trade(rec_b, 1)
-    cross = functools.partial(cross_call, n_src=n_src, n_win=n_win, early=early, c_dev=c_dev, scale=scale)
-    head, rest = (0, head), (head, n_win)
-    own = [(rec_a, head), (rec_b, rest)]
+    own = [(0, 0, 0, head), (1, head, head, n_win)]
     if direct:
-        by_2 = jnp.concatenate([by_2a, trade(src_b, 4)], axis=0)
+        by_2 = join_call(by_2a, trade(src_b, 4))
         by_1 = trade(src, 2)
         by_3 = trade(by_2, 2)
         srcs = [part[None] for part in (src, by_1, by_2, by_3)]
-        split = (srcs[:1], srcs[1:3], srcs[3:])
-        near, sums = [], []
-        for k, part in enumerate(split):
-            after = sums[-1:]
-            near += cross([(part, own, None)], ltab=ltab, after=after)
-            sums += cross([(part, [(far_a, head)], None)], after=near[-1:])
-        runs = [(part, [(far_b, rest)], before) for part, before in zip(split, sums)]
-        far, near = cross(runs, ltab=ltab, done=near)
+        swapped = [(2, 0, 0, head)]
+        runs = [
+            (0, 1, [(1, head, early, n_win)], (0, 0), None),
+            (1, 2, own, None, None),
+            (0, 1, swapped, None, (1, 0)),
+            (1, 2, swapped, None, (1, 1)),
+        ]
+        near, sums = cross(srcs[:3], [rec_a, rec_b, far_a], runs, [[1, 2], 3], befores=begun, ltab=ltab)
+        swapped = [(3, head, head, n_win)]
+        runs = [
+            (0, 1, swapped, (0, 0), None),
+            (1, 2, swapped, (0, 1), None),
+            (3, 1, [(2, 0, 0, head)] + swapped, None, None),
+            (3, 1, own, None, None),
+        ]
+        far, near = cross(
+            srcs, [rec_a, rec_b, far_a, far_b], runs, [[1, 2, 1], ["done", 1]],
+            befores=[sums], done=[near], ltab=ltab,
+        )
     else:
         ranks = [[2 * j + p for j in range(n_group)] for p in range(2)]
         srcs = [lax.all_gather(src, "fibre", axis=0, axis_index_groups=ranks)]
-        near = cross([(srcs, own, None)], ltab=ltab)[0]
-        far = cross([(srcs, [(far_a, head), (far_b, rest)], None)], ltab=ltab)[0]
+        runs = [(0, 1, own, None, None)]
+        near = cross(srcs, [rec_a, rec_b], runs, [[1]], ltab=ltab)[0]
+        far = cross(srcs, [far_a, far_b], runs, [[1]], ltab=ltab)[0]
     near, far = (r.reshape(n_group, n_src, c_dev, LAGS) for r in (near, far))
 
     def piece(lagged, owner):

time: 39.3 us -> 41.5 us (1.056)
  local copies, waits for them, and re-layouts: 0.98 us -> 2.25 us
  Pallas kernels: 14.2 us -> 15.3 us
    unnamed x3 -> x10, local copies, waits for them, and re-layouts: 0.93 us -> 2.21 us
    pallas_call x7 -> x4, Pallas kernels: 8.17 us -> 9.23 us  [the longest x3 7.63 us: cross_call(): pl.pallas_call(functools.partial(cross_kernel, runs, kept, [len(some) for...]
    ppermute x6, waiting for transfers between devices: 2.65 us -> 3.51 us  [trade(): return lax.ppermute(array, 'fibre', [(i, i ^ by) for i in range(n_fibre)])]
    ppermute x1, waiting for transfers between devices: 1.81 us -> 1.06 us  [body(): halo = lax.ppermute(edge, 'tm', [(i, i - 1) for i in range(1, n_tm)])]
  transfers between devices with their start and end apart: 11 -> 11, of which waited for: 8 -> 7; matrix products, arithmetic and copies ran while one was open for 2% -> 0% of each run, Pallas kernels for 22% -> 20%
where the time goes in v10:
time: 41.5 us; the launch traced here: 41.3 us
  Pallas kernels  15.3 us (37%)
  starting transfers between devices  14.9 us (36%)
  waiting for transfers between devices  7.97 us (19%)
  local copies, waits for them, and re-layouts  2.25 us (5%)
  other arithmetic  0.75 us (2%)
    ppermute x6, starting transfers between devices, trade(): return lax.ppermute(array, 'fibre', [(i, i ^ by) for i in range(n_fibre)])  9.57 us
    pallas_call x3, Pallas kernels, cross_call(): pl.pallas_call(functools.partial(cross_kernel, runs, kept, [len(some) for...  7.63 us
    pallas_call x2, Pallas kernels, spectra_call(): pl.pallas_call(functools.partial(spectra_kernel, first, count, late is no...  6.07 us
    ppermute x3, starting transfers between devices, body(): mine = lax.ppermute(mine.astype(jnp.bfloat16), ('fibre', 'tm'), routes)  3.57 us
    ppermute x6, waiting for transfers between devices, trade(): return lax.ppermute(array, 'fibre', [(i, i ^ by) for i in range(n_fibre)])  3.51 us
    ppermute x3, waiting for transfers between devices, body(): mine = lax.ppermute(mine.astype(jnp.bfloat16), ('fibre', 'tm'), routes)  2.42 us
    unnamed x10, local copies, waits for them, and re-layouts  2.21 us
    pallas_call x1, Pallas kernels, join_call(): pl.pallas_call(join_kernel, out_shape=jax.ShapeDtypeStruct((rows, parts[0...  1.6 us
  transfers between devices with their start and end apart: 11, of which 7 were waited for; matrix products, arithmetic and copies ran while one was open for 0% of the time, Pallas kernels for 20%

profile of v10, /device:TPU:0, one launch (start us, length us, event | category | flops | bytes accessed | tf_op | source)
XLA Modules:
  0.0 41.3 jit_solution(5603125908572100943)
XLA Ops:
  0.0 4.2 %spectra.2 = (bf16[384,768]{1,0:T(8,128)(2,1)S(1)}, bf16[64,768]{1,0:T(8,128)(2,1)S(1)}, bf16[112,768]{1,0:T(8,128)(2,1)S(1)}, bf16[16,2048]{1,0:T(8,128)(2,1)S(...) custom-call(s32[32]{0:T(128)} %refs_0_.3, s32[4]{0:T(128)} %refs_1_.3, ...), custom_call_target="tpu_custom_call" | custom-call | flops 43000000 | bytes 1048576 | tf_op jit(solution)/shard_map/spectra/pallas_call | solution.py:175
  4.2 3.0 %collective-permute-start.5 = (bf16[384,768]{1,0:T(8,128)(2,1)S(1)}, bf16[384,768]{1,0:T(8,128)(2,1)S(1)}, u32[]{:S(2)}, u32[]{:S(2)}) collective-permute-start(bf16[384,768]{1,0:T(8,128)(2,1)S(1)} %get-tuple-element.25.refs_1_.refs_3_.refs_4_), channel_id=1, source_target_pairs={{0,4},{4,0},{8,12},{12,8},{16,20},{20,16},{24,28},{28,24},{1,5},{5... | collective-permute-start | bytes 1769480 | tf_op jit(solution)/shard_map/ppermute | solution.py:363
  7.2 2.6 %collective-permute-start.2 = (bf16[112,768]{1,0:T(8,128)(2,1)S(1)}, bf16[112,768]{1,0:T(8,128)(2,1)S(1)}, u32[]{:S(2)}, u32[]{:S(2)}) collective-permute-start(bf16[112,768]{1,0:T(8,128)(2,1)S(1)} %get-tuple-element.24.refs_8_), channel_id=1, source_target_pairs={{0,16},{4,20},{8,24},{12,28},{16,0},{20,4},{24,8},{28,12},{1,17},{... | collective-permute-start | bytes 516104 | tf_op jit(solution)/shard_map/ppermute | solution.py:363
  9.8 1.3 %collective-permute-start = (bf16[16,2048]{1,0:T(8,128)(2,1)S(1)}, bf16[16,2048]{1,0:T(8,128)(2,1)S(1)}, u32[]{:S(2)}, u32[]{:S(2)}) collective-permute-start(bf16[16,2048]{1,0:T(8,128)(2,1)S(1)} %get-tuple-element.19), channel_id=1, source_target_pairs={{1,0},{2,1},{3,2},{5,4},{6,5},{7,6},{9,8},{10,9},{11,10},{13,12},{... | collective-permute-start | bytes 196616 | tf_op jit(solution)/shard_map/ppermute | solution.py:369
  11.1 0.8 %cross.3.refs_9_.refs_6_ = f32[64,768]{1,0:T(8,128)S(1)} custom-call(bf16[1,112,768]{2,1,0:T(8,128)(2,1)S(1)} %bitcast.48, bf16[384,768]{1,0:T(8,128)(2,1)S(1)} %get-tuple-element.25.refs_1_.refs_3_.refs_4_, bf16[64,768]{1,0:T(8,128)(2,1)S(1)} %get-tuple-element.23.refs_2_.refs_7_), custom_call_target="tpu_custom_call" | custom-call | flops 25920000 | bytes 1048576 | tf_op jit(solution)/shard_map/cross/pallas_call | solution.py:309
  11.9 1.1 %collective-permute-done.refs_3_ = bf16[16,2048]{1,0:T(8,128)(2,1)S(1)} collective-permute-done((bf16[16,2048]{1,0:T(8,128)(2,1)S(1)}, bf16[16,2048]{1,0:T(8,128)(2,1)S(1)}, u32[]{:S(2)}, u32[]{:S(2)}) %collective-permute-start) | collective-permute-done | bytes 65568 | tf_op jit(solution)/shard_map/ppermute | solution.py:369
  12.9 0.0 copy-start.2
  12.9 1.9 %spectra.3 = (bf16[128,768]{1,0:T(8,128)(2,1)S(1)}, bf16[16,768]{1,0:T(8,128)(2,1)S(1)}, bf16[128,768]{1,0:T(8,128)(2,1)S(1)}) custom-call(s32[32]{0:T(128)} %refs_0_.3, s32[4]{0:T(128)} %refs_1_.3, bf16[16,32768]{1,0:T(8,128)(2,1)} %refs_2_.3, bf16[16,2048]{1,0:T(8,128)(2,1)S(1)} %collective-permute-done.refs_3_, ...), custom_call_target="tpu_custom_call" | custom-call | flops 19000000 | bytes 1048576 | tf_op jit(solution)/shard_map/spectra/pallas_call | solution.py:175
  14.8 0.4 collective-permute-start.3
  15.2 1.6 %collective-permute-start.1 = (bf16[128,768]{1,0:T(8,128)(2,1)S(1)}, bf16[128,768]{1,0:T(8,128)(2,1)S(1)}, u32[]{:S(2)}, u32[]{:S(2)}) collective-permute-start(bf16[128,768]{1,0:T(8,128)(2,1)S(1)} %get-tuple-element.26), channel_id=1, source_target_pairs={{0,8},{4,12},{8,0},{12,4},{16,24},{20,28},{24,16},{28,20},{1,9},{5... | collective-permute-start | bytes 589832 | tf_op jit(solution)/shard_map/ppermute | solution.py:363
  16.8 0.5 %collective-permute-start.6 = (bf16[128,768]{1,0:T(8,128)(2,1)S(1)}, bf16[128,768]{1,0:T(8,128)(2,1)S(1)}, u32[]{:S(2)}, u32[]{:S(2)}) collective-permute-start(bf16[128,768]{1,0:T(8,128)(2,1)S(1)} %get-tuple-element.28.refs_4_.refs_5_), channel_id=1, source_target_pairs={{0,4},{4,0},{8,12},{12,8},{16,20},{20,16},{24,28},{28,24},{1,5},{5... | collective-permute-start | bytes 589832 | tf_op jit(solution)/shard_map/ppermute | solution.py:363
  17.3 2.4 %collective-permute-done.3.refs_1_ = bf16[16,768]{1,0:T(8,128)(2,1)S(1)} collective-permute-done((bf16[16,768]{1,0:T(8,128)(2,1)S(1)}, bf16[16,768]{1,0:T(8,128)(2,1)S(1)}, u32[]{:S(2)}, u32[]{:S(2)}) %collective-permute-start.3) | collective-permute-done | bytes 24608 | tf_op jit(solution)/shard_map/ppermute | solution.py:363
  19.7 0.0 copy-start.4
  19.7 0.0 collective-permute-done.2.refs_0_
  19.7 0.6 %copy-done.4 = bf16[16,768]{1,0:T(8,128)(2,1)} copy-done((bf16[16,768]{1,0:T(8,128)(2,1)}, bf16[16,768]{1,0:T(8,128)(2,1)S(1)}, u32[]{:S(2)}) %copy-start.4) | copy-done | bytes 24600
  20.3 0.0 copy-start.3
  20.3 0.7 %copy-done.3 = bf16[112,768]{1,0:T(8,128)(2,1)} copy-done((bf16[112,768]{1,0:T(8,128)(2,1)}, bf16[112,768]{1,0:T(8,128)(2,1)S(1)}, u32[]{:S(2)}) %copy-start.3) | copy-done | bytes 172056
  21.0 1.6 %join.1 = bf16[128,768]{1,0:T(8,128)(2,1)} custom-call(bf16[112,768]{1,0:T(8,128)(2,1)} %copy-done.3, bf16[16,768]{1,0:T(8,128)(2,1)} %copy-done.4), custom_call_target="tpu_custom_call" | custom-call | flops 1048576 | bytes 524288 | tf_op jit(solution)/shard_map/join/pallas_call | solution.py:337
  22.6 1.5 %collective-permute-start.4 = (bf16[128,768]{1,0:T(8,128)(2,1)}, bf16[128,768]{1,0:T(8,128)(2,1)S(1)}, u32[]{:S(2)}, u32[]{:S(2)}) collective-permute-start(bf16[128,768]{1,0:T(8,128)(2,1)} %join.1), channel_id=1, source_target_pairs={{0,8},{4,12},{8,0},{12,4},{16,24},{20,28},{24,16},{28,20},{1,9},{5... | collective-permute-start | bytes 589832 | tf_op jit(solution)/shard_map/ppermute | solution.py:363
  24.1 0.0 collective-permute-done.1
  24.1 0.0 collective-permute-done.5.refs_5_.refs_6_
  24.1 0.0 copy-done.2
  24.1 0.0 copy-start
  24.1 0.9 %copy-done = bf16[128,768]{1,0:T(8,128)(2,1)S(1)} copy-done((bf16[128,768]{1,0:T(8,128)(2,1)S(1)}, bf16[128,768]{1,0:T(8,128)(2,1)}, u32[]{:S(2)}) %copy-start) | copy-done | bytes 196632
  25.0 0.0 copy-start.1
  25.0 4.0 %cross.4 = (bf16[192,256]{1,0:T(8,128)(2,1)S(1)}, f32[192,768]{1,0:T(8,128)S(1)}) custom-call(bf16[1,128,768]{2,1,0:T(8,128)(2,1)S(1)} %bitcast.44, bf16[1,128,768]{2,1,0:T(8,128)(2,1)S(1)} %bitcast.46, bf16[1,128,768]{2,1,0:T(8,128)(2,1)S(1)} %bitcast.42, bf16[384,768]{1,0:T(8,128)(2,1)S(1)} %get-tuple-element.25.refs_1_.refs_3_.refs_4_, ...), custom_call_target="tpu_custom_call" | custom-call | flops 97600000 | bytes 1048576 | tf_op jit(solution)/shard_map/cross/pallas_call | solution.py:309
  29.0 0.0 collective-permute-done.6.refs_7_
  29.0 1.1 %collective-permute-done.4 = bf16[128,768]{1,0:T(8,128)(2,1)S(1)} collective-permute-done((bf16[128,768]{1,0:T(8,128)(2,1)}, bf16[128,768]{1,0:T(8,128)(2,1)S(1)}, u32[]{:S(2)}, u32[]{:S(2)}) %collective-permute-start.4) | collective-permute-done | bytes 196640 | tf_op jit(solution)/shard_map/ppermute | solution.py:363
  30.1 0.0 copy-done.1
  30.1 2.9 %cross.5 = (bf16[256,256]{1,0:T(8,128)(2,1)S(1)}, bf16[256,256]{1,0:T(8,128)(2,1)S(1)}) custom-call(bf16[1,128,768]{2,1,0:T(8,128)(2,1)S(1)} %bitcast.45, bf16[1,128,768]{2,1,0:T(8,128)(2,1)S(1)} %bitcast.47, bf16[1,128,768]{2,1,0:T(8,128)(2,1)S(1)} %bitcast.43, bf16[1,128,768]{2,1,0:T(8,128)(2,1)S(1)} %bitcast.49, ...), custom_call_target="tpu_custom_call" | custom-call | flops 64320000 | bytes 1048576 | tf_op jit(solution)/shard_map/cross/pallas_call | solution.py:309
  33.1 0.5 %collective-permute-start.7 = (bf16[4,1,4,16,256]{4,3,2,1,0:T(8,128)(2,1)S(1)}, bf16[4,1,4,16,256]{4,3,2,1,0:T(8,128)(2,1)S(1)}, u32[]{:S(2)}, u32[]{:S(2)}) collective-permute-start(bf16[4,1,4,16,256]{4,3,2,1,0:T(8,128)(2,1)S(1)} %pad_maximum_fusion), channel_id=1, source_target_pairs={{0,1},{1,0},{2,3},{3,2},{4,5},{5,4},{6,7},{7,6},{8,9},{9,8},{10,11... | collective-permute-start | bytes 393224 | tf_op jit(solution)/shard_map/ppermute | solution.py:423
  33.5 1.0 %collective-permute-done.7 = bf16[4,1,4,16,256]{4,3,2,1,0:T(8,128)(2,1)S(1)} collective-permute-done((bf16[4,1,4,16,256]{4,3,2,1,0:T(8,128)(2,1)S(1)}, bf16[4,1,4,16,256]{4,3,2,1,0:T(8,128)(2,1)S(1)}, u32[]{:S(2)}, u32[]{:S(2)}) %collective-permute-start.7) | collective-permute-done | bytes 131104 | tf_op jit(solution)/shard_map/ppermute | solution.py:423
  34.6 1.4 %collective-permute-start.10 = (bf16[1,4,16,256]{3,2,1,0:T(8,128)(2,1)S(1)}, bf16[1,4,16,256]{3,2,1,0:T(8,128)(2,1)S(1)}, u32[]{:S(2)}, u32[]{:S(2)}) collective-permute-start(bf16[1,4,16,256]{3,2,1,0:T(8,128)(2,1)S(1)} %get-tuple-element.38), channel_id=1, source_target_pairs={{0,6},{1,7},{2,4},{3,5},{4,2},{5,3},{6,0},{7,1},{8,14},{9,15},{10,... | collective-permute-start | bytes 98312 | tf_op jit(solution)/shard_map/ppermute | solution.py:436
  36.0 0.7 %collective-permute-start.8 = (bf16[1,4,16,256]{3,2,1,0:T(8,128)(2,1)S(1)}, bf16[1,4,16,256]{3,2,1,0:T(8,128)(2,1)S(1)}, u32[]{:S(2)}, u32[]{:S(2)}) collective-permute-start(bf16[1,4,16,256]{3,2,1,0:T(8,128)(2,1)S(1)} %get-tuple-element.37), channel_id=1, source_target_pairs={{0,2},{1,3},{2,0},{3,1},{4,6},{5,7},{6,4},{7,5},{8,10},{9,11},{10,... | collective-permute-start | bytes 98312 | tf_op jit(solution)/shard_map/ppermute | solution.py:436
  36.7 1.5 %collective-permute-start.9 = (bf16[1,4,16,256]{3,2,1,0:T(8,128)(2,1)S(1)}, bf16[1,4,16,256]{3,2,1,0:T(8,128)(2,1)S(1)}, u32[]{:S(2)}, u32[]{:S(2)}) collective-permute-start(bf16[1,4,16,256]{3,2,1,0:T(8,128)(2,1)S(1)} %get-tuple-element.39), channel_id=1, source_target_pairs={{0,4},{1,5},{2,6},{3,7},{4,0},{5,1},{6,2},{7,3},{8,12},{9,13},{10,... | collective-permute-start | bytes 98312 | tf_op jit(solution)/shard_map/ppermute | solution.py:436
  38.2 1.4 %collective-permute-done.10 = bf16[1,4,16,256]{3,2,1,0:T(8,128)(2,1)S(1)} collective-permute-done((bf16[1,4,16,256]{3,2,1,0:T(8,128)(2,1)S(1)}, bf16[1,4,16,256]{3,2,1,0:T(8,128)(2,1)S(1)}, u32[]{:S(2)}, u32[]{:S(2)}) %collective-permute-start.10) | collective-permute-done | bytes 32800 | tf_op jit(solution)/shard_map/ppermute | solution.py:436
  39.5 0.4 collective-permute-done.8
  39.9 0.7 %collective-permute-done.9 = bf16[1,4,16,256]{3,2,1,0:T(8,128)(2,1)S(1)} collective-permute-done((bf16[1,4,16,256]{3,2,1,0:T(8,128)(2,1)S(1)}, bf16[1,4,16,256]{3,2,1,0:T(8,128)(2,1)S(1)}, u32[]{:S(2)}, u32[]{:S(2)}) %collective-permute-start.9) | collective-permute-done | bytes 32800 | tf_op jit(solution)/shard_map/ppermute | solution.py:436
  40.6 0.7 %pad_maximum_fusion.1 = f32[1,2,4,16,256]{4,3,2,1,0:T(8,128)} fusion(f32[1,1,4,16,256]{4,3,2,1,0:T(8,128)S(1)} %get-tuple-element.34, f32[1,1,4,16,256]{4,3,2,1,0:T(8,128)S(1)} %get-tuple-element.33), kind=kLoop, calls=%fused_computation.2 | loop fusion | flops 32768 | bytes 262144 | tf_op jit(solution)/shard_map/stack | solution.py:442
  (5 shorter events, 0.1 us)
Async XLA Ops:
  4.2 19.9 %collective-permute-start.5 = (bf16[384,768]{1,0:T(8,128)(2,1)S(1)}, bf16[384,768]{1,0:T(8,128)(2,1)S(1)}, u32[]{:S(2)}, u32[]{:S(2)}) collective-permute-start(bf16[384,768]{1,0:T(8,128)(2,1)S(1)} %get-tuple-element.25.refs_1_.refs_3_.refs_4_), channel_id=1, source_target_pairs={{0,4},{4,0},{8,12},{12,8},{16,20},{20,16},{24,28},{28,24},{1,5},{5... | collective-permute-start | bytes 1769480 | tf_op jit(solution)/shard_map/ppermute | solution.py:363
  7.2 12.5 %collective-permute-start.2 = (bf16[112,768]{1,0:T(8,128)(2,1)S(1)}, bf16[112,768]{1,0:T(8,128)(2,1)S(1)}, u32[]{:S(2)}, u32[]{:S(2)}) collective-permute-start(bf16[112,768]{1,0:T(8,128)(2,1)S(1)} %get-tuple-element.24.refs_8_), channel_id=1, source_target_pairs={{0,16},{4,20},{8,24},{12,28},{16,0},{20,4},{24,8},{28,12},{1,17},{... | collective-permute-start | bytes 516104 | tf_op jit(solution)/shard_map/ppermute | solution.py:363
  9.8 3.1 %collective-permute-start = (bf16[16,2048]{1,0:T(8,128)(2,1)S(1)}, bf16[16,2048]{1,0:T(8,128)(2,1)S(1)}, u32[]{:S(2)}, u32[]{:S(2)}) collective-permute-start(bf16[16,2048]{1,0:T(8,128)(2,1)S(1)} %get-tuple-element.19), channel_id=1, source_target_pairs={{1,0},{2,1},{3,2},{5,4},{6,5},{7,6},{9,8},{10,9},{11,10},{13,12},{... | collective-permute-start | bytes 196616 | tf_op jit(solution)/shard_map/ppermute | solution.py:369
  12.9 11.1 %copy-start.2 = (bf16[768,256]{1,0:T(8,128)(2,1)S(1)}, bf16[768,256]{1,0:T(8,128)(2,1)}, u32[]{:S(2)}) copy-start(bf16[768,256]{1,0:T(8,128)(2,1)} %constant.81.clone.refs_7_.refs_10_) | copy-start | bytes 1179652
  14.8 4.9 %collective-permute-start.3 = (bf16[16,768]{1,0:T(8,128)(2,1)S(1)}, bf16[16,768]{1,0:T(8,128)(2,1)S(1)}, u32[]{:S(2)}, u32[]{:S(2)}) collective-permute-start(bf16[16,768]{1,0:T(8,128)(2,1)S(1)} %get-tuple-element.27), channel_id=1, source_target_pairs={{0,16},{4,20},{8,24},{12,28},{16,0},{20,4},{24,8},{28,12},{1,17},{... | collective-permute-start | bytes 73736 | tf_op jit(solution)/shard_map/ppermute | solution.py:363
  15.2 8.8 %collective-permute-start.1 = (bf16[128,768]{1,0:T(8,128)(2,1)S(1)}, bf16[128,768]{1,0:T(8,128)(2,1)S(1)}, u32[]{:S(2)}, u32[]{:S(2)}) collective-permute-start(bf16[128,768]{1,0:T(8,128)(2,1)S(1)} %get-tuple-element.26), channel_id=1, source_target_pairs={{0,8},{4,12},{8,0},{12,4},{16,24},{20,28},{24,16},{28,20},{1,9},{5... | collective-permute-start | bytes 589832 | tf_op jit(solution)/shard_map/ppermute | solution.py:363
  16.8 12.2 %collective-permute-start.6 = (bf16[128,768]{1,0:T(8,128)(2,1)S(1)}, bf16[128,768]{1,0:T(8,128)(2,1)S(1)}, u32[]{:S(2)}, u32[]{:S(2)}) collective-permute-start(bf16[128,768]{1,0:T(8,128)(2,1)S(1)} %get-tuple-element.28.refs_4_.refs_5_), channel_id=1, source_target_pairs={{0,4},{4,0},{8,12},{12,8},{16,20},{20,16},{24,28},{28,24},{1,5},{5... | collective-permute-start | bytes 589832 | tf_op jit(solution)/shard_map/ppermute | solution.py:363
  19.7 0.6 %copy-start.4 = (bf16[16,768]{1,0:T(8,128)(2,1)}, bf16[16,768]{1,0:T(8,128)(2,1)S(1)}, u32[]{:S(2)}) copy-start(bf16[16,768]{1,0:T(8,128)(2,1)S(1)} %collective-permute-done.3.refs_1_) | copy-start | bytes 73732
  20.3 0.7 %copy-start.3 = (bf16[112,768]{1,0:T(8,128)(2,1)}, bf16[112,768]{1,0:T(8,128)(2,1)S(1)}, u32[]{:S(2)}) copy-start(bf16[112,768]{1,0:T(8,128)(2,1)S(1)} %collective-permute-done.2.refs_0_) | copy-start | bytes 516100
  22.6 7.5 %collective-permute-start.4 = (bf16[128,768]{1,0:T(8,128)(2,1)}, bf16[128,768]{1,0:T(8,128)(2,1)S(1)}, u32[]{:S(2)}, u32[]{:S(2)}) collective-permute-start(bf16[128,768]{1,0:T(8,128)(2,1)} %join.1), channel_id=1, source_target_pairs={{0,8},{4,12},{8,0},{12,4},{16,24},{20,28},{24,16},{28,20},{1,9},{5... | collective-permute-start | bytes 589832 | tf_op jit(solution)/shard_map/ppermute | solution.py:363
  24.1 0.9 %copy-start = (bf16[128,768]{1,0:T(8,128)(2,1)S(1)}, bf16[128,768]{1,0:T(8,128)(2,1)}, u32[]{:S(2)}) copy-start(bf16[128,768]{1,0:T(8,128)(2,1)} %join.1) | copy-start | bytes 589828
  25.0 5.1 %copy-start.1 = (bf16[128,768]{1,0:T(8,128)(2,1)S(1)}, bf16[128,768]{1,0:T(8,128)(2,1)}, u32[]{:S(2)}) copy-start(bf16[128,768]{1,0:T(8,128)(2,1)} %join.1) | copy-start | bytes 589828
  33.1 1.5 %collective-permute-start.7 = (bf16[4,1,4,16,256]{4,3,2,1,0:T(8,128)(2,1)S(1)}, bf16[4,1,4,16,256]{4,3,2,1,0:T(8,128)(2,1)S(1)}, u32[]{:S(2)}, u32[]{:S(2)}) collective-permute-start(bf16[4,1,4,16,256]{4,3,2,1,0:T(8,128)(2,1)S(1)} %pad_maximum_fusion), channel_id=1, source_target_pairs={{0,1},{1,0},{2,3},{3,2},{4,5},{5,4},{6,7},{7,6},{8,9},{9,8},{10,11... | collective-permute-start | bytes 393224 | tf_op jit(solution)/shard_map/ppermute | solution.py:423
  34.6 4.9 %collective-permute-start.10 = (bf16[1,4,16,256]{3,2,1,0:T(8,128)(2,1)S(1)}, bf16[1,4,16,256]{3,2,1,0:T(8,128)(2,1)S(1)}, u32[]{:S(2)}, u32[]{:S(2)}) collective-permute-start(bf16[1,4,16,256]{3,2,1,0:T(8,128)(2,1)S(1)} %get-tuple-element.38), channel_id=1, source_target_pairs={{0,6},{1,7},{2,4},{3,5},{4,2},{5,3},{6,0},{7,1},{8,14},{9,15},{10,... | collective-permute-start | bytes 98312 | tf_op jit(solution)/shard_map/ppermute | solution.py:436
  36.0 3.9 %collective-permute-start.8 = (bf16[1,4,16,256]{3,2,1,0:T(8,128)(2,1)S(1)}, bf16[1,4,16,256]{3,2,1,0:T(8,128)(2,1)S(1)}, u32[]{:S(2)}, u32[]{:S(2)}) collective-permute-start(bf16[1,4,16,256]{3,2,1,0:T(8,128)(2,1)S(1)} %get-tuple-element.37), channel_id=1, source_target_pairs={{0,2},{1,3},{2,0},{3,1},{4,6},{5,7},{6,4},{7,5},{8,10},{9,11},{10,... | collective-permute-start | bytes 98312 | tf_op jit(solution)/shard_map/ppermute | solution.py:436
  36.7 3.9 %collective-permute-start.9 = (bf16[1,4,16,256]{3,2,1,0:T(8,128)(2,1)S(1)}, bf16[1,4,16,256]{3,2,1,0:T(8,128)(2,1)S(1)}, u32[]{:S(2)}, u32[]{:S(2)}) collective-permute-start(bf16[1,4,16,256]{3,2,1,0:T(8,128)(2,1)S(1)} %get-tuple-element.39), channel_id=1, source_target_pairs={{0,4},{1,5},{2,6},{3,7},{4,0},{5,1},{6,2},{7,3},{8,12},{9,13},{10,... | collective-permute-start | bytes 98312 | tf_op jit(solution)/shard_map/ppermute | solution.py:436

commit v11 on v10

--- a/solution.py
+++ b/solution.py
@@ -339,6 +339,7 @@
         out_shape=jax.ShapeDtypeStruct((rows, parts[0].shape[1]), parts[0].dtype),
         in_specs=[vmem] * len(parts),
         out_specs=vmem,
+        compiler_params=pltpu.CompilerParams(vmem_limit_bytes=4 << 20),
         cost_estimate=pl.CostEstimate(flops=1 << 20, bytes_accessed=1 << 19, transcendentals=0),
         name="join",
     )(*parts)

time: 41.5 us -> 38.4 us (0.925)
  local copies, waits for them, and re-layouts: 2.25 us -> 0.04 us
  Pallas kernels: 15.3 us -> 13.7 us
  waiting for transfers between devices: 7.97 us -> 8.76 us
    unnamed x10 -> x2, local copies, waits for them, and re-layouts: 2.21 us -> 0.01 us
    pallas_call x1, Pallas kernels: 1.6 us -> 0.01 us  [join_call(): pl.pallas_call(join_kernel, out_shape=jax.ShapeDtypeStruct((rows, parts[0...]
    ppermute x6, waiting for transfers between devices: 3.51 us -> 4.55 us  [trade(): return lax.ppermute(array, 'fibre', [(i, i ^ by) for i in range(n_fibre)])]
  transfers between devices with their start and end apart: 11 -> 11, of which waited for: 7 -> 8; matrix products, arithmetic and copies ran while one was open for 0% -> 0% of each run, Pallas kernels for 20% -> 17%
where the time goes in v11:
time: 38.4 us; the launch traced here: 38.2 us
  starting transfers between devices  14.8 us (39%)
  Pallas kernels  13.7 us (36%)
  waiting for transfers between devices  8.76 us (23%)
  other arithmetic  0.75 us (2%)
    ppermute x6, starting transfers between devices, trade(): return lax.ppermute(array, 'fibre', [(i, i ^ by) for i in range(n_fibre)])  9.64 us
    pallas_call x3, Pallas kernels, cross_call(): pl.pallas_call(functools.partial(cross_kernel, runs, kept, [len(some) for...  7.63 us
    pallas_call x2, Pallas kernels, spectra_call(): pl.pallas_call(functools.partial(spectra_kernel, first, count, late is no...  6.07 us
    ppermute x6, waiting for transfers between devices, trade(): return lax.ppermute(array, 'fibre', [(i, i ^ by) for i in range(n_fibre)])  4.55 us
    ppermute x3, starting transfers between devices, body(): mine = lax.ppermute(mine.astype(jnp.bfloat16), ('fibre', 'tm'), routes)  3.55 us
    ppermute x3, waiting for transfers between devices, body(): mine = lax.ppermute(mine.astype(jnp.bfloat16), ('fibre', 'tm'), routes)  2.11 us
    ppermute x1, starting transfers between devices, body(): halo = lax.ppermute(edge, 'tm', [(i, i - 1) for i in range(1, n_tm)])  1.28 us
    ppermute x1, waiting for transfers between devices, body(): halo = lax.ppermute(edge, 'tm', [(i, i - 1) for i in range(1, n_tm)])  1.06 us
  transfers between devices with their start and end apart: 11, of which 8 were waited for; matrix products, arithmetic and copies ran while one was open for 0% of the time, Pallas kernels for 17%

profile of v11, /device:TPU:0, one launch (start us, length us, event | category | flops | bytes accessed | tf_op | source)
XLA Modules:
  0.0 38.2 jit_solution(14990685601929180285)
XLA Ops:
  0.0 4.2 %spectra.2 = (bf16[384,768]{1,0:T(8,128)(2,1)S(1)}, bf16[64,768]{1,0:T(8,128)(2,1)S(1)}, bf16[112,768]{1,0:T(8,128)(2,1)S(1)}, bf16[16,2048]{1,0:T(8,128)(2,1)S(...) custom-call(s32[32]{0:T(128)} %refs_0_.3, s32[4]{0:T(128)} %refs_1_.3, ...), custom_call_target="tpu_custom_call" | custom-call | flops 43000000 | bytes 1048576 | tf_op jit(solution)/shard_map/spectra/pallas_call | solution.py:175
  4.2 3.0 %collective-permute-start.5 = (bf16[384,768]{1,0:T(8,128)(2,1)S(1)}, bf16[384,768]{1,0:T(8,128)(2,1)S(1)}, u32[]{:S(2)}, u32[]{:S(2)}) collective-permute-start(bf16[384,768]{1,0:T(8,128)(2,1)S(1)} %get-tuple-element.25.refs_1_.refs_3_.refs_4_), channel_id=1, source_target_pairs={{0,4},{4,0},{8,12},{12,8},{16,20},{20,16},{24,28},{28,24},{1,5},{5... | collective-permute-start | bytes 1769480 | tf_op jit(solution)/shard_map/ppermute | solution.py:364
  7.2 2.6 %collective-permute-start.2 = (bf16[112,768]{1,0:T(8,128)(2,1)S(1)}, bf16[112,768]{1,0:T(8,128)(2,1)S(1)}, u32[]{:S(2)}, u32[]{:S(2)}) collective-permute-start(bf16[112,768]{1,0:T(8,128)(2,1)S(1)} %get-tuple-element.24.refs_8_), channel_id=1, source_target_pairs={{0,16},{4,20},{8,24},{12,28},{16,0},{20,4},{24,8},{28,12},{1,17},{... | collective-permute-start | bytes 516104 | tf_op jit(solution)/shard_map/ppermute | solution.py:364
  9.8 1.3 %collective-permute-start = (bf16[16,2048]{1,0:T(8,128)(2,1)S(1)}, bf16[16,2048]{1,0:T(8,128)(2,1)S(1)}, u32[]{:S(2)}, u32[]{:S(2)}) collective-permute-start(bf16[16,2048]{1,0:T(8,128)(2,1)S(1)} %get-tuple-element.19), channel_id=1, source_target_pairs={{1,0},{2,1},{3,2},{5,4},{6,5},{7,6},{9,8},{10,9},{11,10},{13,12},{... | collective-permute-start | bytes 196616 | tf_op jit(solution)/shard_map/ppermute | solution.py:370
  11.1 0.8 %cross.3.refs_9_.refs_6_ = f32[64,768]{1,0:T(8,128)S(1)} custom-call(bf16[1,112,768]{2,1,0:T(8,128)(2,1)S(1)} %bitcast.48, bf16[384,768]{1,0:T(8,128)(2,1)S(1)} %get-tuple-element.25.refs_1_.refs_3_.refs_4_, bf16[64,768]{1,0:T(8,128)(2,1)S(1)} %get-tuple-element.23.refs_2_.refs_7_), custom_call_target="tpu_custom_call" | custom-call | flops 25920000 | bytes 1048576 | tf_op jit(solution)/shard_map/cross/pallas_call | solution.py:309
  11.9 1.1 %collective-permute-done.refs_3_ = bf16[16,2048]{1,0:T(8,128)(2,1)S(1)} collective-permute-done((bf16[16,2048]{1,0:T(8,128)(2,1)S(1)}, bf16[16,2048]{1,0:T(8,128)(2,1)S(1)}, u32[]{:S(2)}, u32[]{:S(2)}) %collective-permute-start) | collective-permute-done | bytes 65568 | tf_op jit(solution)/shard_map/ppermute | solution.py:370
  12.9 0.0 copy-start
  12.9 1.9 %spectra.3 = (bf16[128,768]{1,0:T(8,128)(2,1)S(1)}, bf16[16,768]{1,0:T(8,128)(2,1)S(1)}, bf16[128,768]{1,0:T(8,128)(2,1)S(1)}) custom-call(s32[32]{0:T(128)} %refs_0_.3, s32[4]{0:T(128)} %refs_1_.3, bf16[16,32768]{1,0:T(8,128)(2,1)} %refs_2_.3, bf16[16,2048]{1,0:T(8,128)(2,1)S(1)} %collective-permute-done.refs_3_, ...), custom_call_target="tpu_custom_call" | custom-call | flops 19000000 | bytes 1048576 | tf_op jit(solution)/shard_map/spectra/pallas_call | solution.py:175
  14.8 0.4 %collective-permute-start.3 = (bf16[16,768]{1,0:T(8,128)(2,1)S(1)}, bf16[16,768]{1,0:T(8,128)(2,1)S(1)}, u32[]{:S(2)}, u32[]{:S(2)}) collective-permute-start(bf16[16,768]{1,0:T(8,128)(2,1)S(1)} %get-tuple-element.27), channel_id=1, source_target_pairs={{0,16},{4,20},{8,24},{12,28},{16,0},{20,4},{24,8},{28,12},{1,17},{... | collective-permute-start | bytes 73736 | tf_op jit(solution)/shard_map/ppermute | solution.py:364
  15.2 1.6 %collective-permute-start.1 = (bf16[128,768]{1,0:T(8,128)(2,1)S(1)}, bf16[128,768]{1,0:T(8,128)(2,1)S(1)}, u32[]{:S(2)}, u32[]{:S(2)}) collective-permute-start(bf16[128,768]{1,0:T(8,128)(2,1)S(1)} %get-tuple-element.26), channel_id=1, source_target_pairs={{0,8},{4,12},{8,0},{12,4},{16,24},{20,28},{24,16},{28,20},{1,9},{5... | collective-permute-start | bytes 589832 | tf_op jit(solution)/shard_map/ppermute | solution.py:364
  16.8 0.5 %collective-permute-start.6 = (bf16[128,768]{1,0:T(8,128)(2,1)S(1)}, bf16[128,768]{1,0:T(8,128)(2,1)S(1)}, u32[]{:S(2)}, u32[]{:S(2)}) collective-permute-start(bf16[128,768]{1,0:T(8,128)(2,1)S(1)} %get-tuple-element.28.refs_4_.refs_5_), channel_id=1, source_target_pairs={{0,4},{4,0},{8,12},{12,8},{16,20},{20,16},{24,28},{28,24},{1,5},{5... | collective-permute-start | bytes 589832 | tf_op jit(solution)/shard_map/ppermute | solution.py:364
  17.3 2.4 %collective-permute-done.3.refs_1_ = bf16[16,768]{1,0:T(8,128)(2,1)S(1)} collective-permute-done((bf16[16,768]{1,0:T(8,128)(2,1)S(1)}, bf16[16,768]{1,0:T(8,128)(2,1)S(1)}, u32[]{:S(2)}, u32[]{:S(2)}) %collective-permute-start.3) | collective-permute-done | bytes 24608 | tf_op jit(solution)/shard_map/ppermute | solution.py:364
  19.7 0.0 collective-permute-done.2.refs_0_
  19.7 1.5 %collective-permute-start.4 = (bf16[128,768]{1,0:T(8,128)(2,1)S(1)}, bf16[128,768]{1,0:T(8,128)(2,1)S(1)}, u32[]{:S(2)}, u32[]{:S(2)}) collective-permute-start(bf16[128,768]{1,0:T(8,128)(2,1)S(1)} %join.1), channel_id=1, source_target_pairs={{0,8},{4,12},{8,0},{12,4},{16,24},{20,28},{24,16},{28,20},{1,9},{5... | collective-permute-start | bytes 589832 | tf_op jit(solution)/shard_map/ppermute | solution.py:364
  21.3 1.0 %collective-permute-done.1 = bf16[128,768]{1,0:T(8,128)(2,1)S(1)} collective-permute-done((bf16[128,768]{1,0:T(8,128)(2,1)S(1)}, bf16[128,768]{1,0:T(8,128)(2,1)S(1)}, u32[]{:S(2)}, u32[]{:S(2)}) %collective-permute-start.1) | collective-permute-done | bytes 196640 | tf_op jit(solution)/shard_map/ppermute | solution.py:364
  22.3 0.0 collective-permute-done.5.refs_5_.refs_6_
  22.3 0.0 copy-done
  22.3 4.0 %cross.4 = (bf16[192,256]{1,0:T(8,128)(2,1)S(1)}, f32[192,768]{1,0:T(8,128)S(1)}) custom-call(bf16[1,128,768]{2,1,0:T(8,128)(2,1)S(1)} %bitcast.44, bf16[1,128,768]{2,1,0:T(8,128)(2,1)S(1)} %bitcast.46, bf16[1,128,768]{2,1,0:T(8,128)(2,1)S(1)} %bitcast.42, bf16[384,768]{1,0:T(8,128)(2,1)S(1)} %get-tuple-element.25.refs_1_.refs_3_.refs_4_, ...), custom_call_target="tpu_custom_call" | custom-call | flops 97600000 | bytes 1048576 | tf_op jit(solution)/shard_map/cross/pallas_call | solution.py:309
  26.3 0.0 collective-permute-done.6.refs_7_
  26.3 1.1 %collective-permute-done.4 = bf16[128,768]{1,0:T(8,128)(2,1)S(1)} collective-permute-done((bf16[128,768]{1,0:T(8,128)(2,1)S(1)}, bf16[128,768]{1,0:T(8,128)(2,1)S(1)}, u32[]{:S(2)}, u32[]{:S(2)}) %collective-permute-start.4) | collective-permute-done | bytes 196640 | tf_op jit(solution)/shard_map/ppermute | solution.py:364
  27.4 2.9 %cross.5 = (bf16[256,256]{1,0:T(8,128)(2,1)S(1)}, bf16[256,256]{1,0:T(8,128)(2,1)S(1)}) custom-call(bf16[1,128,768]{2,1,0:T(8,128)(2,1)S(1)} %bitcast.45, bf16[1,128,768]{2,1,0:T(8,128)(2,1)S(1)} %bitcast.47, bf16[1,128,768]{2,1,0:T(8,128)(2,1)S(1)} %bitcast.43, bf16[1,128,768]{2,1,0:T(8,128)(2,1)S(1)} %bitcast.49, ...), custom_call_target="tpu_custom_call" | custom-call | flops 64320000 | bytes 1048576 | tf_op jit(solution)/shard_map/cross/pallas_call | solution.py:309
  30.4 0.4 collective-permute-start.7
  30.7 1.0 %collective-permute-done.7 = bf16[4,1,4,16,256]{4,3,2,1,0:T(8,128)(2,1)S(1)} collective-permute-done((bf16[4,1,4,16,256]{4,3,2,1,0:T(8,128)(2,1)S(1)}, bf16[4,1,4,16,256]{4,3,2,1,0:T(8,128)(2,1)S(1)}, u32[]{:S(2)}, u32[]{:S(2)}) %collective-permute-start.7) | collective-permute-done | bytes 131104 | tf_op jit(solution)/shard_map/ppermute | solution.py:424
  31.9 1.6 %collective-permute-start.10 = (bf16[1,4,16,256]{3,2,1,0:T(8,128)(2,1)S(1)}, bf16[1,4,16,256]{3,2,1,0:T(8,128)(2,1)S(1)}, u32[]{:S(2)}, u32[]{:S(2)}) collective-permute-start(bf16[1,4,16,256]{3,2,1,0:T(8,128)(2,1)S(1)} %get-tuple-element.38), channel_id=1, source_target_pairs={{0,6},{1,7},{2,4},{3,5},{4,2},{5,3},{6,0},{7,1},{8,14},{9,15},{10,... | collective-permute-start | bytes 98312 | tf_op jit(solution)/shard_map/ppermute | solution.py:437
  33.4 0.2 collective-permute-start.8
  33.6 1.8 %collective-permute-start.9 = (bf16[1,4,16,256]{3,2,1,0:T(8,128)(2,1)S(1)}, bf16[1,4,16,256]{3,2,1,0:T(8,128)(2,1)S(1)}, u32[]{:S(2)}, u32[]{:S(2)}) collective-permute-start(bf16[1,4,16,256]{3,2,1,0:T(8,128)(2,1)S(1)} %get-tuple-element.39), channel_id=1, source_target_pairs={{0,4},{1,5},{2,6},{3,7},{4,0},{5,1},{6,2},{7,3},{8,12},{9,13},{10,... | collective-permute-start | bytes 98312 | tf_op jit(solution)/shard_map/ppermute | solution.py:437
  35.4 1.4 %collective-permute-done.10 = bf16[1,4,16,256]{3,2,1,0:T(8,128)(2,1)S(1)} collective-permute-done((bf16[1,4,16,256]{3,2,1,0:T(8,128)(2,1)S(1)}, bf16[1,4,16,256]{3,2,1,0:T(8,128)(2,1)S(1)}, u32[]{:S(2)}, u32[]{:S(2)}) %collective-permute-start.10) | collective-permute-done | bytes 32800 | tf_op jit(solution)/shard_map/ppermute | solution.py:437
  36.8 0.6 %collective-permute-done.8 = bf16[1,4,16,256]{3,2,1,0:T(8,128)(2,1)S(1)} collective-permute-done((bf16[1,4,16,256]{3,2,1,0:T(8,128)(2,1)S(1)}, bf16[1,4,16,256]{3,2,1,0:T(8,128)(2,1)S(1)}, u32[]{:S(2)}, u32[]{:S(2)}) %collective-permute-start.8) | collective-permute-done | bytes 32800 | tf_op jit(solution)/shard_map/ppermute | solution.py:437
  37.4 0.2 collective-permute-done.9
  37.6 0.7 %pad_maximum_fusion.1 = f32[1,2,4,16,256]{4,3,2,1,0:T(8,128)} fusion(f32[1,1,4,16,256]{4,3,2,1,0:T(8,128)S(1)} %get-tuple-element.34, f32[1,1,4,16,256]{4,3,2,1,0:T(8,128)S(1)} %get-tuple-element.33), kind=kLoop, calls=%fused_computation.2 | loop fusion | flops 32768 | bytes 262144 | tf_op jit(solution)/shard_map/stack | solution.py:443
  (6 shorter events, 0.1 us)
Async XLA Ops:
  4.2 18.1 %collective-permute-start.5 = (bf16[384,768]{1,0:T(8,128)(2,1)S(1)}, bf16[384,768]{1,0:T(8,128)(2,1)S(1)}, u32[]{:S(2)}, u32[]{:S(2)}) collective-permute-start(bf16[384,768]{1,0:T(8,128)(2,1)S(1)} %get-tuple-element.25.refs_1_.refs_3_.refs_4_), channel_id=1, source_target_pairs={{0,4},{4,0},{8,12},{12,8},{16,20},{20,16},{24,28},{28,24},{1,5},{5... | collective-permute-start | bytes 1769480 | tf_op jit(solution)/shard_map/ppermute | solution.py:364
  7.2 12.5 %collective-permute-start.2 = (bf16[112,768]{1,0:T(8,128)(2,1)S(1)}, bf16[112,768]{1,0:T(8,128)(2,1)S(1)}, u32[]{:S(2)}, u32[]{:S(2)}) collective-permute-start(bf16[112,768]{1,0:T(8,128)(2,1)S(1)} %get-tuple-element.24.refs_8_), channel_id=1, source_target_pairs={{0,16},{4,20},{8,24},{12,28},{16,0},{20,4},{24,8},{28,12},{1,17},{... | collective-permute-start | bytes 516104 | tf_op jit(solution)/shard_map/ppermute | solution.py:364
  9.8 3.1 %collective-permute-start = (bf16[16,2048]{1,0:T(8,128)(2,1)S(1)}, bf16[16,2048]{1,0:T(8,128)(2,1)S(1)}, u32[]{:S(2)}, u32[]{:S(2)}) collective-permute-start(bf16[16,2048]{1,0:T(8,128)(2,1)S(1)} %get-tuple-element.19), channel_id=1, source_target_pairs={{1,0},{2,1},{3,2},{5,4},{6,5},{7,6},{9,8},{10,9},{11,10},{13,12},{... | collective-permute-start | bytes 196616 | tf_op jit(solution)/shard_map/ppermute | solution.py:370
  12.9 9.4 %copy-start = (bf16[768,256]{1,0:T(8,128)(2,1)S(1)}, bf16[768,256]{1,0:T(8,128)(2,1)}, u32[]{:S(2)}) copy-start(bf16[768,256]{1,0:T(8,128)(2,1)} %constant.81.clone.refs_7_.refs_10_) | copy-start | bytes 1179652
  14.8 4.9 %collective-permute-start.3 = (bf16[16,768]{1,0:T(8,128)(2,1)S(1)}, bf16[16,768]{1,0:T(8,128)(2,1)S(1)}, u32[]{:S(2)}, u32[]{:S(2)}) collective-permute-start(bf16[16,768]{1,0:T(8,128)(2,1)S(1)} %get-tuple-element.27), channel_id=1, source_target_pairs={{0,16},{4,20},{8,24},{12,28},{16,0},{20,4},{24,8},{28,12},{1,17},{... | collective-permute-start | bytes 73736 | tf_op jit(solution)/shard_map/ppermute | solution.py:364
  15.2 7.1 %collective-permute-start.1 = (bf16[128,768]{1,0:T(8,128)(2,1)S(1)}, bf16[128,768]{1,0:T(8,128)(2,1)S(1)}, u32[]{:S(2)}, u32[]{:S(2)}) collective-permute-start(bf16[128,768]{1,0:T(8,128)(2,1)S(1)} %get-tuple-element.26), channel_id=1, source_target_pairs={{0,8},{4,12},{8,0},{12,4},{16,24},{20,28},{24,16},{28,20},{1,9},{5... | collective-permute-start | bytes 589832 | tf_op jit(solution)/shard_map/ppermute | solution.py:364
  16.8 9.5 %collective-permute-start.6 = (bf16[128,768]{1,0:T(8,128)(2,1)S(1)}, bf16[128,768]{1,0:T(8,128)(2,1)S(1)}, u32[]{:S(2)}, u32[]{:S(2)}) collective-permute-start(bf16[128,768]{1,0:T(8,128)(2,1)S(1)} %get-tuple-element.28.refs_4_.refs_5_), channel_id=1, source_target_pairs={{0,4},{4,0},{8,12},{12,8},{16,20},{20,16},{24,28},{28,24},{1,5},{5... | collective-permute-start | bytes 589832 | tf_op jit(solution)/shard_map/ppermute | solution.py:364
  19.7 7.7 %collective-permute-start.4 = (bf16[128,768]{1,0:T(8,128)(2,1)S(1)}, bf16[128,768]{1,0:T(8,128)(2,1)S(1)}, u32[]{:S(2)}, u32[]{:S(2)}) collective-permute-start(bf16[128,768]{1,0:T(8,128)(2,1)S(1)} %join.1), channel_id=1, source_target_pairs={{0,8},{4,12},{8,0},{12,4},{16,24},{20,28},{24,16},{28,20},{1,9},{5... | collective-permute-start | bytes 589832 | tf_op jit(solution)/shard_map/ppermute | solution.py:364
  30.4 1.4 %collective-permute-start.7 = (bf16[4,1,4,16,256]{4,3,2,1,0:T(8,128)(2,1)S(1)}, bf16[4,1,4,16,256]{4,3,2,1,0:T(8,128)(2,1)S(1)}, u32[]{:S(2)}, u32[]{:S(2)}) collective-permute-start(bf16[4,1,4,16,256]{4,3,2,1,0:T(8,128)(2,1)S(1)} %pad_maximum_fusion), channel_id=1, source_target_pairs={{0,1},{1,0},{2,3},{3,2},{4,5},{5,4},{6,7},{7,6},{8,9},{9,8},{10,11... | collective-permute-start | bytes 393224 | tf_op jit(solution)/shard_map/ppermute | solution.py:424
  31.9 4.9 %collective-permute-start.10 = (bf16[1,4,16,256]{3,2,1,0:T(8,128)(2,1)S(1)}, bf16[1,4,16,256]{3,2,1,0:T(8,128)(2,1)S(1)}, u32[]{:S(2)}, u32[]{:S(2)}) collective-permute-start(bf16[1,4,16,256]{3,2,1,0:T(8,128)(2,1)S(1)} %get-tuple-element.38), channel_id=1, source_target_pairs={{0,6},{1,7},{2,4},{3,5},{4,2},{5,3},{6,0},{7,1},{8,14},{9,15},{10,... | collective-permute-start | bytes 98312 | tf_op jit(solution)/shard_map/ppermute | solution.py:437
  33.4 3.9 %collective-permute-start.8 = (bf16[1,4,16,256]{3,2,1,0:T(8,128)(2,1)S(1)}, bf16[1,4,16,256]{3,2,1,0:T(8,128)(2,1)S(1)}, u32[]{:S(2)}, u32[]{:S(2)}) collective-permute-start(bf16[1,4,16,256]{3,2,1,0:T(8,128)(2,1)S(1)} %get-tuple-element.37), channel_id=1, source_target_pairs={{0,2},{1,3},{2,0},{3,1},{4,6},{5,7},{6,4},{7,5},{8,10},{9,11},{10,... | collective-permute-start | bytes 98312 | tf_op jit(solution)/shard_map/ppermute | solution.py:437
  33.6 3.9 %collective-permute-start.9 = (bf16[1,4,16,256]{3,2,1,0:T(8,128)(2,1)S(1)}, bf16[1,4,16,256]{3,2,1,0:T(8,128)(2,1)S(1)}, u32[]{:S(2)}, u32[]{:S(2)}) collective-permute-start(bf16[1,4,16,256]{3,2,1,0:T(8,128)(2,1)S(1)} %get-tuple-element.39), channel_id=1, source_target_pairs={{0,4},{1,5},{2,6},{3,7},{4,0},{5,1},{6,2},{7,3},{8,12},{9,13},{10,... | collective-permute-start | bytes 98312 | tf_op jit(solution)/shard_map/ppermute | solution.py:437

commit v12 on v11

--- a/solution.py
+++ b/solution.py
@@ -269,12 +269,12 @@
         lags = jnp.dot(refs[1][...], tables[0][...], preferred_element_type=jnp.float32)
         lags = (lags * scale).astype(jnp.bfloat16)
         unit = n_src * c_dev
-        start = 0
+        start, done = 0, list(done)
         for out, pieces in zip(outputs, outs):
             at = 0
             for piece in pieces or ():
                 if isinstance(piece, str):
-                    part = done[0][...]
+                    part = done.pop(0)[...]
                 else:
                     part = lags[start * unit : (start + piece) * unit]
                     start += piece
@@ -294,7 +294,7 @@
         if isinstance(out, int):
             shapes.append(jax.ShapeDtypeStruct((out * unit, 2 * NB), jnp.float32))
         else:
-            rows = sum(done[0].shape[0] if isinstance(p, str) else p * unit for p in out)
+            rows = sum(unit if isinstance(p, str) else p * unit for p in out)
             shapes.append(jax.ShapeDtypeStruct((grid * rows, LAGS), jnp.bfloat16))
     out_specs = [whole] * len(shapes)
     if grid > 1:
@@ -386,24 +386,28 @@
         by_1 = trade(src, 2)
         by_3 = trade(by_2, 2)
         srcs = [part[None] for part in (src, by_1, by_2, by_3)]
+        mine = functools.partial(cross, recs=[rec_a, rec_b, far_a], ltab=ltab)
         swapped = [(2, 0, 0, head)]
         runs = [
             (0, 1, [(1, head, early, n_win)], (0, 0), None),
-            (1, 2, own, None, None),
-            (0, 1, swapped, None, (1, 0)),
-            (1, 2, swapped, None, (1, 1)),
+            (1, 1, own, None, None),
+            (0, 1, swapped, None, (2, 0)),
+            (1, 1, swapped, None, (2, 1)),
         ]
-        near, sums = cross(srcs[:3], [rec_a, rec_b, far_a], runs, [[1, 2], 3], befores=begun, ltab=ltab)
+        near_0, near_2, sums = mine([srcs[0], srcs[2]], runs=runs, outs=[[1], [1], 2], befores=begun)
+        runs = [(0, 1, own, None, None), (0, 1, swapped, None, (1, 0))]
+        near_1, sums_1 = mine(srcs[1:2], runs=runs, outs=[[1], 1], after=[sums])
         swapped = [(3, head, head, n_win)]
         runs = [
             (0, 1, swapped, (0, 0), None),
-            (1, 2, swapped, (0, 1), None),
+            (1, 1, swapped, (1, 0), None),
+            (2, 1, swapped, (0, 1), None),
             (3, 1, [(2, 0, 0, head)] + swapped, None, None),
             (3, 1, own, None, None),
         ]
         far, near = cross(
-            srcs, [rec_a, rec_b, far_a, far_b], runs, [[1, 2, 1], ["done", 1]],
-            befores=[sums], done=[near], ltab=ltab,
+            srcs, [rec_a, rec_b, far_a, far_b], runs, [[1, 1, 1, 1], ["done"] * 3 + [1]],
+            befores=[sums, sums_1], done=[near_0, near_1, near_2], ltab=ltab,
         )
     else:
         ranks = [[2 * j + p for j in range(n_group)] for p in range(2)]

time: 38.4 us -> 38.5 us (level)
  Pallas kernels: 13.7 us -> 14.2 us
    pallas_call x3 -> x4, Pallas kernels: 7.63 us -> 8.11 us  [cross_call(): pl.pallas_call(functools.partial(cross_kernel, runs, kept, [len(some) for...]
    ppermute x6, waiting for transfers between devices: 4.55 us -> 4.14 us  [trade(): return lax.ppermute(array, 'fibre', [(i, i ^ by) for i in range(n_fibre)])]
  transfers between devices with their start and end apart: 11 -> 11, of which waited for: 8 -> 7; matrix products, arithmetic and copies ran while one was open for 0% -> 0% of each run, Pallas kernels for 17% -> 18%
where the time goes in v12:
time: 38.5 us; the launch traced here: 38.3 us
  starting transfers between devices  14.7 us (38%)
  Pallas kernels  14.2 us (37%)
  waiting for transfers between devices  8.52 us (22%)
  other arithmetic  0.75 us (2%)
    ppermute x6, starting transfers between devices, trade(): return lax.ppermute(array, 'fibre', [(i, i ^ by) for i in range(n_fibre)])  9.63 us
    pallas_call x4, Pallas kernels, cross_call(): pl.pallas_call(functools.partial(cross_kernel, runs, kept, [len(some) for...  8.11 us
    pallas_call x2, Pallas kernels, spectra_call(): pl.pallas_call(functools.partial(spectra_kernel, first, count, late is no...  6.07 us
    ppermute x6, waiting for transfers between devices, trade(): return lax.ppermute(array, 'fibre', [(i, i ^ by) for i in range(n_fibre)])  4.14 us
    ppermute x3, starting transfers between devices, body(): mine = lax.ppermute(mine.astype(jnp.bfloat16), ('fibre', 'tm'), routes)  3.55 us
    ppermute x3, waiting for transfers between devices, body(): mine = lax.ppermute(mine.astype(jnp.bfloat16), ('fibre', 'tm'), routes)  2.1 us
    ppermute x1, starting transfers between devices, body(): halo = lax.ppermute(edge, 'tm', [(i, i - 1) for i in range(1, n_tm)])  1.28 us
    ppermute x1, waiting for transfers between devices, body(): got = lax.ppermute(give, 'tm', [(i, i ^ 1) for i in range(n_tm)])  1.22 us
  transfers between devices with their start and end apart: 11, of which 7 were waited for; matrix products, arithmetic and copies ran while one was open for 0% of the time, Pallas kernels for 18%

profile of v12, /device:TPU:0, one launch (start us, length us, event | category | flops | bytes accessed | tf_op | source)
XLA Modules:
  0.0 38.3 jit_solution(9348229282049315647)
XLA Ops:
  0.0 4.2 %spectra.2 = (bf16[384,768]{1,0:T(8,128)(2,1)S(1)}, bf16[64,768]{1,0:T(8,128)(2,1)S(1)}, bf16[112,768]{1,0:T(8,128)(2,1)S(1)}, bf16[16,2048]{1,0:T(8,128)(2,1)S(...) custom-call(s32[32]{0:T(128)} %refs_0_.3, s32[4]{0:T(128)} %refs_1_.3, ...), custom_call_target="tpu_custom_call" | custom-call | flops 43000000 | bytes 1048576 | tf_op jit(solution)/shard_map/spectra/pallas_call | solution.py:175
  4.2 3.0 %collective-permute-start.5 = (bf16[384,768]{1,0:T(8,128)(2,1)S(1)}, bf16[384,768]{1,0:T(8,128)(2,1)S(1)}, u32[]{:S(2)}, u32[]{:S(2)}) collective-permute-start(bf16[384,768]{1,0:T(8,128)(2,1)S(1)} %get-tuple-element.28.refs_1_.refs_2_.refs_4_), channel_id=1, source_target_pairs={{0,4},{4,0},{8,12},{12,8},{16,20},{20,16},{24,28},{28,24},{1,5},{5... | collective-permute-start | bytes 1769480 | tf_op jit(solution)/shard_map/ppermute | solution.py:364
  7.2 2.6 %collective-permute-start.2 = (bf16[112,768]{1,0:T(8,128)(2,1)S(1)}, bf16[112,768]{1,0:T(8,128)(2,1)S(1)}, u32[]{:S(2)}, u32[]{:S(2)}) collective-permute-start(bf16[112,768]{1,0:T(8,128)(2,1)S(1)} %get-tuple-element.27.refs_8_), channel_id=1, source_target_pairs={{0,16},{4,20},{8,24},{12,28},{16,0},{20,4},{24,8},{28,12},{1,17},{... | collective-permute-start | bytes 516104 | tf_op jit(solution)/shard_map/ppermute | solution.py:364
  9.8 1.3 %collective-permute-start = (bf16[16,2048]{1,0:T(8,128)(2,1)S(1)}, bf16[16,2048]{1,0:T(8,128)(2,1)S(1)}, u32[]{:S(2)}, u32[]{:S(2)}) collective-permute-start(bf16[16,2048]{1,0:T(8,128)(2,1)S(1)} %get-tuple-element.22), channel_id=1, source_target_pairs={{1,0},{2,1},{3,2},{5,4},{6,5},{7,6},{9,8},{10,9},{11,10},{13,12},{... | collective-permute-start | bytes 196616 | tf_op jit(solution)/shard_map/ppermute | solution.py:370
  11.1 0.8 %cross.4.refs_9_.refs_5_ = f32[64,768]{1,0:T(8,128)S(1)} custom-call(bf16[1,112,768]{2,1,0:T(8,128)(2,1)S(1)} %bitcast.48, bf16[384,768]{1,0:T(8,128)(2,1)S(1)} %get-tuple-element.28.refs_1_.refs_2_.refs_4_, bf16[64,768]{1,0:T(8,128)(2,1)S(1)} %get-tuple-element.26.refs_2_.refs_7_), custom_call_target="tpu_custom_call" | custom-call | flops 25920000 | bytes 1048576 | tf_op jit(solution)/shard_map/cross/pallas_call | solution.py:309
  11.9 1.1 %collective-permute-done.refs_3_ = bf16[16,2048]{1,0:T(8,128)(2,1)S(1)} collective-permute-done((bf16[16,2048]{1,0:T(8,128)(2,1)S(1)}, bf16[16,2048]{1,0:T(8,128)(2,1)S(1)}, u32[]{:S(2)}, u32[]{:S(2)}) %collective-permute-start) | collective-permute-done | bytes 65568 | tf_op jit(solution)/shard_map/ppermute | solution.py:370
  12.9 0.0 copy-start
  12.9 1.9 %spectra.3 = (bf16[128,768]{1,0:T(8,128)(2,1)S(1)}, bf16[16,768]{1,0:T(8,128)(2,1)S(1)}, bf16[128,768]{1,0:T(8,128)(2,1)S(1)}) custom-call(s32[32]{0:T(128)} %refs_0_.3, s32[4]{0:T(128)} %refs_1_.3, bf16[16,32768]{1,0:T(8,128)(2,1)} %refs_2_.3, bf16[16,2048]{1,0:T(8,128)(2,1)S(1)} %collective-permute-done.refs_3_, ...), custom_call_target="tpu_custom_call" | custom-call | flops 19000000 | bytes 1048576 | tf_op jit(solution)/shard_map/spectra/pallas_call | solution.py:175
  14.8 0.4 %collective-permute-start.3 = (bf16[16,768]{1,0:T(8,128)(2,1)S(1)}, bf16[16,768]{1,0:T(8,128)(2,1)S(1)}, u32[]{:S(2)}, u32[]{:S(2)}) collective-permute-start(bf16[16,768]{1,0:T(8,128)(2,1)S(1)} %get-tuple-element.30), channel_id=1, source_target_pairs={{0,16},{4,20},{8,24},{12,28},{16,0},{20,4},{24,8},{28,12},{1,17},{... | collective-permute-start | bytes 73736 | tf_op jit(solution)/shard_map/ppermute | solution.py:364
  15.2 1.6 %collective-permute-start.1 = (bf16[128,768]{1,0:T(8,128)(2,1)S(1)}, bf16[128,768]{1,0:T(8,128)(2,1)S(1)}, u32[]{:S(2)}, u32[]{:S(2)}) collective-permute-start(bf16[128,768]{1,0:T(8,128)(2,1)S(1)} %get-tuple-element.29), channel_id=1, source_target_pairs={{0,8},{4,12},{8,0},{12,4},{16,24},{20,28},{24,16},{28,20},{1,9},{5... | collective-permute-start | bytes 589832 | tf_op jit(solution)/shard_map/ppermute | solution.py:364
  16.8 0.5 %collective-permute-start.6 = (bf16[128,768]{1,0:T(8,128)(2,1)S(1)}, bf16[128,768]{1,0:T(8,128)(2,1)S(1)}, u32[]{:S(2)}, u32[]{:S(2)}) collective-permute-start(bf16[128,768]{1,0:T(8,128)(2,1)S(1)} %get-tuple-element.31.refs_3_.refs_2_.refs_5_), channel_id=1, source_target_pairs={{0,4},{4,0},{8,12},{12,8},{16,20},{20,16},{24,28},{28,24},{1,5},{5... | collective-permute-start | bytes 589832 | tf_op jit(solution)/shard_map/ppermute | solution.py:364
  17.3 2.4 %collective-permute-done.3.refs_1_ = bf16[16,768]{1,0:T(8,128)(2,1)S(1)} collective-permute-done((bf16[16,768]{1,0:T(8,128)(2,1)S(1)}, bf16[16,768]{1,0:T(8,128)(2,1)S(1)}, u32[]{:S(2)}, u32[]{:S(2)}) %collective-permute-start.3) | collective-permute-done | bytes 24608 | tf_op jit(solution)/shard_map/ppermute | solution.py:364
  19.7 0.0 collective-permute-done.2.refs_0_
  19.7 1.5 %collective-permute-start.4 = (bf16[128,768]{1,0:T(8,128)(2,1)S(1)}, bf16[128,768]{1,0:T(8,128)(2,1)S(1)}, u32[]{:S(2)}, u32[]{:S(2)}) collective-permute-start(bf16[128,768]{1,0:T(8,128)(2,1)S(1)} %join.1), channel_id=1, source_target_pairs={{0,8},{4,12},{8,0},{12,4},{16,24},{20,28},{24,16},{28,20},{1,9},{5... | collective-permute-start | bytes 589832 | tf_op jit(solution)/shard_map/ppermute | solution.py:364
  21.3 0.0 collective-permute-done.5.refs_4_.refs_3_.refs_6_
  21.3 0.0 copy-done
  21.3 2.6 %cross.5 = (bf16[64,256]{1,0:T(8,128)(2,1)S(1)}, bf16[64,256]{1,0:T(8,128)(2,1)S(1)}, f32[128,768]{1,0:T(8,128)S(1)}) custom-call(bf16[1,128,768]{2,1,0:T(8,128)(2,1)S(1)} %bitcast.44, bf16[1,128,768]{2,1,0:T(8,128)(2,1)S(1)} %bitcast.42, bf16[384,768]{1,0:T(8,128)(2,1)S(1)} %get-tuple-element.28.refs_1_.refs_2_.refs_4_, ...), custom_call_target="tpu_custom_call" | custom-call | flops 61760000 | bytes 1048576 | tf_op jit(solution)/shard_map/cross/pallas_call | solution.py:309
  23.9 0.0 collective-permute-done.1
  23.9 1.8 %cross.6 = (bf16[64,256]{1,0:T(8,128)(2,1)S(1)}, f32[64,768]{1,0:T(8,128)S(1)}) custom-call(bf16[1,128,768]{2,1,0:T(8,128)(2,1)S(1)} %bitcast.46, bf16[384,768]{1,0:T(8,128)(2,1)S(1)} %get-tuple-element.28.refs_1_.refs_2_.refs_4_, bf16[128,768]{1,0:T(8,128)(2,1)S(1)} %get-tuple-element.31.refs_3_.refs_2_.refs_5_, ...), custom_call_target="tpu_custom_call" | custom-call | flops 43840000 | bytes 1048576 | tf_op jit(solution)/shard_map/cross/pallas_call | solution.py:309
  25.7 0.0 collective-permute-done.6.refs_7_
  25.7 1.7 %collective-permute-done.4 = bf16[128,768]{1,0:T(8,128)(2,1)S(1)} collective-permute-done((bf16[128,768]{1,0:T(8,128)(2,1)S(1)}, bf16[128,768]{1,0:T(8,128)(2,1)S(1)}, u32[]{:S(2)}, u32[]{:S(2)}) %collective-permute-start.4) | collective-permute-done | bytes 196640 | tf_op jit(solution)/shard_map/ppermute | solution.py:364
  27.4 3.0 %cross.7 = (bf16[256,256]{1,0:T(8,128)(2,1)S(1)}, bf16[256,256]{1,0:T(8,128)(2,1)S(1)}) custom-call(bf16[1,128,768]{2,1,0:T(8,128)(2,1)S(1)} %bitcast.45, bf16[1,128,768]{2,1,0:T(8,128)(2,1)S(1)} %bitcast.47, bf16[1,128,768]{2,1,0:T(8,128)(2,1)S(1)} %bitcast.43, bf16[1,128,768]{2,1,0:T(8,128)(2,1)S(1)} %bitcast.49, ...), custom_call_target="tpu_custom_call" | custom-call | flops 64320000 | bytes 1048576 | tf_op jit(solution)/shard_map/cross/pallas_call | solution.py:309
  30.5 0.2 collective-permute-start.7
  30.6 1.2 %collective-permute-done.7 = bf16[4,1,4,16,256]{4,3,2,1,0:T(8,128)(2,1)S(1)} collective-permute-done((bf16[4,1,4,16,256]{4,3,2,1,0:T(8,128)(2,1)S(1)}, bf16[4,1,4,16,256]{4,3,2,1,0:T(8,128)(2,1)S(1)}, u32[]{:S(2)}, u32[]{:S(2)}) %collective-permute-start.7) | collective-permute-done | bytes 131104 | tf_op jit(solution)/shard_map/ppermute | solution.py:428
  31.9 1.4 %collective-permute-start.10 = (bf16[1,4,16,256]{3,2,1,0:T(8,128)(2,1)S(1)}, bf16[1,4,16,256]{3,2,1,0:T(8,128)(2,1)S(1)}, u32[]{:S(2)}, u32[]{:S(2)}) collective-permute-start(bf16[1,4,16,256]{3,2,1,0:T(8,128)(2,1)S(1)} %get-tuple-element.44), channel_id=1, source_target_pairs={{0,6},{1,7},{2,4},{3,5},{4,2},{5,3},{6,0},{7,1},{8,14},{9,15},{10,... | collective-permute-start | bytes 98312 | tf_op jit(solution)/shard_map/ppermute | solution.py:441
  33.4 0.3 collective-permute-start.8
  33.7 1.8 %collective-permute-start.9 = (bf16[1,4,16,256]{3,2,1,0:T(8,128)(2,1)S(1)}, bf16[1,4,16,256]{3,2,1,0:T(8,128)(2,1)S(1)}, u32[]{:S(2)}, u32[]{:S(2)}) collective-permute-start(bf16[1,4,16,256]{3,2,1,0:T(8,128)(2,1)S(1)} %get-tuple-element.45), channel_id=1, source_target_pairs={{0,4},{1,5},{2,6},{3,7},{4,0},{5,1},{6,2},{7,3},{8,12},{9,13},{10,... | collective-permute-start | bytes 98312 | tf_op jit(solution)/shard_map/ppermute | solution.py:441
  35.5 1.3 %collective-permute-done.10 = bf16[1,4,16,256]{3,2,1,0:T(8,128)(2,1)S(1)} collective-permute-done((bf16[1,4,16,256]{3,2,1,0:T(8,128)(2,1)S(1)}, bf16[1,4,16,256]{3,2,1,0:T(8,128)(2,1)S(1)}, u32[]{:S(2)}, u32[]{:S(2)}) %collective-permute-start.10) | collective-permute-done | bytes 32800 | tf_op jit(solution)/shard_map/ppermute | solution.py:441
  36.8 0.5 %collective-permute-done.8 = bf16[1,4,16,256]{3,2,1,0:T(8,128)(2,1)S(1)} collective-permute-done((bf16[1,4,16,256]{3,2,1,0:T(8,128)(2,1)S(1)}, bf16[1,4,16,256]{3,2,1,0:T(8,128)(2,1)S(1)}, u32[]{:S(2)}, u32[]{:S(2)}) %collective-permute-start.8) | collective-permute-done | bytes 32800 | tf_op jit(solution)/shard_map/ppermute | solution.py:441
  37.3 0.3 collective-permute-done.9
  37.6 0.7 %pad_maximum_fusion.1 = f32[1,2,4,16,256]{4,3,2,1,0:T(8,128)} fusion(f32[1,1,4,16,256]{4,3,2,1,0:T(8,128)S(1)} %get-tuple-element.40, f32[1,1,4,16,256]{4,3,2,1,0:T(8,128)S(1)} %get-tuple-element.39), kind=kLoop, calls=%fused_computation.2 | loop fusion | flops 32768 | bytes 262144 | tf_op jit(solution)/shard_map/stack | solution.py:447
  (6 shorter events, 0.1 us)
Async XLA Ops:
  4.2 17.1 %collective-permute-start.5 = (bf16[384,768]{1,0:T(8,128)(2,1)S(1)}, bf16[384,768]{1,0:T(8,128)(2,1)S(1)}, u32[]{:S(2)}, u32[]{:S(2)}) collective-permute-start(bf16[384,768]{1,0:T(8,128)(2,1)S(1)} %get-tuple-element.28.refs_1_.refs_2_.refs_4_), channel_id=1, source_target_pairs={{0,4},{4,0},{8,12},{12,8},{16,20},{20,16},{24,28},{28,24},{1,5},{5... | collective-permute-start | bytes 1769480 | tf_op jit(solution)/shard_map/ppermute | solution.py:364
  7.2 12.5 %collective-permute-start.2 = (bf16[112,768]{1,0:T(8,128)(2,1)S(1)}, bf16[112,768]{1,0:T(8,128)(2,1)S(1)}, u32[]{:S(2)}, u32[]{:S(2)}) collective-permute-start(bf16[112,768]{1,0:T(8,128)(2,1)S(1)} %get-tuple-element.27.refs_8_), channel_id=1, source_target_pairs={{0,16},{4,20},{8,24},{12,28},{16,0},{20,4},{24,8},{28,12},{1,17},{... | collective-permute-start | bytes 516104 | tf_op jit(solution)/shard_map/ppermute | solution.py:364
  9.8 3.1 %collective-permute-start = (bf16[16,2048]{1,0:T(8,128)(2,1)S(1)}, bf16[16,2048]{1,0:T(8,128)(2,1)S(1)}, u32[]{:S(2)}, u32[]{:S(2)}) collective-permute-start(bf16[16,2048]{1,0:T(8,128)(2,1)S(1)} %get-tuple-element.22), channel_id=1, source_target_pairs={{1,0},{2,1},{3,2},{5,4},{6,5},{7,6},{9,8},{10,9},{11,10},{13,12},{... | collective-permute-start | bytes 196616 | tf_op jit(solution)/shard_map/ppermute | solution.py:370
  12.9 8.3 %copy-start = (bf16[768,256]{1,0:T(8,128)(2,1)S(1)}, bf16[768,256]{1,0:T(8,128)(2,1)}, u32[]{:S(2)}) copy-start(bf16[768,256]{1,0:T(8,128)(2,1)} %constant.81.clone.refs_6_.refs_4_.refs_13_) | copy-start | bytes 1179652
  14.8 4.9 %collective-permute-start.3 = (bf16[16,768]{1,0:T(8,128)(2,1)S(1)}, bf16[16,768]{1,0:T(8,128)(2,1)S(1)}, u32[]{:S(2)}, u32[]{:S(2)}) collective-permute-start(bf16[16,768]{1,0:T(8,128)(2,1)S(1)} %get-tuple-element.30), channel_id=1, source_target_pairs={{0,16},{4,20},{8,24},{12,28},{16,0},{20,4},{24,8},{28,12},{1,17},{... | collective-permute-start | bytes 73736 | tf_op jit(solution)/shard_map/ppermute | solution.py:364
  15.2 8.7 %collective-permute-start.1 = (bf16[128,768]{1,0:T(8,128)(2,1)S(1)}, bf16[128,768]{1,0:T(8,128)(2,1)S(1)}, u32[]{:S(2)}, u32[]{:S(2)}) collective-permute-start(bf16[128,768]{1,0:T(8,128)(2,1)S(1)} %get-tuple-element.29), channel_id=1, source_target_pairs={{0,8},{4,12},{8,0},{12,4},{16,24},{20,28},{24,16},{28,20},{1,9},{5... | collective-permute-start | bytes 589832 | tf_op jit(solution)/shard_map/ppermute | solution.py:364
  16.8 8.9 %collective-permute-start.6 = (bf16[128,768]{1,0:T(8,128)(2,1)S(1)}, bf16[128,768]{1,0:T(8,128)(2,1)S(1)}, u32[]{:S(2)}, u32[]{:S(2)}) collective-permute-start(bf16[128,768]{1,0:T(8,128)(2,1)S(1)} %get-tuple-element.31.refs_3_.refs_2_.refs_5_), channel_id=1, source_target_pairs={{0,4},{4,0},{8,12},{12,8},{16,20},{20,16},{24,28},{28,24},{1,5},{5... | collective-permute-start | bytes 589832 | tf_op jit(solution)/shard_map/ppermute | solution.py:364
  19.7 7.7 %collective-permute-start.4 = (bf16[128,768]{1,0:T(8,128)(2,1)S(1)}, bf16[128,768]{1,0:T(8,128)(2,1)S(1)}, u32[]{:S(2)}, u32[]{:S(2)}) collective-permute-start(bf16[128,768]{1,0:T(8,128)(2,1)S(1)} %join.1), channel_id=1, source_target_pairs={{0,8},{4,12},{8,0},{12,4},{16,24},{20,28},{24,16},{28,20},{1,9},{5... | collective-permute-start | bytes 589832 | tf_op jit(solution)/shard_map/ppermute | solution.py:364
  30.5 1.4 %collective-permute-start.7 = (bf16[4,1,4,16,256]{4,3,2,1,0:T(8,128)(2,1)S(1)}, bf16[4,1,4,16,256]{4,3,2,1,0:T(8,128)(2,1)S(1)}, u32[]{:S(2)}, u32[]{:S(2)}) collective-permute-start(bf16[4,1,4,16,256]{4,3,2,1,0:T(8,128)(2,1)S(1)} %pad_maximum_fusion), channel_id=1, source_target_pairs={{0,1},{1,0},{2,3},{3,2},{4,5},{5,4},{6,7},{7,6},{8,9},{9,8},{10,11... | collective-permute-start | bytes 393224 | tf_op jit(solution)/shard_map/ppermute | solution.py:428
  31.9 4.9 %collective-permute-start.10 = (bf16[1,4,16,256]{3,2,1,0:T(8,128)(2,1)S(1)}, bf16[1,4,16,256]{3,2,1,0:T(8,128)(2,1)S(1)}, u32[]{:S(2)}, u32[]{:S(2)}) collective-permute-start(bf16[1,4,16,256]{3,2,1,0:T(8,128)(2,1)S(1)} %get-tuple-element.44), channel_id=1, source_target_pairs={{0,6},{1,7},{2,4},{3,5},{4,2},{5,3},{6,0},{7,1},{8,14},{9,15},{10,... | collective-permute-start | bytes 98312 | tf_op jit(solution)/shard_map/ppermute | solution.py:441
  33.4 3.9 %collective-permute-start.8 = (bf16[1,4,16,256]{3,2,1,0:T(8,128)(2,1)S(1)}, bf16[1,4,16,256]{3,2,1,0:T(8,128)(2,1)S(1)}, u32[]{:S(2)}, u32[]{:S(2)}) collective-permute-start(bf16[1,4,16,256]{3,2,1,0:T(8,128)(2,1)S(1)} %get-tuple-element.43), channel_id=1, source_target_pairs={{0,2},{1,3},{2,0},{3,1},{4,6},{5,7},{6,4},{7,5},{8,10},{9,11},{10,... | collective-permute-start | bytes 98312 | tf_op jit(solution)/shard_map/ppermute | solution.py:441
  33.7 3.9 %collective-permute-start.9 = (bf16[1,4,16,256]{3,2,1,0:T(8,128)(2,1)S(1)}, bf16[1,4,16,256]{3,2,1,0:T(8,128)(2,1)S(1)}, u32[]{:S(2)}, u32[]{:S(2)}) collective-permute-start(bf16[1,4,16,256]{3,2,1,0:T(8,128)(2,1)S(1)} %get-tuple-element.45), channel_id=1, source_target_pairs={{0,4},{1,5},{2,6},{3,7},{4,0},{5,1},{6,2},{7,3},{8,12},{9,13},{10,... | collective-permute-start | bytes 98312 | tf_op jit(solution)/shard_map/ppermute | solution.py:441

commit v13 on v12

--- a/solution.py
+++ b/solution.py
@@ -78,20 +78,21 @@
     fetch(offs, offs_v)
     fetch(sources, sources_v)
     inside = width - (W if late else 0)
-    for at in range(0, inside, inside // 2):
-        fetch(rec.at[:, pl.ds(first * HOP + at, inside // 2)], held.at[:, pl.ds(at, inside // 2)])
+    half = 0 if late else (count + 1) // 2
     if late:
         held[:, inside:] = halo[...]
-        ready = len(copies)
     else:
         fetch(taper, taper_v)
-        ready = len(copies)
+    for start, stop in ((0, (half + 2) * HOP), ((half + 2) * HOP, inside)):
+        fetch(rec.at[:, pl.ds(first * HOP + start, stop - start)], held.at[:, pl.ds(start, stop - start)])
+    ready = len(copies)
+    if not late:
         rows = FOLD // 4
         for at in range(0, FOLD, rows):
             fetch(table.at[pl.ds(at, rows)], table_v.at[pl.ds(at, rows)])
         fetch(smooth, smooth_v)
         fetch(rec.at[:, pl.ds(0, W)], out_edge)
-    for copy in copies[:ready]:
+    for copy in copies[: ready - 1]:
         copy.wait()
 
     lanes = lax.broadcasted_iota(jnp.int32, (c_dev, LANE), 1)
@@ -113,7 +114,11 @@
             sums[row, lo] = (near + far).astype(jnp.bfloat16)
             diffs[row, lo] = (near - far).astype(jnp.bfloat16)
 
-    pl.loop(0, count, unroll=4)(cut)
+    for slot in range(half):
+        cut(slot)
+    copies[ready - 1].wait()
+    for slot in range(half, count):
+        cut(slot)
     for copy in copies[ready:]:
         copy.wait()
 
@@ -317,7 +322,7 @@
         scratch_shapes=scratch,
         compiler_params=pltpu.CompilerParams(vmem_limit_bytes=24 << 20),
         cost_estimate=pl.CostEstimate(
-            flops=int((0.4 + grid * pairs * 0.008) * 0.02e9), bytes_accessed=1 << 20, transcendentals=0
+            flops=int((0.4 + grid * pairs * 0.008) * 1.15e9), bytes_accessed=1 << 20, transcendentals=0
         ),
         name="cross",
     )(*arrays)

time: 38.5 us -> 38 us (0.987)
  Pallas kernels: 14.2 us -> 13.8 us
    pallas_call x2, Pallas kernels: 6.07 us -> 5.64 us  [spectra_call(): pl.pallas_call(functools.partial(spectra_kernel, first, count, late is no...]
  transfers between devices with their start and end apart: 11 -> 11, of which waited for: 7 -> 7; matrix products, arithmetic and copies ran while one was open for 0% -> 0% of each run, Pallas kernels for 18% -> 19%
where the time goes in v13:
time: 38 us; the launch traced here: 37.9 us
  starting transfers between devices  14.7 us (39%)
  Pallas kernels  13.8 us (36%)
  waiting for transfers between devices  8.53 us (22%)
  other arithmetic  0.75 us (2%)
    ppermute x6, starting transfers between devices, trade(): return lax.ppermute(array, 'fibre', [(i, i ^ by) for i in range(n_fibre)])  9.64 us
    pallas_call x4, Pallas kernels, cross_call(): pl.pallas_call(functools.partial(cross_kernel, runs, kept, [len(some) for...  8.11 us
    pallas_call x2, Pallas kernels, spectra_call(): pl.pallas_call(functools.partial(spectra_kernel, first, count, late is no...  5.64 us
    ppermute x6, waiting for transfers between devices, trade(): return lax.ppermute(array, 'fibre', [(i, i ^ by) for i in range(n_fibre)])  4.14 us
    ppermute x3, starting transfers between devices, body(): mine = lax.ppermute(mine.astype(jnp.bfloat16), ('fibre', 'tm'), routes)  3.55 us
    ppermute x3, waiting for transfers between devices, body(): mine = lax.ppermute(mine.astype(jnp.bfloat16), ('fibre', 'tm'), routes)  2.11 us
    ppermute x1, starting transfers between devices, body(): halo = lax.ppermute(edge, 'tm', [(i, i - 1) for i in range(1, n_tm)])  1.28 us
    ppermute x1, waiting for transfers between devices, body(): got = lax.ppermute(give, 'tm', [(i, i ^ 1) for i in range(n_tm)])  1.22 us
  transfers between devices with their start and end apart: 11, of which 7 were waited for; matrix products, arithmetic and copies ran while one was open for 0% of the time, Pallas kernels for 19%

profile of v13, /device:TPU:0, one launch (start us, length us, event | category | flops | bytes accessed | tf_op | source)
XLA Modules:
  0.0 37.9 jit_solution(3250832276950386465)
XLA Ops:
  0.0 3.8 %spectra.2 = (bf16[384,768]{1,0:T(8,128)(2,1)S(1)}, bf16[64,768]{1,0:T(8,128)(2,1)S(1)}, bf16[112,768]{1,0:T(8,128)(2,1)S(1)}, bf16[16,2048]{1,0:T(8,128)(2,1)S(...) custom-call(s32[32]{0:T(128)} %refs_0_.3, s32[4]{0:T(128)} %refs_1_.3, ...), custom_call_target="tpu_custom_call" | custom-call | flops 43000000 | bytes 1048576 | tf_op jit(solution)/shard_map/spectra/pallas_call | solution.py:180
  3.8 3.0 %collective-permute-start.5 = (bf16[384,768]{1,0:T(8,128)(2,1)S(1)}, bf16[384,768]{1,0:T(8,128)(2,1)S(1)}, u32[]{:S(2)}, u32[]{:S(2)}) collective-permute-start(bf16[384,768]{1,0:T(8,128)(2,1)S(1)} %get-tuple-element.28.refs_1_.refs_2_.refs_4_), channel_id=1, source_target_pairs={{0,4},{4,0},{8,12},{12,8},{16,20},{20,16},{24,28},{28,24},{1,5},{5... | collective-permute-start | bytes 1769480 | tf_op jit(solution)/shard_map/ppermute | solution.py:369
  6.8 2.6 %collective-permute-start.2 = (bf16[112,768]{1,0:T(8,128)(2,1)S(1)}, bf16[112,768]{1,0:T(8,128)(2,1)S(1)}, u32[]{:S(2)}, u32[]{:S(2)}) collective-permute-start(bf16[112,768]{1,0:T(8,128)(2,1)S(1)} %get-tuple-element.27.refs_8_), channel_id=1, source_target_pairs={{0,16},{4,20},{8,24},{12,28},{16,0},{20,4},{24,8},{28,12},{1,17},{... | collective-permute-start | bytes 516104 | tf_op jit(solution)/shard_map/ppermute | solution.py:369
  9.4 1.3 %collective-permute-start = (bf16[16,2048]{1,0:T(8,128)(2,1)S(1)}, bf16[16,2048]{1,0:T(8,128)(2,1)S(1)}, u32[]{:S(2)}, u32[]{:S(2)}) collective-permute-start(bf16[16,2048]{1,0:T(8,128)(2,1)S(1)} %get-tuple-element.22), channel_id=1, source_target_pairs={{1,0},{2,1},{3,2},{5,4},{6,5},{7,6},{9,8},{10,9},{11,10},{13,12},{... | collective-permute-start | bytes 196616 | tf_op jit(solution)/shard_map/ppermute | solution.py:375
  10.6 0.8 %cross.4.refs_9_.refs_5_ = f32[64,768]{1,0:T(8,128)S(1)} custom-call(bf16[1,112,768]{2,1,0:T(8,128)(2,1)S(1)} %bitcast.44, bf16[384,768]{1,0:T(8,128)(2,1)S(1)} %get-tuple-element.28.refs_1_.refs_2_.refs_4_, bf16[64,768]{1,0:T(8,128)(2,1)S(1)} %get-tuple-element.26.refs_2_.refs_7_), custom_call_target="tpu_custom_call" | custom-call | flops 1490400000 | bytes 1048576 | tf_op jit(solution)/shard_map/cross/pallas_call | solution.py:314
  11.4 1.1 %collective-permute-done.refs_3_ = bf16[16,2048]{1,0:T(8,128)(2,1)S(1)} collective-permute-done((bf16[16,2048]{1,0:T(8,128)(2,1)S(1)}, bf16[16,2048]{1,0:T(8,128)(2,1)S(1)}, u32[]{:S(2)}, u32[]{:S(2)}) %collective-permute-start) | collective-permute-done | bytes 65568 | tf_op jit(solution)/shard_map/ppermute | solution.py:375
  12.5 0.0 copy-start
  12.5 1.9 %spectra.3 = (bf16[128,768]{1,0:T(8,128)(2,1)S(1)}, bf16[16,768]{1,0:T(8,128)(2,1)S(1)}, bf16[128,768]{1,0:T(8,128)(2,1)S(1)}) custom-call(s32[32]{0:T(128)} %refs_0_.3, s32[4]{0:T(128)} %refs_1_.3, bf16[16,32768]{1,0:T(8,128)(2,1)} %refs_2_.3, bf16[16,2048]{1,0:T(8,128)(2,1)S(1)} %collective-permute-done.refs_3_, ...), custom_call_target="tpu_custom_call" | custom-call | flops 19000000 | bytes 1048576 | tf_op jit(solution)/shard_map/spectra/pallas_call | solution.py:180
  14.4 0.4 %collective-permute-start.3 = (bf16[16,768]{1,0:T(8,128)(2,1)S(1)}, bf16[16,768]{1,0:T(8,128)(2,1)S(1)}, u32[]{:S(2)}, u32[]{:S(2)}) collective-permute-start(bf16[16,768]{1,0:T(8,128)(2,1)S(1)} %get-tuple-element.30), channel_id=1, source_target_pairs={{0,16},{4,20},{8,24},{12,28},{16,0},{20,4},{24,8},{28,12},{1,17},{... | collective-permute-start | bytes 73736 | tf_op jit(solution)/shard_map/ppermute | solution.py:369
  14.8 1.6 %collective-permute-start.1 = (bf16[128,768]{1,0:T(8,128)(2,1)S(1)}, bf16[128,768]{1,0:T(8,128)(2,1)S(1)}, u32[]{:S(2)}, u32[]{:S(2)}) collective-permute-start(bf16[128,768]{1,0:T(8,128)(2,1)S(1)} %get-tuple-element.29), channel_id=1, source_target_pairs={{0,8},{4,12},{8,0},{12,4},{16,24},{20,28},{24,16},{28,20},{1,9},{5... | collective-permute-start | bytes 589832 | tf_op jit(solution)/shard_map/ppermute | solution.py:369
  16.4 0.5 %collective-permute-start.6 = (bf16[128,768]{1,0:T(8,128)(2,1)S(1)}, bf16[128,768]{1,0:T(8,128)(2,1)S(1)}, u32[]{:S(2)}, u32[]{:S(2)}) collective-permute-start(bf16[128,768]{1,0:T(8,128)(2,1)S(1)} %get-tuple-element.31.refs_3_.refs_2_.refs_5_), channel_id=1, source_target_pairs={{0,4},{4,0},{8,12},{12,8},{16,20},{20,16},{24,28},{28,24},{1,5},{5... | collective-permute-start | bytes 589832 | tf_op jit(solution)/shard_map/ppermute | solution.py:369
  16.9 2.4 %collective-permute-done.3.refs_1_ = bf16[16,768]{1,0:T(8,128)(2,1)S(1)} collective-permute-done((bf16[16,768]{1,0:T(8,128)(2,1)S(1)}, bf16[16,768]{1,0:T(8,128)(2,1)S(1)}, u32[]{:S(2)}, u32[]{:S(2)}) %collective-permute-start.3) | collective-permute-done | bytes 24608 | tf_op jit(solution)/shard_map/ppermute | solution.py:369
  19.3 0.0 collective-permute-done.2.refs_0_
  19.3 1.5 %collective-permute-start.4 = (bf16[128,768]{1,0:T(8,128)(2,1)S(1)}, bf16[128,768]{1,0:T(8,128)(2,1)S(1)}, u32[]{:S(2)}, u32[]{:S(2)}) collective-permute-start(bf16[128,768]{1,0:T(8,128)(2,1)S(1)} %join.1), channel_id=1, source_target_pairs={{0,8},{4,12},{8,0},{12,4},{16,24},{20,28},{24,16},{28,20},{1,9},{5... | collective-permute-start | bytes 589832 | tf_op jit(solution)/shard_map/ppermute | solution.py:369
  20.8 0.0 collective-permute-done.5.refs_4_.refs_3_.refs_6_
  20.8 0.0 copy-done
  20.8 2.6 %cross.5 = (bf16[64,256]{1,0:T(8,128)(2,1)S(1)}, bf16[64,256]{1,0:T(8,128)(2,1)S(1)}, f32[128,768]{1,0:T(8,128)S(1)}) custom-call(bf16[1,128,768]{2,1,0:T(8,128)(2,1)S(1)} %bitcast.47, bf16[1,128,768]{2,1,0:T(8,128)(2,1)S(1)} %bitcast.42, bf16[384,768]{1,0:T(8,128)(2,1)S(1)} %get-tuple-element.28.refs_1_.refs_2_.refs_4_, ...), custom_call_target="tpu_custom_call" | custom-call | flops 3551200000 | bytes 1048576 | tf_op jit(solution)/shard_map/cross/pallas_call | solution.py:314
  23.5 0.0 collective-permute-done.1
  23.5 1.8 %cross.6 = (bf16[64,256]{1,0:T(8,128)(2,1)S(1)}, f32[64,768]{1,0:T(8,128)S(1)}) custom-call(bf16[1,128,768]{2,1,0:T(8,128)(2,1)S(1)} %bitcast.49, bf16[384,768]{1,0:T(8,128)(2,1)S(1)} %get-tuple-element.28.refs_1_.refs_2_.refs_4_, bf16[128,768]{1,0:T(8,128)(2,1)S(1)} %get-tuple-element.31.refs_3_.refs_2_.refs_5_, ...), custom_call_target="tpu_custom_call" | custom-call | flops 2520800000 | bytes 1048576 | tf_op jit(solution)/shard_map/cross/pallas_call | solution.py:314
  25.2 0.0 collective-permute-done.6.refs_7_
  25.3 1.7 %collective-permute-done.4 = bf16[128,768]{1,0:T(8,128)(2,1)S(1)} collective-permute-done((bf16[128,768]{1,0:T(8,128)(2,1)S(1)}, bf16[128,768]{1,0:T(8,128)(2,1)S(1)}, u32[]{:S(2)}, u32[]{:S(2)}) %collective-permute-start.4) | collective-permute-done | bytes 196640 | tf_op jit(solution)/shard_map/ppermute | solution.py:369
  27.0 2.9 %cross.7 = (bf16[256,256]{1,0:T(8,128)(2,1)S(1)}, bf16[256,256]{1,0:T(8,128)(2,1)S(1)}) custom-call(bf16[1,128,768]{2,1,0:T(8,128)(2,1)S(1)} %bitcast.48, bf16[1,128,768]{2,1,0:T(8,128)(2,1)S(1)} %bitcast.50, bf16[1,128,768]{2,1,0:T(8,128)(2,1)S(1)} %bitcast.43, bf16[1,128,768]{2,1,0:T(8,128)(2,1)S(1)} %bitcast.51, ...), custom_call_target="tpu_custom_call" | custom-call | flops 3698400000 | bytes 1048576 | tf_op jit(solution)/shard_map/cross/pallas_call | solution.py:314
  30.0 0.2 collective-permute-start.7
  30.2 1.2 %collective-permute-done.7 = bf16[4,1,4,16,256]{4,3,2,1,0:T(8,128)(2,1)S(1)} collective-permute-done((bf16[4,1,4,16,256]{4,3,2,1,0:T(8,128)(2,1)S(1)}, bf16[4,1,4,16,256]{4,3,2,1,0:T(8,128)(2,1)S(1)}, u32[]{:S(2)}, u32[]{:S(2)}) %collective-permute-start.7) | collective-permute-done | bytes 131104 | tf_op jit(solution)/shard_map/ppermute | solution.py:433
  31.5 1.4 %collective-permute-start.10 = (bf16[1,4,16,256]{3,2,1,0:T(8,128)(2,1)S(1)}, bf16[1,4,16,256]{3,2,1,0:T(8,128)(2,1)S(1)}, u32[]{:S(2)}, u32[]{:S(2)}) collective-permute-start(bf16[1,4,16,256]{3,2,1,0:T(8,128)(2,1)S(1)} %get-tuple-element.44), channel_id=1, source_target_pairs={{0,6},{1,7},{2,4},{3,5},{4,2},{5,3},{6,0},{7,1},{8,14},{9,15},{10,... | collective-permute-start | bytes 98312 | tf_op jit(solution)/shard_map/ppermute | solution.py:446
  32.9 0.3 collective-permute-start.8
  33.3 1.8 %collective-permute-start.9 = (bf16[1,4,16,256]{3,2,1,0:T(8,128)(2,1)S(1)}, bf16[1,4,16,256]{3,2,1,0:T(8,128)(2,1)S(1)}, u32[]{:S(2)}, u32[]{:S(2)}) collective-permute-start(bf16[1,4,16,256]{3,2,1,0:T(8,128)(2,1)S(1)} %get-tuple-element.45), channel_id=1, source_target_pairs={{0,4},{1,5},{2,6},{3,7},{4,0},{5,1},{6,2},{7,3},{8,12},{9,13},{10,... | collective-permute-start | bytes 98312 | tf_op jit(solution)/shard_map/ppermute | solution.py:446
  35.1 1.3 %collective-permute-done.10 = bf16[1,4,16,256]{3,2,1,0:T(8,128)(2,1)S(1)} collective-permute-done((bf16[1,4,16,256]{3,2,1,0:T(8,128)(2,1)S(1)}, bf16[1,4,16,256]{3,2,1,0:T(8,128)(2,1)S(1)}, u32[]{:S(2)}, u32[]{:S(2)}) %collective-permute-start.10) | collective-permute-done | bytes 32800 | tf_op jit(solution)/shard_map/ppermute | solution.py:446
  36.4 0.5 %collective-permute-done.8 = bf16[1,4,16,256]{3,2,1,0:T(8,128)(2,1)S(1)} collective-permute-done((bf16[1,4,16,256]{3,2,1,0:T(8,128)(2,1)S(1)}, bf16[1,4,16,256]{3,2,1,0:T(8,128)(2,1)S(1)}, u32[]{:S(2)}, u32[]{:S(2)}) %collective-permute-start.8) | collective-permute-done | bytes 32800 | tf_op jit(solution)/shard_map/ppermute | solution.py:446
  36.9 0.3 collective-permute-done.9
  37.2 0.7 %pad_maximum_fusion.1 = f32[1,2,4,16,256]{4,3,2,1,0:T(8,128)} fusion(f32[1,1,4,16,256]{4,3,2,1,0:T(8,128)S(1)} %get-tuple-element.40, f32[1,1,4,16,256]{4,3,2,1,0:T(8,128)S(1)} %get-tuple-element.39), kind=kLoop, calls=%fused_computation.2 | loop fusion | flops 32768 | bytes 262144 | tf_op jit(solution)/shard_map/stack | solution.py:452
  (6 shorter events, 0.1 us)
Async XLA Ops:
  3.8 17.1 %collective-permute-start.5 = (bf16[384,768]{1,0:T(8,128)(2,1)S(1)}, bf16[384,768]{1,0:T(8,128)(2,1)S(1)}, u32[]{:S(2)}, u32[]{:S(2)}) collective-permute-start(bf16[384,768]{1,0:T(8,128)(2,1)S(1)} %get-tuple-element.28.refs_1_.refs_2_.refs_4_), channel_id=1, source_target_pairs={{0,4},{4,0},{8,12},{12,8},{16,20},{20,16},{24,28},{28,24},{1,5},{5... | collective-permute-start | bytes 1769480 | tf_op jit(solution)/shard_map/ppermute | solution.py:369
  6.8 12.5 %collective-permute-start.2 = (bf16[112,768]{1,0:T(8,128)(2,1)S(1)}, bf16[112,768]{1,0:T(8,128)(2,1)S(1)}, u32[]{:S(2)}, u32[]{:S(2)}) collective-permute-start(bf16[112,768]{1,0:T(8,128)(2,1)S(1)} %get-tuple-element.27.refs_8_), channel_id=1, source_target_pairs={{0,16},{4,20},{8,24},{12,28},{16,0},{20,4},{24,8},{28,12},{1,17},{... | collective-permute-start | bytes 516104 | tf_op jit(solution)/shard_map/ppermute | solution.py:369
  9.4 3.1 %collective-permute-start = (bf16[16,2048]{1,0:T(8,128)(2,1)S(1)}, bf16[16,2048]{1,0:T(8,128)(2,1)S(1)}, u32[]{:S(2)}, u32[]{:S(2)}) collective-permute-start(bf16[16,2048]{1,0:T(8,128)(2,1)S(1)} %get-tuple-element.22), channel_id=1, source_target_pairs={{1,0},{2,1},{3,2},{5,4},{6,5},{7,6},{9,8},{10,9},{11,10},{13,12},{... | collective-permute-start | bytes 196616 | tf_op jit(solution)/shard_map/ppermute | solution.py:375
  12.5 8.4 %copy-start = (bf16[768,256]{1,0:T(8,128)(2,1)S(1)}, bf16[768,256]{1,0:T(8,128)(2,1)}, u32[]{:S(2)}) copy-start(bf16[768,256]{1,0:T(8,128)(2,1)} %constant.81.clone.refs_6_.refs_4_.refs_13_) | copy-start | bytes 1179652
  14.4 4.9 %collective-permute-start.3 = (bf16[16,768]{1,0:T(8,128)(2,1)S(1)}, bf16[16,768]{1,0:T(8,128)(2,1)S(1)}, u32[]{:S(2)}, u32[]{:S(2)}) collective-permute-start(bf16[16,768]{1,0:T(8,128)(2,1)S(1)} %get-tuple-element.30), channel_id=1, source_target_pairs={{0,16},{4,20},{8,24},{12,28},{16,0},{20,4},{24,8},{28,12},{1,17},{... | collective-permute-start | bytes 73736 | tf_op jit(solution)/shard_map/ppermute | solution.py:369
  14.8 8.7 %collective-permute-start.1 = (bf16[128,768]{1,0:T(8,128)(2,1)S(1)}, bf16[128,768]{1,0:T(8,128)(2,1)S(1)}, u32[]{:S(2)}, u32[]{:S(2)}) collective-permute-start(bf16[128,768]{1,0:T(8,128)(2,1)S(1)} %get-tuple-element.29), channel_id=1, source_target_pairs={{0,8},{4,12},{8,0},{12,4},{16,24},{20,28},{24,16},{28,20},{1,9},{5... | collective-permute-start | bytes 589832 | tf_op jit(solution)/shard_map/ppermute | solution.py:369
  16.4 8.9 %collective-permute-start.6 = (bf16[128,768]{1,0:T(8,128)(2,1)S(1)}, bf16[128,768]{1,0:T(8,128)(2,1)S(1)}, u32[]{:S(2)}, u32[]{:S(2)}) collective-permute-start(bf16[128,768]{1,0:T(8,128)(2,1)S(1)} %get-tuple-element.31.refs_3_.refs_2_.refs_5_), channel_id=1, source_target_pairs={{0,4},{4,0},{8,12},{12,8},{16,20},{20,16},{24,28},{28,24},{1,5},{5... | collective-permute-start | bytes 589832 | tf_op jit(solution)/shard_map/ppermute | solution.py:369
  19.3 7.7 %collective-permute-start.4 = (bf16[128,768]{1,0:T(8,128)(2,1)S(1)}, bf16[128,768]{1,0:T(8,128)(2,1)S(1)}, u32[]{:S(2)}, u32[]{:S(2)}) collective-permute-start(bf16[128,768]{1,0:T(8,128)(2,1)S(1)} %join.1), channel_id=1, source_target_pairs={{0,8},{4,12},{8,0},{12,4},{16,24},{20,28},{24,16},{28,20},{1,9},{5... | collective-permute-start | bytes 589832 | tf_op jit(solution)/shard_map/ppermute | solution.py:369
  30.0 1.4 %collective-permute-start.7 = (bf16[4,1,4,16,256]{4,3,2,1,0:T(8,128)(2,1)S(1)}, bf16[4,1,4,16,256]{4,3,2,1,0:T(8,128)(2,1)S(1)}, u32[]{:S(2)}, u32[]{:S(2)}) collective-permute-start(bf16[4,1,4,16,256]{4,3,2,1,0:T(8,128)(2,1)S(1)} %pad_maximum_fusion), channel_id=1, source_target_pairs={{0,1},{1,0},{2,3},{3,2},{4,5},{5,4},{6,7},{7,6},{8,9},{9,8},{10,11... | collective-permute-start | bytes 393224 | tf_op jit(solution)/shard_map/ppermute | solution.py:433
  31.5 4.9 %collective-permute-start.10 = (bf16[1,4,16,256]{3,2,1,0:T(8,128)(2,1)S(1)}, bf16[1,4,16,256]{3,2,1,0:T(8,128)(2,1)S(1)}, u32[]{:S(2)}, u32[]{:S(2)}) collective-permute-start(bf16[1,4,16,256]{3,2,1,0:T(8,128)(2,1)S(1)} %get-tuple-element.44), channel_id=1, source_target_pairs={{0,6},{1,7},{2,4},{3,5},{4,2},{5,3},{6,0},{7,1},{8,14},{9,15},{10,... | collective-permute-start | bytes 98312 | tf_op jit(solution)/shard_map/ppermute | solution.py:446
  32.9 3.9 %collective-permute-start.8 = (bf16[1,4,16,256]{3,2,1,0:T(8,128)(2,1)S(1)}, bf16[1,4,16,256]{3,2,1,0:T(8,128)(2,1)S(1)}, u32[]{:S(2)}, u32[]{:S(2)}) collective-permute-start(bf16[1,4,16,256]{3,2,1,0:T(8,128)(2,1)S(1)} %get-tuple-element.43), channel_id=1, source_target_pairs={{0,2},{1,3},{2,0},{3,1},{4,6},{5,7},{6,4},{7,5},{8,10},{9,11},{10,... | collective-permute-start | bytes 98312 | tf_op jit(solution)/shard_map/ppermute | solution.py:446
  33.3 3.9 %collective-permute-start.9 = (bf16[1,4,16,256]{3,2,1,0:T(8,128)(2,1)S(1)}, bf16[1,4,16,256]{3,2,1,0:T(8,128)(2,1)S(1)}, u32[]{:S(2)}, u32[]{:S(2)}) collective-permute-start(bf16[1,4,16,256]{3,2,1,0:T(8,128)(2,1)S(1)} %get-tuple-element.45), channel_id=1, source_target_pairs={{0,4},{1,5},{2,6},{3,7},{4,0},{5,1},{6,2},{7,3},{8,12},{9,13},{10,... | collective-permute-start | bytes 98312 | tf_op jit(solution)/shard_map/ppermute | solution.py:446

commit v14 on v13

--- a/solution.py
+++ b/solution.py
@@ -60,12 +60,13 @@
 
 def spectra_kernel(first, count, late, c_dev, n_src, n_after, *refs):
     if late:
-        offs, sources, rec, halo, table_v, taper_v, smooth_v, before_r, before_s, *refs = refs
+        offs, sources, rest, halo, table_v, taper_v, smooth_v, before_r, before_s, *refs = refs
         out_r, out_s, out_all, *refs = refs[n_after:]
         sums, diffs, held, offs_v, sources_v, sems = refs
     else:
         offs, sources, rec, table, taper, smooth, *refs = refs
-        out_r, out_mid, out_s, out_edge, table_v, taper_v, smooth_v, *refs = refs
+        out_r, out_mid, out_s, out_edge, out_rest, out_offs, out_sources, *refs = refs
+        table_v, taper_v, smooth_v, *refs = refs
         sums, diffs, held, offs_v, sources_v, sems = refs
     width = (count + 2) * HOP
     copies = []
@@ -80,11 +81,12 @@
     inside = width - (W if late else 0)
     half = 0 if late else (count + 1) // 2
     if late:
+        held[:, :inside] = rest[...]
         held[:, inside:] = halo[...]
     else:
         fetch(taper, taper_v)
-    for start, stop in ((0, (half + 2) * HOP), ((half + 2) * HOP, inside)):
-        fetch(rec.at[:, pl.ds(first * HOP + start, stop - start)], held.at[:, pl.ds(start, stop - start)])
+        for start, stop in ((0, (half + 2) * HOP), ((half + 2) * HOP, inside)):
+            fetch(rec.at[:, pl.ds(start, stop - start)], held.at[:, pl.ds(start, stop - start)])
     ready = len(copies)
     if not late:
         rows = FOLD // 4
@@ -92,6 +94,9 @@
             fetch(table.at[pl.ds(at, rows)], table_v.at[pl.ds(at, rows)])
         fetch(smooth, smooth_v)
         fetch(rec.at[:, pl.ds(0, W)], out_edge)
+        fetch(rec.at[:, pl.ds(count * HOP, out_rest.shape[1])], out_rest)
+        fetch(offs, out_offs)
+        fetch(sources, out_sources)
     for copy in copies[: ready - 1]:
         copy.wait()
 
@@ -162,15 +167,17 @@
     vmem = pl.BlockSpec(memory_space=pltpu.VMEM)
     hbm = pl.BlockSpec(memory_space=pltpu.HBM)
     arrays = [offsets, src_idx, record]
+    n_rest = record.shape[1] - count * HOP
     if late is None:
         arrays += tables
-    arrays = [pltpu.with_memory_space_constraint(a, pltpu.HBM) for a in arrays]
-    specs = [hbm] * len(arrays)
+        arrays = [pltpu.with_memory_space_constraint(a, pltpu.HBM) for a in arrays]
+    specs = [hbm if late is None else vmem] * len(arrays)
     rows = [head, count - head] if late is None else [count + late[1].shape[0] // c_dev]
     out_shape = [jax.ShapeDtypeStruct((n * c_dev, 2 * NB), jnp.bfloat16) for n in rows]
     out_shape.append(jax.ShapeDtypeStruct((n_src * count, 2 * NB), jnp.bfloat16))
     if late is None:
-        out_shape.append(jax.ShapeDtypeStruct((c_dev, W), record.dtype))
+        out_shape += [jax.ShapeDtypeStruct((c_dev, n), record.dtype) for n in (W, n_rest)]
+        out_shape += [jax.ShapeDtypeStruct(a.shape, a.dtype) for a in (offsets, src_idx)]
         out_shape += [jax.ShapeDtypeStruct(t.shape, t.dtype) for t in tables]
     else:
         halo, middle, sources = late
@@ -294,12 +301,12 @@
     lists = [srcs, recs, befores, done, () if ltab is None else (ltab,), after]
     arrays = [a for some in lists for a in some]
     specs = [whole] * (len(arrays) - len(after)) + [pl.BlockSpec(memory_space=pl.ANY)] * len(after)
-    shapes = []
+    shapes, heights = [], [a.shape[0] for a in done]
     for out in outs:
         if isinstance(out, int):
             shapes.append(jax.ShapeDtypeStruct((out * unit, 2 * NB), jnp.float32))
         else:
-            rows = sum(unit if isinstance(p, str) else p * unit for p in out)
+            rows = sum(heights.pop(0) if isinstance(p, str) else p * unit for p in out)
             shapes.append(jax.ShapeDtypeStruct((grid * rows, LAGS), jnp.bfloat16))
     out_specs = [whole] * len(shapes)
     if grid > 1:
@@ -322,7 +329,7 @@
         scratch_shapes=scratch,
         compiler_params=pltpu.CompilerParams(vmem_limit_bytes=24 << 20),
         cost_estimate=pl.CostEstimate(
-            flops=int((0.4 + grid * pairs * 0.008) * 1.15e9), bytes_accessed=1 << 20, transcendentals=0
+            flops=int((0.4 + grid * pairs * 0.008) * 0.02e9), bytes_accessed=1 << 20, transcendentals=0
         ),
         name="cross",
     )(*arrays)
@@ -368,7 +375,7 @@
     def trade(array, by):
         return lax.ppermute(array, "fibre", [(i, i ^ by) for i in range(n_fibre)])
 
-    rec_a, middle, src_a, edge, *tables = spectra_call(record, offsets, src_idx, tables, 0, early, head)
+    rec_a, middle, src_a, edge, rest, offs, sources, *tables = spectra_call(record, offsets, src_idx, tables, 0, early, head)
     far_a = trade(rec_a, 1)
     if direct:
         by_2a = trade(src_a, 4)
@@ -382,7 +389,7 @@
         parts = [(0, 0, 0, head), (1, head, head, early)]
         begun = cross([src_a[None]], [rec_a, middle], [(0, 1, parts, None, (0, 0))], [1])
     rec_b, src_b, src = spectra_call(
-        record, offsets, src_idx, tables, early, n_win - early, late=late, after=begun
+        rest, offs, sources, tables, early, n_win - early, late=late, after=begun
     )
     far_b = trade(rec_b, 1)
     own = [(0, 0, 0, head), (1, head, head, n_win)]
@@ -392,27 +399,20 @@
         by_3 = trade(by_2, 2)
         srcs = [part[None] for part in (src, by_1, by_2, by_3)]
         mine = functools.partial(cross, recs=[rec_a, rec_b, far_a], ltab=ltab)
+        runs = [(0, 1, [(1, head, early, n_win)], (0, 0), None), (1, 1, own, None, None)]
+        ours = functools.partial(cross, recs=[rec_a, rec_b], ltab=ltab)
+        near_0, near_2 = ours([srcs[0], srcs[2]], runs=runs, outs=[[1], [1]], befores=begun)
+        near_1 = ours(srcs[1:2], runs=[(0, 1, own, None, None)], outs=[[1]], after=[near_2])[0]
         swapped = [(2, 0, 0, head)]
-        runs = [
-            (0, 1, [(1, head, early, n_win)], (0, 0), None),
-            (1, 1, own, None, None),
-            (0, 1, swapped, None, (2, 0)),
-            (1, 1, swapped, None, (2, 1)),
-        ]
-        near_0, near_2, sums = mine([srcs[0], srcs[2]], runs=runs, outs=[[1], [1], 2], befores=begun)
-        runs = [(0, 1, own, None, None), (0, 1, swapped, None, (1, 0))]
-        near_1, sums_1 = mine(srcs[1:2], runs=runs, outs=[[1], 1], after=[sums])
+        runs = [(0, 2, swapped, None, (0, 0)), (2, 1, swapped, None, (0, 2))]
+        sums = mine(srcs[:3], runs=runs, outs=[3], after=[near_1])[0]
         swapped = [(3, head, head, n_win)]
-        runs = [
-            (0, 1, swapped, (0, 0), None),
-            (1, 1, swapped, (1, 0), None),
-            (2, 1, swapped, (0, 1), None),
-            (3, 1, [(2, 0, 0, head)] + swapped, None, None),
-            (3, 1, own, None, None),
-        ]
-        far, near = cross(
-            srcs, [rec_a, rec_b, far_a, far_b], runs, [[1, 1, 1, 1], ["done"] * 3 + [1]],
-            befores=[sums, sums_1], done=[near_0, near_1, near_2], ltab=ltab,
+        runs = [(0, 2, swapped, (0, 0), None), (2, 1, swapped, (0, 2), None)]
+        theirs = functools.partial(cross, recs=[rec_a, rec_b, far_a, far_b], ltab=ltab)
+        far = theirs(srcs[:3], runs=runs, outs=[[1, 1, 1]], befores=[sums])[0]
+        runs = [(0, 1, [(2, 0, 0, head)] + swapped, None, None), (0, 1, own, None, None)]
+        far, near = theirs(
+            srcs[3:], runs=runs, outs=[["done", 1], ["done"] * 3 + [1]], done=[far, near_0, near_1, near_2]
         )
     else:
         ranks = [[2 * j + p for j in range(n_group)] for p in range(2)]

time: 38 us -> 37.5 us (0.987)
  waiting for transfers between devices: 8.53 us -> 7.49 us
  starting transfers between devices: 14.7 us -> 15.4 us
    ppermute x6, waiting for transfers between devices: 4.14 us -> 3.04 us  [trade(): return lax.ppermute(array, 'fibre', [(i, i ^ by) for i in range(n_fibre)])]
    ppermute x1, starting transfers between devices: 0.19 us -> 0.93 us  [body(): got = lax.ppermute(give, 'tm', [(i, i ^ 1) for i in range(n_tm)])]
    pallas_call x4 -> x6, Pallas kernels: 8.11 us -> 8.23 us  [cross_call(): pl.pallas_call(functools.partial(cross_kernel, runs, kept, [len(some) for...]
  transfers between devices with their start and end apart: 11 -> 11, of which waited for: 7 -> 7; matrix products, arithmetic and copies ran while one was open for 0% -> 0% of each run, Pallas kernels for 19% -> 21%
where the time goes in v14:
time: 37.5 us; the launch traced here: 37.4 us
  starting transfers between devices  15.4 us (41%)
  Pallas kernels  13.5 us (36%)
  waiting for transfers between devices  7.49 us (20%)
  other arithmetic  0.75 us (2%)
    ppermute x6, starting transfers between devices, trade(): return lax.ppermute(array, 'fibre', [(i, i ^ by) for i in range(n_fibre)])  9.64 us
    pallas_call x6, Pallas kernels, cross_call(): pl.pallas_call(functools.partial(cross_kernel, runs, kept, [len(some) for...  8.23 us
    pallas_call x2, Pallas kernels, spectra_call(): pl.pallas_call(functools.partial(spectra_kernel, first, count, late is no...  5.26 us
    ppermute x3, starting transfers between devices, body(): mine = lax.ppermute(mine.astype(jnp.bfloat16), ('fibre', 'tm'), routes)  3.57 us
    ppermute x6, waiting for transfers between devices, trade(): return lax.ppermute(array, 'fibre', [(i, i ^ by) for i in range(n_fibre)])  3.04 us
    ppermute x3, waiting for transfers between devices, body(): mine = lax.ppermute(mine.astype(jnp.bfloat16), ('fibre', 'tm'), routes)  2.42 us
    ppermute x1, starting transfers between devices, body(): halo = lax.ppermute(edge, 'tm', [(i, i - 1) for i in range(1, n_tm)])  1.28 us
    ppermute x1, waiting for transfers between devices, body(): halo = lax.ppermute(edge, 'tm', [(i, i - 1) for i in range(1, n_tm)])  1.04 us
  transfers between devices with their start and end apart: 11, of which 7 were waited for; matrix products, arithmetic and copies ran while one was open for 0% of the time, Pallas kernels for 21%

profile of v14, /device:TPU:0, one launch (start us, length us, event | category | flops | bytes accessed | tf_op | source)
XLA Modules:
  0.0 37.4 jit_solution(4467617581700824836)
XLA Ops:
  0.0 3.8 %spectra.2 = (bf16[384,768]{1,0:T(8,128)(2,1)S(1)}, bf16[64,768]{1,0:T(8,128)(2,1)S(1)}, bf16[112,768]{1,0:T(8,128)(2,1)S(1)}, bf16[16,2048]{1,0:T(8,128)(2,1)S(...) custom-call(s32[32]{0:T(128)} %refs_0_.1, ...), custom_call_target="tpu_custom_call" | custom-call | flops 43000000 | bytes 1048576 | tf_op jit(solution)/shard_map/spectra/pallas_call | solution.py:187
  3.8 3.0 %collective-permute-start.4 = (bf16[384,768]{1,0:T(8,128)(2,1)S(1)}, bf16[384,768]{1,0:T(8,128)(2,1)S(1)}, u32[]{:S(2)}, u32[]{:S(2)}) collective-permute-start(bf16[384,768]{1,0:T(8,128)(2,1)S(1)} %get-tuple-element.31.refs_1_.refs_2_.refs_3_), channel_id=1, source_target_pairs={{0,4},{4,0},{8,12},{12,8},{16,20},{20,16},{24,28},{28,24},{1,5},{5... | collective-permute-start | bytes 1769480 | tf_op jit(solution)/shard_map/ppermute | solution.py:376
  6.8 2.6 %collective-permute-start = (bf16[112,768]{1,0:T(8,128)(2,1)S(1)}, bf16[112,768]{1,0:T(8,128)(2,1)S(1)}, u32[]{:S(2)}, u32[]{:S(2)}) collective-permute-start(bf16[112,768]{1,0:T(8,128)(2,1)S(1)} %get-tuple-element.22.refs_8_), channel_id=1, source_target_pairs={{0,16},{4,20},{8,24},{12,28},{16,0},{20,4},{24,8},{28,12},{1,17},{... | collective-permute-start | bytes 516104 | tf_op jit(solution)/shard_map/ppermute | solution.py:376
  9.4 1.3 %collective-permute-start.1 = (bf16[16,2048]{1,0:T(8,128)(2,1)S(1)}, bf16[16,2048]{1,0:T(8,128)(2,1)S(1)}, u32[]{:S(2)}, u32[]{:S(2)}) collective-permute-start(bf16[16,2048]{1,0:T(8,128)(2,1)S(1)} %get-tuple-element.26), channel_id=1, source_target_pairs={{1,0},{2,1},{3,2},{5,4},{6,5},{7,6},{9,8},{10,9},{11,10},{13,12},{... | collective-permute-start | bytes 196616 | tf_op jit(solution)/shard_map/ppermute | solution.py:382
  10.7 0.8 %cross.6.refs_9_.refs_4_ = f32[64,768]{1,0:T(8,128)S(1)} custom-call(bf16[1,112,768]{2,1,0:T(8,128)(2,1)S(1)} %bitcast.51, bf16[384,768]{1,0:T(8,128)(2,1)S(1)} %get-tuple-element.31.refs_1_.refs_2_.refs_3_, bf16[64,768]{1,0:T(8,128)(2,1)S(1)} %get-tuple-element.30.refs_2_.refs_7_), custom_call_target="tpu_custom_call" | custom-call | flops 25920000 | bytes 1048576 | tf_op jit(solution)/shard_map/cross/pallas_call | solution.py:321
  11.4 0.0 copy-start
  11.5 1.0 %collective-permute-done.1.refs_3_ = bf16[16,2048]{1,0:T(8,128)(2,1)S(1)} collective-permute-done((bf16[16,2048]{1,0:T(8,128)(2,1)S(1)}, bf16[16,2048]{1,0:T(8,128)(2,1)S(1)}, u32[]{:S(2)}, u32[]{:S(2)}) %collective-permute-start.1) | collective-permute-done | bytes 65568 | tf_op jit(solution)/shard_map/ppermute | solution.py:382
  12.5 1.5 %spectra.3 = (bf16[128,768]{1,0:T(8,128)(2,1)S(1)}, bf16[16,768]{1,0:T(8,128)(2,1)S(1)}, bf16[128,768]{1,0:T(8,128)(2,1)S(1)}) custom-call(s32[32]{0:T(128)S(1)} %get-tuple-element.23.refs_0_, s32[4]{0:T(128)S(1)} %get-tuple-element.24.refs_1_, bf16[16,4096]{1,0:T(8,128)(2,1)S(1)} %get-tuple-element.25.refs_2_, ...), custom_call_target="tpu_custom_call" | custom-call | flops 19000000 | bytes 1048576 | tf_op jit(solution)/shard_map/spectra/pallas_call | solution.py:187
  14.0 0.4 %collective-permute-start.2 = (bf16[16,768]{1,0:T(8,128)(2,1)S(1)}, bf16[16,768]{1,0:T(8,128)(2,1)S(1)}, u32[]{:S(2)}, u32[]{:S(2)}) collective-permute-start(bf16[16,768]{1,0:T(8,128)(2,1)S(1)} %get-tuple-element.32), channel_id=1, source_target_pairs={{0,16},{4,20},{8,24},{12,28},{16,0},{20,4},{24,8},{28,12},{1,17},{... | collective-permute-start | bytes 73736 | tf_op jit(solution)/shard_map/ppermute | solution.py:376
  14.4 1.6 %collective-permute-start.6 = (bf16[128,768]{1,0:T(8,128)(2,1)S(1)}, bf16[128,768]{1,0:T(8,128)(2,1)S(1)}, u32[]{:S(2)}, u32[]{:S(2)}) collective-permute-start(bf16[128,768]{1,0:T(8,128)(2,1)S(1)} %get-tuple-element.34), channel_id=1, source_target_pairs={{0,8},{4,12},{8,0},{12,4},{16,24},{20,28},{24,16},{28,20},{1,9},{5... | collective-permute-start | bytes 589832 | tf_op jit(solution)/shard_map/ppermute | solution.py:376
  16.0 0.5 %collective-permute-start.5 = (bf16[128,768]{1,0:T(8,128)(2,1)S(1)}, bf16[128,768]{1,0:T(8,128)(2,1)S(1)}, u32[]{:S(2)}, u32[]{:S(2)}) collective-permute-start(bf16[128,768]{1,0:T(8,128)(2,1)S(1)} %get-tuple-element.33.refs_3_.refs_2_.refs_4_), channel_id=1, source_target_pairs={{0,4},{4,0},{8,12},{12,8},{16,20},{20,16},{24,28},{28,24},{1,5},{5... | collective-permute-start | bytes 589832 | tf_op jit(solution)/shard_map/ppermute | solution.py:376
  16.5 2.4 %collective-permute-done.2.refs_1_ = bf16[16,768]{1,0:T(8,128)(2,1)S(1)} collective-permute-done((bf16[16,768]{1,0:T(8,128)(2,1)S(1)}, bf16[16,768]{1,0:T(8,128)(2,1)S(1)}, u32[]{:S(2)}, u32[]{:S(2)}) %collective-permute-start.2) | collective-permute-done | bytes 24608 | tf_op jit(solution)/shard_map/ppermute | solution.py:376
  18.9 0.0 collective-permute-done.refs_0_
  18.9 1.5 %collective-permute-start.3 = (bf16[128,768]{1,0:T(8,128)(2,1)S(1)}, bf16[128,768]{1,0:T(8,128)(2,1)S(1)}, u32[]{:S(2)}, u32[]{:S(2)}) collective-permute-start(bf16[128,768]{1,0:T(8,128)(2,1)S(1)} %join.1), channel_id=1, source_target_pairs={{0,8},{4,12},{8,0},{12,4},{16,24},{20,28},{24,16},{28,20},{1,9},{5... | collective-permute-start | bytes 589832 | tf_op jit(solution)/shard_map/ppermute | solution.py:376
  20.5 0.0 copy-done
  20.5 1.3 %cross.7 = (bf16[64,256]{1,0:T(8,128)(2,1)S(1)}, bf16[64,256]{1,0:T(8,128)(2,1)S(1)}) custom-call(bf16[1,128,768]{2,1,0:T(8,128)(2,1)S(1)} %bitcast.45, bf16[1,128,768]{2,1,0:T(8,128)(2,1)S(1)} %bitcast.42, bf16[384,768]{1,0:T(8,128)(2,1)S(1)} %get-tuple-element.31.refs_1_.refs_2_.refs_3_, bf16[128,768]{1,0:T(8,128)(2,1)S(1)} %get-tuple-element.33.refs_3_.refs_2_.refs_4_, ...), custom_call_target="tpu_custom_call" | custom-call | flops 31040000 | bytes 1048576 | tf_op jit(solution)/shard_map/cross/pallas_call | solution.py:321
  21.8 0.0 collective-permute-done.6
  21.8 1.1 %cross.8.refs_7_ = bf16[64,256]{1,0:T(8,128)(2,1)S(1)} custom-call(bf16[1,128,768]{2,1,0:T(8,128)(2,1)S(1)} %bitcast.48, bf16[384,768]{1,0:T(8,128)(2,1)S(1)} %get-tuple-element.31.refs_1_.refs_2_.refs_3_, bf16[128,768]{1,0:T(8,128)(2,1)S(1)} %get-tuple-element.33.refs_3_.refs_2_.refs_4_, bf16[768,256]{1,0:T(8,128)(2,1)S(1)} %copy-done, ...), custom_call_target="tpu_custom_call" | custom-call | flops 28480000 | bytes 1048576 | tf_op jit(solution)/shard_map/cross/pallas_call | solution.py:321
  22.9 0.0 collective-permute-done.4.refs_5_.refs_3_
  22.9 2.0 %cross.9.refs_7_ = f32[192,768]{1,0:T(8,128)S(1)} custom-call(bf16[1,128,768]{2,1,0:T(8,128)(2,1)S(1)} %bitcast.46, bf16[1,128,768]{2,1,0:T(8,128)(2,1)S(1)} %bitcast.49, bf16[1,128,768]{2,1,0:T(8,128)(2,1)S(1)} %bitcast.43, bf16[384,768]{1,0:T(8,128)(2,1)S(1)} %get-tuple-element.31.refs_1_.refs_2_.refs_3_, ...), custom_call_target="tpu_custom_call" | custom-call | flops 54080000 | bytes 1048576 | tf_op jit(solution)/shard_map/cross/pallas_call | solution.py:321
  24.9 0.0 collective-permute-done.5.refs_6_.refs_4_
  24.9 1.0 %cross.10.refs_5_ = bf16[192,256]{1,0:T(8,128)(2,1)S(1)} custom-call(bf16[1,128,768]{2,1,0:T(8,128)(2,1)S(1)} %bitcast.47, bf16[1,128,768]{2,1,0:T(8,128)(2,1)S(1)} %bitcast.50, bf16[1,128,768]{2,1,0:T(8,128)(2,1)S(1)} %bitcast.44, bf16[384,768]{1,0:T(8,128)(2,1)S(1)} %get-tuple-element.31.refs_1_.refs_2_.refs_3_, ...), custom_call_target="tpu_custom_call" | custom-call | flops 23360000 | bytes 1048576 | tf_op jit(solution)/shard_map/cross/pallas_call | solution.py:321
  26.0 0.6 %collective-permute-done.3 = bf16[128,768]{1,0:T(8,128)(2,1)S(1)} collective-permute-done((bf16[128,768]{1,0:T(8,128)(2,1)S(1)}, bf16[128,768]{1,0:T(8,128)(2,1)S(1)}, u32[]{:S(2)}, u32[]{:S(2)}) %collective-permute-start.3) | collective-permute-done | bytes 196640 | tf_op jit(solution)/shard_map/ppermute | solution.py:376
  26.6 2.0 %cross.11 = (bf16[256,256]{1,0:T(8,128)(2,1)S(1)}, bf16[256,256]{1,0:T(8,128)(2,1)S(1)}) custom-call(bf16[1,128,768]{2,1,0:T(8,128)(2,1)S(1)} %bitcast.52, bf16[384,768]{1,0:T(8,128)(2,1)S(1)} %get-tuple-element.31.refs_1_.refs_2_.refs_3_, bf16[128,768]{1,0:T(8,128)(2,1)S(1)} %get-tuple-element.33.refs_3_.refs_2_.refs_4_, ...), custom_call_target="tpu_custom_call" | custom-call | flops 48960000 | bytes 1048576 | tf_op jit(solution)/shard_map/cross/pallas_call | solution.py:321
  28.7 0.9 %collective-permute-start.7 = (bf16[4,1,4,16,256]{4,3,2,1,0:T(8,128)(2,1)S(1)}, bf16[4,1,4,16,256]{4,3,2,1,0:T(8,128)(2,1)S(1)}, u32[]{:S(2)}, u32[]{:S(2)}) collective-permute-start(bf16[4,1,4,16,256]{4,3,2,1,0:T(8,128)(2,1)S(1)} %pad_maximum_fusion), channel_id=1, source_target_pairs={{0,1},{1,0},{2,3},{3,2},{4,5},{5,4},{6,7},{7,6},{8,9},{9,8},{10,11... | collective-permute-start | bytes 393224 | tf_op jit(solution)/shard_map/ppermute | solution.py:433
  29.6 1.0 %collective-permute-done.7 = bf16[4,1,4,16,256]{4,3,2,1,0:T(8,128)(2,1)S(1)} collective-permute-done((bf16[4,1,4,16,256]{4,3,2,1,0:T(8,128)(2,1)S(1)}, bf16[4,1,4,16,256]{4,3,2,1,0:T(8,128)(2,1)S(1)}, u32[]{:S(2)}, u32[]{:S(2)}) %collective-permute-start.7) | collective-permute-done | bytes 131104 | tf_op jit(solution)/shard_map/ppermute | solution.py:433
  30.7 1.8 %collective-permute-start.10 = (bf16[1,4,16,256]{3,2,1,0:T(8,128)(2,1)S(1)}, bf16[1,4,16,256]{3,2,1,0:T(8,128)(2,1)S(1)}, u32[]{:S(2)}, u32[]{:S(2)}) collective-permute-start(bf16[1,4,16,256]{3,2,1,0:T(8,128)(2,1)S(1)} %get-tuple-element.44), channel_id=1, source_target_pairs={{0,6},{1,7},{2,4},{3,5},{4,2},{5,3},{6,0},{7,1},{8,14},{9,15},{10,... | collective-permute-start | bytes 98312 | tf_op jit(solution)/shard_map/ppermute | solution.py:446
  32.5 0.3 collective-permute-start.8
  32.7 1.5 %collective-permute-start.9 = (bf16[1,4,16,256]{3,2,1,0:T(8,128)(2,1)S(1)}, bf16[1,4,16,256]{3,2,1,0:T(8,128)(2,1)S(1)}, u32[]{:S(2)}, u32[]{:S(2)}) collective-permute-start(bf16[1,4,16,256]{3,2,1,0:T(8,128)(2,1)S(1)} %get-tuple-element.45), channel_id=1, source_target_pairs={{0,4},{1,5},{2,6},{3,7},{4,0},{5,1},{6,2},{7,3},{8,12},{9,13},{10,... | collective-permute-start | bytes 98312 | tf_op jit(solution)/shard_map/ppermute | solution.py:446
  34.2 1.4 %collective-permute-done.10 = bf16[1,4,16,256]{3,2,1,0:T(8,128)(2,1)S(1)} collective-permute-done((bf16[1,4,16,256]{3,2,1,0:T(8,128)(2,1)S(1)}, bf16[1,4,16,256]{3,2,1,0:T(8,128)(2,1)S(1)}, u32[]{:S(2)}, u32[]{:S(2)}) %collective-permute-start.10) | collective-permute-done | bytes 32800 | tf_op jit(solution)/shard_map/ppermute | solution.py:446
  35.6 0.8 %collective-permute-done.8 = bf16[1,4,16,256]{3,2,1,0:T(8,128)(2,1)S(1)} collective-permute-done((bf16[1,4,16,256]{3,2,1,0:T(8,128)(2,1)S(1)}, bf16[1,4,16,256]{3,2,1,0:T(8,128)(2,1)S(1)}, u32[]{:S(2)}, u32[]{:S(2)}) %collective-permute-start.8) | collective-permute-done | bytes 32800 | tf_op jit(solution)/shard_map/ppermute | solution.py:446
  36.4 0.3 collective-permute-done.9
  36.7 0.7 %pad_maximum_fusion.1 = f32[1,2,4,16,256]{4,3,2,1,0:T(8,128)} fusion(f32[1,1,4,16,256]{4,3,2,1,0:T(8,128)S(1)} %get-tuple-element.40, f32[1,1,4,16,256]{4,3,2,1,0:T(8,128)S(1)} %get-tuple-element.39), kind=kLoop, calls=%fused_computation.2 | loop fusion | flops 32768 | bytes 262144 | tf_op jit(solution)/shard_map/stack | solution.py:452
  (6 shorter events, 0.1 us)
Async XLA Ops:
  3.8 19.2 %collective-permute-start.4 = (bf16[384,768]{1,0:T(8,128)(2,1)S(1)}, bf16[384,768]{1,0:T(8,128)(2,1)S(1)}, u32[]{:S(2)}, u32[]{:S(2)}) collective-permute-start(bf16[384,768]{1,0:T(8,128)(2,1)S(1)} %get-tuple-element.31.refs_1_.refs_2_.refs_3_), channel_id=1, source_target_pairs={{0,4},{4,0},{8,12},{12,8},{16,20},{20,16},{24,28},{28,24},{1,5},{5... | collective-permute-start | bytes 1769480 | tf_op jit(solution)/shard_map/ppermute | solution.py:376
  6.8 12.1 %collective-permute-start = (bf16[112,768]{1,0:T(8,128)(2,1)S(1)}, bf16[112,768]{1,0:T(8,128)(2,1)S(1)}, u32[]{:S(2)}, u32[]{:S(2)}) collective-permute-start(bf16[112,768]{1,0:T(8,128)(2,1)S(1)} %get-tuple-element.22.refs_8_), channel_id=1, source_target_pairs={{0,16},{4,20},{8,24},{12,28},{16,0},{20,4},{24,8},{28,12},{1,17},{... | collective-permute-start | bytes 516104 | tf_op jit(solution)/shard_map/ppermute | solution.py:376
  9.4 3.1 %collective-permute-start.1 = (bf16[16,2048]{1,0:T(8,128)(2,1)S(1)}, bf16[16,2048]{1,0:T(8,128)(2,1)S(1)}, u32[]{:S(2)}, u32[]{:S(2)}) collective-permute-start(bf16[16,2048]{1,0:T(8,128)(2,1)S(1)} %get-tuple-element.26), channel_id=1, source_target_pairs={{1,0},{2,1},{3,2},{5,4},{6,5},{7,6},{9,8},{10,9},{11,10},{13,12},{... | collective-permute-start | bytes 196616 | tf_op jit(solution)/shard_map/ppermute | solution.py:382
  11.4 9.0 %copy-start = (bf16[768,256]{1,0:T(8,128)(2,1)S(1)}, bf16[768,256]{1,0:T(8,128)(2,1)}, u32[]{:S(2)}) copy-start(bf16[768,256]{1,0:T(8,128)(2,1)} %constant.81.clone.refs_5_.refs_3_.refs_6_.refs_8_.refs_9_) | copy-start | bytes 1179652
  14.0 4.9 %collective-permute-start.2 = (bf16[16,768]{1,0:T(8,128)(2,1)S(1)}, bf16[16,768]{1,0:T(8,128)(2,1)S(1)}, u32[]{:S(2)}, u32[]{:S(2)}) collective-permute-start(bf16[16,768]{1,0:T(8,128)(2,1)S(1)} %get-tuple-element.32), channel_id=1, source_target_pairs={{0,16},{4,20},{8,24},{12,28},{16,0},{20,4},{24,8},{28,12},{1,17},{... | collective-permute-start | bytes 73736 | tf_op jit(solution)/shard_map/ppermute | solution.py:376
  14.4 7.4 %collective-permute-start.6 = (bf16[128,768]{1,0:T(8,128)(2,1)S(1)}, bf16[128,768]{1,0:T(8,128)(2,1)S(1)}, u32[]{:S(2)}, u32[]{:S(2)}) collective-permute-start(bf16[128,768]{1,0:T(8,128)(2,1)S(1)} %get-tuple-element.34), channel_id=1, source_target_pairs={{0,8},{4,12},{8,0},{12,4},{16,24},{20,28},{24,16},{28,20},{1,9},{5... | collective-permute-start | bytes 589832 | tf_op jit(solution)/shard_map/ppermute | solution.py:376
  16.0 8.9 %collective-permute-start.5 = (bf16[128,768]{1,0:T(8,128)(2,1)S(1)}, bf16[128,768]{1,0:T(8,128)(2,1)S(1)}, u32[]{:S(2)}, u32[]{:S(2)}) collective-permute-start(bf16[128,768]{1,0:T(8,128)(2,1)S(1)} %get-tuple-element.33.refs_3_.refs_2_.refs_4_), channel_id=1, source_target_pairs={{0,4},{4,0},{8,12},{12,8},{16,20},{20,16},{24,28},{28,24},{1,5},{5... | collective-permute-start | bytes 589832 | tf_op jit(solution)/shard_map/ppermute | solution.py:376
  18.9 7.7 %collective-permute-start.3 = (bf16[128,768]{1,0:T(8,128)(2,1)S(1)}, bf16[128,768]{1,0:T(8,128)(2,1)S(1)}, u32[]{:S(2)}, u32[]{:S(2)}) collective-permute-start(bf16[128,768]{1,0:T(8,128)(2,1)S(1)} %join.1), channel_id=1, source_target_pairs={{0,8},{4,12},{8,0},{12,4},{16,24},{20,28},{24,16},{28,20},{1,9},{5... | collective-permute-start | bytes 589832 | tf_op jit(solution)/shard_map/ppermute | solution.py:376
  28.7 1.9 %collective-permute-start.7 = (bf16[4,1,4,16,256]{4,3,2,1,0:T(8,128)(2,1)S(1)}, bf16[4,1,4,16,256]{4,3,2,1,0:T(8,128)(2,1)S(1)}, u32[]{:S(2)}, u32[]{:S(2)}) collective-permute-start(bf16[4,1,4,16,256]{4,3,2,1,0:T(8,128)(2,1)S(1)} %pad_maximum_fusion), channel_id=1, source_target_pairs={{0,1},{1,0},{2,3},{3,2},{4,5},{5,4},{6,7},{7,6},{8,9},{9,8},{10,11... | collective-permute-start | bytes 393224 | tf_op jit(solution)/shard_map/ppermute | solution.py:433
  30.7 4.9 %collective-permute-start.10 = (bf16[1,4,16,256]{3,2,1,0:T(8,128)(2,1)S(1)}, bf16[1,4,16,256]{3,2,1,0:T(8,128)(2,1)S(1)}, u32[]{:S(2)}, u32[]{:S(2)}) collective-permute-start(bf16[1,4,16,256]{3,2,1,0:T(8,128)(2,1)S(1)} %get-tuple-element.44), channel_id=1, source_target_pairs={{0,6},{1,7},{2,4},{3,5},{4,2},{5,3},{6,0},{7,1},{8,14},{9,15},{10,... | collective-permute-start | bytes 98312 | tf_op jit(solution)/shard_map/ppermute | solution.py:446
  32.5 3.9 %collective-permute-start.8 = (bf16[1,4,16,256]{3,2,1,0:T(8,128)(2,1)S(1)}, bf16[1,4,16,256]{3,2,1,0:T(8,128)(2,1)S(1)}, u32[]{:S(2)}, u32[]{:S(2)}) collective-permute-start(bf16[1,4,16,256]{3,2,1,0:T(8,128)(2,1)S(1)} %get-tuple-element.43), channel_id=1, source_target_pairs={{0,2},{1,3},{2,0},{3,1},{4,6},{5,7},{6,4},{7,5},{8,10},{9,11},{10,... | collective-permute-start | bytes 98312 | tf_op jit(solution)/shard_map/ppermute | solution.py:446
  32.7 3.9 %collective-permute-start.9 = (bf16[1,4,16,256]{3,2,1,0:T(8,128)(2,1)S(1)}, bf16[1,4,16,256]{3,2,1,0:T(8,128)(2,1)S(1)}, u32[]{:S(2)}, u32[]{:S(2)}) collective-permute-start(bf16[1,4,16,256]{3,2,1,0:T(8,128)(2,1)S(1)} %get-tuple-element.45), channel_id=1, source_target_pairs={{0,4},{1,5},{2,6},{3,7},{4,0},{5,1},{6,2},{7,3},{8,12},{9,13},{10,... | collective-permute-start | bytes 98312 | tf_op jit(solution)/shard_map/ppermute | solution.py:446

commit v15 on v14

--- a/solution.py
+++ b/solution.py
@@ -84,9 +84,10 @@
         held[:, :inside] = rest[...]
         held[:, inside:] = halo[...]
     else:
-        fetch(taper, taper_v)
         for start, stop in ((0, (half + 2) * HOP), ((half + 2) * HOP, inside)):
             fetch(rec.at[:, pl.ds(start, stop - start)], held.at[:, pl.ds(start, stop - start)])
+            if not start:
+                fetch(taper, taper_v)
     ready = len(copies)
     if not late:
         rows = FOLD // 4

time: 37.5 us -> 37.5 us (level)
  no operation moved by 1% of the time
where the time goes in v15:
time: 37.5 us; the launch traced here: 37.3 us
  starting transfers between devices  15.4 us (41%)
  Pallas kernels  13.5 us (36%)
  waiting for transfers between devices  7.49 us (20%)
  other arithmetic  0.75 us (2%)
    ppermute x6, starting transfers between devices, trade(): return lax.ppermute(array, 'fibre', [(i, i ^ by) for i in range(n_fibre)])  9.64 us
    pallas_call x6, Pallas kernels, cross_call(): pl.pallas_call(functools.partial(cross_kernel, runs, kept, [len(some) for...  8.23 us
    pallas_call x2, Pallas kernels, spectra_call(): pl.pallas_call(functools.partial(spectra_kernel, first, count, late is no...  5.25 us
    ppermute x3, starting transfers between devices, body(): mine = lax.ppermute(mine.astype(jnp.bfloat16), ('fibre', 'tm'), routes)  3.57 us
    ppermute x6, waiting for transfers between devices, trade(): return lax.ppermute(array, 'fibre', [(i, i ^ by) for i in range(n_fibre)])  3.05 us
    ppermute x3, waiting for transfers between devices, body(): mine = lax.ppermute(mine.astype(jnp.bfloat16), ('fibre', 'tm'), routes)  2.42 us
    ppermute x1, starting transfers between devices, body(): halo = lax.ppermute(edge, 'tm', [(i, i - 1) for i in range(1, n_tm)])  1.28 us
    ppermute x1, waiting for transfers between devices, body(): halo = lax.ppermute(edge, 'tm', [(i, i - 1) for i in range(1, n_tm)])  1.04 us
  transfers between devices with their start and end apart: 11, of which 7 were waited for; matrix products, arithmetic and copies ran while one was open for 0% of the time, Pallas kernels for 21%

profile of v15, /device:TPU:0, one launch (start us, length us, event | category | flops | bytes accessed | tf_op | source)
XLA Modules:
  0.0 37.3 jit_solution(6169248913796476148)
XLA Ops:
  0.0 3.7 %spectra.2 = (bf16[384,768]{1,0:T(8,128)(2,1)S(1)}, bf16[64,768]{1,0:T(8,128)(2,1)S(1)}, bf16[112,768]{1,0:T(8,128)(2,1)S(1)}, bf16[16,2048]{1,0:T(8,128)(2,1)S(...) custom-call(s32[32]{0:T(128)} %refs_0_.1, ...), custom_call_target="tpu_custom_call" | custom-call | flops 43000000 | bytes 1048576 | tf_op jit(solution)/shard_map/spectra/pallas_call | solution.py:188
  3.8 3.0 %collective-permute-start.4 = (bf16[384,768]{1,0:T(8,128)(2,1)S(1)}, bf16[384,768]{1,0:T(8,128)(2,1)S(1)}, u32[]{:S(2)}, u32[]{:S(2)}) collective-permute-start(bf16[384,768]{1,0:T(8,128)(2,1)S(1)} %get-tuple-element.31.refs_1_.refs_2_.refs_3_), channel_id=1, source_target_pairs={{0,4},{4,0},{8,12},{12,8},{16,20},{20,16},{24,28},{28,24},{1,5},{5... | collective-permute-start | bytes 1769480 | tf_op jit(solution)/shard_map/ppermute | solution.py:377
  6.8 2.6 %collective-permute-start = (bf16[112,768]{1,0:T(8,128)(2,1)S(1)}, bf16[112,768]{1,0:T(8,128)(2,1)S(1)}, u32[]{:S(2)}, u32[]{:S(2)}) collective-permute-start(bf16[112,768]{1,0:T(8,128)(2,1)S(1)} %get-tuple-element.22.refs_8_), channel_id=1, source_target_pairs={{0,16},{4,20},{8,24},{12,28},{16,0},{20,4},{24,8},{28,12},{1,17},{... | collective-permute-start | bytes 516104 | tf_op jit(solution)/shard_map/ppermute | solution.py:377
  9.3 1.3 %collective-permute-start.1 = (bf16[16,2048]{1,0:T(8,128)(2,1)S(1)}, bf16[16,2048]{1,0:T(8,128)(2,1)S(1)}, u32[]{:S(2)}, u32[]{:S(2)}) collective-permute-start(bf16[16,2048]{1,0:T(8,128)(2,1)S(1)} %get-tuple-element.26), channel_id=1, source_target_pairs={{1,0},{2,1},{3,2},{5,4},{6,5},{7,6},{9,8},{10,9},{11,10},{13,12},{... | collective-permute-start | bytes 196616 | tf_op jit(solution)/shard_map/ppermute | solution.py:383
  10.6 0.8 %cross.6.refs_9_.refs_4_ = f32[64,768]{1,0:T(8,128)S(1)} custom-call(bf16[1,112,768]{2,1,0:T(8,128)(2,1)S(1)} %bitcast.51, bf16[384,768]{1,0:T(8,128)(2,1)S(1)} %get-tuple-element.31.refs_1_.refs_2_.refs_3_, bf16[64,768]{1,0:T(8,128)(2,1)S(1)} %get-tuple-element.30.refs_2_.refs_7_), custom_call_target="tpu_custom_call" | custom-call | flops 25920000 | bytes 1048576 | tf_op jit(solution)/shard_map/cross/pallas_call | solution.py:322
  11.4 0.0 copy-start
  11.4 1.0 %collective-permute-done.1.refs_3_ = bf16[16,2048]{1,0:T(8,128)(2,1)S(1)} collective-permute-done((bf16[16,2048]{1,0:T(8,128)(2,1)S(1)}, bf16[16,2048]{1,0:T(8,128)(2,1)S(1)}, u32[]{:S(2)}, u32[]{:S(2)}) %collective-permute-start.1) | collective-permute-done | bytes 65568 | tf_op jit(solution)/shard_map/ppermute | solution.py:383
  12.5 1.5 %spectra.3 = (bf16[128,768]{1,0:T(8,128)(2,1)S(1)}, bf16[16,768]{1,0:T(8,128)(2,1)S(1)}, bf16[128,768]{1,0:T(8,128)(2,1)S(1)}) custom-call(s32[32]{0:T(128)S(1)} %get-tuple-element.23.refs_0_, s32[4]{0:T(128)S(1)} %get-tuple-element.24.refs_1_, bf16[16,4096]{1,0:T(8,128)(2,1)S(1)} %get-tuple-element.25.refs_2_, ...), custom_call_target="tpu_custom_call" | custom-call | flops 19000000 | bytes 1048576 | tf_op jit(solution)/shard_map/spectra/pallas_call | solution.py:188
  14.0 0.4 %collective-permute-start.2 = (bf16[16,768]{1,0:T(8,128)(2,1)S(1)}, bf16[16,768]{1,0:T(8,128)(2,1)S(1)}, u32[]{:S(2)}, u32[]{:S(2)}) collective-permute-start(bf16[16,768]{1,0:T(8,128)(2,1)S(1)} %get-tuple-element.32), channel_id=1, source_target_pairs={{0,16},{4,20},{8,24},{12,28},{16,0},{20,4},{24,8},{28,12},{1,17},{... | collective-permute-start | bytes 73736 | tf_op jit(solution)/shard_map/ppermute | solution.py:377
  14.4 1.6 %collective-permute-start.6 = (bf16[128,768]{1,0:T(8,128)(2,1)S(1)}, bf16[128,768]{1,0:T(8,128)(2,1)S(1)}, u32[]{:S(2)}, u32[]{:S(2)}) collective-permute-start(bf16[128,768]{1,0:T(8,128)(2,1)S(1)} %get-tuple-element.34), channel_id=1, source_target_pairs={{0,8},{4,12},{8,0},{12,4},{16,24},{20,28},{24,16},{28,20},{1,9},{5... | collective-permute-start | bytes 589832 | tf_op jit(solution)/shard_map/ppermute | solution.py:377
  16.0 0.5 %collective-permute-start.5 = (bf16[128,768]{1,0:T(8,128)(2,1)S(1)}, bf16[128,768]{1,0:T(8,128)(2,1)S(1)}, u32[]{:S(2)}, u32[]{:S(2)}) collective-permute-start(bf16[128,768]{1,0:T(8,128)(2,1)S(1)} %get-tuple-element.33.refs_3_.refs_2_.refs_4_), channel_id=1, source_target_pairs={{0,4},{4,0},{8,12},{12,8},{16,20},{20,16},{24,28},{28,24},{1,5},{5... | collective-permute-start | bytes 589832 | tf_op jit(solution)/shard_map/ppermute | solution.py:377
  16.5 2.4 %collective-permute-done.2.refs_1_ = bf16[16,768]{1,0:T(8,128)(2,1)S(1)} collective-permute-done((bf16[16,768]{1,0:T(8,128)(2,1)S(1)}, bf16[16,768]{1,0:T(8,128)(2,1)S(1)}, u32[]{:S(2)}, u32[]{:S(2)}) %collective-permute-start.2) | collective-permute-done | bytes 24608 | tf_op jit(solution)/shard_map/ppermute | solution.py:377
  18.9 0.0 collective-permute-done.refs_0_
  18.9 1.5 %collective-permute-start.3 = (bf16[128,768]{1,0:T(8,128)(2,1)S(1)}, bf16[128,768]{1,0:T(8,128)(2,1)S(1)}, u32[]{:S(2)}, u32[]{:S(2)}) collective-permute-start(bf16[128,768]{1,0:T(8,128)(2,1)S(1)} %join.1), channel_id=1, source_target_pairs={{0,8},{4,12},{8,0},{12,4},{16,24},{20,28},{24,16},{28,20},{1,9},{5... | collective-permute-start | bytes 589832 | tf_op jit(solution)/shard_map/ppermute | solution.py:377
  20.4 0.0 copy-done
  20.4 1.3 %cross.7 = (bf16[64,256]{1,0:T(8,128)(2,1)S(1)}, bf16[64,256]{1,0:T(8,128)(2,1)S(1)}) custom-call(bf16[1,128,768]{2,1,0:T(8,128)(2,1)S(1)} %bitcast.45, bf16[1,128,768]{2,1,0:T(8,128)(2,1)S(1)} %bitcast.42, bf16[384,768]{1,0:T(8,128)(2,1)S(1)} %get-tuple-element.31.refs_1_.refs_2_.refs_3_, bf16[128,768]{1,0:T(8,128)(2,1)S(1)} %get-tuple-element.33.refs_3_.refs_2_.refs_4_, ...), custom_call_target="tpu_custom_call" | custom-call | flops 31040000 | bytes 1048576 | tf_op jit(solution)/shard_map/cross/pallas_call | solution.py:322
  21.8 0.0 collective-permute-done.6
  21.8 1.1 %cross.8.refs_7_ = bf16[64,256]{1,0:T(8,128)(2,1)S(1)} custom-call(bf16[1,128,768]{2,1,0:T(8,128)(2,1)S(1)} %bitcast.48, bf16[384,768]{1,0:T(8,128)(2,1)S(1)} %get-tuple-element.31.refs_1_.refs_2_.refs_3_, bf16[128,768]{1,0:T(8,128)(2,1)S(1)} %get-tuple-element.33.refs_3_.refs_2_.refs_4_, bf16[768,256]{1,0:T(8,128)(2,1)S(1)} %copy-done, ...), custom_call_target="tpu_custom_call" | custom-call | flops 28480000 | bytes 1048576 | tf_op jit(solution)/shard_map/cross/pallas_call | solution.py:322
  22.9 0.0 collective-permute-done.4.refs_5_.refs_3_
  22.9 2.0 %cross.9.refs_7_ = f32[192,768]{1,0:T(8,128)S(1)} custom-call(bf16[1,128,768]{2,1,0:T(8,128)(2,1)S(1)} %bitcast.46, bf16[1,128,768]{2,1,0:T(8,128)(2,1)S(1)} %bitcast.49, bf16[1,128,768]{2,1,0:T(8,128)(2,1)S(1)} %bitcast.43, bf16[384,768]{1,0:T(8,128)(2,1)S(1)} %get-tuple-element.31.refs_1_.refs_2_.refs_3_, ...), custom_call_target="tpu_custom_call" | custom-call | flops 54080000 | bytes 1048576 | tf_op jit(solution)/shard_map/cross/pallas_call | solution.py:322
  24.9 0.0 collective-permute-done.5.refs_6_.refs_4_
  24.9 1.0 %cross.10.refs_5_ = bf16[192,256]{1,0:T(8,128)(2,1)S(1)} custom-call(bf16[1,128,768]{2,1,0:T(8,128)(2,1)S(1)} %bitcast.47, bf16[1,128,768]{2,1,0:T(8,128)(2,1)S(1)} %bitcast.50, bf16[1,128,768]{2,1,0:T(8,128)(2,1)S(1)} %bitcast.44, bf16[384,768]{1,0:T(8,128)(2,1)S(1)} %get-tuple-element.31.refs_1_.refs_2_.refs_3_, ...), custom_call_target="tpu_custom_call" | custom-call | flops 23360000 | bytes 1048576 | tf_op jit(solution)/shard_map/cross/pallas_call | solution.py:322
  26.0 0.7 %collective-permute-done.3 = bf16[128,768]{1,0:T(8,128)(2,1)S(1)} collective-permute-done((bf16[128,768]{1,0:T(8,128)(2,1)S(1)}, bf16[128,768]{1,0:T(8,128)(2,1)S(1)}, u32[]{:S(2)}, u32[]{:S(2)}) %collective-permute-start.3) | collective-permute-done | bytes 196640 | tf_op jit(solution)/shard_map/ppermute | solution.py:377
  26.6 2.0 %cross.11 = (bf16[256,256]{1,0:T(8,128)(2,1)S(1)}, bf16[256,256]{1,0:T(8,128)(2,1)S(1)}) custom-call(bf16[1,128,768]{2,1,0:T(8,128)(2,1)S(1)} %bitcast.52, bf16[384,768]{1,0:T(8,128)(2,1)S(1)} %get-tuple-element.31.refs_1_.refs_2_.refs_3_, bf16[128,768]{1,0:T(8,128)(2,1)S(1)} %get-tuple-element.33.refs_3_.refs_2_.refs_4_, ...), custom_call_target="tpu_custom_call" | custom-call | flops 48960000 | bytes 1048576 | tf_op jit(solution)/shard_map/cross/pallas_call | solution.py:322
  28.7 0.9 %collective-permute-start.7 = (bf16[4,1,4,16,256]{4,3,2,1,0:T(8,128)(2,1)S(1)}, bf16[4,1,4,16,256]{4,3,2,1,0:T(8,128)(2,1)S(1)}, u32[]{:S(2)}, u32[]{:S(2)}) collective-permute-start(bf16[4,1,4,16,256]{4,3,2,1,0:T(8,128)(2,1)S(1)} %pad_maximum_fusion), channel_id=1, source_target_pairs={{0,1},{1,0},{2,3},{3,2},{4,5},{5,4},{6,7},{7,6},{8,9},{9,8},{10,11... | collective-permute-start | bytes 393224 | tf_op jit(solution)/shard_map/ppermute | solution.py:434
  29.6 1.0 %collective-permute-done.7 = bf16[4,1,4,16,256]{4,3,2,1,0:T(8,128)(2,1)S(1)} collective-permute-done((bf16[4,1,4,16,256]{4,3,2,1,0:T(8,128)(2,1)S(1)}, bf16[4,1,4,16,256]{4,3,2,1,0:T(8,128)(2,1)S(1)}, u32[]{:S(2)}, u32[]{:S(2)}) %collective-permute-start.7) | collective-permute-done | bytes 131104 | tf_op jit(solution)/shard_map/ppermute | solution.py:434
  30.7 1.8 %collective-permute-start.10 = (bf16[1,4,16,256]{3,2,1,0:T(8,128)(2,1)S(1)}, bf16[1,4,16,256]{3,2,1,0:T(8,128)(2,1)S(1)}, u32[]{:S(2)}, u32[]{:S(2)}) collective-permute-start(bf16[1,4,16,256]{3,2,1,0:T(8,128)(2,1)S(1)} %get-tuple-element.44), channel_id=1, source_target_pairs={{0,6},{1,7},{2,4},{3,5},{4,2},{5,3},{6,0},{7,1},{8,14},{9,15},{10,... | collective-permute-start | bytes 98312 | tf_op jit(solution)/shard_map/ppermute | solution.py:447
  32.4 0.3 collective-permute-start.8
  32.7 1.5 %collective-permute-start.9 = (bf16[1,4,16,256]{3,2,1,0:T(8,128)(2,1)S(1)}, bf16[1,4,16,256]{3,2,1,0:T(8,128)(2,1)S(1)}, u32[]{:S(2)}, u32[]{:S(2)}) collective-permute-start(bf16[1,4,16,256]{3,2,1,0:T(8,128)(2,1)S(1)} %get-tuple-element.45), channel_id=1, source_target_pairs={{0,4},{1,5},{2,6},{3,7},{4,0},{5,1},{6,2},{7,3},{8,12},{9,13},{10,... | collective-permute-start | bytes 98312 | tf_op jit(solution)/shard_map/ppermute | solution.py:447
  34.2 1.4 %collective-permute-done.10 = bf16[1,4,16,256]{3,2,1,0:T(8,128)(2,1)S(1)} collective-permute-done((bf16[1,4,16,256]{3,2,1,0:T(8,128)(2,1)S(1)}, bf16[1,4,16,256]{3,2,1,0:T(8,128)(2,1)S(1)}, u32[]{:S(2)}, u32[]{:S(2)}) %collective-permute-start.10) | collective-permute-done | bytes 32800 | tf_op jit(solution)/shard_map/ppermute | solution.py:447
  35.6 0.8 %collective-permute-done.8 = bf16[1,4,16,256]{3,2,1,0:T(8,128)(2,1)S(1)} collective-permute-done((bf16[1,4,16,256]{3,2,1,0:T(8,128)(2,1)S(1)}, bf16[1,4,16,256]{3,2,1,0:T(8,128)(2,1)S(1)}, u32[]{:S(2)}, u32[]{:S(2)}) %collective-permute-start.8) | collective-permute-done | bytes 32800 | tf_op jit(solution)/shard_map/ppermute | solution.py:447
  36.4 0.3 collective-permute-done.9
  36.7 0.7 %pad_maximum_fusion.1 = f32[1,2,4,16,256]{4,3,2,1,0:T(8,128)} fusion(f32[1,1,4,16,256]{4,3,2,1,0:T(8,128)S(1)} %get-tuple-element.40, f32[1,1,4,16,256]{4,3,2,1,0:T(8,128)S(1)} %get-tuple-element.39), kind=kLoop, calls=%fused_computation.2 | loop fusion | flops 32768 | bytes 262144 | tf_op jit(solution)/shard_map/stack | solution.py:453
  (6 shorter events, 0.1 us)
Async XLA Ops:
  3.8 19.2 %collective-permute-start.4 = (bf16[384,768]{1,0:T(8,128)(2,1)S(1)}, bf16[384,768]{1,0:T(8,128)(2,1)S(1)}, u32[]{:S(2)}, u32[]{:S(2)}) collective-permute-start(bf16[384,768]{1,0:T(8,128)(2,1)S(1)} %get-tuple-element.31.refs_1_.refs_2_.refs_3_), channel_id=1, source_target_pairs={{0,4},{4,0},{8,12},{12,8},{16,20},{20,16},{24,28},{28,24},{1,5},{5... | collective-permute-start | bytes 1769480 | tf_op jit(solution)/shard_map/ppermute | solution.py:377
  6.8 12.1 %collective-permute-start = (bf16[112,768]{1,0:T(8,128)(2,1)S(1)}, bf16[112,768]{1,0:T(8,128)(2,1)S(1)}, u32[]{:S(2)}, u32[]{:S(2)}) collective-permute-start(bf16[112,768]{1,0:T(8,128)(2,1)S(1)} %get-tuple-element.22.refs_8_), channel_id=1, source_target_pairs={{0,16},{4,20},{8,24},{12,28},{16,0},{20,4},{24,8},{28,12},{1,17},{... | collective-permute-start | bytes 516104 | tf_op jit(solution)/shard_map/ppermute | solution.py:377
  9.3 3.1 %collective-permute-start.1 = (bf16[16,2048]{1,0:T(8,128)(2,1)S(1)}, bf16[16,2048]{1,0:T(8,128)(2,1)S(1)}, u32[]{:S(2)}, u32[]{:S(2)}) collective-permute-start(bf16[16,2048]{1,0:T(8,128)(2,1)S(1)} %get-tuple-element.26), channel_id=1, source_target_pairs={{1,0},{2,1},{3,2},{5,4},{6,5},{7,6},{9,8},{10,9},{11,10},{13,12},{... | collective-permute-start | bytes 196616 | tf_op jit(solution)/shard_map/ppermute | solution.py:383
  11.4 9.0 %copy-start = (bf16[768,256]{1,0:T(8,128)(2,1)S(1)}, bf16[768,256]{1,0:T(8,128)(2,1)}, u32[]{:S(2)}) copy-start(bf16[768,256]{1,0:T(8,128)(2,1)} %constant.81.clone.refs_5_.refs_3_.refs_6_.refs_8_.refs_9_) | copy-start | bytes 1179652
  14.0 4.9 %collective-permute-start.2 = (bf16[16,768]{1,0:T(8,128)(2,1)S(1)}, bf16[16,768]{1,0:T(8,128)(2,1)S(1)}, u32[]{:S(2)}, u32[]{:S(2)}) collective-permute-start(bf16[16,768]{1,0:T(8,128)(2,1)S(1)} %get-tuple-element.32), channel_id=1, source_target_pairs={{0,16},{4,20},{8,24},{12,28},{16,0},{20,4},{24,8},{28,12},{1,17},{... | collective-permute-start | bytes 73736 | tf_op jit(solution)/shard_map/ppermute | solution.py:377
  14.4 7.4 %collective-permute-start.6 = (bf16[128,768]{1,0:T(8,128)(2,1)S(1)}, bf16[128,768]{1,0:T(8,128)(2,1)S(1)}, u32[]{:S(2)}, u32[]{:S(2)}) collective-permute-start(bf16[128,768]{1,0:T(8,128)(2,1)S(1)} %get-tuple-element.34), channel_id=1, source_target_pairs={{0,8},{4,12},{8,0},{12,4},{16,24},{20,28},{24,16},{28,20},{1,9},{5... | collective-permute-start | bytes 589832 | tf_op jit(solution)/shard_map/ppermute | solution.py:377
  16.0 8.9 %collective-permute-start.5 = (bf16[128,768]{1,0:T(8,128)(2,1)S(1)}, bf16[128,768]{1,0:T(8,128)(2,1)S(1)}, u32[]{:S(2)}, u32[]{:S(2)}) collective-permute-start(bf16[128,768]{1,0:T(8,128)(2,1)S(1)} %get-tuple-element.33.refs_3_.refs_2_.refs_4_), channel_id=1, source_target_pairs={{0,4},{4,0},{8,12},{12,8},{16,20},{20,16},{24,28},{28,24},{1,5},{5... | collective-permute-start | bytes 589832 | tf_op jit(solution)/shard_map/ppermute | solution.py:377
  18.9 7.7 %collective-permute-start.3 = (bf16[128,768]{1,0:T(8,128)(2,1)S(1)}, bf16[128,768]{1,0:T(8,128)(2,1)S(1)}, u32[]{:S(2)}, u32[]{:S(2)}) collective-permute-start(bf16[128,768]{1,0:T(8,128)(2,1)S(1)} %join.1), channel_id=1, source_target_pairs={{0,8},{4,12},{8,0},{12,4},{16,24},{20,28},{24,16},{28,20},{1,9},{5... | collective-permute-start | bytes 589832 | tf_op jit(solution)/shard_map/ppermute | solution.py:377
  28.7 1.9 %collective-permute-start.7 = (bf16[4,1,4,16,256]{4,3,2,1,0:T(8,128)(2,1)S(1)}, bf16[4,1,4,16,256]{4,3,2,1,0:T(8,128)(2,1)S(1)}, u32[]{:S(2)}, u32[]{:S(2)}) collective-permute-start(bf16[4,1,4,16,256]{4,3,2,1,0:T(8,128)(2,1)S(1)} %pad_maximum_fusion), channel_id=1, source_target_pairs={{0,1},{1,0},{2,3},{3,2},{4,5},{5,4},{6,7},{7,6},{8,9},{9,8},{10,11... | collective-permute-start | bytes 393224 | tf_op jit(solution)/shard_map/ppermute | solution.py:434
  30.7 4.9 %collective-permute-start.10 = (bf16[1,4,16,256]{3,2,1,0:T(8,128)(2,1)S(1)}, bf16[1,4,16,256]{3,2,1,0:T(8,128)(2,1)S(1)}, u32[]{:S(2)}, u32[]{:S(2)}) collective-permute-start(bf16[1,4,16,256]{3,2,1,0:T(8,128)(2,1)S(1)} %get-tuple-element.44), channel_id=1, source_target_pairs={{0,6},{1,7},{2,4},{3,5},{4,2},{5,3},{6,0},{7,1},{8,14},{9,15},{10,... | collective-permute-start | bytes 98312 | tf_op jit(solution)/shard_map/ppermute | solution.py:447
  32.4 3.9 %collective-permute-start.8 = (bf16[1,4,16,256]{3,2,1,0:T(8,128)(2,1)S(1)}, bf16[1,4,16,256]{3,2,1,0:T(8,128)(2,1)S(1)}, u32[]{:S(2)}, u32[]{:S(2)}) collective-permute-start(bf16[1,4,16,256]{3,2,1,0:T(8,128)(2,1)S(1)} %get-tuple-element.43), channel_id=1, source_target_pairs={{0,2},{1,3},{2,0},{3,1},{4,6},{5,7},{6,4},{7,5},{8,10},{9,11},{10,... | collective-permute-start | bytes 98312 | tf_op jit(solution)/shard_map/ppermute | solution.py:447
  32.7 3.9 %collective-permute-start.9 = (bf16[1,4,16,256]{3,2,1,0:T(8,128)(2,1)S(1)}, bf16[1,4,16,256]{3,2,1,0:T(8,128)(2,1)S(1)}, u32[]{:S(2)}, u32[]{:S(2)}) collective-permute-start(bf16[1,4,16,256]{3,2,1,0:T(8,128)(2,1)S(1)} %get-tuple-element.45), channel_id=1, source_target_pairs={{0,4},{1,5},{2,6},{3,7},{4,0},{5,1},{6,2},{7,3},{8,12},{9,13},{10,... | collective-permute-start | bytes 98312 | tf_op jit(solution)/shard_map/ppermute | solution.py:447
